TPU v7x, 32 devices: a whole 2x2x4 slice. The times are simulated.
32 devices in a mesh: rows: 8 (over y, x, core), batch: 4 (over z).
Axes of the slice: x: 2, y: 2, z: 4, core: 2. Of those that a mesh axis runs over, the one named last changes fastest.
Arguments:
- inputs: bfloat16 [8, 16, 128, 512], P('batch', 'rows'), may hold values from -12 to 12
- image_counts: int32 [4], replicated, may hold values from 1 to 2, as said below
- w_down: bfloat16 [3, 3, 512, 1024], replicated, may hold values from -0.09375 to 0.09375
- w_short: bfloat16 [1024, 512], replicated, may hold values from -0.1875 to 0.1875
- w_main: bfloat16 [1024, 512], replicated, may hold values from -0.1875 to 0.1875
- w_inner: bfloat16 [512, 512], replicated, may hold values from -0.25 to 0.25
- w_spatial: bfloat16 [3, 3, 512, 512], replicated, may hold values from -0.09375 to 0.09375
- w_trans: bfloat16 [512, 512], replicated, may hold values from -0.25 to 0.25
- w_unite: bfloat16 [1024, 1024], replicated, may hold values from -0.1875 to 0.1875
- gains_wide: float32 [2, 1024], replicated, may hold values from 0.25 to 1.75
- gains_narrow: float32 [5, 512], replicated, may hold values from 0.25 to 1.75
- shifts_wide: float32 [2, 1024], replicated, may hold values from -3 to 3
- shifts_narrow: float32 [5, 512], replicated, may hold values from -3 to 3
- grad_output: bfloat16 [8, 8, 64, 1024], P('batch', 'rows'), may hold values from -6 to 6
Outputs:
- output: bfloat16 [8, 8, 64, 1024], P('batch', 'rows')
- grad_inputs: float32 [8, 16, 128, 512], P('batch', 'rows')
- grad_w_down: float32 [3, 3, 512, 1024], P(None, None, None, 'rows')
- grad_w_short: float32 [1024, 512], P(None, 'rows')
- grad_w_main: float32 [1024, 512], P(None, 'rows')
- grad_w_inner: float32 [512, 512], P(None, 'rows')
- grad_w_spatial: float32 [3, 3, 512, 512], P(None, None, None, 'rows')
- grad_w_trans: float32 [512, 512], P(None, 'rows')
- grad_w_unite: float32 [1024, 1024], P(None, 'rows')
- grad_gains_wide: float32 [2, 1024], replicated
- grad_gains_narrow: float32 [5, 512], replicated
- grad_shifts_wide: float32 [2, 1024], replicated
- grad_shifts_narrow: float32 [5, 512], replicated
Inputs may be any that keep to these rules, and one draw needn't show every extreme that they name: `image_counts`: each batch group holds 1 to 2 images in its first slots; in every draw at least one group is full and one other holds a single image.
All inputs are finite; a program needn't handle non-finite values.
Results may differ from a plain program's by a relative error of at most 0.024.
Values may be sent and summed in bfloat16 or wider, within the bound.
No kernel may reach another device: no remote copies, remote signals or barrier semaphores. Data moves between devices by JAX's collectives and lax.ppermute only.
A program may use at most 192 MiB of HBM per device.

v0:
```python
import jax
import jax.numpy as jnp
from jax import lax
from jax.sharding import PartitionSpec as P

EPSILON = 1e-05
LAYOUT = ("NHWC", "HWIO", "NHWC")


def from_behind(value, axis, steps):
    count = lax.axis_size(axis)
    first, last = (max(0, -steps), min(count, count - steps))
    return lax.ppermute(value, axis, [(source, source + steps) for source in range(first, last)])


def padded(block, sides, width):
    for axis, dim in sides:
        count = lax.axis_size(axis)
        forward = [(i, i + 1) for i in range(count - 1)]
        backward = [(target, source) for source, target in forward]
        low = lax.ppermute(
            lax.slice_in_dim(block, block.shape[dim] - width, None, axis=dim), axis, forward
        )
        high = lax.ppermute(lax.slice_in_dim(block, 0, width, axis=dim), axis, backward)
        block = jnp.concatenate([low, block, high], axis=dim)
    return block


def mish_act(values):
    return values * jnp.tanh(jax.nn.softplus(values))


def normalize(pre_norm, weights, pixels, gain, offset):
    totals = lax.psum(jnp.sum(pre_norm * weights, axis=(0, 1, 2)), ("rows", "batch"))
    centered = pre_norm - totals / pixels
    squares = lax.psum(jnp.sum(centered * centered * weights, axis=(0, 1, 2)), ("rows", "batch"))
    scaled = lax.rsqrt(squares / pixels + EPSILON)
    unit_map = centered * scaled
    shifted = unit_map * gain + offset
    return (mish_act(shifted), (unit_map, shifted, scaled))


def local_terms(grad_act, saved):
    unit_map, shifted, scaled = saved
    grad_pre = jax.vjp(mish_act, shifted)[1](grad_act)[0]
    return (
        grad_pre,
        jnp.sum(grad_pre, axis=(0, 1, 2)),
        jnp.sum(grad_pre * unit_map, axis=(0, 1, 2)),
    )


def finish(grad_pre, saved, gain, weights, pixels, grad_shift, grad_gain):
    unit_map, shifted, scaled = saved
    return (
        weights * (gain * scaled) * (grad_pre - (grad_shift + unit_map * grad_gain) / pixels)
    ).astype(jnp.bfloat16)


def norm_back(grad_act, saved, gain, weights, pixels):
    grad_pre, sum_first, sum_second = local_terms(grad_act, saved)
    grad_shift, grad_gain = lax.psum((sum_first, sum_second), ("rows", "batch"))
    return (
        finish(grad_pre, saved, gain, weights, pixels, grad_shift, grad_gain),
        grad_gain,
        grad_shift,
    )


def project(values, matrix):
    return jnp.einsum("bhwc,cd->bhwd", values, matrix, preferred_element_type=jnp.float32)


def project_back(grad_pre, matrix):
    return jnp.einsum("bhwd,cd->bhwc", grad_pre, matrix, preferred_element_type=jnp.float32)


def outer_sum(values, grad_pre):
    return jnp.einsum("bhwc,bhwd->cd", values, grad_pre, preferred_element_type=jnp.float32)


def flipped(kernel):
    return jnp.swapaxes(jnp.flip(kernel, (0, 1)), 2, 3)


def tap_grads(source, grad_pre, stride):
    images, height, columns, _ = grad_pre.shape
    tap_list = []
    for row_tap in range(3):
        for col_tap in range(3):
            window = lax.slice(
                source,
                (0, row_tap, col_tap, 0),
                (
                    images,
                    row_tap + stride * (height - 1) + 1,
                    col_tap + stride * (columns - 1) + 1,
                    source.shape[3],
                ),
                (1, stride, stride, 1),
            )
            tap_list.append(outer_sum(window, grad_pre))
    return jnp.concatenate(tap_list, axis=0)


def record(store, label, grad_flat):
    store[label] = grad_flat


def on_device(
    inputs,
    image_counts,
    w_down,
    w_short,
    w_main,
    w_inner,
    w_spatial,
    w_trans,
    w_unite,
    gains_wide,
    gains_narrow,
    shifts_wide,
    shifts_narrow,
    grad_output,
):
    half = w_short.shape[1]
    own_group = lax.axis_index("batch")
    groups = image_counts.shape[0]
    own_count = jnp.sum(
        jnp.where(jnp.arange(groups, dtype=jnp.int32) == own_group, image_counts, 0)
    )
    per_group = inputs.shape[0]
    weights = (
        (jnp.arange(per_group, dtype=jnp.int32) < own_count)
        .astype(jnp.float32)
        .reshape(-1, 1, 1, 1)
    )
    pixels = jnp.sum(image_counts).astype(jnp.float32) * (
        grad_output.shape[1] * lax.axis_size("rows") * grad_output.shape[2]
    )
    borrowed = from_behind(inputs[:, -1:], "rows", 1)
    down_source = jnp.pad(
        jnp.concatenate([borrowed, inputs], axis=1), ((0, 0), (0, 0), (1, 0), (0, 0))
    )
    down_pre = lax.conv_general_dilated(
        down_source,
        w_down,
        (2, 2),
        ((0, 0), (0, 0)),
        dimension_numbers=LAYOUT,
        preferred_element_type=jnp.float32,
    )
    sectioned, down_saved = normalize(down_pre, weights, pixels, gains_wide[0], shifts_wide[0])
    sectioned = sectioned.astype(jnp.bfloat16)
    split_pre = jnp.concatenate([project(sectioned, w_short), project(sectioned, w_main)], axis=3)
    split_act, split_saved = normalize(
        split_pre,
        weights,
        pixels,
        jnp.concatenate([gains_narrow[0], gains_narrow[1]]),
        jnp.concatenate([shifts_narrow[0], shifts_narrow[1]]),
    )
    split_act = split_act.astype(jnp.bfloat16)
    shortcut = split_act[..., :half]
    mainline = split_act[..., half:]
    short_saved = (split_saved[0][..., :half], split_saved[1][..., :half], split_saved[2][:half])
    main_saved = (split_saved[0][..., half:], split_saved[1][..., half:], split_saved[2][half:])
    inner_act, inner_saved = normalize(
        project(mainline, w_inner), weights, pixels, gains_narrow[2], shifts_narrow[2]
    )
    inner_act = inner_act.astype(jnp.bfloat16)
    inner_rim = padded(inner_act, (("rows", 1),), 1)
    spatial_source = jnp.pad(inner_rim, ((0, 0), (0, 0), (1, 1), (0, 0)))
    spatial_pre = lax.conv_general_dilated(
        spatial_source,
        w_spatial,
        (1, 1),
        ((0, 0), (0, 0)),
        dimension_numbers=LAYOUT,
        preferred_element_type=jnp.float32,
    )
    branch, spatial_saved = normalize(
        spatial_pre, weights, pixels, gains_narrow[3], shifts_narrow[3]
    )
    merged = (mainline.astype(jnp.float32) + branch).astype(jnp.bfloat16)
    transition, trans_saved = normalize(
        project(merged, w_trans), weights, pixels, gains_narrow[4], shifts_narrow[4]
    )
    transition = transition.astype(jnp.bfloat16)
    joined = jnp.concatenate([shortcut, transition], axis=3)
    united, unite_saved = normalize(
        project(joined, w_unite), weights, pixels, gains_wide[1], shifts_wide[1]
    )
    output = (united * weights).astype(jnp.bfloat16)
    store = {}
    grad_unite_pre, gain_unite, shift_unite = norm_back(
        grad_output.astype(jnp.float32) * weights, unite_saved, gains_wide[1], weights, pixels
    )
    record(store, "unite", outer_sum(joined, grad_unite_pre))
    grad_joined = project_back(grad_unite_pre, w_unite)
    short_pre_grad, short_first, short_second = local_terms(grad_joined[..., :half], short_saved)
    shift_short, gain_short = lax.psum((short_first, short_second), ("rows", "batch"))
    grad_short_pre = finish(
        short_pre_grad, short_saved, gains_narrow[0], weights, pixels, shift_short, gain_short
    )
    record(store, "short", outer_sum(sectioned, grad_short_pre))
    grad_trans_pre, gain_trans, shift_trans = norm_back(
        grad_joined[..., half:], trans_saved, gains_narrow[4], weights, pixels
    )
    record(store, "trans", outer_sum(merged, grad_trans_pre))
    grad_merged = project_back(grad_trans_pre, w_trans)
    grad_spatial_pre, gain_spatial, shift_spatial = norm_back(
        grad_merged, spatial_saved, gains_narrow[3], weights, pixels
    )
    grad_rim = padded(grad_spatial_pre, (("rows", 1),), 1)
    grad_inner_act = lax.conv_general_dilated(
        grad_rim,
        flipped(w_spatial),
        (1, 1),
        ((0, 0), (1, 1)),
        dimension_numbers=LAYOUT,
        preferred_element_type=jnp.float32,
    )
    record(store, "spatial", tap_grads(spatial_source, grad_spatial_pre, 1))
    grad_inner_pre, gain_inner, shift_inner = norm_back(
        grad_inner_act, inner_saved, gains_narrow[2], weights, pixels
    )
    record(store, "inner", outer_sum(mainline, grad_inner_pre))
    grad_mainline = grad_merged + project_back(grad_inner_pre, w_inner)
    main_pre_grad, main_first, main_second = local_terms(grad_mainline, main_saved)
    shift_main, gain_main = lax.psum((main_first, main_second), ("rows", "batch"))
    grad_main_pre = finish(
        main_pre_grad, main_saved, gains_narrow[1], weights, pixels, shift_main, gain_main
    )
    record(store, "main", outer_sum(sectioned, grad_main_pre))
    grad_sectioned = project_back(grad_short_pre, w_short) + project_back(grad_main_pre, w_main)
    grad_down_pre, gain_down, shift_down = norm_back(
        grad_sectioned, down_saved, gains_wide[0], weights, pixels
    )
    record(store, "down", tap_grads(down_source, grad_down_pre, 2))
    widened = lax.conv_general_dilated(
        grad_down_pre,
        flipped(w_down),
        (1, 1),
        ((2, 2), (2, 2)),
        lhs_dilation=(2, 2),
        dimension_numbers=LAYOUT,
        preferred_element_type=jnp.float32,
    )
    returned = from_behind(widened[:, :1, 1:].astype(jnp.bfloat16), "rows", -1).astype(jnp.float32)
    grad_inputs = widened[:, 1:, 1:] + jnp.pad(
        returned, ((0, 0), (widened.shape[1] - 2, 0), (0, 0), (0, 0))
    )
    row_shares = (
        lax.psum_scatter(
            store["down"].astype(jnp.bfloat16), "rows", scatter_dimension=1, tiled=True
        ).astype(jnp.float32),
        lax.psum_scatter(
            store["short"].astype(jnp.bfloat16), "rows", scatter_dimension=1, tiled=True
        ).astype(jnp.float32),
        lax.psum_scatter(
            store["main"].astype(jnp.bfloat16), "rows", scatter_dimension=1, tiled=True
        ).astype(jnp.float32),
        lax.psum_scatter(
            store["inner"].astype(jnp.bfloat16), "rows", scatter_dimension=1, tiled=True
        ).astype(jnp.float32),
        lax.psum_scatter(
            store["spatial"].astype(jnp.bfloat16), "rows", scatter_dimension=1, tiled=True
        ).astype(jnp.float32),
        lax.psum_scatter(
            store["trans"].astype(jnp.bfloat16), "rows", scatter_dimension=1, tiled=True
        ).astype(jnp.float32),
        lax.psum_scatter(
            store["unite"].astype(jnp.bfloat16), "rows", scatter_dimension=1, tiled=True
        ).astype(jnp.float32),
    )
    settled = (
        lax.psum(row_shares[0].astype(jnp.bfloat16), "batch").astype(jnp.float32),
        lax.psum(row_shares[1].astype(jnp.bfloat16), "batch").astype(jnp.float32),
        lax.psum(row_shares[2].astype(jnp.bfloat16), "batch").astype(jnp.float32),
        lax.psum(row_shares[3].astype(jnp.bfloat16), "batch").astype(jnp.float32),
        lax.psum(row_shares[4].astype(jnp.bfloat16), "batch").astype(jnp.float32),
        lax.psum(row_shares[5].astype(jnp.bfloat16), "batch").astype(jnp.float32),
        lax.psum(row_shares[6].astype(jnp.bfloat16), "batch").astype(jnp.float32),
    )
    grad_w_down = settled[0].reshape(3, 3, half, -1)
    grad_w_spatial = settled[4].reshape(3, 3, half, -1)
    grad_gains_wide = jnp.stack([gain_down, gain_unite])
    grad_gains_narrow = jnp.stack([gain_short, gain_main, gain_inner, gain_spatial, gain_trans])
    grad_shifts_wide = jnp.stack([shift_down, shift_unite])
    grad_shifts_narrow = jnp.stack(
        [shift_short, shift_main, shift_inner, shift_spatial, shift_trans]
    )
    return (
        output,
        grad_inputs,
        grad_w_down,
        settled[1],
        settled[2],
        settled[3],
        grad_w_spatial,
        settled[5],
        settled[6],
        grad_gains_wide,
        grad_gains_narrow,
        grad_shifts_wide,
        grad_shifts_narrow,
    )


def solution(mesh):
    placed = (
        P("batch", "rows", None, None),
        P(),
        P(),
        P(),
        P(),
        P(),
        P(),
        P(),
        P(),
        P(),
        P(),
        P(),
        P(),
        P("batch", "rows", None, None),
    )
    return jax.shard_map(
        on_device,
        mesh=mesh,
        in_specs=placed,
        out_specs=(
            P("batch", "rows", None, None),
            P("batch", "rows", None, None),
            P(None, None, None, "rows"),
            P(None, "rows"),
            P(None, "rows"),
            P(None, "rows"),
            P(None, None, None, "rows"),
            P(None, "rows"),
            P(None, "rows"),
            P(),
            P(),
            P(),
            P(),
        ),
        check_vma=False,
    )
```

profile of v0, /device:TPU:0, one launch (start us, length us, event | category | flops | bytes accessed | tf_op | source)
XLA Modules:
  0.0 1241.9 jit_solution(9995371178752502694)
XLA Ops:
  8.4 2.4 collective-permute-start
  11.6 1.5 fusion.245
  13.1 1.5 fusion.246
  23.4 6.2 select_reduce_fusion.1
  29.6 41.5 %psum.231 = f32[1024]{0:T(1024)S(1)} all-reduce(f32[1024]{0:T(1024)S(1)} %get-tuple-element.168), channel_id=1, replica_groups=mesh['rows'=8,'batch'=4] {'rows','batch'}, use_global_device_ids=true, to_apply=%region_2.3 | all-reduce | flops 1024 | bytes 8192 | tf_op jit(solution)/shard_map/psum | solution.py:34
  72.4 40.2 %psum.232 = f32[1024]{0:T(1024)S(1)} all-reduce(f32[1024]{0:T(1024)S(1)} %select_reduce_fusion), channel_id=1, replica_groups=mesh['rows'=8,'batch'=4] {'rows','batch'}, use_global_device_ids=true, to_apply=%region_5.6 | all-reduce | flops 1024 | bytes 8192 | tf_op jit(solution)/shard_map/psum | solution.py:36
  113.2 2.5 fusion.50
  116.0 1.6 convolution_bitcast_fusion.11
  117.7 1.5 convolution_bitcast_fusion.12
  119.3 39.8 %psum.233 = f32[1024]{0:T(1024)S(1)} all-reduce(f32[1024]{0:T(1024)S(1)} %multiply_reduce_fusion.3), channel_id=1, replica_groups=mesh['rows'=8,'batch'=4] {'rows','batch'}, use_global_device_ids=true, to_apply=%region_7.8 | all-reduce | flops 1024 | bytes 8192 | tf_op jit(solution)/shard_map/psum | solution.py:34
  159.4 40.4 %psum.234 = f32[1024]{0:T(1024)S(1)} all-reduce(f32[1024]{0:T(1024)S(1)} %multiply_reduce_fusion.2), channel_id=1, replica_groups=mesh['rows'=8,'batch'=4] {'rows','batch'}, use_global_device_ids=true, to_apply=%region_9.10 | all-reduce | flops 1024 | bytes 8192 | tf_op jit(solution)/shard_map/psum | solution.py:36
  203.2 39.7 %psum.235 = f32[512]{0:T(512)S(1)} all-reduce(f32[512]{0:T(512)S(1)} %get-tuple-element.170), channel_id=1, replica_groups=mesh['rows'=8,'batch'=4] {'rows','batch'}, use_global_device_ids=true, to_apply=%region_11.12 | all-reduce | flops 512 | bytes 4096 | tf_op jit(solution)/shard_map/psum | solution.py:34
  242.9 40.4 %psum.236 = f32[512]{0:T(512)S(1)} all-reduce(f32[512]{0:T(512)S(1)} %multiply_reduce_fusion.8), channel_id=1, replica_groups=mesh['rows'=8,'batch'=4] {'rows','batch'}, use_global_device_ids=true, to_apply=%region_13.14 | all-reduce | flops 512 | bytes 4096 | tf_op jit(solution)/shard_map/psum | solution.py:36
  285.5 3.5 collective-permute-start.1
  292.5 3.9 select_reduce_fusion.3
  296.5 42.3 %psum.237 = f32[512]{0:T(512)S(1)} all-reduce(f32[512]{0:T(512)S(1)} %get-tuple-element.172), channel_id=1, replica_groups=mesh['rows'=8,'batch'=4] {'rows','batch'}, use_global_device_ids=true, to_apply=%region_15.16 | all-reduce | flops 512 | bytes 4096 | tf_op jit(solution)/shard_map/psum | solution.py:34
  339.9 41.4 %psum.238 = f32[512]{0:T(512)S(1)} all-reduce(f32[512]{0:T(512)S(1)} %select_reduce_fusion.2), channel_id=1, replica_groups=mesh['rows'=8,'batch'=4] {'rows','batch'}, use_global_device_ids=true, to_apply=%region_17.18 | all-reduce | flops 512 | bytes 4096 | tf_op jit(solution)/shard_map/psum | solution.py:36
  381.9 2.0 fusion.101
  385.6 38.7 %psum.239 = f32[512]{0:T(512)S(1)} all-reduce(f32[512]{0:T(512)S(1)} %get-tuple-element.174), channel_id=1, replica_groups=mesh['rows'=8,'batch'=4] {'rows','batch'}, use_global_device_ids=true, to_apply=%region_19.20 | all-reduce | flops 512 | bytes 4096 | tf_op jit(solution)/shard_map/psum | solution.py:34
  424.5 41.4 %psum.240 = f32[512]{0:T(512)S(1)} all-reduce(f32[512]{0:T(512)S(1)} %multiply_reduce_fusion.6), channel_id=1, replica_groups=mesh['rows'=8,'batch'=4] {'rows','batch'}, use_global_device_ids=true, to_apply=%region_21.22 | all-reduce | flops 512 | bytes 4096 | tf_op jit(solution)/shard_map/psum | solution.py:36
  468.7 2.0 multiply_reduce_fusion.1
  470.6 38.9 %psum.241 = f32[1024]{0:T(1024)} all-reduce(f32[1024]{0:T(1024)} %get-tuple-element.176), channel_id=1, replica_groups=mesh['rows'=8,'batch'=4] {'rows','batch'}, use_global_device_ids=true, to_apply=%region_23.24 | all-reduce | flops 1024 | bytes 8192 | tf_op jit(solution)/shard_map/psum | solution.py:34
  511.0 41.9 %psum.242 = f32[1024]{0:T(1024)} all-reduce(f32[1024]{0:T(1024)} %multiply_reduce_fusion), channel_id=1, replica_groups=mesh['rows'=8,'batch'=4] {'rows','batch'}, use_global_device_ids=true, to_apply=%region_25.26 | all-reduce | flops 1024 | bytes 8192 | tf_op jit(solution)/shard_map/psum | solution.py:36
  554.9 3.1 fusion.231
  558.0 39.4 %all-reduce.8 = (f32[1024]{0:T(1024)}, f32[1024]{0:T(1024)}) all-reduce(f32[1024]{0:T(1024)} %get-tuple-element.85, f32[1024]{0:T(1024)} %get-tuple-element.84), channel_id=1, replica_groups=mesh['rows'=8,'batch'=4] {'rows','batch'}, use_global_device_ids=true, to_apply=%region_29.31 | all-reduce | flops 2048 | bytes 16384 | tf_op jit(solution)/shard_map/psum | solution.py:62
  599.5 1.9 bitcast_convert_fusion
  603.5 2.3 fusion.233
  605.8 2.5 copy.120
  608.4 42.0 %all-reduce.7 = (f32[512]{0:T(512)S(1)}, f32[512]{0:T(512)S(1)}) all-reduce(f32[512]{0:T(512)} %get-tuple-element.93, f32[512]{0:T(512)} %get-tuple-element.92), channel_id=1, replica_groups=mesh['rows'=8,'batch'=4] {'rows','batch'}, use_global_device_ids=true, to_apply=%region_37.40 | all-reduce | flops 1024 | bytes 8192 | tf_op jit(solution)/shard_map/psum | solution.py:62
  652.3 2.4 fusion.132
  654.7 38.7 %all-reduce.6 = (f32[512]{0:T(512)S(1)}, f32[512]{0:T(512)S(1)}) all-reduce(f32[512]{0:T(512)S(1)} %get-tuple-element.91, f32[512]{0:T(512)S(1)} %get-tuple-element.90), channel_id=1, replica_groups=mesh['rows'=8,'batch'=4] {'rows','batch'}, use_global_device_ids=true, to_apply=%region_39.42 | all-reduce | flops 1024 | bytes 8192 | tf_op jit(solution)/shard_map/psum | solution.py:62
  704.2 6.7 copy.118
  712.4 3.2 collective-permute-start.3
  728.4 4.1 convolution_select_fusion.2
  733.1 41.6 %all-reduce.5 = (f32[512]{0:T(512)S(1)}, f32[512]{0:T(512)S(1)}) all-reduce(f32[512]{0:T(512)S(1)} %get-tuple-element.89, f32[512]{0:T(512)S(1)} %get-tuple-element.88), channel_id=1, replica_groups=mesh['rows'=8,'batch'=4] {'rows','batch'}, use_global_device_ids=true, to_apply=%region_45.48 | all-reduce | flops 1024 | bytes 8192 | tf_op jit(solution)/shard_map/psum | solution.py:62
  774.8 2.7 multiply_reduce_fusion.4
  777.5 38.8 %all-reduce.4 = (f32[512]{0:T(512)S(1)}, f32[512]{0:T(512)S(1)}, f32[512]{0:T(512)S(1)}, f32[512]{0:T(512)S(1)}) all-reduce(f32[512]{0:T(512)S(1)} %get-tuple-element.83, f32[512]{0:T(512)S(1)} %get-tuple-element.86, f32[512]{0:T(512)S(1)} %get-tuple-element.82, ...), channel_id=1, replica_groups=mesh['rows'=8,'batch'=4] {'rows','batch'}, use_global_device_ids=true, to_apply=%region_33.36 | all-reduce | flops 2048 | bytes 16384 | tf_op jit(solution)/shard_map/psum | solution.py:202
  817.9 2.5 fusion.76
  820.4 41.7 %all-reduce.3 = (f32[1024]{0:T(1024)S(1)}, f32[1024]{0:T(1024)S(1)}) all-reduce(f32[1024]{0:T(1024)S(1)} %get-tuple-element.81, f32[1024]{0:T(1024)S(1)} %get-tuple-element.80), channel_id=1, replica_groups=mesh['rows'=8,'batch'=4] {'rows','batch'}, use_global_device_ids=true, to_apply=%region_51.54 | all-reduce | flops 2048 | bytes 16384 | tf_op jit(solution)/shard_map/psum | solution.py:62
  867.3 1.5 fusion.7
  871.7 1.5 fusion.10
  873.2 1.5 fusion.11
  874.6 1.5 fusion.12
  876.1 12.7 %copy.116 = bf16[4608,1024]{0,1:T(8,128)(2,1)} copy(bf16[4608,1024]{1,0:T(8,128)(2,1)} %fusion.12) | data formatting | bytes 18874368
  892.3 1.5 bitcast_convert_fusion.1
  893.9 1.5 bitcast_convert_fusion.2
  895.4 1.8 copy.121
  897.2 1.7 copy.119
  900.3 64.8 %reduce-scatter.22.cloned.1.call-done = bf16[128,4608]{1,0:T(8,128)(2,1)} async-done(((bf16[1024,4608]{1,0:T(8,128)(2,1)}), bf16[128,4608]{1,0:T(8,128)(2,1)}) %reduce-scatter.22.cloned.1.call-update) | async-done | bytes 1179664
  965.1 2.4 copy.117
  967.4 34.7 %reduce-scatter.20.cloned.1.call-done = bf16[512,64]{0,1:T(8,128)(2,1)} async-done(((bf16[512,512]{0,1:T(8,128)(2,1)}), bf16[512,64]{0,1:T(8,128)(2,1)}) %reduce-scatter.20.cloned.1.call-update) | async-done | bytes 65552 | tf_op jit(solution)/shard_map/reduce_scatter | solution.py:270
  1002.1 38.0 %reduce-scatter.18.cloned.1.call-done = bf16[512,64]{0,1:T(8,128)(2,1)} async-done(((bf16[512,512]{0,1:T(8,128)(2,1)}), bf16[512,64]{0,1:T(8,128)(2,1)}) %reduce-scatter.18.cloned.1.call-update) | async-done | bytes 65552 | tf_op jit(solution)/shard_map/reduce_scatter | solution.py:264
  1040.1 39.1 %reduce-scatter.16.cloned.1.call-done = bf16[1024,64]{0,1:T(8,128)(2,1)} async-done(((bf16[1024,512]{0,1:T(8,128)(2,1)}), bf16[1024,64]{0,1:T(8,128)(2,1)}) %reduce-scatter.16.cloned.1.call-update) | async-done | bytes 131088 | tf_op jit(solution)/shard_map/reduce_scatter | solution.py:261
  1079.2 39.8 %reduce-scatter.14.cloned.1.call-done = bf16[1024,64]{0,1:T(8,128)(2,1)} async-done(((bf16[1024,512]{0,1:T(8,128)(2,1)}), bf16[1024,64]{0,1:T(8,128)(2,1)}) %reduce-scatter.14.cloned.1.call-update) | async-done | bytes 131088 | tf_op jit(solution)/shard_map/reduce_scatter | solution.py:258
  1121.0 6.4 fusion.249
  1129.7 2.5 copy.111
  1136.1 1.6 slice_bitcast_fusion
  1139.0 83.5 %all-reduce.12.cloned.1.call-done = (bf16[3,3,512,128]{3,2,1,0:T(8,128)(2,1)}, bf16[1024,64]{0,1:T(8,128)(2,1)}, bf16[1024,64]{0,1:T(8,128)(2,1)}, bf16[512,64]{...) async-done(((bf16[3,3,512,128]{3,2,1,0:T(8,128)(2,1)}, bf16[1024,64]{0,1:T(8,128)(2,1)}, ...) | async-done | bytes 2424848 | tf_op jit(solution)/shard_map/psum | solution.py:278
  1222.5 1.6 convert_element_type.152
  1224.0 1.5 convert_element_type.154
  1225.5 1.6 convert_element_type.148
  1227.2 1.6 convert_element_type.150
  1228.8 1.8 convert_element_type.156
  1230.6 2.9 reshape.716
  (267 shorter events, 88.2 us)
Async XLA Ops:
  7.2 461.5 %copy-start = (bf16[1024,1024]{1,0:T(8,128)(2,1)S(1)}, bf16[1024,1024]{1,0:T(8,128)(2,1)}, u32[]{:S(2)}) copy-start(bf16[1024,1024]{1,0:T(8,128)(2,1)} %param.24) | copy-start | bytes 6291460
  7.2 16.2 %copy-start.50 = (pred[16,9]{0,1:T(8,128)(4,1)S(1)}, pred[16,9]{0,1:T(8,128)(4,1)}, u32[]{:S(2)}) copy-start(pred[16,9]{0,1:T(8,128)(4,1)} %constant.64) | copy-start | bytes 436
  7.2 888.2 %reduce-scatter.26.cloned.1.call-start = ((), (), s32[]{:S(2)}) async-start(), calls=%async_computation.13 | async-start | bytes 2359296
  8.4 10.2 collective-permute-start
  13.1 270.9 %copy-start.44 = (f32[1,512]{1,0:T(1,128)}, f32[1,512]{1,0:T(1,128)S(1)}, u32[]{:S(2)}) copy-start(f32[1,512]{1,0:T(1,128)S(1)} %get-tuple-element.145) | copy-start | bytes 6148
  14.6 269.4 %copy-start.46 = (f32[1,512]{1,0:T(1,128)}, f32[1,512]{1,0:T(1,128)S(1)}, u32[]{:S(2)}) copy-start(f32[1,512]{1,0:T(1,128)S(1)} %get-tuple-element.150) | copy-start | bytes 6148
  116.0 174.7 %copy-start.2 = (bf16[1,2,72,1024]{3,2,1,0:T(8,128)(2,1)}, bf16[1,2,72,1024]{3,2,1,0:T(8,128)(2,1)S(1)}, u32[]{:S(2)}) copy-start(bf16[1,2,72,1024]{3,2,1,0:T(8,128)(2,1)S(1)} %reshape.739) | copy-start | bytes 884740
  242.8 53.6 %copy-start.36 = (f32[512]{0:T(512)}, f32[512]{0:T(512)S(1)}, u32[]{:S(2)}) copy-start(f32[512]{0:T(512)S(1)} %broadcast_divide_fusion.5) | copy-start | bytes 6148
  284.0 12.5 %copy-start.40 = (f32[512]{0:T(512)}, f32[512]{0:T(512)S(1)}, u32[]{:S(2)}) copy-start(f32[512]{0:T(512)S(1)} %get-tuple-element.121) | copy-start | bytes 6148
  284.2 5.4 collective-permute-start.2
  285.5 4.1 collective-permute-start.1
  291.6 92.6 %copy-start.8 = (bf16[2,1,64,1024]{3,2,0,1:T(8,128)(2,1)S(1)}, bf16[2,1,64,1024]{3,2,0,1:T(8,128)(2,1)}, u32[]{:S(2)}) copy-start(bf16[2,1,64,1024]{3,2,0,1:T(8,128)(2,1)} %copy-done.7) | copy-start | bytes 786436
  384.2 82.9 %copy-start.13 = (f32[1,2,64,512]{3,0,2,1:T(1,128)}, f32[1,2,64,512]{3,0,2,1:T(1,128)S(1)}, u32[]{:S(2)}) copy-start(f32[1,2,64,512]{3,0,2,1:T(1,128)S(1)} %slice.212) | copy-start | bytes 786436
  424.4 46.3 %copy-start.38 = (f32[512]{0:T(512)}, f32[512]{0:T(512)S(1)}, u32[]{:S(2)}) copy-start(f32[512]{0:T(512)S(1)} %broadcast_divide_fusion.3) | copy-start | bytes 6148
  467.1 85.8 %copy-start.42 = (f32[512]{0:T(512)}, f32[512]{0:T(512)S(1)}, u32[]{:S(2)}) copy-start(f32[512]{0:T(512)S(1)} %get-tuple-element.127) | copy-start | bytes 6148
  597.4 4.0 copy-start.19
  597.4 5.0 copy-start.10
  599.5 4.0 copy-start.18
  608.4 85.0 %copy-start.11 = (f32[1,16,9,512]{3,1,2,0:T(8,128)S(1)}, f32[1,16,9,512]{3,1,2,0:T(8,128)}, u32[]{:S(2)}) copy-start(f32[1,16,9,512]{3,1,2,0:T(8,128)} %get-tuple-element.134) | copy-start | bytes 884740
  608.4 86.6 %copy-start.26 = (bf16[2,1,64,512]{3,2,0,1:T(8,128)(2,1)S(1)}, bf16[2,1,64,512]{3,2,0,1:T(8,128)(2,1)}, u32[]{:S(2)}) copy-start(bf16[2,1,64,512]{3,2,0,1:T(8,128)(2,1)} %copy-done.25) | copy-start | bytes 393220
  608.4 288.8 %reduce-scatter.24.cloned.1.call-start = ((), (), s32[]{:S(2)}) async-start(), calls=%async_computation.12 | async-start | bytes 5308416
  650.5 47.9 %copy-start.52 = (f32[512]{0:T(512)}, f32[512]{0:T(512)S(1)}, u32[]{:S(2)}) copy-start(f32[512]{0:T(512)S(1)} %get-tuple-element.106) | copy-start | bytes 6148
  650.5 47.9 %copy-start.54 = (f32[512]{0:T(512)}, f32[512]{0:T(512)S(1)}, u32[]{:S(2)}) copy-start(f32[512]{0:T(512)S(1)} %get-tuple-element.107) | copy-start | bytes 6148
  651.3 47.1 %copy-start.37 = (f32[512]{0:T(512)S(1)}, f32[512]{0:T(512)}, u32[]{:S(2)}) copy-start(f32[512]{0:T(512)} %copy-done.36) | copy-start | bytes 6148
  651.3 47.1 %copy-start.41 = (f32[512]{0:T(512)S(1)}, f32[512]{0:T(512)}, u32[]{:S(2)}) copy-start(f32[512]{0:T(512)} %copy-done.40) | copy-start | bytes 6148
  651.3 47.1 %copy-start.45 = (f32[1,512]{1,0:T(1,128)S(1)}, f32[1,512]{1,0:T(1,128)}, u32[]{:S(2)}) copy-start(f32[1,512]{1,0:T(1,128)} %copy-done.44) | copy-start | bytes 6148
  651.3 47.1 %copy-start.47 = (f32[1,512]{1,0:T(1,128)S(1)}, f32[1,512]{1,0:T(1,128)}, u32[]{:S(2)}) copy-start(f32[1,512]{1,0:T(1,128)} %copy-done.46) | copy-start | bytes 6148
  652.3 41.1 %copy-start.21 = (bf16[2,1,64,512]{3,2,0,1:T(8,128)(2,1)}, bf16[2,1,64,512]{3,2,0,1:T(8,128)(2,1)S(1)}, u32[]{:S(2)}) copy-start(bf16[2,1,64,512]{3,2,0,1:T(8,128)(2,1)S(1)} %fusion.155) | copy-start | bytes 393220
  693.5 8.5 copy-start.24
  710.9 13.3 %copy-start.12 = (f32[1,16,9,1024]{3,1,2,0:T(8,128)S(1)}, f32[1,16,9,1024]{3,1,2,0:T(8,128)}, u32[]{:S(2)}) copy-start(f32[1,16,9,1024]{3,1,2,0:T(8,128)} %get-tuple-element.139) | copy-start | bytes 1769476
  710.9 14.7 %copy-start.4 = (f32[1,16,9,1024]{3,1,2,0:T(8,128)S(1)}, f32[1,16,9,1024]{3,1,2,0:T(8,128)}, u32[]{:S(2)}) copy-start(f32[1,16,9,1024]{3,1,2,0:T(8,128)} %get-tuple-element.140) | copy-start | bytes 1769476
  710.9 254.2 %reduce-scatter.22.cloned.1.call-start = ((), (), s32[]{:S(2)}) async-start(), calls=%async_computation.11 | async-start | bytes 10616832
  710.9 16.1 %collective-permute-start.4 = (bf16[2,1,64,512]{3,2,0,1:T(8,128)(2,1)S(1)}, bf16[2,1,64,512]{3,2,0,1:T(8,128)(2,1)S(1)}, u32[]{:S(2)}, u32[]{:S(2)}) collective-permute-start(bf16[2,1,64,512]{3,2,0,1:T(8,128)(2,1)S(1)} %fusion.130), channel_id=1, source_target_pairs={{4,0},{8,4},{12,8},{16,12},{20,16},{24,20},{28,24},{5,1},{9,5},{13... | collective-permute-start | bytes 393224 | tf_op jit(solution)/shard_map/ppermute | solution.py:24
  712.4 14.6 %collective-permute-start.3 = (bf16[2,1,64,512]{3,2,0,1:T(8,128)(2,1)S(1)}, bf16[2,1,64,512]{3,2,0,1:T(8,128)(2,1)S(1)}, u32[]{:S(2)}, u32[]{:S(2)}) collective-permute-start(bf16[2,1,64,512]{3,2,0,1:T(8,128)(2,1)S(1)} %fusion.130), channel_id=1, source_target_pairs={{0,4},{4,8},{8,12},{12,16},{16,20},{20,24},{24,28},{1,5},{5,9},{9,... | collective-permute-start | bytes 393224 | tf_op jit(solution)/shard_map/ppermute | solution.py:21
  720.2 8.2 copy-start.51
  728.4 46.5 %copy-start.15 = (f32[2,1,64,1024]{3,2,0,1:T(8,128)S(1)}, f32[2,1,64,1024]{3,2,0,1:T(8,128)}, u32[]{:S(2)}) copy-start(f32[2,1,64,1024]{3,2,0,1:T(8,128)} %get-tuple-element.137) | copy-start | bytes 1572868
  732.4 85.0 %copy-start.6 = (bf16[1024,512]{1,0:T(8,128)(2,1)S(1)}, bf16[1024,512]{1,0:T(8,128)(2,1)}, u32[]{:S(2)}) copy-start(bf16[1024,512]{1,0:T(8,128)(2,1)} %param.19) | copy-start | bytes 3145732
  817.4 45.4 %copy-start.43 = (f32[2,1024]{1,0:T(2,128)S(1)}, f32[2,1024]{1,0:T(2,128)}, u32[]{:S(2)}) copy-start(f32[2,1024]{1,0:T(2,128)} %get-tuple-element.161) | copy-start | bytes 24580
  817.9 45.1 %copy-start.35 = (bf16[2,1,64,512]{3,2,0,1:T(8,128)(2,1)S(1)}, bf16[2,1,64,512]{3,2,0,1:T(8,128)(2,1)}, u32[]{:S(2)}) copy-start(bf16[2,1,64,512]{3,2,0,1:T(8,128)(2,1)} %slice.176) | copy-start | bytes 393220
  817.9 46.5 %copy-start.34 = (bf16[2,1,64,512]{3,2,0,1:T(8,128)(2,1)S(1)}, bf16[2,1,64,512]{3,2,0,1:T(8,128)(2,1)}, u32[]{:S(2)}) copy-start(bf16[2,1,64,512]{3,2,0,1:T(8,128)(2,1)} %slice.177) | copy-start | bytes 393220
  820.4 45.5 %copy-start.33 = (bf16[2,1,64,512]{3,2,0,1:T(8,128)(2,1)S(1)}, bf16[2,1,64,512]{3,2,0,1:T(8,128)(2,1)}, u32[]{:S(2)}) copy-start(bf16[2,1,64,512]{3,2,0,1:T(8,128)(2,1)} %slice.178) | copy-start | bytes 393220
  862.1 5.2 copy-start.32
  862.8 6.1 copy-start.31
  862.8 7.4 copy-start.30
  863.0 8.7 copy-start.29
  864.5 8.7 copy-start.28
  865.9 8.7 copy-start.27
  888.8 1.0 copy-start.14
  888.8 1.1 copy-start.22
  888.8 3.5 copy-start.3
  888.9 113.3 %reduce-scatter.20.cloned.1.call-start = ((), (), s32[]{:S(2)}) async-start(), calls=%async_computation.10 | async-start | bytes 589824 | tf_op jit(solution)/shard_map/reduce_scatter | solution.py:270
  891.1 149.1 %reduce-scatter.18.cloned.1.call-start = ((), (), s32[]{:S(2)}) async-start(), calls=%async_computation.9 | async-start | bytes 589824 | tf_op jit(solution)/shard_map/reduce_scatter | solution.py:264
  892.3 186.9 %reduce-scatter.16.cloned.1.call-start = ((), (), s32[]{:S(2)}) async-start(), calls=%async_computation.8 | async-start | bytes 1179648 | tf_op jit(solution)/shard_map/reduce_scatter | solution.py:261
  893.8 225.2 %reduce-scatter.14.cloned.1.call-start = ((), (), s32[]{:S(2)}) async-start(), calls=%async_computation.7 | async-start | bytes 1179648 | tf_op jit(solution)/shard_map/reduce_scatter | solution.py:258
  895.3 223.7 %copy-start.39 = (f32[1,1024]{1,0:T(1,128)S(1)}, f32[1,1024]{1,0:T(1,128)}, u32[]{:S(2)}) copy-start(f32[1,1024]{1,0:T(1,128)} %get-tuple-element.158) | copy-start | bytes 12292
  895.3 327.1 %all-reduce.12.cloned.1.call-start = ((), (), s32[]{:S(2)}) async-start(), calls=%async_computation.14 | async-start | bytes 4849664 | tf_op jit(solution)/shard_map/psum | solution.py:278
  899.0 222.0 %copy-start.56 = (pred[16,18]{0,1:T(8,128)(4,1)S(1)}, pred[16,18]{0,1:T(8,128)(4,1)}, u32[]{:S(2)}) copy-start(pred[16,18]{0,1:T(8,128)(4,1)} %constant.70) | copy-start | bytes 868
  1128.3 5.4 copy-start.55
  1128.3 6.0 copy-start.53
  1128.3 6.6 copy-start.49
  1128.3 7.2 copy-start.48
  1128.4 9.4 collective-permute-start.5
  1137.8 96.8 %copy-start.1 = (bf16[1024,1024]{1,0:T(8,128)(2,1)S(1)}, bf16[1024,1024]{1,0:T(8,128)(2,1)}, u32[]{:S(2)}) copy-start(bf16[1024,1024]{1,0:T(8,128)(2,1)} %param.24) | copy-start | bytes 6291460
  1222.5 11.0 copy-start.20
  (7 other events, 5.3 us)
Sparse Core Ops, SparseCore 0:
  608.5 43.1 reduce-scatter.25
  711.0 55.7 reduce-scatter.23
  889.0 76.0 reduce-scatter.21
  968.0 34.1 reduce-scatter.19
  1005.9 34.1 reduce-scatter.17
  1043.1 35.9 reduce-scatter.15
  1082.9 36.0 reduce-scatter.13
  1122.5 99.9 all-reduce.11
where the time goes:
time: 1250 us; the launch traced here: 1240 us
  blocking collectives  729 us (58%)
  waiting for transfers between devices  300 us (24%)
  local copies, waits for them, and re-layouts  69.6 us (6%)
  matrix products  67.6 us (5%)
  other arithmetic  46.1 us (4%)
  between operations  16.2 us (1%)
  starting transfers between devices  13.5 us (1%)
    psum x6, blocking collectives, normalize(): lax.psum(jnp.sum(centered * centered * weights, axis=(0, 1, 2)), ('rows',...  246 us
    psum x6, blocking collectives, normalize(): lax.psum(jnp.sum(pre_norm * weights, axis=(0, 1, 2)), ('rows', 'batch'))  241 us
    psum x5, blocking collectives, norm_back(): grad_shift, grad_gain = lax.psum((sum_first, sum_second), ('rows', 'batch'))  203 us
    psum x1, waiting for transfers between devices, on_device(): lax.psum(row_shares[0].astype(jnp.bfloat16), 'batch').astype(jnp.float32)  83.5 us
    unnamed x11, waiting for transfers between devices  64.9 us
    reduce_scatter x1, waiting for transfers between devices, on_device(): lax.psum_scatter(store['short'].astype(jnp.bfloat16), 'rows', scatter_dim...  39.8 us
    reduce_scatter x1, waiting for transfers between devices, on_device(): lax.psum_scatter(store['main'].astype(jnp.bfloat16), 'rows', scatter_dime...  39.1 us
    psum x1, blocking collectives, on_device(): lax.psum((short_first, short_second), ('rows', 'batch'))  38.8 us
  transfers between devices with their start and end apart: 14, of which 6 were waited for; matrix products, arithmetic and copies ran while one was open for 9% of the time, Pallas kernels for 0%

commit v1 on v0

v1 whole, which is shorter than its diff:
```python
import jax
import jax.numpy as jnp
from jax import lax
from jax.sharding import PartitionSpec as P

EPSILON = 1e-05
LAYOUT = ("NHWC", "HWIO", "NHWC")
FAR = 20.0


def mish(values):
    grown = jnp.exp(jnp.minimum(values, FAR))
    wide = grown * (grown + 2.0)
    return values * (wide / (wide + 2.0))


def mish_slope(values):
    grown = jnp.exp(jnp.minimum(values, FAR))
    wide = grown * (grown + 2.0)
    share = 1.0 / (wide + 2.0)
    return wide * share + 4.0 * values * (grown * (grown + 1.0) * share) * share


def tree_sum(parts):
    while len(parts) > 1:
        parts = [parts[i] + parts[i + 1] for i in range(0, len(parts), 2)]
    return parts[0]


class Plane:
    def __init__(self):
        self.rows = lax.axis_size("rows")
        self.groups = lax.axis_size("batch")
        self.chips = self.rows // 2
        self.place = lax.axis_index("rows")
        self.core = self.place % 2
        self.chip = self.place // 2

    def swap(self, value):
        return lax.ppermute(value, "rows", [(i, i ^ 1) for i in range(self.rows)])

    def chip_hop(self, value, step):
        return lax.ppermute(value, "rows", [(i, i ^ (2 * step)) for i in range(self.rows)])

    def plane_hop(self, value, step):
        return lax.ppermute(value, "batch", [(i, i ^ step) for i in range(self.groups)])

    def by_core(self, mine, got):
        first = self.core == 0
        return jnp.where(first, mine, got), jnp.where(first, got, mine)

    def image_of(self, block):
        mine = lax.dynamic_index_in_dim(block, self.core, 0, keepdims=False)
        other = lax.dynamic_index_in_dim(block, 1 - self.core, 0, keepdims=False)
        piece = jnp.concatenate(self.by_core(mine, self.swap(other)), axis=0)
        height = piece.shape[0]
        image = jnp.zeros((self.chips * height,) + piece.shape[1:], piece.dtype)
        for step in range(self.chips):
            part = piece if step == 0 else self.chip_hop(piece, step)
            image = lax.dynamic_update_slice_in_dim(image, part, (self.chip ^ step) * height, 0)
        return image

    def rows_of(self, mine, other):
        return jnp.stack(self.by_core(mine, self.swap(other)), axis=0)

    def group_sum(self, value):
        value = value + self.swap(value)
        return tree_sum(
            [value] + [self.plane_hop(value, step) for step in range(1, self.groups)]
        )

    def group_moments(self, sums, count_here, count_pair, pixels):
        got = self.swap(sums)
        total = sums[0] + got[0]
        count_there = count_pair - count_here
        gap = sums[0] / jnp.maximum(count_here, 1.0) - got[0] / jnp.maximum(count_there, 1.0)
        spread = sums[1] + got[1] + gap * gap * (count_here * count_there / count_pair)
        pair = jnp.stack([total, spread, total * total / count_pair])
        pairs = [pair[:2]] + [self.plane_hop(pair[:2], step) for step in range(1, self.groups)]
        counts = [count_pair] + [
            self.counts[lax.axis_index("batch") ^ step] for step in range(1, self.groups)
        ]
        center = tree_sum([p[0] for p in pairs]) / pixels
        total = tree_sum(
            [p[1] + n * jnp.square(p[0] / n - center) for p, n in zip(pairs, counts)]
        )
        return center, lax.rsqrt(total / pixels + EPSILON)


def moments(pre, weight):
    cells = pre.shape[0]
    total = jnp.sum(pre, axis=0)
    centered = pre - total / cells
    return jnp.stack([total, jnp.sum(centered * centered, axis=0)]) * weight


def dot(a, b):
    return jnp.dot(a, b, preferred_element_type=jnp.float32)


def dot_back(a, b):
    return lax.dot_general(a, b, (((1,), (1,)), ((), ())), preferred_element_type=jnp.float32)


def dot_cells(a, b):
    return lax.dot_general(a, b, (((0,), (0,)), ((), ())), preferred_element_type=jnp.float32)


def flipped(kernel):
    return jnp.swapaxes(jnp.flip(kernel, (0, 1)), 2, 3)


class Norm:
    def __init__(self, pre, center, rstd, gain, offset):
        self.pre, self.center, self.rstd, self.gain = pre, center, rstd, gain
        self.unit = (pre - center) * rstd
        self.shifted = self.unit * gain + offset

    def act(self):
        return mish(self.shifted)

    def incoming(self, grad):
        self.pushed = grad * mish_slope(self.shifted)
        return jnp.stack(
            [jnp.sum(self.pushed, axis=0), jnp.sum(self.pushed * self.unit, axis=0)]
        )

    def outgoing(self, sums, weight, pixels):
        return (
            weight
            * (self.gain * self.rstd)
            * (self.pushed - (sums[0] + self.unit * sums[1]) / pixels)
        ).astype(jnp.bfloat16)


def on_device(
    inputs,
    image_counts,
    w_down,
    w_short,
    w_main,
    w_inner,
    w_spatial,
    w_trans,
    w_unite,
    gains_wide,
    gains_narrow,
    shifts_wide,
    shifts_narrow,
    grad_output,
):
    half = w_short.shape[1]
    full = 2 * half
    slots, height_dev, width, _ = grad_output.shape
    here = Plane()
    height = here.rows * height_dev
    cells = height * width
    row_cells = height_dev * width
    batch = lax.axis_index("batch")
    own_count = image_counts[batch]
    pixels = jnp.sum(image_counts).astype(jnp.float32) * cells
    here.counts = image_counts.astype(jnp.float32) * cells
    weight = (here.core < own_count).astype(jnp.float32)
    count_here = weight * cells
    count_pair = here.counts[batch]

    below = [(i, i + 1) for i in range(here.rows - 1)]
    borrowed = lax.ppermute(inputs[:, -1:], "rows", below)
    down_source = jnp.pad(
        jnp.concatenate([borrowed, inputs], axis=1), ((0, 0), (0, 0), (1, 0), (0, 0))
    )
    down_rows = lax.conv_general_dilated(
        down_source,
        w_down,
        (2, 2),
        ((0, 0), (0, 0)),
        dimension_numbers=LAYOUT,
        preferred_element_type=jnp.float32,
    )
    slot_weight = (jnp.arange(slots) < own_count).astype(jnp.float32).reshape(-1, 1, 1, 1)
    group_rows = image_counts.astype(jnp.float32) * row_cells
    total = jnp.sum(down_rows * slot_weight, axis=(0, 1, 2))
    centered = down_rows - total / group_rows[batch]
    sums = jnp.stack([total, jnp.sum(centered * centered * slot_weight, axis=(0, 1, 2))])
    down_pre = here.image_of(down_rows.astype(jnp.bfloat16))
    devices = here.rows * here.groups
    spread_out = jnp.broadcast_to(sums[None], (devices,) + sums.shape)
    gathered = lax.all_to_all(spread_out, ("rows", "batch"), 0, 0, tiled=True)
    gathered = gathered.reshape(here.rows, here.groups, 2, full)
    center = jnp.sum(gathered[:, :, 0], axis=(0, 1)) / pixels
    gaps = gathered[:, :, 0] / group_rows[None, :, None] - center
    squares = jnp.sum(gathered[:, :, 1] + group_rows[None, :, None] * gaps * gaps, axis=(0, 1))
    rstd = lax.rsqrt(squares / pixels + EPSILON)
    down = Norm(
        down_pre.reshape(cells, full).astype(jnp.float32),
        center,
        rstd,
        gains_wide[0],
        shifts_wide[0],
    )
    grad_out = here.image_of(grad_output).reshape(cells, full)
    source = here.image_of(inputs)

    def normed(pre, gain, offset):
        sums = moments(pre, weight)
        return Norm(pre, *here.group_moments(sums, count_here, count_pair, pixels), gain, offset)

    sectioned = down.act().astype(jnp.bfloat16)
    split_pre = jnp.concatenate([dot(sectioned, w_short), dot(sectioned, w_main)], axis=1)
    split_sums = moments(split_pre, weight)
    split_center, split_rstd = here.group_moments(split_sums, count_here, count_pair, pixels)
    short = Norm(
        split_pre[:, :half], split_center[:half], split_rstd[:half], gains_narrow[0], shifts_narrow[0]
    )
    main = Norm(
        split_pre[:, half:], split_center[half:], split_rstd[half:], gains_narrow[1], shifts_narrow[1]
    )
    mainline = main.act().astype(jnp.bfloat16)
    inner = normed(dot(mainline, w_inner), gains_narrow[2], shifts_narrow[2])
    inner_act = inner.act().astype(jnp.bfloat16).reshape(height, width, half)
    rim = jnp.pad(inner_act, ((1, 1), (1, 1), (0, 0)))
    spatial_pre = lax.conv_general_dilated(
        rim[None],
        w_spatial,
        (1, 1),
        ((0, 0), (0, 0)),
        dimension_numbers=LAYOUT,
        preferred_element_type=jnp.float32,
    ).reshape(cells, half)
    spatial = normed(spatial_pre, gains_narrow[3], shifts_narrow[3])
    merged = (mainline.astype(jnp.float32) + spatial.act()).astype(jnp.bfloat16)
    trans = normed(dot(merged, w_trans), gains_narrow[4], shifts_narrow[4])
    joined = jnp.concatenate(
        [short.act().astype(jnp.bfloat16), trans.act().astype(jnp.bfloat16)], axis=1
    )
    unite = normed(dot(joined, w_unite), gains_wide[1], shifts_wide[1])
    out_image = (unite.act() * weight).astype(jnp.bfloat16).reshape(height, width, full)

    def own_rows(image, per_device):
        return [
            lax.dynamic_slice_in_dim(image, place * per_device, per_device, 0)
            for place in (here.place, here.place ^ 1)
        ]

    output = here.rows_of(*own_rows(out_image, height_dev))

    def share(values, grad):
        columns = grad.shape[1] // here.chips
        grad = lax.dynamic_slice_in_dim(grad, here.chip * columns, columns, 1)
        part = jnp.concatenate([dot_cells(v, grad) for v in values], axis=0)
        part = part.reshape(part.shape[0], 2, columns // 2)
        mine = lax.dynamic_index_in_dim(part, here.core, 1, keepdims=False)
        other = lax.dynamic_index_in_dim(part, 1 - here.core, 1, keepdims=False)
        return (mine + here.swap(other.astype(jnp.bfloat16)).astype(jnp.float32)).astype(
            jnp.bfloat16
        )

    unite_sums = here.group_sum(unite.incoming(grad_out.astype(jnp.float32) * weight))
    grad_unite_pre = unite.outgoing(unite_sums, weight, pixels)
    grad_joined = dot_back(grad_unite_pre, w_unite)
    pair_sums = here.group_sum(
        jnp.stack([short.incoming(grad_joined[:, :half]), trans.incoming(grad_joined[:, half:])])
    )
    short_sums, trans_sums = pair_sums[0], pair_sums[1]
    grad_short_pre = short.outgoing(short_sums, weight, pixels)
    grad_trans_pre = trans.outgoing(trans_sums, weight, pixels)
    grad_merged = dot_back(grad_trans_pre, w_trans)
    spatial_sums = here.group_sum(spatial.incoming(grad_merged))
    grad_spatial_pre = spatial.outgoing(spatial_sums, weight, pixels)
    grad_inner_act = lax.conv_general_dilated(
        grad_spatial_pre.reshape(1, height, width, half),
        flipped(w_spatial),
        (1, 1),
        ((1, 1), (1, 1)),
        dimension_numbers=LAYOUT,
        preferred_element_type=jnp.float32,
    ).reshape(cells, half)
    inner_sums = here.group_sum(inner.incoming(grad_inner_act))
    grad_inner_pre = inner.outgoing(inner_sums, weight, pixels)
    grad_mainline = grad_merged + dot_back(grad_inner_pre, w_inner)
    main_sums = here.group_sum(main.incoming(grad_mainline))
    grad_main_pre = main.outgoing(main_sums, weight, pixels)

    windows = [
        rim[i : i + height, j : j + width].reshape(cells, half) for i in range(3) for j in range(3)
    ]
    early = lax.psum(
        (
            share([sectioned], grad_short_pre),
            share([sectioned], grad_main_pre),
            share([mainline], grad_inner_pre),
            share(windows, grad_spatial_pre),
            share([merged], grad_trans_pre),
            share([joined], grad_unite_pre),
        ),
        "batch",
    )
    early = [e.astype(jnp.float32) for e in early]

    grad_sectioned = dot_back(grad_short_pre, w_short) + dot_back(grad_main_pre, w_main)
    down_sums = here.group_sum(down.incoming(grad_sectioned))
    grad_down_pre = down.outgoing(down_sums, weight, pixels)

    frame = jnp.pad(source, ((1, 0), (1, 0), (0, 0)))
    taps = [
        lax.slice(
            frame,
            (i, j, 0),
            (i + 2 * (height - 1) + 1, j + 2 * (width - 1) + 1, half),
            (2, 2, 1),
        ).reshape(cells, half)
        for i in range(3)
        for j in range(3)
    ]
    grad_w_down = lax.psum(share(taps, grad_down_pre), "batch").astype(jnp.float32)

    pair_rows = 2 * height_dev
    grad_image = jnp.pad(grad_down_pre.reshape(height, width, full), ((0, 1), (0, 0), (0, 0)))
    grad_block = lax.dynamic_slice_in_dim(grad_image, here.chip * pair_rows, pair_rows + 1, 0)
    widened = lax.conv_general_dilated(
        grad_block[None],
        flipped(w_down),
        (1, 1),
        ((1, 0), (1, 2)),
        lhs_dilation=(2, 2),
        dimension_numbers=LAYOUT,
        preferred_element_type=jnp.float32,
    )[0]
    mine = lax.dynamic_slice_in_dim(widened, here.core * pair_rows, pair_rows, 0)
    other = lax.dynamic_slice_in_dim(widened, (1 - here.core) * pair_rows, pair_rows, 0)
    grad_inputs = here.rows_of(mine, other)

    return (
        output,
        grad_inputs,
        grad_w_down.reshape(3, 3, half, -1),
        early[0],
        early[1],
        early[2],
        early[3].reshape(3, 3, half, -1),
        early[4],
        early[5],
        jnp.stack([down_sums[1], unite_sums[1]]),
        jnp.stack([short_sums[1], main_sums[1], inner_sums[1], spatial_sums[1], trans_sums[1]]),
        jnp.stack([down_sums[0], unite_sums[0]]),
        jnp.stack([short_sums[0], main_sums[0], inner_sums[0], spatial_sums[0], trans_sums[0]]),
    )


def solution(mesh):
    placed = (P("batch", "rows", None, None),) + (P(),) * 12 + (P("batch", "rows", None, None),)
    return jax.shard_map(
        on_device,
        mesh=mesh,
        in_specs=placed,
        out_specs=(
            P("batch", "rows", None, None),
            P("batch", "rows", None, None),
            P(None, None, None, "rows"),
            P(None, "rows"),
            P(None, "rows"),
            P(None, "rows"),
            P(None, None, None, "rows"),
            P(None, "rows"),
            P(None, "rows"),
            P(),
            P(),
            P(),
            P(),
        ),
        check_vma=False,
    )
```

time: 1250 us -> 545 us (0.44)
  blocking collectives: 729 us -> 0 us
  waiting for transfers between devices: 300 us -> 123 us
  local copies, waits for them, and re-layouts: 69.6 us -> 178 us
  starting transfers between devices: 13.5 us -> 72.7 us
  other arithmetic: 46.1 us -> 86.3 us
    psum x18 -> x0, blocking collectives: 729 us -> none  [the longest x6 246 us: normalize(): lax.psum(jnp.sum(centered * centered * weights, axis=(0, 1, 2)), ('rows',...]
    reduce_scatter x4 -> x0, waiting for transfers between devices: 152 us -> none  [the longest x1 39.8 us: on_device(): lax.psum_scatter(store['short'].astype(jnp.bfloat16), 'rows', scatter_dim...]
    slice x16 -> x22, local copies, waits for them, and re-layouts: 14.2 us -> 90.3 us  [the longest x9 83.8 us: on_device(): lax.slice(frame, (i, j, 0), (i + 2 * (height - 1) + 1, j + 2 * (width - 1...]
    unnamed x11 -> x1, waiting for transfers between devices: 64.9 us -> 0.02 us
    ppermute x6 -> x66, starting transfers between devices: 13.1 us -> 67.5 us  [the longest x33 48.8 us: plane_hop(): lax.ppermute(value, 'batch', [(i, i ^ step) for i in range(self.groups)])]
    ppermute x6 -> x66, waiting for transfers between devices: 0.02 us -> 30.4 us  [the longest x33 18.2 us: plane_hop(): lax.ppermute(value, 'batch', [(i, i ^ step) for i in range(self.groups)])]
    unnamed x127 -> x266, local copies, waits for them, and re-layouts: 34.9 us -> 7.61 us
    convert_element_type x16 -> x26, other arithmetic: 17.3 us -> 34.8 us  [the longest x7 10.5 us: share(): (mine + here.swap(other.astype(jnp.bfloat16)).astype(jnp.float32)).astype...]
  transfers between devices with their start and end apart: 14 -> 68, of which waited for: 6 -> 16; matrix products, arithmetic and copies ran while one was open for 9% -> 55% of each run, Pallas kernels for 0% -> 0%
where the time goes in v1:
time: 545 us; the launch traced here: 536 us
  local copies, waits for them, and re-layouts  178 us (33%)
  waiting for transfers between devices  123 us (23%)
  other arithmetic  86.3 us (16%)
  starting transfers between devices  72.7 us (13%)
  matrix products  56.5 us (10%)
  between operations  19.7 us (4%)
    psum x1, waiting for transfers between devices, on_device(): lax.psum((share([sectioned], grad_short_pre), share([sectioned], grad_mai...  92.8 us
    slice x9, local copies, waits for them, and re-layouts, on_device(): lax.slice(frame, (i, j, 0), (i + 2 * (height - 1) + 1, j + 2 * (width - 1...  83.8 us
    ppermute x33, starting transfers between devices, plane_hop(): lax.ppermute(value, 'batch', [(i, i ^ step) for i in range(self.groups)])  48.8 us
    dot_general x23, matrix products, dot_cells(): lax.dot_general(a, b, (((0,), (0,)), ((), ())), preferred_element_type=jn...  21.4 us
    ppermute x33, waiting for transfers between devices, plane_hop(): lax.ppermute(value, 'batch', [(i, i ^ step) for i in range(self.groups)])  18.2 us
    mul x7, other arithmetic, outgoing(): weight * (self.gain * self.rstd)  14.4 us
  transfers between devices with their start and end apart: 68, of which 16 were waited for; matrix products, arithmetic and copies ran while one was open for 55% of the time, Pallas kernels for 0%

profile of v1, /device:TPU:0, one launch (start us, length us, event | category | flops | bytes accessed | tf_op | source)
XLA Modules:
  0.0 536.0 jit_solution(7299727400941146364)
XLA Ops:
  8.3 2.4 collective-permute-start
  11.7 2.7 collective-permute-start.26
  30.3 5.4 %select_reduce_fusion.3 = (f32[1024]{0:T(1024)S(1)}, f32[1,16,9,1024]{3,1,2,0:T(8,128)S(1)}) fusion(f32[1,16,9,1024]{3,0,2,1:T(1,128)S(1)} %bitcast.327, pred[16,9]{0,1:T(8,128)(4,1)S(1)} %copy-done.126, bf16[3,3,512,1024]{3,2,1,0:T(8,128)(2,1)} %param.16, bf16[3,2,8,20,512]{4,1,3,2,0:T(2,128)(2,1)S(1)} %fusion.58), kind=kOutput, calls=%fused_computation.193 | convolution fusion | flops 1359543296 | bytes 11604112 | tf_op jit(solution)/shard_map/conv_general_dilated | solution.py:172
  43.7 4.9 all-to-all-start
  58.3 4.7 collective-permute-done.2
  64.4 3.6 collective-permute-done.3
  70.6 2.3 fusion.15
  79.1 2.7 collective-permute-start.7
  83.6 3.6 collective-permute-done.8
  87.2 2.7 add_rsqrt_fusion
  92.3 2.9 convert_multiply_fusion
  96.0 3.7 collective-permute-start.12
  101.7 2.5 copy.152
  105.6 3.3 multiply_multiply_fusion.4
  108.9 2.6 fusion.28
  115.7 2.7 reshape.361
  120.2 5.0 select_reduce_fusion.1
  128.3 3.7 collective-permute-start.16
  136.2 2.5 copy.158
  138.7 3.3 multiply_multiply_fusion.3
  142.1 2.2 fusion.57
  148.1 3.9 pad.16
  151.9 9.3 %slice.511 = bf16[8,64,512]{2,1,0:T(8,128)(2,1)} slice(bf16[17,129,512]{2,1,0:T(8,128)(2,1)} %pad.16), slice={[0:15:2], [0:127:2], [0:512:1]} | slice | bytes 1048576 | tf_op jit(solution)/shard_map/slice | solution.py:306
  161.2 9.3 %slice.512 = bf16[8,64,512]{2,1,0:T(8,128)(2,1)} slice(bf16[17,129,512]{2,1,0:T(8,128)(2,1)} %pad.16), slice={[0:15:2], [1:128:2], [0:512:1]} | slice | bytes 1048576 | tf_op jit(solution)/shard_map/slice | solution.py:306
  170.5 9.4 %slice.513 = bf16[8,64,512]{2,1,0:T(8,128)(2,1)} slice(bf16[17,129,512]{2,1,0:T(8,128)(2,1)} %pad.16), slice={[0:15:2], [2:129:2], [0:512:1]} | slice | bytes 1048576 | tf_op jit(solution)/shard_map/slice | solution.py:306
  179.9 9.3 %slice.514 = bf16[8,64,512]{2,1,0:T(8,128)(2,1)} slice(bf16[17,129,512]{2,1,0:T(8,128)(2,1)} %pad.16), slice={[1:16:2], [0:127:2], [0:512:1]} | slice | bytes 1048576 | tf_op jit(solution)/shard_map/slice | solution.py:306
  189.2 9.3 %slice.515 = bf16[8,64,512]{2,1,0:T(8,128)(2,1)} slice(bf16[17,129,512]{2,1,0:T(8,128)(2,1)} %pad.16), slice={[1:16:2], [1:128:2], [0:512:1]} | slice | bytes 1048576 | tf_op jit(solution)/shard_map/slice | solution.py:306
  198.5 9.4 %slice.516 = bf16[8,64,512]{2,1,0:T(8,128)(2,1)} slice(bf16[17,129,512]{2,1,0:T(8,128)(2,1)} %pad.16), slice={[1:16:2], [2:129:2], [0:512:1]} | slice | bytes 1048576 | tf_op jit(solution)/shard_map/slice | solution.py:306
  207.9 9.2 %slice.517 = bf16[8,64,512]{2,1,0:T(8,128)(2,1)} slice(bf16[17,129,512]{2,1,0:T(8,128)(2,1)} %pad.16), slice={[2:17:2], [0:127:2], [0:512:1]} | slice | bytes 1048576 | tf_op jit(solution)/shard_map/slice | solution.py:306
  217.1 9.2 %slice.518 = bf16[8,64,512]{2,1,0:T(8,128)(2,1)} slice(bf16[17,129,512]{2,1,0:T(8,128)(2,1)} %pad.16), slice={[2:17:2], [1:128:2], [0:512:1]} | slice | bytes 1048576 | tf_op jit(solution)/shard_map/slice | solution.py:306
  226.3 9.4 %slice.519 = bf16[8,64,512]{2,1,0:T(8,128)(2,1)} slice(bf16[17,129,512]{2,1,0:T(8,128)(2,1)} %pad.16), slice={[2:17:2], [2:129:2], [0:512:1]} | slice | bytes 1048576 | tf_op jit(solution)/shard_map/slice | solution.py:306
  236.5 3.7 collective-permute-start.20
  240.2 2.6 fusion.24
  242.8 2.6 copy.159
  245.4 3.3 multiply_multiply_fusion.5
  250.5 2.3 fusion.213
  255.2 3.6 collective-permute-start.24
  260.7 2.7 multiply_multiply_fusion.1
  263.5 2.2 fusion.190
  265.8 2.3 pad_slice_fusion
  268.5 3.8 collective-permute-start.32
  274.0 3.8 collective-permute-done.33
  280.0 3.0 fusion.195
  285.9 3.6 collective-permute-start.37
  289.6 2.1 copy.179
  299.3 3.0 collective-permute-start.40
  304.3 3.4 collective-permute-done.41
  309.0 5.2 convolution_select_fusion.1
  316.6 2.5 copy.169
  319.3 3.1 fusion.192
  332.4 3.2 copy.178
  338.5 2.5 collective-permute-start.45
  340.9 2.2 fusion.76
  348.3 3.0 collective-permute-start.48
  353.3 3.4 collective-permute-done.49
  361.1 3.4 fusion.189
  367.8 2.5 collective-permute-start.53
  373.3 2.3 multiply_convert_fusion
  385.9 6.7 %reshape.332 = f32[4608,2,128]{2,1,0:T(2,128)} reshape(f32[4608,256]{1,0:T(8,128)} %convolution_dynamic-update-slice_fusion) | data formatting | bytes 9437184 | tf_op jit(solution)/shard_map/reshape | solution.py:251
  392.7 8.5 %constant_dynamic-slice_fusion.5 = (f32[4608,1,128]{2,1,0:T(1,128)S(1)}, f32[4608,1,128]{2,1,0:T(1,128)}) fusion(f32[4608,2,128]{2,1,0:T(2,128)} %reshape.332, s32[]{:T(128)S(6)} %select_n.175, s32[]{:T(128)S(6)} %select_n.174), kind=kLoop, calls=%fused_computation.278 | loop fusion | bytes 9437192 | tf_op jit(solution)/shard_map/jit(dynamic_index_in_dim)/dynamic_slice | solution.py:253
  411.9 3.2 add_convert_fusion
  416.0 6.2 %convolution_select_fusion = f32[4,8,18,512]{3,1,2,0:T(8,128)S(1)} fusion(bf16[3,3,512,1024]{3,2,1,0:T(8,128)(2,1)} %param.16, pred[8,18]{0,1:T(8,128)(4,1)S(1)} %copy-done.129, bf16[3,1,7,1,1024]{4,2,3,0,1:T(8,128)(2,1)S(1)} %slice.620, bf16[3,1,8,9,1024]{4,2,3,0,1:T(8,128)(2,1)S(1)} %copy.173), kind=kOutput, calls=%fused_computation.71 | convolution fusion | flops 1360723968 | bytes 11102352 | tf_op jit(solution)/shard_map/conv_general_dilated | solution.py:320
  428.0 92.8 %all-reduce.6.cloned.1.call-done = (bf16[3,3,512,64]{2,1,0,3:T(4,128)(2,1)}, bf16[3,3,512,128]{3,2,1,0:T(8,128)(2,1)}, bf16[1024,64]{0,1:T(8,128)(2,1)}, bf16[10...) async-done(((bf16[3,3,512,64]{2,1,0,3:T(4,128)(2,1)}, bf16[3,3,512,128]{3,2,1,0:T(8,128)(2,1)}, ...) | async-done | bytes 2424848 | tf_op jit(solution)/shard_map/psum | solution.py:287
  520.8 3.0 reshape.334
  (579 shorter events, 157.5 us)
Async XLA Ops:
  8.3 19.0 %collective-permute-start = (bf16[2,1,128,512]{3,2,1,0:T(8,128)(2,1)S(1)}, bf16[2,1,128,512]{3,2,1,0:T(8,128)(2,1)S(1)}, u32[]{:S(2)}, u32[]{:S(2)}) collective-permute-start(bf16[2,1,128,512]{3,2,1,0:T(8,128)(2,1)S(1)} %slice.422), channel_id=1, source_target_pairs={{0,4},{4,8},{8,12},{12,16},{16,20},{20,24},{24,28},{1,5},{5,9},{9,... | collective-permute-start | bytes 786440 | tf_op jit(solution)/shard_map/ppermute | solution.py:168
  11.7 14.7 %collective-permute-start.26 = (bf16[1,64,1024]{2,1,0:T(8,128)(2,1)S(1)}, bf16[1,64,1024]{2,1,0:T(8,128)(2,1)}, u32[]{:S(2)}, u32[]{:S(2)}) collective-permute-start(bf16[1,64,1024]{2,1,0:T(8,128)(2,1)S(1)} %dynamic-slice_bitcast_fusion.2), channel_id=1, source_target_pairs={{0,4},{4,0},{8,12},{12,8},{16,20},{20,16},{24,28},{28,24},{1,5},{5... | collective-permute-start | bytes 393224 | tf_op jit(solution)/shard_map/ppermute | solution.py:40
  16.0 35.0 %collective-permute-start.55 = (bf16[2,128,512]{2,1,0:T(8,128)(2,1)}, bf16[2,128,512]{2,1,0:T(8,128)(2,1)}, u32[]{:S(2)}, u32[]{:S(2)}) collective-permute-start(bf16[2,128,512]{2,1,0:T(8,128)(2,1)} %dynamic-slice_bitcast_fusion), channel_id=1, source_target_pairs={{0,4},{4,0},{8,12},{12,8},{16,20},{20,16},{24,28},{28,24},{1,5},{5... | collective-permute-start | bytes 786440 | tf_op jit(solution)/shard_map/ppermute | solution.py:40
  36.9 12.0 %collective-permute-start.1 = (bf16[1,64,1024]{2,1,0:T(8,128)(2,1)S(1)}, bf16[1,64,1024]{2,1,0:T(8,128)(2,1)S(1)}, u32[]{:S(2)}, u32[]{:S(2)}) collective-permute-start(bf16[1,64,1024]{2,1,0:T(8,128)(2,1)S(1)} %dynamic-slice_bitcast_fusion.1), channel_id=1, source_target_pairs={{0,4},{4,0},{8,12},{12,8},{16,20},{20,16},{24,28},{28,24},{1,5},{5... | collective-permute-start | bytes 393224 | tf_op jit(solution)/shard_map/ppermute | solution.py:40
  39.5 16.8 %collective-permute-start.27 = (bf16[2,64,1024]{2,1,0:T(8,128)(2,1)}, bf16[2,64,1024]{2,1,0:T(8,128)(2,1)}, u32[]{:S(2)}, u32[]{:S(2)}) collective-permute-start(bf16[2,64,1024]{2,1,0:T(8,128)(2,1)} %get-tuple-element.137), channel_id=1, source_target_pairs={{0,8},{4,12},{8,0},{12,4},{16,24},{20,28},{24,16},{28,20},{1,9},{5... | collective-permute-start | bytes 786440 | tf_op jit(solution)/shard_map/ppermute | solution.py:43
  40.9 34.8 %collective-permute-start.28 = (bf16[2,64,1024]{2,1,0:T(8,128)(2,1)}, bf16[2,64,1024]{2,1,0:T(8,128)(2,1)}, u32[]{:S(2)}, u32[]{:S(2)}) collective-permute-start(bf16[2,64,1024]{2,1,0:T(8,128)(2,1)} %get-tuple-element.137), channel_id=1, source_target_pairs={{0,16},{4,20},{8,24},{12,28},{16,0},{20,4},{24,8},{28,12},{1,17},{... | collective-permute-start | bytes 786440 | tf_op jit(solution)/shard_map/ppermute | solution.py:43
  41.0 40.8 %collective-permute-start.29 = (bf16[2,64,1024]{2,1,0:T(8,128)(2,1)}, bf16[2,64,1024]{2,1,0:T(8,128)(2,1)}, u32[]{:S(2)}, u32[]{:S(2)}) collective-permute-start(bf16[2,64,1024]{2,1,0:T(8,128)(2,1)} %get-tuple-element.137), channel_id=1, source_target_pairs={{0,24},{4,28},{8,16},{12,20},{16,8},{20,12},{24,0},{28,4},{1,25},{... | collective-permute-start | bytes 786440 | tf_op jit(solution)/shard_map/ppermute | solution.py:43
  43.7 25.9 %all-to-all-start = ((f32[32,2,1024]{2,1,0:T(2,128)}), f32[32,2,1024]{2,1,0:T(2,128)S(1)}, u32[]{:S(2)}, u32[]{:S(2)}) async-start(f32[32,2,1024]{2,1,0:T(2,128)} %broadcast_in_dim.8), calls=%async_computation | async-start | bytes 524288 | tf_op jit(solution)/shard_map/all_to_all | solution.py:188
  48.7 472.1 %all-reduce.6.cloned.1.call-start = ((), (), s32[]{:S(2)}) async-start(), calls=%async_computation.1 | async-start | bytes 5242880 | tf_op jit(solution)/shard_map/psum | solution.py:287
  49.1 13.8 %collective-permute-start.2 = (bf16[2,64,1024]{2,1,0:T(8,128)(2,1)S(1)}, bf16[2,64,1024]{2,1,0:T(8,128)(2,1)S(1)}, u32[]{:S(2)}, u32[]{:S(2)}) collective-permute-start(bf16[2,64,1024]{2,1,0:T(8,128)(2,1)S(1)} %get-tuple-element.142), channel_id=1, source_target_pairs={{0,8},{4,12},{8,0},{12,4},{16,24},{20,28},{24,16},{28,20},{1,9},{5... | collective-permute-start | bytes 786440 | tf_op jit(solution)/shard_map/ppermute | solution.py:43
  52.0 16.0 %collective-permute-start.3 = (bf16[2,64,1024]{2,1,0:T(8,128)(2,1)S(1)}, bf16[2,64,1024]{2,1,0:T(8,128)(2,1)S(1)}, u32[]{:S(2)}, u32[]{:S(2)}) collective-permute-start(bf16[2,64,1024]{2,1,0:T(8,128)(2,1)S(1)} %get-tuple-element.142), channel_id=1, source_target_pairs={{0,16},{4,20},{8,24},{12,28},{16,0},{20,4},{24,8},{28,12},{1,17},{... | collective-permute-start | bytes 786440 | tf_op jit(solution)/shard_map/ppermute | solution.py:43
  56.2 13.3 %collective-permute-start.4 = (bf16[2,64,1024]{2,1,0:T(8,128)(2,1)S(1)}, bf16[2,64,1024]{2,1,0:T(8,128)(2,1)S(1)}, u32[]{:S(2)}, u32[]{:S(2)}) collective-permute-start(bf16[2,64,1024]{2,1,0:T(8,128)(2,1)S(1)} %get-tuple-element.142), channel_id=1, source_target_pairs={{0,24},{4,28},{8,16},{12,20},{16,8},{20,12},{24,0},{28,4},{1,25},{... | collective-permute-start | bytes 786440 | tf_op jit(solution)/shard_map/ppermute | solution.py:43
  62.9 62.6 %collective-permute-start.56 = (bf16[4,128,512]{2,1,0:T(8,128)(2,1)}, bf16[4,128,512]{2,1,0:T(8,128)(2,1)}, u32[]{:S(2)}, u32[]{:S(2)}) collective-permute-start(bf16[4,128,512]{2,1,0:T(8,128)(2,1)} %get-tuple-element.123), channel_id=1, source_target_pairs={{0,8},{4,12},{8,0},{12,4},{16,24},{20,28},{24,16},{28,20},{1,9},{5... | collective-permute-start | bytes 1572872 | tf_op jit(solution)/shard_map/ppermute | solution.py:43
  68.1 63.9 %collective-permute-start.57 = (bf16[4,128,512]{2,1,0:T(8,128)(2,1)}, bf16[4,128,512]{2,1,0:T(8,128)(2,1)}, u32[]{:S(2)}, u32[]{:S(2)}) collective-permute-start(bf16[4,128,512]{2,1,0:T(8,128)(2,1)} %get-tuple-element.123), channel_id=1, source_target_pairs={{0,16},{4,20},{8,24},{12,28},{16,0},{20,4},{24,8},{28,12},{1,17},{... | collective-permute-start | bytes 1572872 | tf_op jit(solution)/shard_map/ppermute | solution.py:43
  75.6 1.8 collective-permute-start.5
  77.5 6.1 %collective-permute-start.6 = (f32[2,1024]{1,0:T(2,128)S(1)}, f32[2,1024]{1,0:T(2,128)S(1)}, u32[]{:S(2)}, u32[]{:S(2)}) collective-permute-start(f32[2,1024]{1,0:T(2,128)S(1)} %pad_maximum_fusion.10), channel_id=1, source_target_pairs={{0,1},{1,0},{2,3},{3,2},{4,5},{5,4},{6,7},{7,6},{8,9},{9,8},{10,11... | collective-permute-start | bytes 24584 | tf_op jit(solution)/shard_map/ppermute | solution.py:46
  79.1 4.5 collective-permute-start.7
  81.8 5.4 %collective-permute-start.8 = (f32[2,1024]{1,0:T(2,128)S(1)}, f32[2,1024]{1,0:T(2,128)S(1)}, u32[]{:S(2)}, u32[]{:S(2)}) collective-permute-start(f32[2,1024]{1,0:T(2,128)S(1)} %pad_maximum_fusion.10), channel_id=1, source_target_pairs={{0,3},{1,2},{2,1},{3,0},{4,7},{5,6},{6,5},{7,4},{8,11},{9,10},{10,... | collective-permute-start | bytes 24584 | tf_op jit(solution)/shard_map/ppermute | solution.py:46
  92.2 3.0 collective-permute-start.9
  95.2 9.0 %collective-permute-start.10 = (f32[2,512]{1,0:T(2,128)S(1)}, f32[2,512]{1,0:T(2,128)S(1)}, u32[]{:S(2)}, u32[]{:S(2)}) collective-permute-start(f32[2,512]{1,0:T(2,128)S(1)} %pad_maximum_fusion.17), channel_id=1, source_target_pairs={{0,1},{1,0},{2,3},{3,2},{4,5},{5,4},{6,7},{7,6},{8,9},{9,8},{10,11... | collective-permute-start | bytes 12296 | tf_op jit(solution)/shard_map/ppermute | solution.py:46
  95.3 10.3 %collective-permute-start.11 = (f32[2,512]{1,0:T(2,128)S(1)}, f32[2,512]{1,0:T(2,128)S(1)}, u32[]{:S(2)}, u32[]{:S(2)}) collective-permute-start(f32[2,512]{1,0:T(2,128)S(1)} %pad_maximum_fusion.17), channel_id=1, source_target_pairs={{0,2},{1,3},{2,0},{3,1},{4,6},{5,7},{6,4},{7,5},{8,10},{9,11},{10,... | collective-permute-start | bytes 12296 | tf_op jit(solution)/shard_map/ppermute | solution.py:46
  96.0 9.6 %collective-permute-start.12 = (f32[2,512]{1,0:T(2,128)S(1)}, f32[2,512]{1,0:T(2,128)S(1)}, u32[]{:S(2)}, u32[]{:S(2)}) collective-permute-start(f32[2,512]{1,0:T(2,128)S(1)} %pad_maximum_fusion.17), channel_id=1, source_target_pairs={{0,3},{1,2},{2,1},{3,0},{4,7},{5,6},{6,5},{7,4},{8,11},{9,10},{10,... | collective-permute-start | bytes 12296 | tf_op jit(solution)/shard_map/ppermute | solution.py:46
  104.2 41.9 %collective-permute-start.58 = (bf16[4,128,512]{2,1,0:T(8,128)(2,1)}, bf16[4,128,512]{2,1,0:T(8,128)(2,1)}, u32[]{:S(2)}, u32[]{:S(2)}) collective-permute-start(bf16[4,128,512]{2,1,0:T(8,128)(2,1)} %get-tuple-element.123), channel_id=1, source_target_pairs={{0,24},{4,28},{8,16},{12,20},{16,8},{20,12},{24,0},{28,4},{1,25},{... | collective-permute-start | bytes 1572872 | tf_op jit(solution)/shard_map/ppermute | solution.py:43
  125.5 2.0 collective-permute-start.13
  127.5 11.2 %collective-permute-start.14 = (f32[2,512]{1,0:T(2,128)S(1)}, f32[2,512]{1,0:T(2,128)S(1)}, u32[]{:S(2)}, u32[]{:S(2)}) collective-permute-start(f32[2,512]{1,0:T(2,128)S(1)} %pad_maximum_fusion.18), channel_id=1, source_target_pairs={{0,1},{1,0},{2,3},{3,2},{4,5},{5,4},{6,7},{7,6},{8,9},{9,8},{10,11... | collective-permute-start | bytes 12296 | tf_op jit(solution)/shard_map/ppermute | solution.py:46
  127.6 11.2 %collective-permute-start.15 = (f32[2,512]{1,0:T(2,128)S(1)}, f32[2,512]{1,0:T(2,128)S(1)}, u32[]{:S(2)}, u32[]{:S(2)}) collective-permute-start(f32[2,512]{1,0:T(2,128)S(1)} %pad_maximum_fusion.18), channel_id=1, source_target_pairs={{0,2},{1,3},{2,0},{3,1},{4,6},{5,7},{6,4},{7,5},{8,10},{9,11},{10,... | collective-permute-start | bytes 12296 | tf_op jit(solution)/shard_map/ppermute | solution.py:46
  128.3 10.4 %collective-permute-start.16 = (f32[2,512]{1,0:T(2,128)S(1)}, f32[2,512]{1,0:T(2,128)S(1)}, u32[]{:S(2)}, u32[]{:S(2)}) collective-permute-start(f32[2,512]{1,0:T(2,128)S(1)} %pad_maximum_fusion.18), channel_id=1, source_target_pairs={{0,3},{1,2},{2,1},{3,0},{4,7},{5,6},{6,5},{7,4},{8,11},{9,10},{10,... | collective-permute-start | bytes 12296 | tf_op jit(solution)/shard_map/ppermute | solution.py:46
  146.0 89.7 %collective-permute-start.17 = (f32[2,512]{1,0:T(2,128)S(1)}, f32[2,512]{1,0:T(2,128)S(1)}, u32[]{:S(2)}, u32[]{:S(2)}) collective-permute-start(f32[2,512]{1,0:T(2,128)S(1)} %maximum_multiply_fusion.4), channel_id=1, source_target_pairs={{0,4},{4,0},{8,12},{12,8},{16,20},{20,16},{24,28},{28,24},{1,5},{5... | collective-permute-start | bytes 12296 | tf_op jit(solution)/shard_map/ppermute | solution.py:40
  235.7 9.6 %collective-permute-start.18 = (f32[2,512]{1,0:T(2,128)S(1)}, f32[2,512]{1,0:T(2,128)S(1)}, u32[]{:S(2)}, u32[]{:S(2)}) collective-permute-start(f32[2,512]{1,0:T(2,128)S(1)} %pad_maximum_fusion.19), channel_id=1, source_target_pairs={{0,1},{1,0},{2,3},{3,2},{4,5},{5,4},{6,7},{7,6},{8,9},{9,8},{10,11... | collective-permute-start | bytes 12296 | tf_op jit(solution)/shard_map/ppermute | solution.py:46
  235.8 9.6 %collective-permute-start.19 = (f32[2,512]{1,0:T(2,128)S(1)}, f32[2,512]{1,0:T(2,128)S(1)}, u32[]{:S(2)}, u32[]{:S(2)}) collective-permute-start(f32[2,512]{1,0:T(2,128)S(1)} %pad_maximum_fusion.19), channel_id=1, source_target_pairs={{0,2},{1,3},{2,0},{3,1},{4,6},{5,7},{6,4},{7,5},{8,10},{9,11},{10,... | collective-permute-start | bytes 12296 | tf_op jit(solution)/shard_map/ppermute | solution.py:46
  236.5 8.8 %collective-permute-start.20 = (f32[2,512]{1,0:T(2,128)S(1)}, f32[2,512]{1,0:T(2,128)S(1)}, u32[]{:S(2)}, u32[]{:S(2)}) collective-permute-start(f32[2,512]{1,0:T(2,128)S(1)} %pad_maximum_fusion.19), channel_id=1, source_target_pairs={{0,3},{1,2},{2,1},{3,0},{4,7},{5,6},{6,5},{7,4},{8,11},{9,10},{10,... | collective-permute-start | bytes 12296 | tf_op jit(solution)/shard_map/ppermute | solution.py:46
  254.4 5.0 collective-permute-start.22
  254.5 4.9 collective-permute-start.23
  255.2 5.4 %collective-permute-start.24 = (f32[2,1024]{1,0:T(2,128)S(1)}, f32[2,1024]{1,0:T(2,128)S(1)}, u32[]{:S(2)}, u32[]{:S(2)}) collective-permute-start(f32[2,1024]{1,0:T(2,128)S(1)} %pad_maximum_fusion.11), channel_id=1, source_target_pairs={{0,3},{1,2},{2,1},{3,0},{4,7},{5,6},{6,5},{7,4},{8,11},{9,10},{10,... | collective-permute-start | bytes 24584 | tf_op jit(solution)/shard_map/ppermute | solution.py:46
  265.7 2.4 collective-permute-start.30
  268.1 4.6 collective-permute-start.31
  268.5 5.4 %collective-permute-start.32 = (f32[2,1024]{1,0:T(2,128)S(1)}, f32[2,1024]{1,0:T(2,128)S(1)}, u32[]{:S(2)}, u32[]{:S(2)}) collective-permute-start(f32[2,1024]{1,0:T(2,128)S(1)} %fusion.188), channel_id=1, source_target_pairs={{0,2},{1,3},{2,0},{3,1},{4,6},{5,7},{6,4},{7,5},{8,10},{9,11},{10,... | collective-permute-start | bytes 24584 | tf_op jit(solution)/shard_map/ppermute | solution.py:46
  272.4 5.4 %collective-permute-start.33 = (f32[2,1024]{1,0:T(2,128)S(1)}, f32[2,1024]{1,0:T(2,128)S(1)}, u32[]{:S(2)}, u32[]{:S(2)}) collective-permute-start(f32[2,1024]{1,0:T(2,128)S(1)} %fusion.188), channel_id=1, source_target_pairs={{0,3},{1,2},{2,1},{3,0},{4,7},{5,6},{6,5},{7,4},{8,11},{9,10},{10,... | collective-permute-start | bytes 24584 | tf_op jit(solution)/shard_map/ppermute | solution.py:46
  272.6 152.4 %collective-permute-start.25 = (bf16[1,64,1024]{2,1,0:T(8,128)(2,1)S(1)}, bf16[1,64,1024]{2,1,0:T(8,128)(2,1)}, u32[]{:S(2)}, u32[]{:S(2)}) collective-permute-start(bf16[1,64,1024]{2,1,0:T(8,128)(2,1)S(1)} %constant_dynamic-slice_fusion.9), channel_id=1, source_target_pairs={{0,4},{4,0},{8,12},{12,8},{16,20},{20,16},{24,28},{28,24},{1,5},{5... | collective-permute-start | bytes 393224 | tf_op jit(solution)/shard_map/ppermute | solution.py:40
  283.0 1.5 collective-permute-start.34
  285.1 7.5 %collective-permute-start.35 = (f32[2,2,512]{2,1,0:T(2,128)}, f32[2,2,512]{2,1,0:T(2,128)}, u32[]{:S(2)}, u32[]{:S(2)}) collective-permute-start(f32[2,2,512]{2,1,0:T(2,128)} %fusion.187), channel_id=1, source_target_pairs={{0,1},{1,0},{2,3},{3,2},{4,5},{5,4},{6,7},{7,6},{8,9},{9,8},{10,11... | collective-permute-start | bytes 24584 | tf_op jit(solution)/shard_map/ppermute | solution.py:46
  285.1 7.5 %collective-permute-start.36 = (f32[2,2,512]{2,1,0:T(2,128)}, f32[2,2,512]{2,1,0:T(2,128)}, u32[]{:S(2)}, u32[]{:S(2)}) collective-permute-start(f32[2,2,512]{2,1,0:T(2,128)} %fusion.187), channel_id=1, source_target_pairs={{0,2},{1,3},{2,0},{3,1},{4,6},{5,7},{6,4},{7,5},{8,10},{9,11},{10,... | collective-permute-start | bytes 24584 | tf_op jit(solution)/shard_map/ppermute | solution.py:46
  285.9 6.8 %collective-permute-start.37 = (f32[2,2,512]{2,1,0:T(2,128)}, f32[2,2,512]{2,1,0:T(2,128)}, u32[]{:S(2)}, u32[]{:S(2)}) collective-permute-start(f32[2,2,512]{2,1,0:T(2,128)} %fusion.187), channel_id=1, source_target_pairs={{0,3},{1,2},{2,1},{3,0},{4,7},{5,6},{6,5},{7,4},{8,11},{9,10},{10,... | collective-permute-start | bytes 24584 | tf_op jit(solution)/shard_map/ppermute | solution.py:46
  292.6 115.3 %collective-permute-start.65 = (bf16[1024,128]{1,0:T(8,128)(2,1)}, bf16[1024,128]{1,0:T(8,128)(2,1)}, u32[]{:S(2)}, u32[]{:S(2)}) collective-permute-start(bf16[1024,128]{1,0:T(8,128)(2,1)} %bitcast.360), channel_id=1, source_target_pairs={{0,4},{4,0},{8,12},{12,8},{16,20},{20,16},{24,28},{28,24},{1,5},{5... | collective-permute-start | bytes 786440 | tf_op jit(solution)/shard_map/ppermute | solution.py:40
  299.2 5.1 collective-permute-start.39
  299.3 5.0 collective-permute-start.40
  302.3 5.4 %collective-permute-start.41 = (f32[2,512]{1,0:T(2,128)S(1)}, f32[2,512]{1,0:T(2,128)S(1)}, u32[]{:S(2)}, u32[]{:S(2)}) collective-permute-start(f32[2,512]{1,0:T(2,128)S(1)} %fusion.185), channel_id=1, source_target_pairs={{0,3},{1,2},{2,1},{3,0},{4,7},{5,6},{6,5},{7,4},{8,11},{9,10},{10,... | collective-permute-start | bytes 12296 | tf_op jit(solution)/shard_map/ppermute | solution.py:46
  323.0 12.7 %collective-permute-start.42 = (f32[2,512]{1,0:T(2,128)}, f32[2,512]{1,0:T(2,128)}, u32[]{:S(2)}, u32[]{:S(2)}) collective-permute-start(f32[2,512]{1,0:T(2,128)} %pad_maximum_fusion.21), channel_id=1, source_target_pairs={{0,4},{4,0},{8,12},{12,8},{16,20},{20,16},{24,28},{28,24},{1,5},{5... | collective-permute-start | bytes 12296 | tf_op jit(solution)/shard_map/ppermute | solution.py:40
  336.5 6.6 %collective-permute-start.43 = (f32[2,512]{1,0:T(2,128)S(1)}, f32[2,512]{1,0:T(2,128)S(1)}, u32[]{:S(2)}, u32[]{:S(2)}) collective-permute-start(f32[2,512]{1,0:T(2,128)S(1)} %fusion.184), channel_id=1, source_target_pairs={{0,1},{1,0},{2,3},{3,2},{4,5},{5,4},{6,7},{7,6},{8,9},{9,8},{10,11... | collective-permute-start | bytes 12296 | tf_op jit(solution)/shard_map/ppermute | solution.py:46
  336.6 6.5 %collective-permute-start.44 = (f32[2,512]{1,0:T(2,128)S(1)}, f32[2,512]{1,0:T(2,128)S(1)}, u32[]{:S(2)}, u32[]{:S(2)}) collective-permute-start(f32[2,512]{1,0:T(2,128)S(1)} %fusion.184), channel_id=1, source_target_pairs={{0,2},{1,3},{2,0},{3,1},{4,6},{5,7},{6,4},{7,5},{8,10},{9,11},{10,... | collective-permute-start | bytes 12296 | tf_op jit(solution)/shard_map/ppermute | solution.py:46
  338.5 5.4 %collective-permute-start.45 = (f32[2,512]{1,0:T(2,128)S(1)}, f32[2,512]{1,0:T(2,128)S(1)}, u32[]{:S(2)}, u32[]{:S(2)}) collective-permute-start(f32[2,512]{1,0:T(2,128)S(1)} %fusion.184), channel_id=1, source_target_pairs={{0,3},{1,2},{2,1},{3,0},{4,7},{5,6},{6,5},{7,4},{8,11},{9,10},{10,... | collective-permute-start | bytes 12296 | tf_op jit(solution)/shard_map/ppermute | solution.py:46
  348.2 5.1 collective-permute-start.47
  348.3 5.0 collective-permute-start.48
  351.3 5.4 %collective-permute-start.49 = (f32[2,512]{1,0:T(2,128)S(1)}, f32[2,512]{1,0:T(2,128)S(1)}, u32[]{:S(2)}, u32[]{:S(2)}) collective-permute-start(f32[2,512]{1,0:T(2,128)S(1)} %fusion.183), channel_id=1, source_target_pairs={{0,3},{1,2},{2,1},{3,0},{4,7},{5,6},{6,5},{7,4},{8,11},{9,10},{10,... | collective-permute-start | bytes 12296 | tf_op jit(solution)/shard_map/ppermute | solution.py:46
  365.8 6.4 %collective-permute-start.51 = (f32[2,1024]{1,0:T(2,128)S(1)}, f32[2,1024]{1,0:T(2,128)S(1)}, u32[]{:S(2)}, u32[]{:S(2)}) collective-permute-start(f32[2,1024]{1,0:T(2,128)S(1)} %fusion.186), channel_id=1, source_target_pairs={{0,1},{1,0},{2,3},{3,2},{4,5},{5,4},{6,7},{7,6},{8,9},{9,8},{10,11... | collective-permute-start | bytes 24584 | tf_op jit(solution)/shard_map/ppermute | solution.py:46
  365.9 6.3 %collective-permute-start.52 = (f32[2,1024]{1,0:T(2,128)S(1)}, f32[2,1024]{1,0:T(2,128)S(1)}, u32[]{:S(2)}, u32[]{:S(2)}) collective-permute-start(f32[2,1024]{1,0:T(2,128)S(1)} %fusion.186), channel_id=1, source_target_pairs={{0,2},{1,3},{2,0},{3,1},{4,6},{5,7},{6,4},{7,5},{8,10},{9,11},{10,... | collective-permute-start | bytes 24584 | tf_op jit(solution)/shard_map/ppermute | solution.py:46
  367.8 5.4 %collective-permute-start.53 = (f32[2,1024]{1,0:T(2,128)S(1)}, f32[2,1024]{1,0:T(2,128)S(1)}, u32[]{:S(2)}, u32[]{:S(2)}) collective-permute-start(f32[2,1024]{1,0:T(2,128)S(1)} %fusion.186), channel_id=1, source_target_pairs={{0,3},{1,2},{2,1},{3,0},{4,7},{5,6},{6,5},{7,4},{8,11},{9,10},{10,... | collective-permute-start | bytes 24584 | tf_op jit(solution)/shard_map/ppermute | solution.py:46
  372.2 30.1 %collective-permute-start.64 = (bf16[512,64]{0,1:T(8,128)(2,1)}, bf16[512,64]{0,1:T(8,128)(2,1)}, u32[]{:S(2)}, u32[]{:S(2)}) collective-permute-start(bf16[512,64]{0,1:T(8,128)(2,1)} %fusion.105), channel_id=1, source_target_pairs={{0,4},{4,0},{8,12},{12,8},{16,20},{20,16},{24,28},{28,24},{1,5},{5... | collective-permute-start | bytes 196616 | tf_op jit(solution)/shard_map/ppermute | solution.py:40
  372.2 37.4 %collective-permute-start.63 = (bf16[4608,64]{0,1:T(8,128)(2,1)}, bf16[4608,64]{0,1:T(8,128)(2,1)}, u32[]{:S(2)}, u32[]{:S(2)}) collective-permute-start(bf16[4608,64]{0,1:T(8,128)(2,1)} %fusion.76), channel_id=1, source_target_pairs={{0,4},{4,0},{8,12},{12,8},{16,20},{20,16},{24,28},{28,24},{1,5},{5... | collective-permute-start | bytes 1769480 | tf_op jit(solution)/shard_map/ppermute | solution.py:40
  373.2 31.3 %collective-permute-start.62 = (bf16[512,64]{0,1:T(8,128)(2,1)}, bf16[512,64]{0,1:T(8,128)(2,1)}, u32[]{:S(2)}, u32[]{:S(2)}) collective-permute-start(bf16[512,64]{0,1:T(8,128)(2,1)} %fusion.104), channel_id=1, source_target_pairs={{0,4},{4,0},{8,12},{12,8},{16,20},{20,16},{24,28},{28,24},{1,5},{5... | collective-permute-start | bytes 196616 | tf_op jit(solution)/shard_map/ppermute | solution.py:40
  402.3 3.7 collective-permute-start.61
  404.5 2.7 collective-permute-start.60
  406.0 5.9 %collective-permute-start.59 = (bf16[4608,128]{1,0:T(8,128)(2,1)}, bf16[4608,128]{1,0:T(8,128)(2,1)}, u32[]{:S(2)}, u32[]{:S(2)}) collective-permute-start(bf16[4608,128]{1,0:T(8,128)(2,1)} %convert_bitcast_fusion), channel_id=1, source_target_pairs={{0,4},{4,0},{8,12},{12,8},{16,20},{20,16},{24,28},{28,24},{1,5},{5... | collective-permute-start | bytes 3538952 | tf_op jit(solution)/shard_map/ppermute | solution.py:40
  423.7 3.1 collective-permute-start.54
  (135 other events, 2225.9 us)
Sparse Core Ops, SparseCore 0:
  415.3 105.4 all-reduce.5

commit v2 on v1

v2 whole, which is shorter than its diff:
```python
import functools

import jax
import jax.numpy as jnp
from jax import lax
from jax.experimental import pallas as pl
from jax.experimental.pallas import tpu as pltpu
from jax.sharding import PartitionSpec as P

EPSILON = 1e-05
FAR = 20.0
CHUNK = 32
COLS = 256
BF = jnp.bfloat16
F32 = jnp.float32


def mish(values):
    grown = jnp.exp(jnp.minimum(values, FAR))
    wide = grown * (grown + 2.0)
    return values * (wide / (wide + 2.0))


def mish_slope(values):
    grown = jnp.exp(jnp.minimum(values, FAR))
    wide = grown * (grown + 2.0)
    share = 1.0 / (wide + 2.0)
    return wide * share + 4.0 * values * (grown * (grown + 1.0) * share) * share


def tree_sum(parts):
    while len(parts) > 1:
        parts = [parts[i] + parts[i + 1] for i in range(0, len(parts), 2)]
    return parts[0]


def dot(a, b):
    return jnp.dot(a, b, preferred_element_type=F32)


def dot_back(a, b):
    return lax.dot_general(a, b, (((1,), (1,)), ((), ())), preferred_element_type=F32)


def dot_cells(a, b):
    return lax.dot_general(a, b, (((0,), (0,)), ((), ())), preferred_element_type=F32)


class Plane:
    def __init__(self):
        self.rows = lax.axis_size("rows")
        self.groups = lax.axis_size("batch")
        self.chips = self.rows // 2
        self.place = lax.axis_index("rows")
        self.core = self.place % 2
        self.chip = self.place // 2

    def swap(self, value):
        return lax.ppermute(value, "rows", [(i, i ^ 1) for i in range(self.rows)])

    def chip_hops(self, value):
        return [value] + [
            lax.ppermute(value, "rows", [(i, i ^ (2 * step)) for i in range(self.rows)])
            for step in range(1, self.chips)
        ]

    def plane_hops(self, value):
        return [value] + [
            lax.ppermute(value, "batch", [(i, i ^ step) for i in range(self.groups)])
            for step in range(1, self.groups)
        ]

    def by_core(self, mine, got):
        first = self.core == 0
        return jnp.where(first, mine, got), jnp.where(first, got, mine)

    def split(self, block, axis=0):
        mine = lax.dynamic_index_in_dim(block, self.core, axis, keepdims=False)
        other = lax.dynamic_index_in_dim(block, 1 - self.core, axis, keepdims=False)
        return mine, other

    def pieces(self, mine, other):
        return self.chip_hops(jnp.concatenate([mine, self.swap(other)], axis=0))

    def everywhere(self, pay):
        return self.plane_hops(jnp.concatenate([pay, self.swap(pay)], axis=0))


def rows_loop(total, body, carry=None, step=CHUNK):
    def turn(index, state):
        return body(pl.ds(pl.multiple_of(index * step, step), step), state)

    return lax.fori_loop(0, total // step, turn, carry)


def finish_moments(scal, refs, cols=slice(None)):
    pixels = scal[1]
    center = tree_sum([r[0:1, cols] + r[2:3, cols] for r in refs]) / pixels
    terms = []
    for k, r in enumerate(refs):
        ends = []
        for side in range(2):
            count, over = scal[2 + 4 * k + 2 * side], scal[3 + 4 * k + 2 * side]
            gap = r[2 * side : 2 * side + 1, cols] * over - center
            ends.append(gap * gap * count)
        terms.append((r[1:2, cols] + r[3:4, cols]) + (ends[0] + ends[1]))
    return center, lax.rsqrt(tree_sum(terms) / pixels + EPSILON)


def finish_sums(refs, cols=slice(None)):
    return (
        tree_sum([r[0:1, cols] + r[2:3, cols] for r in refs]),
        tree_sum([r[1:2, cols] + r[3:4, cols] for r in refs]),
    )


def put_moments(values, pay, cols, weight):
    total = jnp.sum(values, axis=0, keepdims=True)
    off = values - total * (1.0 / values.shape[0])
    pay[0:1, cols] = total * weight
    pay[1:2, cols] = jnp.sum(off * off, axis=0, keepdims=True) * weight


def project(left, weights, pre, pay, weight, add=None):
    for start in range(0, pre.shape[1], COLS):
        cols = slice(start, start + COLS)
        out = dot(left[...], weights[:, cols])
        if add is not None:
            out = out + add[:, cols]
        pre[:, cols] = out
        put_moments(out, pay, cols, weight)


def fold(values):
    return jnp.sum(values.reshape(-1, 8, values.shape[-1]), axis=0)


def push(grad_of, pre, center, rstd, gain, offset, pushed, pay):
    def body(rows, sums):
        unit = (pre[rows, :].astype(F32) - center) * rstd
        out = grad_of(rows) * mish_slope(unit * gain + offset)
        pushed[rows, :] = out
        return sums[0] + fold(out), sums[1] + fold(out * unit)

    zero = jnp.zeros((8, pre.shape[1]), F32)
    first, second = rows_loop(pre.shape[0], body, (zero, zero), 16)
    pay[0:1, :] = jnp.sum(first, axis=0, keepdims=True)
    pay[1:2, :] = jnp.sum(second, axis=0, keepdims=True)


def settle(scal, refs, pushed, pre, coef, gain, out, sums):
    first, second = finish_sums(refs)
    sums[0:1, :] = first
    sums[1:2, :] = second
    over = 1.0 / scal[1]
    center, rstd = coef[0:1, :], coef[1:2, :]
    scale = gain * rstd * scal[0]
    level, tilt = first * over, second * over * rstd

    def body(rows, _):
        x = pre[rows, :].astype(F32) - center
        out[rows, :] = (scale * (pushed[rows, :] - level - x * tilt)).astype(BF)

    rows_loop(pre.shape[0], body)


def own_taps(x, w, out):
    slots = x.shape[0]
    for tap in (1, 2):
        blocks = []
        for slot in range(slots):
            both = x[slot, tap - 1]
            blocks.append(shifted_row(both))
        left = jnp.concatenate(blocks, axis=0)
        part = dot(left, w[tap - 1])
        out[...] = part if tap == 1 else out[...] + part


def shifted_row(both):
    half = both.shape[1] // 2
    odd = both[:, half:].astype(F32)
    first = lax.broadcasted_iota(jnp.int32, odd.shape, 0) == 0
    before = jnp.where(first, 0.0, pltpu.roll(odd, 1, 0)).astype(BF)
    return jnp.concatenate([before, both], axis=1)


def borrowed_taps(scal, x, w, part, rows, pay):
    slots, cells = x.shape[0], x.shape[1]
    left = jnp.concatenate([shifted_row(x[slot]) for slot in range(slots)], axis=0)
    out = dot(left, w[...]) + part[...]
    rows[...] = out.astype(BF)
    total = sum(
        jnp.sum(out[slot * cells : (slot + 1) * cells], axis=0, keepdims=True) * scal[slot]
        for slot in range(slots)
    )
    mean = total * scal[slots]
    spread = 0.0
    for slot in range(slots):
        off = out[slot * cells : (slot + 1) * cells] - mean
        spread += jnp.sum(off * off, axis=0, keepdims=True) * scal[slot]
    pay[0:1, :] = total
    pay[1:2, :] = spread


def main_kernel(pieces, scal, spots, got, counts, over, gains, shifts, *rest):
    parts = rest[:pieces]
    w_main, down_pre, sectioned, main_pre, pay, coef = rest[pieces:]
    pixels = scal[1]
    firsts, seconds = got[:, 0, :], got[:, 1, :]
    center = jnp.sum(firsts, axis=0, keepdims=True) / pixels
    gap = firsts * over[...] - center
    total = jnp.sum(seconds + gap * gap * counts[...], axis=0, keepdims=True)
    rstd = lax.rsqrt(total / pixels + EPSILON)
    coef[0:1, :] = center
    coef[1:2, :] = rstd
    scale, offset = rstd * gains[0:1, :], shifts[0:1, :]
    for k, part in enumerate(parts):
        width = part.shape[0] // 2
        for side in range(2):
            start = spots[2 * k + side] * width

            def body(index, _, part=part, side=side, start=start, width=width):
                src = pl.ds(pl.multiple_of(side * width + index * CHUNK, CHUNK), CHUNK)
                dst = pl.ds(pl.multiple_of(start + index * CHUNK, CHUNK), CHUNK)
                x = part[src, :]
                down_pre[dst, :] = x
                value = (x.astype(F32) - center) * scale + offset
                sectioned[dst, :] = mish(value).astype(BF)

            lax.fori_loop(0, width // CHUNK, body, None)
    project(sectioned, w_main, main_pre, pay, scal[0])


def short_kernel(scal, sectioned, w_short, short_pre, pay):
    project(sectioned, w_short, short_pre, pay, scal[0])


def inner_kernel(groups, scal, *rest):
    refs = rest[:groups]
    pre, gains, shifts, w_inner, mainline, inner_pre, pay, coef = rest[groups:]
    center, rstd = finish_moments(scal, refs)
    coef[0:1, :] = center
    coef[1:2, :] = rstd
    scale, offset = rstd * gains[1:2, :], shifts[1:2, :]

    def body(rows, _):
        mainline[rows, :] = mish((pre[rows, :] - center) * scale + offset).astype(BF)

    rows_loop(pre.shape[0], body)
    project(mainline, w_inner, inner_pre, pay, scal[0])


def three_shifts(values, rim, start, forward):
    width, half = values.shape
    place = lax.broadcasted_iota(jnp.int32, values.shape, 0)
    before = jnp.where(place == 0, 0.0, pltpu.roll(values, 1, 0)).astype(BF)
    after = jnp.where(place == width - 1, 0.0, pltpu.roll(values, width - 1, 0)).astype(BF)
    sides = (before, after) if forward else (after, before)
    rows = pl.ds(start, width)
    rim[rows, 0:half] = sides[0]
    rim[rows, half : 2 * half] = values.astype(BF)
    rim[rows, 2 * half : 3 * half] = sides[1]


def spatial_kernel(groups, width, scal, *rest):
    refs = rest[:groups]
    pre, gains, shifts, w_spatial, rim, spatial_pre, pay, coef = rest[groups:]
    cells, half = pre.shape
    center, rstd = finish_moments(scal, refs)
    coef[0:1, :] = center
    coef[1:2, :] = rstd
    scale, offset = rstd * gains[2:3, :], shifts[2:3, :]
    blank = jnp.zeros((width, 3 * half), BF)
    rim[0:width, :] = blank
    rim[width + cells :, :] = blank

    def body(index, _):
        start = pl.multiple_of(index * width, width)
        act = mish((pre[pl.ds(start, width), :] - center) * scale + offset)
        three_shifts(act, rim, pl.multiple_of(start + width, width), True)

    lax.fori_loop(0, cells // width, body, None)
    for begin in range(0, half, COLS):
        cols = slice(begin, begin + COLS)
        out = sum(
            dot(
                rim[i * width : i * width + cells, :],
                w_spatial[i * 3 * half : (i + 1) * 3 * half, cols],
            )
            for i in range(3)
        )
        spatial_pre[:, cols] = out
        put_moments(out, pay, cols, scal[0])


def trans_kernel(groups, scal, *rest):
    refs = rest[:groups]
    pre, mainline, gains, shifts, w_trans, merged, trans_pre, pay, coef = rest[groups:]
    center, rstd = finish_moments(scal, refs)
    coef[0:1, :] = center
    coef[1:2, :] = rstd
    scale, offset = rstd * gains[3:4, :], shifts[3:4, :]

    def body(rows, _):
        act = mish((pre[rows, :] - center) * scale + offset)
        merged[rows, :] = (mainline[rows, :].astype(F32) + act).astype(BF)

    rows_loop(pre.shape[0], body)
    project(merged, w_trans, trans_pre, pay, scal[0])


def shortcut_kernel(groups, scal, *rest):
    refs = rest[:groups]
    pre, gains, shifts, w_unite, shortcut, part, coef = rest[groups:]
    half = pre.shape[1]
    center, rstd = finish_moments(scal, refs)
    coef[0:1, :] = center
    coef[1:2, :] = rstd
    scale, offset = rstd * gains[0:1, :], shifts[0:1, :]

    def body(rows, _):
        shortcut[rows, :] = mish((pre[rows, :] - center) * scale + offset).astype(BF)

    rows_loop(pre.shape[0], body)
    for start in range(0, part.shape[1], COLS):
        cols = slice(start, start + COLS)
        part[:, cols] = dot(shortcut[...], w_unite[0:half, cols])


def unite_kernel(groups, scal, *rest):
    refs = rest[:groups]
    pre, part, gains, shifts, w_unite, transition, unite_pre, pay, coef = rest[groups:]
    half = pre.shape[1]
    center, rstd = finish_moments(scal, refs)
    coef[0:1, :] = center
    coef[1:2, :] = rstd
    scale, offset = rstd * gains[4:5, :], shifts[4:5, :]

    def body(rows, _):
        transition[rows, :] = mish((pre[rows, :] - center) * scale + offset).astype(BF)

    rows_loop(pre.shape[0], body)
    project(transition, w_unite.at[half:, :], unite_pre, pay, scal[0], part)


def turn_kernel(groups, pieces, scal, spots, *rest):
    refs = rest[:groups]
    parts = rest[groups : groups + pieces]
    pre, gains, shifts, pushed, output, pay, coef = rest[groups + pieces :]
    center, rstd = finish_moments(scal, refs)
    coef[0:1, :] = center
    coef[1:2, :] = rstd
    gain, offset, weight = gains[1:2, :], shifts[1:2, :], scal[0]
    sums = (jnp.zeros((8, pre.shape[1]), F32),) * 2
    for k, part in enumerate(parts):
        width = part.shape[0] // 2
        for side in range(2):
            start = spots[2 * k + side] * width

            def body(index, sums, part=part, side=side, start=start, width=width):
                src = pl.ds(pl.multiple_of(side * width + index * 16, 16), 16)
                dst = pl.ds(pl.multiple_of(start + index * 16, 16), 16)
                unit = (pre[dst, :] - center) * rstd
                value = unit * gain + offset
                grown = jnp.exp(jnp.minimum(value, FAR))
                wide = grown * (grown + 2.0)
                share = 1.0 / (wide + 2.0)
                level = wide * share
                output[dst, :] = (value * level * weight).astype(BF)
                slope = level + 4.0 * value * (grown * (grown + 1.0) * share) * share
                out = part[src, :].astype(F32) * weight * slope
                pushed[dst, :] = out
                return sums[0] + fold(out), sums[1] + fold(out * unit)

            sums = lax.fori_loop(0, width // 16, body, sums)
    pay[0:1, :] = jnp.sum(sums[0], axis=0, keepdims=True)
    pay[1:2, :] = jnp.sum(sums[1], axis=0, keepdims=True)


def back_trans_kernel(groups, scal, *rest):
    refs = rest[:groups]
    (
        unite_pushed, unite_pre, unite_coef, gains_wide, w_unite, trans_pre, trans_coef, gains, shifts,
        grad_unite, sums, pushed, pay, scratch,
    ) = rest[groups:]
    half = trans_pre.shape[1]
    settle(scal, refs, unite_pushed, unite_pre, unite_coef, gains_wide[1:2, :], grad_unite, sums)
    for start in range(0, half, COLS):
        scratch[:, start : start + COLS] = dot_back(
            grad_unite[...], w_unite[half + start : half + start + COLS, :]
        )
    push(
        lambda rows: scratch[rows, :],
        trans_pre, trans_coef[0:1, :], trans_coef[1:2, :], gains[4:5, :], shifts[4:5, :],
        pushed, pay,
    )


def back_short_kernel(grad_unite, w_unite, pre, coef, gains, shifts, pushed, pay, scratch):
    half = pre.shape[1]
    for start in range(0, half, COLS):
        scratch[:, start : start + COLS] = dot_back(
            grad_unite[...], w_unite[start : start + COLS, :]
        )
    push(
        lambda rows: scratch[rows, :],
        pre, coef[0:1, :], coef[1:2, :], gains[0:1, :], shifts[0:1, :], pushed, pay,
    )


def back_spatial_kernel(groups, scal, *rest):
    refs = rest[:groups]
    (
        trans_pushed, trans_pre, trans_coef, w_trans, spatial_pre, spatial_coef, gains, shifts,
        grad_trans, sums, grad_merged, pushed, pay,
    ) = rest[groups:]
    half = trans_pre.shape[1]
    settle(scal, refs, trans_pushed, trans_pre, trans_coef, gains[4:5, :], grad_trans, sums)
    for start in range(0, half, COLS):
        grad_merged[:, start : start + COLS] = dot_back(
            grad_trans[...], w_trans[start : start + COLS, :]
        )
    push(
        lambda rows: grad_merged[rows, :],
        spatial_pre, spatial_coef[0:1, :], spatial_coef[1:2, :], gains[3:4, :], shifts[3:4, :],
        pushed, pay,
    )


def back_inner_kernel(groups, width, scal, *rest):
    refs = rest[:groups]
    (
        spatial_pushed, spatial_pre, spatial_coef, w_spatial, inner_pre, inner_coef, gains, shifts,
        grad_spatial, sums, pushed, pay, rim, scratch,
    ) = rest[groups:]
    cells, half = spatial_pre.shape
    settle(scal, refs, spatial_pushed, spatial_pre, spatial_coef, gains[3:4, :], grad_spatial, sums)
    blank = jnp.zeros((width, 3 * half), BF)
    rim[0:width, :] = blank
    rim[width + cells :, :] = blank

    def body(index, _):
        start = pl.multiple_of(index * width, width)
        values = grad_spatial[pl.ds(start, width), :].astype(F32)
        three_shifts(values, rim, pl.multiple_of(start + width, width), False)

    lax.fori_loop(0, cells // width, body, None)
    for start in range(0, half, COLS):
        scratch[:, start : start + COLS] = sum(
            dot_back(
                rim[(2 - i) * width : (2 - i) * width + cells, j * half : (j + 1) * half],
                w_spatial[(3 * i + j) * half + start : (3 * i + j) * half + start + COLS, :],
            )
            for i in range(3)
            for j in range(3)
        )
    push(
        lambda rows: scratch[rows, :],
        inner_pre, inner_coef[0:1, :], inner_coef[1:2, :], gains[2:3, :], shifts[2:3, :],
        pushed, pay,
    )


def back_main_kernel(groups, scal, *rest):
    refs = rest[:groups]
    (
        inner_pushed, inner_pre, inner_coef, w_inner, grad_merged, main_pre, main_coef, gains, shifts,
        grad_inner, sums, pushed, pay, scratch,
    ) = rest[groups:]
    half = inner_pre.shape[1]
    settle(scal, refs, inner_pushed, inner_pre, inner_coef, gains[2:3, :], grad_inner, sums)
    for start in range(0, half, COLS):
        cols = slice(start, start + COLS)
        scratch[:, cols] = grad_merged[:, cols] + dot_back(grad_inner[...], w_inner[cols, :])
    push(
        lambda rows: scratch[rows, :],
        main_pre, main_coef[0:1, :], main_coef[1:2, :], gains[1:2, :], shifts[1:2, :],
        pushed, pay,
    )


def settle_short_kernel(groups, scal, *rest):
    refs = rest[:groups]
    pushed, pre, coef, gains, w_short, grad_short, sums, part = rest[groups:]
    settle(scal, refs, pushed, pre, coef, gains[0:1, :], grad_short, sums)
    for start in range(0, part.shape[1], COLS):
        part[:, start : start + COLS] = dot_back(grad_short[...], w_short[start : start + COLS, :])


def back_down_kernel(groups, scal, *rest):
    refs = rest[:groups]
    (
        main_pushed, main_pre, main_coef, w_main, part, down_pre, down_coef, gains, gains_wide, shifts_wide,
        grad_main, sums, pushed, pay, scratch,
    ) = rest[groups:]
    settle(scal, refs, main_pushed, main_pre, main_coef, gains[1:2, :], grad_main, sums)
    for start in range(0, part.shape[1], COLS):
        cols = slice(start, start + COLS)
        scratch[:, cols] = part[:, cols] + dot_back(grad_main[...], w_main[cols, :])
    push(
        lambda rows: scratch[rows, :],
        down_pre, down_coef[0:1, :], down_coef[1:2, :], gains_wide[0:1, :], shifts_wide[0:1, :],
        pushed, pay,
    )


def settle_down_kernel(groups, scal, *rest):
    refs = rest[:groups]
    pushed, pre, coef, gains_wide, grad_down, sums = rest[groups:]
    settle(scal, refs, pushed, pre, coef, gains_wide[0:1, :], grad_down, sums)


SMEM = pl.BlockSpec(memory_space=pltpu.SMEM)
VMEM = pl.BlockSpec(memory_space=pltpu.VMEM)


def shape(dims, dtype=F32):
    return jax.ShapeDtypeStruct(dims, dtype)


def nbytes(dims, dtype):
    count = 1
    for d in dims:
        count *= d
    return count * jnp.dtype(dtype).itemsize


def call(kernel, name, scalars, arrays, outs, flops, scratch=()):
    moved = sum(nbytes(a.shape, a.dtype) for a in (*arrays, *outs))
    held = moved + sum(nbytes(s.shape, s.dtype) for s in scratch)
    return pl.pallas_call(
        kernel,
        name=name,
        out_shape=tuple(outs),
        in_specs=[SMEM] * len(scalars) + [VMEM] * len(arrays),
        out_specs=tuple([VMEM] * len(outs)),
        scratch_shapes=tuple(pltpu.VMEM(s.shape, s.dtype) for s in scratch),
        compiler_params=pltpu.CompilerParams(vmem_limit_bytes=held + (10 << 20)),
        cost_estimate=pl.CostEstimate(flops=flops, bytes_accessed=moved, transcendentals=0),
    )(*scalars, *arrays)


def first_conv(scal, view, above, w_down):
    slots, _, cells, both = view.shape
    half = both // 2
    full = w_down.shape[-1]
    taps = w_down.reshape(3, 3 * half, full)
    wide = 256
    part = pl.pallas_call(
        own_taps,
        name="own_taps",
        grid=(full // wide,),
        out_shape=shape((slots * cells, full)),
        in_specs=[
            pl.BlockSpec((slots, 2, cells, both), lambda n: (0, 0, 0, 0)),
            pl.BlockSpec((pl.Element(2), pl.Element(3 * half), pl.Element(wide)), lambda n: (1, 0, n * wide)),
        ],
        out_specs=pl.BlockSpec((slots * cells, wide), lambda n: (0, n)),
        compiler_params=pltpu.CompilerParams(vmem_limit_bytes=24 << 20),
        cost_estimate=pl.CostEstimate(
            flops=4 * slots * cells * 3 * half * full, bytes_accessed=2 * 2 * 3 * half * full, transcendentals=0
        ),
    )(view, taps)
    rows, pay = pl.pallas_call(
        borrowed_taps,
        name="borrowed_taps",
        grid=(full // wide,),
        out_shape=(shape((slots * cells, full), BF), shape((2, full))),
        in_specs=[
            SMEM,
            pl.BlockSpec((slots, cells, both), lambda n: (0, 0, 0)),
            pl.BlockSpec((None, 3 * half, wide), lambda n: (0, 0, n)),
            pl.BlockSpec((slots * cells, wide), lambda n: (0, n)),
        ],
        out_specs=(
            pl.BlockSpec((slots * cells, wide), lambda n: (0, n)),
            pl.BlockSpec((2, wide), lambda n: (0, n)),
        ),
        compiler_params=pltpu.CompilerParams(vmem_limit_bytes=24 << 20),
        cost_estimate=pl.CostEstimate(
            flops=2 * slots * cells * 3 * half * full, bytes_accessed=2 * 3 * half * full, transcendentals=0
        ),
    )(scal, above, taps, part)
    return rows.reshape(slots, cells, full), pay


def flipped(kernel):
    return jnp.swapaxes(jnp.flip(kernel, (0, 1)), 2, 3)


def on_device(
    inputs,
    image_counts,
    w_down,
    w_short,
    w_main,
    w_inner,
    w_spatial,
    w_trans,
    w_unite,
    gains_wide,
    gains_narrow,
    shifts_wide,
    shifts_narrow,
    grad_output,
):
    half = w_short.shape[1]
    full = 2 * half
    slots, height_dev, width, _ = grad_output.shape
    here = Plane()
    groups, chips = here.groups, here.chips
    height = here.rows * height_dev
    cells = height * width
    batch = lax.axis_index("batch")
    counts = image_counts.astype(F32)
    own_count = image_counts[batch]
    pixels = jnp.sum(counts) * cells
    weight = (here.core < own_count).astype(F32)

    scal = [weight, pixels]
    for step in range(groups):
        plane = batch ^ step
        for slot in (here.core, 1 - here.core):
            count = (slot < image_counts[plane]).astype(F32) * cells
            scal += [count, 1.0 / jnp.maximum(count, 1.0)]
    scal = jnp.stack(scal)
    spots = jnp.stack(
        [2 * (here.chip ^ step) + (here.core ^ side) for step in range(chips) for side in range(2)]
    ).astype(jnp.int32)
    slot_scal = jnp.concatenate(
        [
            (jnp.arange(slots) < own_count).astype(F32),
            (1.0 / (own_count.astype(F32) * height_dev * width))[None],
        ]
    )
    device_counts = jnp.tile(counts * (height_dev * width), here.rows).reshape(-1, 1)

    view = inputs.reshape(slots, 2, width, 2 * half)
    below = [(i, i + 1) for i in range(here.rows - 1)]
    above = lax.ppermute(view[:, 1], "rows", below)
    down_rows, sums = first_conv(slot_scal, view, above, w_down)
    devices = here.rows * groups
    gathered = lax.all_to_all(
        jnp.broadcast_to(sums[None], (devices,) + sums.shape), ("rows", "batch"), 0, 0, tiled=True
    )
    down_pieces = here.pieces(*here.split(down_rows))
    grad_pieces = here.pieces(*here.split(grad_output.reshape(slots, width, full)))
    down_pre, sectioned, main_pre, main_pay, down_coef = call(
        functools.partial(main_kernel, chips),
        "main",
        [scal, spots],
        [gathered, device_counts, 1.0 / device_counts, gains_wide, shifts_wide, *down_pieces, w_main],
        [
            shape((cells, full), BF), shape((cells, full), BF), shape((cells, half)),
            shape((2, half)), shape((2, full)),
        ],
        2 * cells * full * half,
    )
    narrow = [gains_narrow, shifts_narrow]

    main_all = here.everywhere(main_pay)
    short_pre, short_pay = call(
        short_kernel,
        "short",
        [scal],
        [sectioned, w_short],
        [shape((cells, half)), shape((2, half))],
        2 * cells * full * half,
    )
    mainline, inner_pre, inner_pay, main_coef = call(
        functools.partial(inner_kernel, groups),
        "inner",
        [scal],
        [*main_all, main_pre, *narrow, w_inner],
        [shape((cells, half), BF), shape((cells, half)), shape((2, half)), shape((2, half))],
        2 * cells * half * half,
    )
    inner_all = here.everywhere(inner_pay)
    rim, spatial_pre, spatial_pay, inner_coef = call(
        functools.partial(spatial_kernel, groups, width),
        "spatial",
        [scal],
        [*inner_all, inner_pre, *narrow, w_spatial.reshape(9 * half, half)],
        [
            shape((cells + 2 * width, 3 * half), BF), shape((cells, half)),
            shape((2, half)), shape((2, half)),
        ],
        18 * cells * half * half,
    )
    both_all = here.everywhere(jnp.concatenate([spatial_pay, short_pay], axis=1))
    spatial_all = [b[:, :half] for b in both_all]
    short_all = [b[:, half:] for b in both_all]
    merged, trans_pre, trans_pay, spatial_coef = call(
        functools.partial(trans_kernel, groups),
        "trans",
        [scal],
        [*spatial_all, spatial_pre, mainline, *narrow, w_trans],
        [shape((cells, half), BF), shape((cells, half)), shape((2, half)), shape((2, half))],
        2 * cells * half * half,
    )
    trans_all = here.everywhere(trans_pay)
    shortcut, unite_part, short_coef = call(
        functools.partial(shortcut_kernel, groups),
        "shortcut",
        [scal],
        [*short_all, short_pre, *narrow, w_unite],
        [shape((cells, half), BF), shape((cells, full)), shape((2, half))],
        2 * cells * half * full,
    )
    transition, unite_pre, unite_pay, trans_coef = call(
        functools.partial(unite_kernel, groups),
        "unite",
        [scal],
        [*trans_all, trans_pre, unite_part, *narrow, w_unite],
        [shape((cells, half), BF), shape((cells, full)), shape((2, full)), shape((2, half))],
        2 * cells * half * full,
    )
    unite_all = here.everywhere(unite_pay)
    unite_pushed, out_image, unite_pay, unite_coef = call(
        functools.partial(turn_kernel, groups, chips),
        "turn",
        [scal, spots],
        [*unite_all, *grad_pieces, unite_pre, gains_wide, shifts_wide],
        [shape((cells, full)), shape((cells, full), BF), shape((2, full)), shape((2, full))],
        40 * cells * full,
    )

    def own_rows(image, per_device):
        return [
            lax.dynamic_slice_in_dim(image, place * per_device, per_device, 0)
            for place in (here.place, here.place ^ 1)
        ]

    mine, other = own_rows(out_image, height_dev * width)
    output = jnp.stack(here.by_core(mine, here.swap(other))).reshape(grad_output.shape)

    unite_all = here.everywhere(unite_pay)
    grad_unite_pre, unite_sums, trans_pushed, trans_pay = call(
        functools.partial(back_trans_kernel, groups),
        "back_trans",
        [scal],
        [*unite_all, unite_pushed, unite_pre, unite_coef, gains_wide, w_unite, trans_pre, trans_coef, *narrow],
        [shape((cells, full), BF), shape((2, full)), shape((cells, half)), shape((2, half))],
        2 * cells * half * full,
        [shape((cells, half))],
    )
    trans_all = here.everywhere(trans_pay)
    short_pushed, short_pay = call(
        back_short_kernel,
        "back_short",
        [],
        [grad_unite_pre, w_unite, short_pre, short_coef, *narrow],
        [shape((cells, half)), shape((2, half))],
        2 * cells * half * full,
        [shape((cells, half))],
    )
    grad_trans_pre, trans_sums, grad_merged, spatial_pushed, spatial_pay = call(
        functools.partial(back_spatial_kernel, groups),
        "back_spatial",
        [scal],
        [*trans_all, trans_pushed, trans_pre, trans_coef, w_trans, spatial_pre, spatial_coef, *narrow],
        [
            shape((cells, half), BF), shape((2, half)), shape((cells, half)), shape((cells, half)),
            shape((2, half)),
        ],
        2 * cells * half * half,
    )
    both_all = here.everywhere(jnp.concatenate([spatial_pay, short_pay], axis=1))
    spatial_all = [b[:, :half] for b in both_all]
    short_all = [b[:, half:] for b in both_all]
    grad_spatial_pre, spatial_sums, inner_pushed, inner_pay = call(
        functools.partial(back_inner_kernel, groups, width),
        "back_inner",
        [scal],
        [
            *spatial_all, spatial_pushed, spatial_pre, spatial_coef, w_spatial.reshape(9 * half, half),
            inner_pre, inner_coef, *narrow,
        ],
        [shape((cells, half), BF), shape((2, half)), shape((cells, half)), shape((2, half))],
        18 * cells * half * half,
        [shape((cells + 2 * width, 3 * half), BF), shape((cells, half))],
    )
    inner_all = here.everywhere(inner_pay)
    grad_short_pre, short_sums, sectioned_part = call(
        functools.partial(settle_short_kernel, groups),
        "settle_short",
        [scal],
        [*short_all, short_pushed, short_pre, short_coef, gains_narrow, w_short],
        [shape((cells, half), BF), shape((2, half)), shape((cells, full))],
        2 * cells * half * full,
    )
    grad_inner_pre, inner_sums, main_pushed, main_pay = call(
        functools.partial(back_main_kernel, groups),
        "back_main",
        [scal],
        [*inner_all, inner_pushed, inner_pre, inner_coef, w_inner, grad_merged, main_pre, main_coef, *narrow],
        [shape((cells, half), BF), shape((2, half)), shape((cells, half)), shape((2, half))],
        2 * cells * half * half,
        [shape((cells, half))],
    )
    main_all = here.everywhere(main_pay)
    grad_main_pre, main_sums, down_pushed, down_pay = call(
        functools.partial(back_down_kernel, groups),
        "back_down",
        [scal],
        [
            *main_all, main_pushed, main_pre, main_coef, w_main, sectioned_part, down_pre, down_coef,
            gains_narrow, gains_wide, shifts_wide,
        ],
        [shape((cells, half), BF), shape((2, half)), shape((cells, full)), shape((2, full))],
        2 * cells * half * full,
        [shape((cells, full))],
    )
    down_all = here.everywhere(down_pay)
    grad_down_pre, down_sums = call(
        functools.partial(settle_down_kernel, groups),
        "settle_down",
        [scal],
        [*down_all, down_pushed, down_pre, down_coef, gains_wide],
        [shape((cells, full), BF), shape((2, full))],
        10 * cells * full,
    )

    def share(values, grad):
        columns = grad.shape[1] // chips
        grad = lax.dynamic_slice_in_dim(grad, here.chip * columns, columns, 1)
        part = jnp.concatenate([dot_cells(v, grad) for v in values], axis=0)
        mine, other = here.split(part.reshape(part.shape[0], 2, columns // 2), 1)
        return (mine + here.swap(other.astype(BF)).astype(F32)).astype(BF)

    windows = [rim[i * width : i * width + cells] for i in range(3)]
    early = lax.psum(
        (
            share([sectioned], grad_short_pre),
            share([sectioned], grad_main_pre),
            share([mainline], grad_inner_pre),
            share(windows, grad_spatial_pre),
            share([merged], grad_trans_pre),
            jnp.concatenate([share([shortcut], grad_unite_pre), share([transition], grad_unite_pre)]),
        ),
        "batch",
    )
    early = [e.astype(F32) for e in early]

    mine, other = here.split(view)
    got = here.chip_hops(jnp.stack([mine, here.swap(other)], axis=1))
    source = jnp.zeros((2, here.rows, width, full), BF)
    for step, piece in enumerate(got):
        for side in range(2):
            source = lax.dynamic_update_slice_in_dim(
                source, piece[:, side : side + 1], spots[2 * step + side], 1
            )
    grad_map = grad_down_pre.reshape(height, width, full)
    columns = full // chips
    grad_cut = lax.dynamic_slice_in_dim(grad_map, here.chip * columns, columns, 2)
    ahead = jnp.pad(grad_cut[:, 1:], ((0, 0), (0, 1), (0, 0)))
    upper = jnp.pad(grad_cut[1:], ((0, 1), (0, 0), (0, 0)))
    both_ahead = jnp.pad(ahead[1:], ((0, 1), (0, 0), (0, 0)))
    even_rows = source[0].reshape(cells, full)
    odd_rows = source[1].reshape(cells, full)

    def taps_of(rows, here_grad, ahead_grad):
        plain = dot_cells(rows, here_grad.reshape(cells, columns))
        before = dot_cells(rows[:, half:], ahead_grad.reshape(cells, columns))
        return [before, plain]

    part = jnp.concatenate(
        taps_of(odd_rows, upper, both_ahead)
        + taps_of(even_rows, grad_cut, ahead)
        + taps_of(odd_rows, grad_cut, ahead),
        axis=0,
    )
    mine, other = here.split(part.reshape(9 * half, 2, columns // 2), 1)
    part = (mine + here.swap(other.astype(BF)).astype(F32)).astype(BF)
    grad_w_down = lax.psum(part, "batch").astype(F32)

    pair_rows = 2 * height_dev
    grad_image = jnp.pad(grad_map, ((0, 1), (0, 0), (0, 0)))
    grad_block = lax.dynamic_slice_in_dim(grad_image, here.chip * pair_rows, pair_rows + 1, 0)
    widened = lax.conv_general_dilated(
        grad_block[None],
        flipped(w_down),
        (1, 1),
        ((1, 0), (1, 2)),
        lhs_dilation=(2, 2),
        dimension_numbers=("NHWC", "HWIO", "NHWC"),
        preferred_element_type=F32,
    )[0]
    mine = lax.dynamic_slice_in_dim(widened, here.core * pair_rows, pair_rows, 0)
    other = lax.dynamic_slice_in_dim(widened, (1 - here.core) * pair_rows, pair_rows, 0)
    grad_inputs = jnp.stack(here.by_core(mine, here.swap(other)))

    narrow_sums = [short_sums, main_sums, inner_sums, spatial_sums, trans_sums]
    return (
        output,
        grad_inputs,
        grad_w_down.reshape(3, 3, half, -1),
        early[0],
        early[1],
        early[2],
        early[3].reshape(3, 3, half, -1),
        early[4],
        early[5],
        jnp.stack([down_sums[1], unite_sums[1]]),
        jnp.stack([s[1] for s in narrow_sums]),
        jnp.stack([down_sums[0], unite_sums[0]]),
        jnp.stack([s[0] for s in narrow_sums]),
    )


def solution(mesh):
    placed = (P("batch", "rows", None, None),) + (P(),) * 12 + (P("batch", "rows", None, None),)
    return jax.shard_map(
        on_device,
        mesh=mesh,
        in_specs=placed,
        out_specs=(
            P("batch", "rows", None, None),
            P("batch", "rows", None, None),
            P(None, None, None, "rows"),
            P(None, "rows"),
            P(None, "rows"),
            P(None, "rows"),
            P(None, None, None, "rows"),
            P(None, "rows"),
            P(None, "rows"),
            P(),
            P(),
            P(),
            P(),
        ),
        check_vma=False,
    )
```

time: 545 us -> 391 us (0.72); the launches traced: 536 us -> 389 us
  local copies, waits for them, and re-layouts: 178 us -> 86.5 us
  other arithmetic: 86.3 us -> 30.1 us
  Pallas kernels: 0 us -> 47.5 us
  matrix products: 56.5 us -> 17.5 us
  waiting for transfers between devices: 123 us -> 114 us
    slice x22 -> x17, local copies, waits for them, and re-layouts: 90.3 us -> 3.71 us  [the longest x1 3.41 us: on_device(): even_rows = source[0].reshape(cells, full)]
    pallas_call x0 -> x18, Pallas kernels: none -> 47.5 us  [the longest x16 42.8 us: call(): pl.pallas_call(kernel, name=name, out_shape=tuple(outs), in_specs=[SMEM]...]
    unnamed x266 -> x161, local copies, waits for them, and re-layouts: 7.61 us -> 35.4 us
    dot_general x33 -> x15, matrix products: 34.7 us -> 11.6 us  [dot_cells(): lax.dot_general(a, b, (((0,), (0,)), ((), ())), preferred_element_type=F32)]
    mul x15 -> x1, other arithmetic: 20.3 us -> 0.6 us  [on_device(): counts * (height_dev * width)]
    convert_element_type x26 -> x15, other arithmetic: 34.8 us -> 19 us  [the longest x7 7.48 us: share(): return (mine + here.swap(other.astype(BF)).astype(F32)).astype(BF)]
    conv_general_dilated x3 -> x0, matrix products: 15.6 us -> none  [the longest x1 5.4 us: on_device(): lax.conv_general_dilated(down_source, w_down, (2, 2), ((0, 0), (0, 0)), d...]
    reduce_sum x13 -> x0, other arithmetic: 11.7 us -> none  [the longest x3 8.27 us: incoming(): jnp.sum(self.pushed, axis=0)]
  transfers between devices with their start and end apart: 68 -> 69, of which waited for: 16 -> 24; matrix products, arithmetic and copies ran while one was open for 55% -> 24% of each run, Pallas kernels for 0% -> 11%
where the time goes in v2:
time: 391 us; the launch traced here: 389 us
  waiting for transfers between devices  114 us (29%)
  local copies, waits for them, and re-layouts  86.5 us (22%)
  starting transfers between devices  71.7 us (18%)
  Pallas kernels  47.5 us (12%)
  other arithmetic  30.1 us (8%)
  between operations  22.3 us (6%)
  matrix products  17.5 us (4%)
    psum x1, waiting for transfers between devices, on_device(): lax.psum((share([sectioned], grad_short_pre), share([sectioned], grad_mai...  93.8 us
    ppermute x33, starting transfers between devices, plane_hops(): lax.ppermute(value, 'batch', [(i, i ^ step) for i in range(self.groups)])  49 us
    pallas_call x16, Pallas kernels, call(): pl.pallas_call(kernel, name=name, out_shape=tuple(outs), in_specs=[SMEM]...  42.8 us
    unnamed x161, local copies, waits for them, and re-layouts  35.4 us
    ppermute x33, waiting for transfers between devices, plane_hops(): lax.ppermute(value, 'batch', [(i, i ^ step) for i in range(self.groups)])  17 us
    dot_general x15, matrix products, dot_cells(): lax.dot_general(a, b, (((0,), (0,)), ((), ())), preferred_element_type=F32)  11.6 us
    ppermute x9, starting transfers between devices, chip_hops(): lax.ppermute(value, 'rows', [(i, i ^ 2 * step) for i in range(self.rows)])  9.76 us
    dynamic_slice x2, local copies, waits for them, and re-layouts, split(): other = lax.dynamic_index_in_dim(block, 1 - self.core, axis, keepdims=False)  8.55 us
  transfers between devices with their start and end apart: 69, of which 24 were waited for; matrix products, arithmetic and copies ran while one was open for 24% of the time, Pallas kernels for 11%

profile of v2, /device:TPU:0, one launch (start us, length us, event | category | flops | bytes accessed | tf_op | source)
XLA Modules:
  0.0 389.3 jit_solution(15098562324754767963)
XLA Ops:
  7.2 1.7 dynamic-slice_bitcast_fusion.3
  11.4 2.4 collective-permute-start
  15.8 3.7 copy-done
  19.5 2.5 own_taps.1.part
  22.7 2.2 borrowed_taps.1
  24.9 2.7 collective-permute-start.1
  28.3 4.9 %all-to-all-start = ((f32[32,2,1024]{2,1,0:T(2,128)}), f32[32,2,1024]{2,1,0:T(2,128)S(1)}, u32[]{:S(2)}, u32[]{:S(2)}) async-start(f32[32,2,1024]{2,1,0:T(2,128)} %broadcast_in_dim.16), calls=%async_computation | async-start | bytes 524288 | tf_op jit(solution)/shard_map/all_to_all | solution.py:643
  33.4 2.7 collective-permute-start.4
  45.9 1.9 pad_maximum_fusion.2
  47.8 1.8 collective-permute-start.56
  58.1 3.4 main.1
  62.7 3.4 collective-permute-start.8
  68.9 1.7 collective-permute-done.7.rest_2_
  71.7 1.9 inner.1
  73.7 1.9 slice_dynamic-update-slice_fusion.5
  75.6 2.0 collective-permute-start.12
  77.8 2.3 collective-permute-start.10
  80.1 1.7 slice_dynamic-update-slice_fusion.4
  83.2 2.3 copy-done.55
  85.5 4.0 %spatial.1 = (bf16[640,1536]{1,0:T(8,128)(2,1)S(1)}, f32[512,512]{1,0:T(8,128)S(1)}, f32[2,512]{1,0:T(2,128)S(1)}, f32[2,512]{1,0:T(2,128)S(1)}) custom-call(f32[18]{0:T(128)S(1)} %stack.145.scal, f32[4,512]{1,0:T(4,128)S(1)} %pad_maximum_fusion.12.rest_0_, f32[4,512]{1,0:T(4,128)S(1)} %collective-permute-done.10.rest_1_, ...), custom_call_target="tpu_custom_call" | custom-call | flops 2415919104 | bytes 8843264 | tf_op jit(solution)/shard_map/spatial/pallas_call | solution.py:531
  92.4 2.0 collective-permute-start.14
  96.1 3.8 collective-permute-done.16
  100.0 1.9 trans.1
  104.9 3.5 collective-permute-start.18
  108.3 2.0 shortcut.1
  111.5 2.2 unite.1
  115.0 2.0 collective-permute-start.24
  117.0 2.4 collective-permute-start.22
  121.6 3.3 turn.1
  124.9 3.4 fusion.62
  128.4 2.0 collective-permute-start.33
  135.2 3.3 back_trans.1
  141.4 1.8 copy.85
  143.2 1.6 copy.95
  145.7 1.7 copy.94
  147.9 2.0 collective-permute-start.37
  150.8 1.6 collective-permute-start.35
  154.8 2.0 back_short.1
  156.9 2.6 back_spatial.1
  163.3 1.9 collective-permute-start.41
  165.7 3.2 collective-permute-done.41
  168.9 2.3 copy-done.56
  171.2 5.0 %back_inner.1 = (bf16[512,512]{1,0:T(8,128)(2,1)S(1)}, f32[2,512]{1,0:T(2,128)S(1)}, f32[512,512]{1,0:T(8,128)S(1)}, f32[2,512]{1,0:T(2,128)S(1)}) custom-call(f32[18]{0:T(128)S(1)} %stack.145.scal, f32[4,512]{1,0:T(4,128)S(1)} %get-tuple-element.215.rest_0_, f32[4,512]{1,0:T(4,128)S(1)} %get-tuple-element.213.rest_1_, ...), custom_call_target="tpu_custom_call" | custom-call | flops 2415919104 | bytes 9506816 | tf_op jit(solution)/shard_map/back_inner/pallas_call | solution.py:531
  178.4 1.6 settle_short.1
  183.4 3.2 copy.82
  186.5 2.3 fusion.8
  188.8 2.0 collective-permute-start.45
  190.8 2.5 collective-permute-start.43
  198.9 2.6 back_main.1
  203.0 2.0 collective-permute-start.49
  209.8 4.1 %back_down.1 = (bf16[512,512]{1,0:T(8,128)(2,1)S(1)}, f32[2,512]{1,0:T(2,128)S(1)}, f32[512,1024]{1,0:T(8,128)S(1)}, f32[2,1024]{1,0:T(2,128)S(1)}) custom-call(f32[18]{0:T(128)S(1)} %stack.145.scal, f32[4,512]{1,0:T(4,128)S(1)} %pad_maximum_fusion.16.rest_0_, f32[4,512]{1,0:T(4,128)S(1)} %collective-permute-done.47.rest_1_, ...), custom_call_target="tpu_custom_call" | custom-call | flops 536870912 | bytes 8996864 | tf_op jit(solution)/shard_map/back_down/pallas_call | solution.py:531
  218.4 2.0 collective-permute-start.53
  225.7 1.6 copy-done.28
  237.8 6.8 %reshape.135 = f32[4608,2,128]{2,1,0:T(2,128)} reshape(f32[4608,256]{1,0:T(8,128)} %convolution_dynamic-update-slice_fusion) | data formatting | bytes 9437184 | tf_op jit(solution)/shard_map/reshape | solution.py:873
  244.5 7.8 %constant_dynamic-slice_fusion.6 = (f32[4608,1,128]{2,1,0:T(1,128)S(1)}, f32[4608,1,128]{2,1,0:T(1,128)S(1)}) fusion(f32[4608,2,128]{2,1,0:T(2,128)} %reshape.135, s32[]{:T(128)S(6)} %select_n.144, s32[]{:T(128)S(6)} %select_n.143), kind=kLoop, calls=%fused_computation.128 | loop fusion | bytes 9437192 | tf_op jit(solution)/shard_map/jit(dynamic_index_in_dim)/dynamic_slice | solution.py:79
  254.6 1.8 fusion.32
  263.1 2.5 add_convert_fusion
  266.3 5.9 %convolution_select_fusion = f32[4,8,18,512]{3,1,2,0:T(8,128)S(1)} fusion(bf16[3,3,512,1024]{3,2,1,0:T(8,128)(2,1)} %param.16, pred[8,18]{0,1:T(8,128)(4,1)S(1)} %copy-done.77, bf16[3,1,7,1,1024]{4,2,3,0,1:T(8,128)(2,1)S(1)} %slice.212, bf16[3,1,8,9,1024]{4,2,3,0,1:T(8,128)(2,1)S(1)} %copy.77), kind=kOutput, calls=%fused_computation.11 | convolution fusion | flops 1360723968 | bytes 11102352 | tf_op jit(solution)/shard_map/conv_general_dilated | solution.py:880
  277.5 93.8 %all-reduce.7.cloned.1.call-done = (bf16[3,3,512,64]{2,1,0,3:T(4,128)(2,1)}, bf16[3,3,512,128]{3,2,1,0:T(8,128)(2,1)}, bf16[1024,64]{0,1:T(8,128)(2,1)}, bf16[10...) async-done(((bf16[3,3,512,64]{2,1,0,3:T(4,128)(2,1)}, bf16[3,3,512,128]{3,2,1,0:T(8,128)(2,1)}, ...) | async-done | bytes 2424848 | tf_op jit(solution)/shard_map/psum | solution.py:832
  371.3 1.6 convert_element_type.159
  374.4 1.6 convert_element_type.149
  376.0 1.6 convert_element_type.154
  377.7 2.3 copy.88
  380.8 1.6 reshape.137
  (381 shorter events, 107.5 us)
Async XLA Ops:
  8.9 40.7 %collective-permute-start.25 = (bf16[64,1024]{1,0:T(8,128)(2,1)}, bf16[64,1024]{1,0:T(8,128)(2,1)}, u32[]{:S(2)}, u32[]{:S(2)}) collective-permute-start(bf16[64,1024]{1,0:T(8,128)(2,1)} %get-tuple-element.205), channel_id=1, source_target_pairs={{0,4},{4,0},{8,12},{12,8},{16,20},{20,16},{24,28},{28,24},{1,5},{5... | collective-permute-start | bytes 393224 | tf_op jit(solution)/shard_map/ppermute | solution.py:59
  11.3 34.6 %collective-permute-start.55 = (bf16[2,64,1024]{2,1,0:T(8,128)(2,1)}, bf16[2,64,1024]{2,1,0:T(8,128)(2,1)S(1)}, u32[]{:S(2)}, u32[]{:S(2)}) collective-permute-start(bf16[2,64,1024]{2,1,0:T(8,128)(2,1)} %dynamic-slice_bitcast_fusion), channel_id=1, source_target_pairs={{0,4},{4,0},{8,12},{12,8},{16,20},{20,16},{24,28},{28,24},{1,5},{5... | collective-permute-start | bytes 786440 | tf_op jit(solution)/shard_map/ppermute | solution.py:59
  11.4 11.3 %collective-permute-start = (bf16[2,64,1024]{2,1,0:T(8,128)(2,1)S(1)}, bf16[2,64,1024]{2,1,0:T(8,128)(2,1)S(1)}, u32[]{:S(2)}, u32[]{:S(2)}) collective-permute-start(bf16[2,64,1024]{2,1,0:T(8,128)(2,1)S(1)} %slice_bitcast_fusion), channel_id=1, source_target_pairs={{0,4},{4,8},{8,12},{12,16},{16,20},{20,24},{24,28},{1,5},{5,9},{9,... | collective-permute-start | bytes 786440 | tf_op jit(solution)/shard_map/ppermute | solution.py:640
  24.9 8.4 %collective-permute-start.1 = (bf16[64,1024]{1,0:T(8,128)(2,1)S(1)}, bf16[64,1024]{1,0:T(8,128)(2,1)S(1)}, u32[]{:S(2)}, u32[]{:S(2)}) collective-permute-start(bf16[64,1024]{1,0:T(8,128)(2,1)S(1)} %get-tuple-element.207), channel_id=1, source_target_pairs={{0,4},{4,0},{8,12},{12,8},{16,20},{20,16},{24,28},{28,24},{1,5},{5... | collective-permute-start | bytes 393224 | tf_op jit(solution)/shard_map/ppermute | solution.py:59
  28.3 25.2 %all-to-all-start = ((f32[32,2,1024]{2,1,0:T(2,128)}), f32[32,2,1024]{2,1,0:T(2,128)S(1)}, u32[]{:S(2)}, u32[]{:S(2)}) async-start(f32[32,2,1024]{2,1,0:T(2,128)} %broadcast_in_dim.16), calls=%async_computation | async-start | bytes 524288 | tf_op jit(solution)/shard_map/all_to_all | solution.py:643
  33.3 338.0 %all-reduce.7.cloned.1.call-start = ((), (), s32[]{:S(2)}) async-start(), calls=%async_computation.1 | async-start | bytes 5242880 | tf_op jit(solution)/shard_map/psum | solution.py:832
  33.4 18.7 %collective-permute-start.4 = (bf16[128,1024]{1,0:T(8,128)(2,1)S(1)}, bf16[128,1024]{1,0:T(8,128)(2,1)S(1)}, u32[]{:S(2)}, u32[]{:S(2)}) collective-permute-start(bf16[128,1024]{1,0:T(8,128)(2,1)S(1)} %pad_maximum_fusion.3.rest_0_), channel_id=1, source_target_pairs={{0,24},{4,28},{8,16},{12,20},{16,8},{20,12},{24,0},{28,4},{1,25},{... | collective-permute-start | bytes 786440 | tf_op jit(solution)/shard_map/ppermute | solution.py:63
  36.2 16.6 %collective-permute-start.3 = (bf16[128,1024]{1,0:T(8,128)(2,1)S(1)}, bf16[128,1024]{1,0:T(8,128)(2,1)S(1)}, u32[]{:S(2)}, u32[]{:S(2)}) collective-permute-start(bf16[128,1024]{1,0:T(8,128)(2,1)S(1)} %pad_maximum_fusion.3.rest_0_), channel_id=1, source_target_pairs={{0,16},{4,20},{8,24},{12,28},{16,0},{20,4},{24,8},{28,12},{1,17},{... | collective-permute-start | bytes 786440 | tf_op jit(solution)/shard_map/ppermute | solution.py:63
  36.7 16.8 %collective-permute-start.2 = (bf16[128,1024]{1,0:T(8,128)(2,1)S(1)}, bf16[128,1024]{1,0:T(8,128)(2,1)}, u32[]{:S(2)}, u32[]{:S(2)}) collective-permute-start(bf16[128,1024]{1,0:T(8,128)(2,1)S(1)} %pad_maximum_fusion.3.rest_0_), channel_id=1, source_target_pairs={{0,8},{4,12},{8,0},{12,4},{16,24},{20,28},{24,16},{28,20},{1,9},{5... | collective-permute-start | bytes 786440 | tf_op jit(solution)/shard_map/ppermute | solution.py:63
  47.8 25.9 %collective-permute-start.56 = (bf16[2,2,64,1024]{3,2,0,1:T(8,128)(2,1)}, bf16[2,2,64,1024]{3,2,0,1:T(8,128)(2,1)}, u32[]{:S(2)}, u32[]{:S(2)}) collective-permute-start(bf16[2,2,64,1024]{3,2,0,1:T(8,128)(2,1)} %pad_maximum_fusion.2), channel_id=1, source_target_pairs={{0,8},{4,12},{8,0},{12,4},{16,24},{20,28},{24,16},{28,20},{1,9},{5... | collective-permute-start | bytes 1572872 | tf_op jit(solution)/shard_map/ppermute | solution.py:63
  50.6 66.4 %collective-permute-start.28 = (bf16[128,1024]{1,0:T(8,128)(2,1)S(1)}, bf16[128,1024]{1,0:T(8,128)(2,1)}, u32[]{:S(2)}, u32[]{:S(2)}) collective-permute-start(bf16[128,1024]{1,0:T(8,128)(2,1)S(1)} %pad_maximum_fusion.4.rest_4_), channel_id=1, source_target_pairs={{0,24},{4,28},{8,16},{12,20},{16,8},{20,12},{24,0},{28,4},{1,25},{... | collective-permute-start | bytes 786440 | tf_op jit(solution)/shard_map/ppermute | solution.py:63
  62.7 5.9 %collective-permute-start.8 = (f32[4,512]{1,0:T(4,128)S(1)}, f32[4,512]{1,0:T(4,128)S(1)}, u32[]{:S(2)}, u32[]{:S(2)}) collective-permute-start(f32[4,512]{1,0:T(4,128)S(1)} %pad_maximum_fusion.11.rest_0_), channel_id=1, source_target_pairs={{0,3},{1,2},{2,1},{3,0},{4,7},{5,6},{6,5},{7,4},{8,11},{9,10},{10,... | collective-permute-start | bytes 24584 | tf_op jit(solution)/shard_map/ppermute | solution.py:69
  66.1 4.5 %collective-permute-start.7 = (f32[4,512]{1,0:T(4,128)S(1)}, f32[4,512]{1,0:T(4,128)S(1)}, u32[]{:S(2)}, u32[]{:S(2)}) collective-permute-start(f32[4,512]{1,0:T(4,128)S(1)} %pad_maximum_fusion.11.rest_0_), channel_id=1, source_target_pairs={{0,2},{1,3},{2,0},{3,1},{4,6},{5,7},{6,4},{7,5},{8,10},{9,11},{10,... | collective-permute-start | bytes 24584 | tf_op jit(solution)/shard_map/ppermute | solution.py:69
  66.1 4.5 %collective-permute-start.6 = (f32[4,512]{1,0:T(4,128)S(1)}, f32[4,512]{1,0:T(4,128)S(1)}, u32[]{:S(2)}, u32[]{:S(2)}) collective-permute-start(f32[4,512]{1,0:T(4,128)S(1)} %pad_maximum_fusion.11.rest_0_), channel_id=1, source_target_pairs={{0,1},{1,0},{2,3},{3,2},{4,5},{5,4},{6,7},{7,6},{8,9},{9,8},{10,11... | collective-permute-start | bytes 24584 | tf_op jit(solution)/shard_map/ppermute | solution.py:69
  68.6 21.1 %collective-permute-start.57 = (bf16[2,2,64,1024]{3,2,0,1:T(8,128)(2,1)}, bf16[2,2,64,1024]{3,2,0,1:T(8,128)(2,1)S(1)}, u32[]{:S(2)}, u32[]{:S(2)}) collective-permute-start(bf16[2,2,64,1024]{3,2,0,1:T(8,128)(2,1)} %pad_maximum_fusion.2), channel_id=1, source_target_pairs={{0,16},{4,20},{8,24},{12,28},{16,0},{20,4},{24,8},{28,12},{1,17},{... | collective-permute-start | bytes 1572872 | tf_op jit(solution)/shard_map/ppermute | solution.py:63
  73.6 2.0 collective-permute-start.9
  75.6 6.1 %collective-permute-start.12 = (f32[4,512]{1,0:T(4,128)S(1)}, f32[4,512]{1,0:T(4,128)S(1)}, u32[]{:S(2)}, u32[]{:S(2)}) collective-permute-start(f32[4,512]{1,0:T(4,128)S(1)} %pad_maximum_fusion.12.rest_0_), channel_id=1, source_target_pairs={{0,3},{1,2},{2,1},{3,0},{4,7},{5,6},{6,5},{7,4},{8,11},{9,10},{10,... | collective-permute-start | bytes 24584 | tf_op jit(solution)/shard_map/ppermute | solution.py:69
  77.6 5.6 %collective-permute-start.11 = (f32[4,512]{1,0:T(4,128)S(1)}, f32[4,512]{1,0:T(4,128)S(1)}, u32[]{:S(2)}, u32[]{:S(2)}) collective-permute-start(f32[4,512]{1,0:T(4,128)S(1)} %pad_maximum_fusion.12.rest_0_), channel_id=1, source_target_pairs={{0,2},{1,3},{2,0},{3,1},{4,6},{5,7},{6,4},{7,5},{8,10},{9,11},{10,... | collective-permute-start | bytes 24584 | tf_op jit(solution)/shard_map/ppermute | solution.py:69
  77.8 5.4 %collective-permute-start.10 = (f32[4,512]{1,0:T(4,128)S(1)}, f32[4,512]{1,0:T(4,128)S(1)}, u32[]{:S(2)}, u32[]{:S(2)}) collective-permute-start(f32[4,512]{1,0:T(4,128)S(1)} %pad_maximum_fusion.12.rest_0_), channel_id=1, source_target_pairs={{0,1},{1,0},{2,3},{3,2},{4,5},{5,4},{6,7},{7,6},{8,9},{9,8},{10,11... | collective-permute-start | bytes 24584 | tf_op jit(solution)/shard_map/ppermute | solution.py:69
  81.7 32.1 %collective-permute-start.58 = (bf16[2,2,64,1024]{3,2,0,1:T(8,128)(2,1)}, bf16[2,2,64,1024]{3,2,0,1:T(8,128)(2,1)S(1)}, u32[]{:S(2)}, u32[]{:S(2)}) collective-permute-start(bf16[2,2,64,1024]{3,2,0,1:T(8,128)(2,1)} %pad_maximum_fusion.2), channel_id=1, source_target_pairs={{0,24},{4,28},{8,16},{12,20},{16,8},{20,12},{24,0},{28,4},{1,25},{... | collective-permute-start | bytes 1572872 | tf_op jit(solution)/shard_map/ppermute | solution.py:63
  89.6 1.2 collective-permute-start.13
  90.9 4.9 %collective-permute-start.15 = (f32[4,1024]{1,0:T(4,128)S(1)}, f32[4,1024]{1,0:T(4,128)S(1)}, u32[]{:S(2)}, u32[]{:S(2)}) collective-permute-start(f32[4,1024]{1,0:T(4,128)S(1)} %pad_maximum_fusion.6), channel_id=1, source_target_pairs={{0,2},{1,3},{2,0},{3,1},{4,6},{5,7},{6,4},{7,5},{8,10},{9,11},{10,... | collective-permute-start | bytes 49160 | tf_op jit(solution)/shard_map/ppermute | solution.py:69
  92.4 3.7 collective-permute-start.14
  94.4 5.5 %collective-permute-start.16 = (f32[4,1024]{1,0:T(4,128)S(1)}, f32[4,1024]{1,0:T(4,128)S(1)}, u32[]{:S(2)}, u32[]{:S(2)}) collective-permute-start(f32[4,1024]{1,0:T(4,128)S(1)} %pad_maximum_fusion.6), channel_id=1, source_target_pairs={{0,3},{1,2},{2,1},{3,0},{4,7},{5,6},{6,5},{7,4},{8,11},{9,10},{10,... | collective-permute-start | bytes 49160 | tf_op jit(solution)/shard_map/ppermute | solution.py:69
  103.9 6.4 %collective-permute-start.20 = (f32[4,512]{1,0:T(4,128)S(1)}, f32[4,512]{1,0:T(4,128)S(1)}, u32[]{:S(2)}, u32[]{:S(2)}) collective-permute-start(f32[4,512]{1,0:T(4,128)S(1)} %pad_maximum_fusion.13.rest_0_), channel_id=1, source_target_pairs={{0,3},{1,2},{2,1},{3,0},{4,7},{5,6},{6,5},{7,4},{8,11},{9,10},{10,... | collective-permute-start | bytes 24584 | tf_op jit(solution)/shard_map/ppermute | solution.py:69
  104.9 6.1 %collective-permute-start.19 = (f32[4,512]{1,0:T(4,128)S(1)}, f32[4,512]{1,0:T(4,128)S(1)}, u32[]{:S(2)}, u32[]{:S(2)}) collective-permute-start(f32[4,512]{1,0:T(4,128)S(1)} %pad_maximum_fusion.13.rest_0_), channel_id=1, source_target_pairs={{0,2},{1,3},{2,0},{3,1},{4,6},{5,7},{6,4},{7,5},{8,10},{9,11},{10,... | collective-permute-start | bytes 24584 | tf_op jit(solution)/shard_map/ppermute | solution.py:69
  104.9 6.6 %collective-permute-start.18 = (f32[4,512]{1,0:T(4,128)S(1)}, f32[4,512]{1,0:T(4,128)S(1)}, u32[]{:S(2)}, u32[]{:S(2)}) collective-permute-start(f32[4,512]{1,0:T(4,128)S(1)} %pad_maximum_fusion.13.rest_0_), channel_id=1, source_target_pairs={{0,1},{1,0},{2,3},{3,2},{4,5},{5,4},{6,7},{7,6},{8,9},{9,8},{10,11... | collective-permute-start | bytes 24584 | tf_op jit(solution)/shard_map/ppermute | solution.py:69
  110.3 9.8 %collective-permute-start.27 = (bf16[128,1024]{1,0:T(8,128)(2,1)S(1)}, bf16[128,1024]{1,0:T(8,128)(2,1)S(1)}, u32[]{:S(2)}, u32[]{:S(2)}) collective-permute-start(bf16[128,1024]{1,0:T(8,128)(2,1)S(1)} %pad_maximum_fusion.4.rest_4_), channel_id=1, source_target_pairs={{0,16},{4,20},{8,24},{12,28},{16,0},{20,4},{24,8},{28,12},{1,17},{... | collective-permute-start | bytes 786440 | tf_op jit(solution)/shard_map/ppermute | solution.py:63
  110.9 9.2 %collective-permute-start.26 = (bf16[128,1024]{1,0:T(8,128)(2,1)S(1)}, bf16[128,1024]{1,0:T(8,128)(2,1)S(1)}, u32[]{:S(2)}, u32[]{:S(2)}) collective-permute-start(bf16[128,1024]{1,0:T(8,128)(2,1)S(1)} %pad_maximum_fusion.4.rest_4_), channel_id=1, source_target_pairs={{0,8},{4,12},{8,0},{12,4},{16,24},{20,28},{24,16},{28,20},{1,9},{5... | collective-permute-start | bytes 786440 | tf_op jit(solution)/shard_map/ppermute | solution.py:63
  115.0 5.7 %collective-permute-start.24 = (f32[4,1024]{1,0:T(4,128)S(1)}, f32[4,1024]{1,0:T(4,128)S(1)}, u32[]{:S(2)}, u32[]{:S(2)}) collective-permute-start(f32[4,1024]{1,0:T(4,128)S(1)} %pad_maximum_fusion.8.rest_0_), channel_id=1, source_target_pairs={{0,3},{1,2},{2,1},{3,0},{4,7},{5,6},{6,5},{7,4},{8,11},{9,10},{10,... | collective-permute-start | bytes 49160 | tf_op jit(solution)/shard_map/ppermute | solution.py:69
  116.9 4.6 %collective-permute-start.23 = (f32[4,1024]{1,0:T(4,128)S(1)}, f32[4,1024]{1,0:T(4,128)S(1)}, u32[]{:S(2)}, u32[]{:S(2)}) collective-permute-start(f32[4,1024]{1,0:T(4,128)S(1)} %pad_maximum_fusion.8.rest_0_), channel_id=1, source_target_pairs={{0,2},{1,3},{2,0},{3,1},{4,6},{5,7},{6,4},{7,5},{8,10},{9,11},{10,... | collective-permute-start | bytes 49160 | tf_op jit(solution)/shard_map/ppermute | solution.py:69
  117.0 4.6 %collective-permute-start.22 = (f32[4,1024]{1,0:T(4,128)S(1)}, f32[4,1024]{1,0:T(4,128)S(1)}, u32[]{:S(2)}, u32[]{:S(2)}) collective-permute-start(f32[4,1024]{1,0:T(4,128)S(1)} %pad_maximum_fusion.8.rest_0_), channel_id=1, source_target_pairs={{0,1},{1,0},{2,3},{3,2},{4,5},{5,4},{6,7},{7,6},{8,9},{9,8},{10,11... | collective-permute-start | bytes 49160 | tf_op jit(solution)/shard_map/ppermute | solution.py:69
  124.8 3.5 collective-permute-start.30
  128.4 5.8 %collective-permute-start.33 = (f32[4,1024]{1,0:T(4,128)S(1)}, f32[4,1024]{1,0:T(4,128)S(1)}, u32[]{:S(2)}, u32[]{:S(2)}) collective-permute-start(f32[4,1024]{1,0:T(4,128)S(1)} %pad_maximum_fusion.9.rest_0_), channel_id=1, source_target_pairs={{0,3},{1,2},{2,1},{3,0},{4,7},{5,6},{6,5},{7,4},{8,11},{9,10},{10,... | collective-permute-start | bytes 49160 | tf_op jit(solution)/shard_map/ppermute | solution.py:69
  130.3 4.6 %collective-permute-start.32 = (f32[4,1024]{1,0:T(4,128)S(1)}, f32[4,1024]{1,0:T(4,128)S(1)}, u32[]{:S(2)}, u32[]{:S(2)}) collective-permute-start(f32[4,1024]{1,0:T(4,128)S(1)} %pad_maximum_fusion.9.rest_0_), channel_id=1, source_target_pairs={{0,2},{1,3},{2,0},{3,1},{4,6},{5,7},{6,4},{7,5},{8,10},{9,11},{10,... | collective-permute-start | bytes 49160 | tf_op jit(solution)/shard_map/ppermute | solution.py:69
  131.5 3.7 collective-permute-start.31
  133.5 141.0 %collective-permute-start.29 = (bf16[64,1024]{1,0:T(8,128)(2,1)}, bf16[64,1024]{1,0:T(8,128)(2,1)}, u32[]{:S(2)}, u32[]{:S(2)}) collective-permute-start(bf16[64,1024]{1,0:T(8,128)(2,1)} %constant_dynamic-slice_fusion.11), channel_id=1, source_target_pairs={{0,4},{4,0},{8,12},{12,8},{16,20},{20,16},{24,28},{28,24},{1,5},{5... | collective-permute-start | bytes 393224 | tf_op jit(solution)/shard_map/ppermute | solution.py:59
  139.9 8.0 %collective-permute-start.34 = (f32[2,512]{1,0:T(2,128)S(1)}, f32[2,512]{1,0:T(2,128)S(1)}, u32[]{:S(2)}, u32[]{:S(2)}) collective-permute-start(f32[2,512]{1,0:T(2,128)S(1)} %get-tuple-element.95), channel_id=1, source_target_pairs={{0,4},{4,0},{8,12},{12,8},{16,20},{20,16},{24,28},{28,24},{1,5},{5... | collective-permute-start | bytes 12296 | tf_op jit(solution)/shard_map/ppermute | solution.py:59
  147.4 109.0 %collective-permute-start.65 = (bf16[512,128]{1,0:T(8,128)(2,1)}, bf16[512,128]{1,0:T(8,128)(2,1)}, u32[]{:S(2)}, u32[]{:S(2)}) collective-permute-start(bf16[512,128]{1,0:T(8,128)(2,1)} %bitcast.150), channel_id=1, source_target_pairs={{0,4},{4,0},{8,12},{12,8},{16,20},{20,16},{24,28},{28,24},{1,5},{5... | collective-permute-start | bytes 393224 | tf_op jit(solution)/shard_map/ppermute | solution.py:59
  147.9 8.9 %collective-permute-start.37 = (f32[4,512]{1,0:T(4,128)S(1)}, f32[4,512]{1,0:T(4,128)S(1)}, u32[]{:S(2)}, u32[]{:S(2)}) collective-permute-start(f32[4,512]{1,0:T(4,128)S(1)} %pad_maximum_fusion.14.rest_0_), channel_id=1, source_target_pairs={{0,3},{1,2},{2,1},{3,0},{4,7},{5,6},{6,5},{7,4},{8,11},{9,10},{10,... | collective-permute-start | bytes 24584 | tf_op jit(solution)/shard_map/ppermute | solution.py:69
  149.9 7.0 %collective-permute-start.36 = (f32[4,512]{1,0:T(4,128)S(1)}, f32[4,512]{1,0:T(4,128)S(1)}, u32[]{:S(2)}, u32[]{:S(2)}) collective-permute-start(f32[4,512]{1,0:T(4,128)S(1)} %pad_maximum_fusion.14.rest_0_), channel_id=1, source_target_pairs={{0,2},{1,3},{2,0},{3,1},{4,6},{5,7},{6,4},{7,5},{8,10},{9,11},{10,... | collective-permute-start | bytes 24584 | tf_op jit(solution)/shard_map/ppermute | solution.py:69
  150.8 6.1 %collective-permute-start.35 = (f32[4,512]{1,0:T(4,128)S(1)}, f32[4,512]{1,0:T(4,128)S(1)}, u32[]{:S(2)}, u32[]{:S(2)}) collective-permute-start(f32[4,512]{1,0:T(4,128)S(1)} %pad_maximum_fusion.14.rest_0_), channel_id=1, source_target_pairs={{0,1},{1,0},{2,3},{3,2},{4,5},{5,4},{6,7},{7,6},{8,9},{9,8},{10,11... | collective-permute-start | bytes 24584 | tf_op jit(solution)/shard_map/ppermute | solution.py:69
  160.8 4.9 %collective-permute-start.40 = (f32[4,1024]{1,0:T(4,128)S(1)}, f32[4,1024]{1,0:T(4,128)S(1)}, u32[]{:S(2)}, u32[]{:S(2)}) collective-permute-start(f32[4,1024]{1,0:T(4,128)S(1)} %pad_maximum_fusion.7), channel_id=1, source_target_pairs={{0,2},{1,3},{2,0},{3,1},{4,6},{5,7},{6,4},{7,5},{8,10},{9,11},{10,... | collective-permute-start | bytes 49160 | tf_op jit(solution)/shard_map/ppermute | solution.py:69
  161.8 3.9 %collective-permute-start.39 = (f32[4,1024]{1,0:T(4,128)S(1)}, f32[4,1024]{1,0:T(4,128)S(1)}, u32[]{:S(2)}, u32[]{:S(2)}) collective-permute-start(f32[4,1024]{1,0:T(4,128)S(1)} %pad_maximum_fusion.7), channel_id=1, source_target_pairs={{0,1},{1,0},{2,3},{3,2},{4,5},{5,4},{6,7},{7,6},{8,9},{9,8},{10,11... | collective-permute-start | bytes 49160 | tf_op jit(solution)/shard_map/ppermute | solution.py:69
  163.3 5.5 %collective-permute-start.41 = (f32[4,1024]{1,0:T(4,128)S(1)}, f32[4,1024]{1,0:T(4,128)S(1)}, u32[]{:S(2)}, u32[]{:S(2)}) collective-permute-start(f32[4,1024]{1,0:T(4,128)S(1)} %pad_maximum_fusion.7), channel_id=1, source_target_pairs={{0,3},{1,2},{2,1},{3,0},{4,7},{5,6},{6,5},{7,4},{8,11},{9,10},{10,... | collective-permute-start | bytes 49160 | tf_op jit(solution)/shard_map/ppermute | solution.py:69
  178.2 10.6 %collective-permute-start.42 = (f32[2,512]{1,0:T(2,128)S(1)}, f32[2,512]{1,0:T(2,128)S(1)}, u32[]{:S(2)}, u32[]{:S(2)}) collective-permute-start(f32[2,512]{1,0:T(2,128)S(1)} %get-tuple-element.104), channel_id=1, source_target_pairs={{0,4},{4,0},{8,12},{12,8},{16,20},{20,16},{24,28},{28,24},{1,5},{5... | collective-permute-start | bytes 12296 | tf_op jit(solution)/shard_map/ppermute | solution.py:59
  188.8 5.5 %collective-permute-start.45 = (f32[4,512]{1,0:T(4,128)S(1)}, f32[4,512]{1,0:T(4,128)S(1)}, u32[]{:S(2)}, u32[]{:S(2)}) collective-permute-start(f32[4,512]{1,0:T(4,128)S(1)} %pad_maximum_fusion.15.rest_0_), channel_id=1, source_target_pairs={{0,3},{1,2},{2,1},{3,0},{4,7},{5,6},{6,5},{7,4},{8,11},{9,10},{10,... | collective-permute-start | bytes 24584 | tf_op jit(solution)/shard_map/ppermute | solution.py:69
  190.8 4.5 %collective-permute-start.44 = (f32[4,512]{1,0:T(4,128)S(1)}, f32[4,512]{1,0:T(4,128)S(1)}, u32[]{:S(2)}, u32[]{:S(2)}) collective-permute-start(f32[4,512]{1,0:T(4,128)S(1)} %pad_maximum_fusion.15.rest_0_), channel_id=1, source_target_pairs={{0,2},{1,3},{2,0},{3,1},{4,6},{5,7},{6,4},{7,5},{8,10},{9,11},{10,... | collective-permute-start | bytes 24584 | tf_op jit(solution)/shard_map/ppermute | solution.py:69
  190.8 4.5 %collective-permute-start.43 = (f32[4,512]{1,0:T(4,128)S(1)}, f32[4,512]{1,0:T(4,128)S(1)}, u32[]{:S(2)}, u32[]{:S(2)}) collective-permute-start(f32[4,512]{1,0:T(4,128)S(1)} %pad_maximum_fusion.15.rest_0_), channel_id=1, source_target_pairs={{0,1},{1,0},{2,3},{3,2},{4,5},{5,4},{6,7},{7,6},{8,9},{9,8},{10,11... | collective-permute-start | bytes 24584 | tf_op jit(solution)/shard_map/ppermute | solution.py:69
  203.0 5.6 %collective-permute-start.49 = (f32[4,512]{1,0:T(4,128)S(1)}, f32[4,512]{1,0:T(4,128)S(1)}, u32[]{:S(2)}, u32[]{:S(2)}) collective-permute-start(f32[4,512]{1,0:T(4,128)S(1)} %pad_maximum_fusion.16.rest_0_), channel_id=1, source_target_pairs={{0,3},{1,2},{2,1},{3,0},{4,7},{5,6},{6,5},{7,4},{8,11},{9,10},{10,... | collective-permute-start | bytes 24584 | tf_op jit(solution)/shard_map/ppermute | solution.py:69
  205.0 4.5 %collective-permute-start.48 = (f32[4,512]{1,0:T(4,128)S(1)}, f32[4,512]{1,0:T(4,128)S(1)}, u32[]{:S(2)}, u32[]{:S(2)}) collective-permute-start(f32[4,512]{1,0:T(4,128)S(1)} %pad_maximum_fusion.16.rest_0_), channel_id=1, source_target_pairs={{0,2},{1,3},{2,0},{3,1},{4,6},{5,7},{6,4},{7,5},{8,10},{9,11},{10,... | collective-permute-start | bytes 24584 | tf_op jit(solution)/shard_map/ppermute | solution.py:69
  206.1 3.7 collective-permute-start.47
  208.6 12.7 %collective-permute-start.64 = (bf16[512,64]{0,1:T(8,128)(2,1)}, bf16[512,64]{0,1:T(8,128)(2,1)}, u32[]{:S(2)}, u32[]{:S(2)}) collective-permute-start(bf16[512,64]{0,1:T(8,128)(2,1)} %fusion.45), channel_id=1, source_target_pairs={{0,4},{4,0},{8,12},{12,8},{16,20},{20,16},{24,28},{28,24},{1,5},{5... | collective-permute-start | bytes 196616 | tf_op jit(solution)/shard_map/ppermute | solution.py:59
  215.2 3.1 collective-permute-start.50
  218.4 5.9 %collective-permute-start.53 = (f32[4,1024]{1,0:T(4,128)S(1)}, f32[4,1024]{1,0:T(4,128)S(1)}, u32[]{:S(2)}, u32[]{:S(2)}) collective-permute-start(f32[4,1024]{1,0:T(4,128)S(1)} %pad_maximum_fusion.10.rest_0_), channel_id=1, source_target_pairs={{0,3},{1,2},{2,1},{3,0},{4,7},{5,6},{6,5},{7,4},{8,11},{9,10},{10,... | collective-permute-start | bytes 49160 | tf_op jit(solution)/shard_map/ppermute | solution.py:69
  220.3 4.8 %collective-permute-start.52 = (f32[4,1024]{1,0:T(4,128)S(1)}, f32[4,1024]{1,0:T(4,128)S(1)}, u32[]{:S(2)}, u32[]{:S(2)}) collective-permute-start(f32[4,1024]{1,0:T(4,128)S(1)} %pad_maximum_fusion.10.rest_0_), channel_id=1, source_target_pairs={{0,2},{1,3},{2,0},{3,1},{4,6},{5,7},{6,4},{7,5},{8,10},{9,11},{10,... | collective-permute-start | bytes 49160 | tf_op jit(solution)/shard_map/ppermute | solution.py:69
  221.3 3.9 %collective-permute-start.51 = (f32[4,1024]{1,0:T(4,128)S(1)}, f32[4,1024]{1,0:T(4,128)S(1)}, u32[]{:S(2)}, u32[]{:S(2)}) collective-permute-start(f32[4,1024]{1,0:T(4,128)S(1)} %pad_maximum_fusion.10.rest_0_), channel_id=1, source_target_pairs={{0,1},{1,0},{2,3},{3,2},{4,5},{5,4},{6,7},{7,6},{8,9},{9,8},{10,11... | collective-permute-start | bytes 49160 | tf_op jit(solution)/shard_map/ppermute | solution.py:69
  224.3 33.2 %collective-permute-start.66 = (bf16[512,128]{1,0:T(8,128)(2,1)}, bf16[512,128]{1,0:T(8,128)(2,1)}, u32[]{:S(2)}, u32[]{:S(2)}) collective-permute-start(bf16[512,128]{1,0:T(8,128)(2,1)} %bitcast.149), channel_id=1, source_target_pairs={{0,4},{4,0},{8,12},{12,8},{16,20},{20,16},{24,28},{28,24},{1,5},{5... | collective-permute-start | bytes 393224 | tf_op jit(solution)/shard_map/ppermute | solution.py:59
  225.1 34.4 %collective-permute-start.60 = (bf16[1024,64]{0,1:T(8,128)(2,1)}, bf16[1024,64]{0,1:T(8,128)(2,1)}, u32[]{:S(2)}, u32[]{:S(2)}) collective-permute-start(bf16[1024,64]{0,1:T(8,128)(2,1)} %fusion.29), channel_id=1, source_target_pairs={{0,4},{4,0},{8,12},{12,8},{16,20},{20,16},{24,28},{28,24},{1,5},{5... | collective-permute-start | bytes 393224 | tf_op jit(solution)/shard_map/ppermute | solution.py:59
  225.2 29.2 %collective-permute-start.62 = (bf16[512,64]{0,1:T(8,128)(2,1)}, bf16[512,64]{0,1:T(8,128)(2,1)}, u32[]{:S(2)}, u32[]{:S(2)}) collective-permute-start(bf16[512,64]{0,1:T(8,128)(2,1)} %fusion.44), channel_id=1, source_target_pairs={{0,4},{4,0},{8,12},{12,8},{16,20},{20,16},{24,28},{28,24},{1,5},{5... | collective-permute-start | bytes 196616 | tf_op jit(solution)/shard_map/ppermute | solution.py:59
  254.5 7.3 %collective-permute-start.63 = (bf16[4608,64]{0,1:T(8,128)(2,1)S(1)}, bf16[4608,64]{0,1:T(8,128)(2,1)S(1)}, u32[]{:S(2)}, u32[]{:S(2)}) collective-permute-start(bf16[4608,64]{0,1:T(8,128)(2,1)S(1)} %copy-done.73), channel_id=1, source_target_pairs={{0,4},{4,0},{8,12},{12,8},{16,20},{20,16},{24,28},{28,24},{1,5},{5... | collective-permute-start | bytes 1769480 | tf_op jit(solution)/shard_map/ppermute | solution.py:59
  256.4 4.8 %collective-permute-start.61 = (bf16[1024,64]{0,1:T(8,128)(2,1)S(1)}, bf16[1024,64]{0,1:T(8,128)(2,1)S(1)}, u32[]{:S(2)}, u32[]{:S(2)}) collective-permute-start(bf16[1024,64]{0,1:T(8,128)(2,1)S(1)} %copy-done.75), channel_id=1, source_target_pairs={{0,4},{4,0},{8,12},{12,8},{16,20},{20,16},{24,28},{28,24},{1,5},{5... | collective-permute-start | bytes 393224 | tf_op jit(solution)/shard_map/ppermute | solution.py:59
  257.5 5.7 %collective-permute-start.59 = (bf16[4608,128]{1,0:T(8,128)(2,1)}, bf16[4608,128]{1,0:T(8,128)(2,1)}, u32[]{:S(2)}, u32[]{:S(2)}) collective-permute-start(bf16[4608,128]{1,0:T(8,128)(2,1)} %convert_bitcast_fusion), channel_id=1, source_target_pairs={{0,4},{4,0},{8,12},{12,8},{16,20},{20,16},{24,28},{28,24},{1,5},{5... | collective-permute-start | bytes 3538952 | tf_op jit(solution)/shard_map/ppermute | solution.py:59
  273.7 2.6 collective-permute-start.54
  (83 other events, 599.5 us)
Sparse Core Ops, SparseCore 0:
  265.8 105.4 all-reduce.6

commit v3 on v2

v3 whole, which is shorter than its diff:
```python
import functools

import jax
import jax.numpy as jnp
from jax import lax
from jax.experimental import pallas as pl
from jax.experimental.pallas import tpu as pltpu
from jax.sharding import PartitionSpec as P

EPSILON = 1e-05
FAR = 20.0
CHUNK = 32
COLS = 256
BF = jnp.bfloat16
F32 = jnp.float32


def mish(values):
    grown = jnp.exp(jnp.minimum(values, FAR))
    wide = grown * (grown + 2.0)
    return values * (wide / (wide + 2.0))


def mish_slope(values):
    grown = jnp.exp(jnp.minimum(values, FAR))
    wide = grown * (grown + 2.0)
    share = 1.0 / (wide + 2.0)
    return wide * share + 4.0 * values * (grown * (grown + 1.0) * share) * share


def after(value, *others):
    return lax.optimization_barrier((value,) + others)[0]


def tree_sum(parts):
    while len(parts) > 1:
        parts = [parts[i] + parts[i + 1] for i in range(0, len(parts), 2)]
    return parts[0]


def dot(a, b):
    return jnp.dot(a, b, preferred_element_type=F32)


def dot_back(a, b):
    return lax.dot_general(a, b, (((1,), (1,)), ((), ())), preferred_element_type=F32)


def dot_cells(a, b):
    return lax.dot_general(a, b, (((0,), (0,)), ((), ())), preferred_element_type=F32)


class Plane:
    def __init__(self):
        self.rows = lax.axis_size("rows")
        self.groups = lax.axis_size("batch")
        self.chips = self.rows // 2
        self.place = lax.axis_index("rows")
        self.core = self.place % 2
        self.chip = self.place // 2

    def swap(self, value):
        return lax.ppermute(value, "rows", [(i, i ^ 1) for i in range(self.rows)])

    def chip_hops(self, value):
        return [value] + [
            lax.ppermute(value, "rows", [(i, i ^ (2 * step)) for i in range(self.rows)])
            for step in range(1, self.chips)
        ]

    def two_ways(self, first, second):
        hop = lambda value, step: lax.ppermute(
            value, "rows", [(i, i ^ (2 * step)) for i in range(self.rows)]
        )
        first_near, second_near = hop(first, 1), hop(second, 2)
        return first_near, second_near, lambda: (
            [first, first_near, hop(first, 2), hop(first_near, 2)],
            [second, hop(second, 1), second_near, hop(second_near, 1)],
        )

    def plane_hops(self, value):
        return [value] + [
            lax.ppermute(value, "batch", [(i, i ^ step) for i in range(self.groups)])
            for step in range(1, self.groups)
        ]

    def by_core(self, mine, got):
        first = self.core == 0
        return jnp.where(first, mine, got), jnp.where(first, got, mine)

    def split(self, block, axis=0):
        mine = lax.dynamic_index_in_dim(block, self.core, axis, keepdims=False)
        other = lax.dynamic_index_in_dim(block, 1 - self.core, axis, keepdims=False)
        return mine, other

    def row_pieces(self, mine, other):
        got = self.swap(other)
        if self.chips == 4:
            firsts, seconds = self.two_ways(mine, got)[2]()
        else:
            firsts, seconds = self.chip_hops(mine), self.chip_hops(got)
        return [piece for pair in zip(firsts, seconds) for piece in pair]

    def everywhere(self, pay):
        return self.plane_hops(jnp.concatenate([pay, self.swap(pay)], axis=0))


class Far:
    def __init__(self, source, target, semaphore):
        self.copy = pltpu.make_async_copy(source, target, semaphore)
        self.copy.start()
        self.target, self.waits = target, True

    def ready(self):
        if self.waits:
            self.copy.wait()
            self.waits = False
        return self.target


def rows_loop(total, body, carry=None, step=CHUNK):
    def turn(index, state):
        return body(pl.ds(pl.multiple_of(index * step, step), step), state)

    return lax.fori_loop(0, total // step, turn, carry)


GAIN_WIDE, SHIFT_WIDE, GAIN, SHIFT = 0, 2, 4, 9


def row_of(params, first, index, half=None):
    return params[first + index : first + index + 1, 0 : (half or params.shape[1])]


def finish_moments(scal, refs, cols=slice(None)):
    pixels = scal[1]
    center = tree_sum([r[0:1, cols] + r[2:3, cols] for r in refs]) / pixels
    terms = []
    for k, r in enumerate(refs):
        ends = []
        for side in range(2):
            count, over = scal[2 + 4 * k + 2 * side], scal[3 + 4 * k + 2 * side]
            gap = r[2 * side : 2 * side + 1, cols] * over - center
            ends.append(gap * gap * count)
        terms.append((r[1:2, cols] + r[3:4, cols]) + (ends[0] + ends[1]))
    return center, lax.rsqrt(tree_sum(terms) / pixels + EPSILON)


def finish_sums(refs, cols=slice(None)):
    return (
        tree_sum([r[0:1, cols] + r[2:3, cols] for r in refs]),
        tree_sum([r[1:2, cols] + r[3:4, cols] for r in refs]),
    )


def put_moments(values, pay, cols, weight):
    total = jnp.sum(values, axis=0, keepdims=True)
    off = values - total * (1.0 / values.shape[0])
    pay[0:1, cols] = total * weight
    pay[1:2, cols] = jnp.sum(off * off, axis=0, keepdims=True) * weight


def project(left, weights, pre, pay, weight, add=None):
    weights = weights.ready() if isinstance(weights, Far) else weights
    for start in range(0, pre.shape[1], COLS):
        cols = slice(start, start + COLS)
        out = dot(left[...], weights[:, cols])
        if add is not None:
            out = out + add[:, cols]
        pre[:, cols] = out
        put_moments(out, pay, cols, weight)


def fold(values):
    return jnp.sum(values.reshape(-1, 8, values.shape[-1]), axis=0)


def push(grad_of, pre, center, rstd, gain, offset, pushed, pay):
    def body(rows, sums):
        unit = (pre[rows, :].astype(F32) - center) * rstd
        out = grad_of(rows) * mish_slope(unit * gain + offset)
        pushed[rows, :] = out
        return sums[0] + fold(out), sums[1] + fold(out * unit)

    zero = jnp.zeros((8, pre.shape[1]), F32)
    first, second = rows_loop(pre.shape[0], body, (zero, zero), 16)
    pay[0:1, :] = jnp.sum(first, axis=0, keepdims=True)
    pay[1:2, :] = jnp.sum(second, axis=0, keepdims=True)


def settle(scal, refs, pushed, pre, coef, gain, out, sums):
    first, second = finish_sums(refs)
    sums[0:1, :] = first
    sums[1:2, :] = second
    over = 1.0 / scal[1]
    center, rstd = coef[0:1, :], coef[1:2, :]
    scale = gain * rstd * scal[0]
    level, tilt = first * over, second * over * rstd

    def body(rows, _):
        x = pre[rows, :].astype(F32) - center
        out[rows, :] = (scale * (pushed[rows, :] - level - x * tilt)).astype(BF)

    rows_loop(pre.shape[0], body)


def shifted_row(both):
    half = both.shape[1] // 2
    odd = both[:, half:].astype(F32)
    first = lax.broadcasted_iota(jnp.int32, odd.shape, 0) == 0
    before = jnp.where(first, 0.0, pltpu.roll(odd, 1, 0)).astype(BF)
    return jnp.concatenate([before, both], axis=1)


def first_kernel(scal, x, above, w, rows, pay, held, semaphores):
    slots, cells = above.shape[0], above.shape[1]
    count, _, _, wide = held.shape
    copies = [
        pltpu.make_async_copy(w.at[:, :, n * wide : (n + 1) * wide], held.at[n], semaphores.at[n])
        for n in range(count)
    ]
    for copy in copies:
        copy.start()
    sources = [above[...]] + [x[:, row] for row in range(2)]
    lefts = [
        jnp.concatenate([shifted_row(source[slot]) for slot in range(slots)], axis=0)
        for source in sources
    ]
    for n, copy in enumerate(copies):
        cols = slice(n * wide, (n + 1) * wide)
        copy.wait()
        out = sum(dot(left, held[n, tap]) for tap, left in enumerate(lefts))
        for slot in range(slots):
            rows[slot, :, cols] = out[slot * cells : (slot + 1) * cells].astype(BF)
        total = sum(
            jnp.sum(out[slot * cells : (slot + 1) * cells], axis=0, keepdims=True) * scal[slot]
            for slot in range(slots)
        )
        mean = total * scal[slots]
        spread = 0.0
        for slot in range(slots):
            off = out[slot * cells : (slot + 1) * cells] - mean
            spread += jnp.sum(off * off, axis=0, keepdims=True) * scal[slot]
        both = jnp.concatenate([total, spread], axis=0)
        pay[:, :, cols] = jnp.broadcast_to(both[None], (pay.shape[0],) + both.shape)


def main_kernel(pieces, scal, spots, got, counts, over, params, *rest):
    parts = rest[:pieces]
    w_main, down_pre, sectioned, main_pre, pay, coef = rest[pieces:]
    pixels = scal[1]
    firsts, seconds = got[:, 0, :], got[:, 1, :]
    center = jnp.sum(firsts, axis=0, keepdims=True) / pixels
    gap = firsts * over[...] - center
    total = jnp.sum(seconds + gap * gap * counts[...], axis=0, keepdims=True)
    rstd = lax.rsqrt(total / pixels + EPSILON)
    coef[0:1, :] = center
    coef[1:2, :] = rstd
    scale, offset = rstd * row_of(params, GAIN_WIDE, 0), row_of(params, SHIFT_WIDE, 0)
    for k, part in enumerate(parts):
        part = part.ready()
        width = part.shape[0]
        start = spots[k] * width

        def body(index, _, part=part, start=start):
            src = pl.ds(pl.multiple_of(index * CHUNK, CHUNK), CHUNK)
            dst = pl.ds(pl.multiple_of(start + index * CHUNK, CHUNK), CHUNK)
            x = part[src, :]
            down_pre[dst, :] = x
            value = (x.astype(F32) - center) * scale + offset
            sectioned[dst, :] = mish(value).astype(BF)

        lax.fori_loop(0, width // CHUNK, body, None)
    project(sectioned, w_main, main_pre, pay, scal[0])


def short_kernel(scal, sectioned, w_short, short_pre, pay):
    project(sectioned, w_short, short_pre, pay, scal[0])


def inner_kernel(groups, scal, *rest):
    refs = rest[:groups]
    pre, params, w_inner, mainline, inner_pre, pay, coef = rest[groups:]
    half = pre.shape[1]
    center, rstd = finish_moments(scal, refs)
    coef[0:1, :] = center
    coef[1:2, :] = rstd
    scale, offset = rstd * row_of(params, GAIN, 1, half), row_of(params, SHIFT, 1, half)

    def body(rows, _):
        mainline[rows, :] = mish((pre[rows, :] - center) * scale + offset).astype(BF)

    rows_loop(pre.shape[0], body)
    project(mainline, w_inner, inner_pre, pay, scal[0])


def three_shifts(values, rim, start, forward):
    width, half = values.shape
    place = lax.broadcasted_iota(jnp.int32, values.shape, 0)
    before = jnp.where(place == 0, 0.0, pltpu.roll(values, 1, 0)).astype(BF)
    after = jnp.where(place == width - 1, 0.0, pltpu.roll(values, width - 1, 0)).astype(BF)
    sides = (before, after) if forward else (after, before)
    rows = pl.ds(start, width)
    rim[rows, 0:half] = sides[0]
    rim[rows, half : 2 * half] = values.astype(BF)
    rim[rows, 2 * half : 3 * half] = sides[1]


def spatial_kernel(groups, width, scal, *rest):
    refs = rest[:groups]
    pre, params, w_spatial, rim, spatial_pre, pay, coef = rest[groups:]
    cells, half = pre.shape
    center, rstd = finish_moments(scal, refs)
    coef[0:1, :] = center
    coef[1:2, :] = rstd
    scale, offset = rstd * row_of(params, GAIN, 2, half), row_of(params, SHIFT, 2, half)
    blank = jnp.zeros((width, 3 * half), BF)
    rim[0:width, :] = blank
    rim[width + cells :, :] = blank

    def body(index, _):
        start = pl.multiple_of(index * width, width)
        act = mish((pre[pl.ds(start, width), :] - center) * scale + offset)
        three_shifts(act, rim, pl.multiple_of(start + width, width), True)

    lax.fori_loop(0, cells // width, body, None)
    w_spatial = w_spatial.ready()
    for begin in range(0, half, COLS):
        cols = slice(begin, begin + COLS)
        out = sum(
            dot(
                rim[i * width : i * width + cells, :],
                w_spatial[i * 3 * half : (i + 1) * 3 * half, cols],
            )
            for i in range(3)
        )
        spatial_pre[:, cols] = out
        put_moments(out, pay, cols, scal[0])


def trans_kernel(groups, scal, *rest):
    refs = rest[:groups]
    pre, mainline, params, w_trans, merged, trans_pre, pay, coef = rest[groups:]
    half = pre.shape[1]
    center, rstd = finish_moments(scal, refs)
    coef[0:1, :] = center
    coef[1:2, :] = rstd
    scale, offset = rstd * row_of(params, GAIN, 3, half), row_of(params, SHIFT, 3, half)

    def body(rows, _):
        act = mish((pre[rows, :] - center) * scale + offset)
        merged[rows, :] = (mainline[rows, :].astype(F32) + act).astype(BF)

    rows_loop(pre.shape[0], body)
    project(merged, w_trans, trans_pre, pay, scal[0])


def shortcut_kernel(groups, scal, *rest):
    refs = rest[:groups]
    pre, params, w_unite, shortcut, part, coef = rest[groups:]
    half = pre.shape[1]
    center, rstd = finish_moments(scal, refs)
    coef[0:1, :] = center
    coef[1:2, :] = rstd
    scale, offset = rstd * row_of(params, GAIN, 0, half), row_of(params, SHIFT, 0, half)

    def body(rows, _):
        shortcut[rows, :] = mish((pre[rows, :] - center) * scale + offset).astype(BF)

    rows_loop(pre.shape[0], body)
    w_unite = w_unite.ready()
    for start in range(0, part.shape[1], COLS):
        cols = slice(start, start + COLS)
        part[:, cols] = dot(shortcut[...], w_unite[0:half, cols])


def unite_kernel(groups, scal, *rest):
    refs = rest[:groups]
    pre, part, params, w_unite, transition, unite_pre, pay, coef = rest[groups:]
    half = pre.shape[1]
    center, rstd = finish_moments(scal, refs)
    coef[0:1, :] = center
    coef[1:2, :] = rstd
    scale, offset = rstd * row_of(params, GAIN, 4, half), row_of(params, SHIFT, 4, half)

    def body(rows, _):
        transition[rows, :] = mish((pre[rows, :] - center) * scale + offset).astype(BF)

    rows_loop(pre.shape[0], body)
    project(transition, w_unite.ready().at[half:, :], unite_pre, pay, scal[0], part)


def turn_kernel(groups, pieces, scal, spots, *rest):
    refs = rest[:groups]
    pre, params = rest[groups : groups + 2]
    parts = rest[groups + 2 : groups + 2 + pieces]
    pushed, *outputs, pay, coef = rest[groups + 2 + pieces :]
    center, rstd = finish_moments(scal, refs)
    coef[0:1, :] = center
    coef[1:2, :] = rstd
    gain, offset, weight = row_of(params, GAIN_WIDE, 1), row_of(params, SHIFT_WIDE, 1), scal[0]
    sums = (jnp.zeros((8, pre.shape[1]), F32),) * 2
    for k, part in enumerate(parts):
        part = part.ready()
        width = part.shape[0]
        start = spots[k] * width

        def body(index, sums, k=k, part=part, start=start):
            src = pl.ds(pl.multiple_of(index * 16, 16), 16)
            dst = pl.ds(pl.multiple_of(start + index * 16, 16), 16)
            unit = (pre[dst, :] - center) * rstd
            value = unit * gain + offset
            grown = jnp.exp(jnp.minimum(value, FAR))
            wide = grown * (grown + 2.0)
            share = 1.0 / (wide + 2.0)
            level = wide * share
            if k < 2:
                outputs[k][src, :] = (value * level * weight).astype(BF)
            slope = level + 4.0 * value * (grown * (grown + 1.0) * share) * share
            out = part[src, :].astype(F32) * weight * slope
            pushed[dst, :] = out
            return sums[0] + fold(out), sums[1] + fold(out * unit)

        sums = lax.fori_loop(0, width // 16, body, sums)
    pay[0:1, :] = jnp.sum(sums[0], axis=0, keepdims=True)
    pay[1:2, :] = jnp.sum(sums[1], axis=0, keepdims=True)


def back_trans_kernel(groups, scal, *rest):
    refs = rest[:groups]
    (
        unite_pushed, unite_pre, unite_coef, params, trans_pre, trans_coef, w_unite,
        grad_unite, sums, pushed, pay, scratch,
    ) = rest[groups:]
    half = trans_pre.shape[1]
    settle(scal, refs, unite_pushed, unite_pre, unite_coef, row_of(params, GAIN_WIDE, 1), grad_unite, sums)
    w_unite = w_unite.ready()
    for start in range(0, half, COLS):
        scratch[:, start : start + COLS] = dot_back(
            grad_unite[...], w_unite[half + start : half + start + COLS, :]
        )
    push(
        lambda rows: scratch[rows, :],
        trans_pre, trans_coef[0:1, :], trans_coef[1:2, :], row_of(params, GAIN, 4, half), row_of(params, SHIFT, 4, half),
        pushed, pay,
    )


def back_short_kernel(grad_unite, pre, coef, params, w_unite, pushed, pay, scratch):
    half = pre.shape[1]
    w_unite = w_unite.ready()
    for start in range(0, half, COLS):
        scratch[:, start : start + COLS] = dot_back(
            grad_unite[...], w_unite[start : start + COLS, :]
        )
    push(
        lambda rows: scratch[rows, :],
        pre, coef[0:1, :], coef[1:2, :], row_of(params, GAIN, 0, half), row_of(params, SHIFT, 0, half), pushed, pay,
    )


def back_spatial_kernel(groups, scal, *rest):
    refs = rest[:groups]
    (
        trans_pushed, trans_pre, trans_coef, spatial_pre, spatial_coef, params, w_trans,
        grad_trans, sums, grad_merged, pushed, pay,
    ) = rest[groups:]
    half = trans_pre.shape[1]
    settle(scal, refs, trans_pushed, trans_pre, trans_coef, row_of(params, GAIN, 4, half), grad_trans, sums)
    w_trans = w_trans.ready()
    for start in range(0, half, COLS):
        grad_merged[:, start : start + COLS] = dot_back(
            grad_trans[...], w_trans[start : start + COLS, :]
        )
    push(
        lambda rows: grad_merged[rows, :],
        spatial_pre, spatial_coef[0:1, :], spatial_coef[1:2, :], row_of(params, GAIN, 3, half), row_of(params, SHIFT, 3, half),
        pushed, pay,
    )


def back_inner_kernel(groups, width, scal, *rest):
    refs = rest[:groups]
    (
        spatial_pushed, spatial_pre, spatial_coef, inner_pre, inner_coef, params, w_spatial,
        grad_spatial, sums, pushed, pay, rim, scratch,
    ) = rest[groups:]
    cells, half = spatial_pre.shape
    settle(scal, refs, spatial_pushed, spatial_pre, spatial_coef, row_of(params, GAIN, 3, half), grad_spatial, sums)
    blank = jnp.zeros((width, 3 * half), BF)
    rim[0:width, :] = blank
    rim[width + cells :, :] = blank

    def body(index, _):
        start = pl.multiple_of(index * width, width)
        values = grad_spatial[pl.ds(start, width), :].astype(F32)
        three_shifts(values, rim, pl.multiple_of(start + width, width), False)

    lax.fori_loop(0, cells // width, body, None)
    w_spatial = w_spatial.ready()
    for start in range(0, half, COLS):
        scratch[:, start : start + COLS] = sum(
            dot_back(
                rim[(2 - i) * width : (2 - i) * width + cells, j * half : (j + 1) * half],
                w_spatial[(3 * i + j) * half + start : (3 * i + j) * half + start + COLS, :],
            )
            for i in range(3)
            for j in range(3)
        )
    push(
        lambda rows: scratch[rows, :],
        inner_pre, inner_coef[0:1, :], inner_coef[1:2, :], row_of(params, GAIN, 2, half), row_of(params, SHIFT, 2, half),
        pushed, pay,
    )


def back_main_kernel(groups, scal, *rest):
    refs = rest[:groups]
    (
        inner_pushed, inner_pre, inner_coef, grad_merged, main_pre, main_coef, params, w_inner,
        grad_inner, sums, pushed, pay, scratch,
    ) = rest[groups:]
    half = inner_pre.shape[1]
    settle(scal, refs, inner_pushed, inner_pre, inner_coef, row_of(params, GAIN, 2, half), grad_inner, sums)
    w_inner = w_inner.ready()
    for start in range(0, half, COLS):
        cols = slice(start, start + COLS)
        scratch[:, cols] = grad_merged[:, cols] + dot_back(grad_inner[...], w_inner[cols, :])
    push(
        lambda rows: scratch[rows, :],
        main_pre, main_coef[0:1, :], main_coef[1:2, :], row_of(params, GAIN, 1, half), row_of(params, SHIFT, 1, half),
        pushed, pay,
    )


def settle_short_kernel(groups, scal, *rest):
    refs = rest[:groups]
    pushed, pre, coef, params, w_short, grad_short, sums, part = rest[groups:]
    half = pre.shape[1]
    settle(scal, refs, pushed, pre, coef, row_of(params, GAIN, 0, half), grad_short, sums)
    w_short = w_short.ready()
    for start in range(0, part.shape[1], COLS):
        part[:, start : start + COLS] = dot_back(grad_short[...], w_short[start : start + COLS, :])


def back_down_kernel(groups, scal, *rest):
    refs = rest[:groups]
    (
        main_pushed, main_pre, main_coef, part, down_pre, down_coef, params, w_main,
        grad_main, sums, pushed, pay, scratch,
    ) = rest[groups:]
    half = main_pre.shape[1]
    settle(scal, refs, main_pushed, main_pre, main_coef, row_of(params, GAIN, 1, half), grad_main, sums)
    w_main = w_main.ready()
    for start in range(0, part.shape[1], COLS):
        cols = slice(start, start + COLS)
        scratch[:, cols] = part[:, cols] + dot_back(grad_main[...], w_main[cols, :])
    push(
        lambda rows: scratch[rows, :],
        down_pre, down_coef[0:1, :], down_coef[1:2, :], row_of(params, GAIN_WIDE, 0), row_of(params, SHIFT_WIDE, 0),
        pushed, pay,
    )


def settle_down_kernel(groups, scal, *rest):
    refs = rest[:groups]
    pushed, pre, coef, params, grad_down, sums = rest[groups:]
    settle(scal, refs, pushed, pre, coef, row_of(params, GAIN_WIDE, 0), grad_down, sums)
    cells = pre.shape[0]
    grad_down[cells:, :] = jnp.zeros((grad_down.shape[0] - cells, pre.shape[1]), BF)


def cut_down_kernel(groups, scal, spots, *rest):
    refs = rest[:groups]
    pushed, pre, coef, params, cut = rest[groups:]
    width = cut.shape[1]
    cols = pl.ds(pl.multiple_of(spots[1] * width, width), width)
    first, second = finish_sums(refs, cols)
    over = 1.0 / scal[1]
    center, rstd = coef[0:1, cols], coef[1:2, cols]
    scale = params[GAIN_WIDE : GAIN_WIDE + 1, cols] * rstd * scal[0]
    level, tilt = first * over, second * over * rstd

    def body(rows, _):
        x = pre[rows, cols].astype(F32) - center
        cut[rows, :] = (scale * (pushed[rows, cols] - level - x * tilt)).astype(BF)

    rows_loop(pre.shape[0], body)


def by_place(spots, first, second):
    low = spots[0] == 0
    return jnp.where(low, first, second), jnp.where(low, second, first)


def share_unite_kernel(spots, shortcut, transition, grad, mine, other):
    width = 2 * mine.shape[1]
    cut = grad[:, pl.ds(pl.multiple_of(spots[1] * width, width), width)]
    half = shortcut.shape[1]
    for k, values in enumerate((shortcut, transition)):
        out = dot_cells(values[...], cut)
        near, far = by_place(spots, out[:, : width // 2], out[:, width // 2 :])
        mine[k * half : (k + 1) * half, :] = near.astype(BF)
        other[k * half : (k + 1) * half, :] = far.astype(BF)


def put_halves(spots, cut, values, start, mine, other):
    out = dot_cells(cut, values)
    rows, cols = mine.shape[0], slice(start, start + out.shape[1])
    near, far = by_place(spots, out[:rows], out[rows:])
    mine[:, cols] = near.astype(BF)
    other[:, cols] = far.astype(BF)


def chip_columns(spots, mine):
    width = 2 * mine.shape[0]
    return pl.ds(pl.multiple_of(spots[1] * width, width), width)


def share_pack_kernel(spots, sectioned, grad_short, merged, grad_trans, mainline, grad_inner, mine, other):
    cols = chip_columns(spots, mine)
    start = 0
    for values, grad in ((sectioned, grad_short), (merged, grad_trans), (mainline, grad_inner)):
        put_halves(spots, grad[:, cols], values[...], start, mine, other)
        start += values.shape[1]


def share_spatial_kernel(cells, spots, rim, grad, mine, other):
    cut = grad[:, chip_columns(spots, mine)]
    line, side = (rim.shape[0] - cells) // 2, rim.shape[1]
    for row in range(3):
        put_halves(spots, cut, rim[row * line : row * line + cells, :], row * side, mine, other)


def share_main_kernel(spots, sectioned, grad, mine, other):
    put_halves(spots, grad[:, chip_columns(spots, mine)], sectioned[...], 0, mine, other)


def finish_kernel(unite, pack, taps, main, w_unite, w_short, w_trans, w_inner, w_spatial, w_main):
    w_unite[...] = unite[...].astype(F32)
    w_main[...] = main[...].astype(F32)
    start = 0
    for out in (w_short, w_trans, w_inner):
        out[...] = pack[:, start : start + out.shape[1]].astype(F32)
        start += out.shape[1]
    half = w_trans.shape[1]
    for tap in range(w_spatial.shape[0]):
        w_spatial[tap] = taps[:, tap * half : (tap + 1) * half].astype(F32)


def norm_sums_kernel(wide_count, *refs):
    sums, outs = refs[:-4], refs[-4:]
    for k, pair in enumerate(sums):
        index = k if k < wide_count else k - wide_count
        for row, out in ((1, outs[0 if k < wide_count else 1]), (0, outs[2 if k < wide_count else 3])):
            out[index : index + 1, :] = pair[row : row + 1, :]


def share_down_kernel(steps, chips, width, last_call, spots, *rest):
    grads = rest[: len(steps)]
    earlier = rest[len(steps) : len(steps) + 2 * last_call]
    rest = rest[len(steps) + 2 * last_call :]
    source, outs, rest = rest[0], rest[1:3], rest[3:]
    if last_call:
        odd_acc, even_acc = rest[:2]
        rest = rest[2:]
    else:
        odd_acc, even_acc = outs
    padded, sides, held, semaphores = rest
    cells, columns = grads[0].shape
    half = source.shape[-1] // 2
    planes = source.shape[0] // (2 * chips)
    copies = []
    for k, step in enumerate(steps):
        plane = spots[2 + step]
        copies.append(
            [
                pltpu.make_async_copy(
                    source.at[row * planes + plane, spots[0]], held.at[k, row], semaphores.at[k, row]
                )
                for row in range(2 * chips)
            ]
        )
        for copy in copies[-1]:
            copy.start()
    padded[cells:, :] = jnp.zeros((padded.shape[0] - cells, columns), BF)
    last = lax.broadcasted_iota(jnp.int32, (width, columns), 0) == width - 1

    def ahead(values):
        return jnp.where(last, 0.0, pltpu.roll(values.astype(F32), width - 1, 0)).astype(BF)

    for k in range(len(steps)):
        padded[0:cells, :] = grads[k][...]
        for block in range(2 * chips):
            rows = slice(block * width, (block + 1) * width)
            here = padded[rows, :]
            upper = padded[(block + 1) * width : (block + 2) * width, :]
            sides[rows, 0:columns] = upper
            sides[rows, columns : 2 * columns] = here
            sides[rows, 2 * columns : 3 * columns] = ahead(here)
            sides[rows, 3 * columns : 4 * columns] = ahead(upper)
        for copy in copies[k]:
            copy.wait()

        def add(which, side, start, values, k=k):
            rows, cols = slice(side * half, (side + 1) * half), slice(start, start + columns)
            acc = (even_acc, odd_acc)[which]
            if k > 0:
                values = values + acc[rows, cols]
            elif last_call:
                values = values + earlier[1 - which][rows, cols]
            acc[rows, cols] = values

        for which in range(2):
            for side in range(2):
                left = held[k, :, which, :, side * half : (side + 1) * half].reshape(cells, half)
                for block in range(4):
                    if (which == 0 and block in (0, 3)) or (side == 0 and block in (2, 3)):
                        continue
                    start = block * columns
                    add(which, side, start, dot_cells(left, sides[:, start : start + columns]))
    if not last_call:
        return
    mine, other = outs
    places = (
        (odd_acc, 1, 3), (odd_acc, 0, 0), (odd_acc, 1, 0),
        (even_acc, 1, 2), (even_acc, 0, 1), (even_acc, 1, 1),
        (odd_acc, 1, 2), (odd_acc, 0, 1), (odd_acc, 1, 1),
    )
    for tap, (acc, side, block) in enumerate(places):
        values = acc[side * half : (side + 1) * half, block * columns : (block + 1) * columns]
        near, far = by_place(spots, values[:, : columns // 2], values[:, columns // 2 :])
        mine[tap * half : (tap + 1) * half, :] = near.astype(BF)
        other[tap * half : (tap + 1) * half, :] = far.astype(BF)


def back_input_kernel(width, spots, grad, w, out, near, far):
    cells = 2 * width
    full = grad.shape[1]

    @pl.when(pl.program_id(0) == 0)
    def _():
        last = lax.broadcasted_iota(jnp.int32, (width, full), 0) == width - 1
        for block in range(3):
            start = pl.multiple_of(spots[1] * cells + block * width, width)
            values = grad[pl.ds(start, width), :]
            rows = slice(block * width, (block + 1) * width)
            near[rows, :] = values
            far[rows, :] = jnp.where(
                last, 0.0, pltpu.roll(values.astype(F32), width - 1, 0)
            ).astype(BF)

    low, high = slice(0, cells), slice(width, width + cells)

    def term(values, rows, i, j):
        return dot_back(values[rows, :], w[3 * i + j])

    def put(parity, column, values):
        for row in range(2):
            out[2 * row + parity, pl.ds(column, width, stride=2), :] = values[
                row * width : (row + 1) * width
            ]

    put(0, 0, term(near, low, 1, 1))
    put(0, 1, term(near, low, 1, 2) + term(far, low, 1, 0))
    put(1, 0, term(near, high, 0, 1) + term(near, low, 2, 1))
    put(
        1,
        1,
        term(near, high, 0, 2) + term(far, high, 0, 0) + term(near, low, 2, 2) + term(far, low, 2, 0),
    )


SMEM = pl.BlockSpec(memory_space=pltpu.SMEM)
VMEM = pl.BlockSpec(memory_space=pltpu.VMEM)
ANY = pl.BlockSpec(memory_space=pl.ANY)


def shape(dims, dtype=F32):
    return jax.ShapeDtypeStruct(dims, dtype)


def nbytes(dims, dtype):
    count = 1
    for d in dims:
        count *= d
    return count * jnp.dtype(dtype).itemsize


def in_vmem(value):
    return pltpu.with_memory_space_constraint(value, pltpu.VMEM)


def in_hbm(value):
    return pltpu.with_memory_space_constraint(value, pltpu.HBM)


def call(kernel, name, scalars, near, outs, flops, scratch=(), far=(), pin=False, spill=()):
    moved = sum(nbytes(a.shape, a.dtype) for a in (*near, *far, *outs))
    held = moved + sum(nbytes(s.shape, s.dtype) for s in scratch)
    if pin:
        held -= moved - sum(nbytes(a.shape, a.dtype) for a in far)
        held += sum(nbytes(outs[k].shape, outs[k].dtype) for k in spill)
        near, far = [in_vmem(a) for a in near], [in_hbm(a) for a in far]
        outs = [
            o if k in spill else pltpu.VMEM(o.shape, o.dtype) for k, o in enumerate(outs)
        ]
    before, after_far, last = len(scalars) + len(near), len(far), len(outs) + len(scratch)

    def body(*refs):
        sources, rest = refs[before : before + after_far], refs[before + after_far :]
        targets = rest[last : last + after_far]
        fars = [Far(a, b, rest[-1].at[k]) for k, (a, b) in enumerate(zip(sources, targets))]
        kernel(*refs[:before], *fars, *rest[:last])
        for one in fars:
            one.ready()

    return pl.pallas_call(
        body if far else kernel,
        name=name,
        out_shape=tuple(outs),
        in_specs=[SMEM] * len(scalars) + [VMEM] * len(near) + [ANY] * len(far),
        out_specs=tuple([VMEM] * len(outs)),
        scratch_shapes=[pltpu.VMEM(s.shape, s.dtype) for s in scratch]
        + [pltpu.VMEM(a.shape, a.dtype) for a in far]
        + ([pltpu.SemaphoreType.DMA((len(far),))] if far else []),
        compiler_params=pltpu.CompilerParams(vmem_limit_bytes=held + (8 << 20)),
        cost_estimate=pl.CostEstimate(flops=flops, bytes_accessed=moved, transcendentals=0),
    )(*scalars, *near, *far)


def first_conv(scal, view, above, w_down, devices, pin):
    slots, _, cells, both = view.shape
    half = both // 2
    full = w_down.shape[-1]
    taps = w_down.reshape(3, 3 * half, full)
    if pin:
        view, above, taps = in_vmem(view), in_vmem(above), in_hbm(taps)
    wide = 256
    count = full // wide
    return pl.pallas_call(
        first_kernel,
        name="first",
        out_shape=(shape((slots, cells, full), BF), shape((devices, 2, full))),
        in_specs=[SMEM, VMEM, VMEM, ANY],
        out_specs=(VMEM, VMEM),
        scratch_shapes=[
            pltpu.VMEM((count, 3, 3 * half, wide), BF), pltpu.SemaphoreType.DMA((count,))
        ],
        compiler_params=pltpu.CompilerParams(vmem_limit_bytes=32 << 20),
        cost_estimate=pl.CostEstimate(
            flops=18 * slots * cells * half * full, bytes_accessed=18 * half * full, transcendentals=0
        ),
    )(scal, view, above, taps)


def flipped(kernel):
    return jnp.swapaxes(jnp.flip(kernel, (0, 1)), 2, 3)


def on_device(
    inputs,
    image_counts,
    w_down,
    w_short,
    w_main,
    w_inner,
    w_spatial,
    w_trans,
    w_unite,
    gains_wide,
    gains_narrow,
    shifts_wide,
    shifts_narrow,
    grad_output,
):
    half = w_short.shape[1]
    full = 2 * half
    slots, height_dev, width, _ = grad_output.shape
    here = Plane()
    wide = here.chips == 4 and half % (128 * here.chips) == 0
    stage = functools.partial(call, pin=wide)
    groups, chips = here.groups, here.chips
    height = here.rows * height_dev
    cells = height * width
    batch = lax.axis_index("batch")
    counts = image_counts.astype(F32)
    own_count = image_counts[batch]
    pixels = jnp.sum(counts) * cells
    weight = (here.core < own_count).astype(F32)

    scal = [weight, pixels]
    for step in range(groups):
        plane = batch ^ step
        for slot in (here.core, 1 - here.core):
            count = (slot < image_counts[plane]).astype(F32) * cells
            scal += [count, 1.0 / jnp.maximum(count, 1.0)]
    scal = jnp.stack(scal)
    spots = jnp.stack(
        [2 * (here.chip ^ step) + (here.core ^ side) for step in range(chips) for side in range(2)]
    ).astype(jnp.int32)
    slot_scal = jnp.concatenate(
        [
            (jnp.arange(slots) < own_count).astype(F32),
            (1.0 / (own_count.astype(F32) * height_dev * width))[None],
        ]
    )
    device_counts = jnp.tile(counts * (height_dev * width), here.rows).reshape(-1, 1)

    view = inputs.reshape(slots, 2, width, 2 * half)
    below = [(i, i + 1) for i in range(here.rows - 1)]
    above = lax.ppermute(view[:, 1], "rows", below)
    params = jnp.concatenate(
        [gains_wide, shifts_wide]
        + [jnp.pad(p, ((0, 0), (0, half))) for p in (gains_narrow, shifts_narrow)]
    )
    down_rows, sums = first_conv(slot_scal, view, above, w_down, here.rows * groups, wide)
    gathered = lax.all_to_all(sums, ("rows", "batch"), 0, 0, tiled=True)
    down_pieces = here.row_pieces(*here.split(down_rows))
    grad_mine, grad_other = here.split(grad_output.reshape(slots, width, full))
    spot_pair = jnp.stack([here.core, here.chip]).astype(jnp.int32)
    planes = jnp.stack([here.core, here.chip] + [batch ^ step for step in range(groups)]).astype(jnp.int32)
    over_counts = 1.0 / device_counts
    gathered, scal, spots, spot_pair, planes, device_counts, over_counts, params, grad_mine, grad_other = (
        lax.optimization_barrier(
            (gathered, scal, spots, spot_pair, planes, device_counts, over_counts, params, grad_mine, grad_other)
        )
    )
    if wide:
        source = lax.all_gather(view, ("rows", "batch"))
    down_pre, sectioned, main_pre, main_pay, down_coef = stage(
        functools.partial(main_kernel, 2 * chips),
        "main",
        [scal, spots],
        [gathered, device_counts, over_counts, params],
        [
            shape((cells, full), BF), shape((cells, full), BF), shape((cells, half)),
            shape((2, half)), shape((2, full)),
        ],
        2 * cells * full * half,
        far=[*down_pieces, w_main],
    )

    grad_pieces = here.row_pieces(after(grad_mine, main_pay), after(grad_other, main_pay))

    main_all = here.everywhere(main_pay)
    short_pre, short_pay = stage(
        short_kernel,
        "short",
        [scal],
        [sectioned],
        [shape((cells, half)), shape((2, half))],
        2 * cells * full * half,
        far=[w_short],
    )
    mainline, inner_pre, inner_pay, main_coef = stage(
        functools.partial(inner_kernel, groups),
        "inner",
        [scal],
        [*main_all, main_pre, params],
        [shape((cells, half), BF), shape((cells, half)), shape((2, half)), shape((2, half))],
        2 * cells * half * half,
        far=[w_inner],
    )
    inner_all = here.everywhere(inner_pay)
    rim, spatial_pre, spatial_pay, inner_coef = stage(
        functools.partial(spatial_kernel, groups, width),
        "spatial",
        [scal],
        [*inner_all, inner_pre, params],
        [
            shape((cells + 2 * width, 3 * half), BF), shape((cells, half)),
            shape((2, half)), shape((2, half)),
        ],
        18 * cells * half * half,
        far=[w_spatial.reshape(9 * half, half)],
    )
    if wide:
        spatial_pay = after(spatial_pay, *grad_pieces)
    both_all = here.everywhere(jnp.concatenate([spatial_pay, short_pay], axis=1))
    spatial_all = [b[:, :half] for b in both_all]
    short_all = [b[:, half:] for b in both_all]
    merged, trans_pre, trans_pay, spatial_coef = stage(
        functools.partial(trans_kernel, groups),
        "trans",
        [scal],
        [*spatial_all, spatial_pre, mainline, params],
        [shape((cells, half), BF), shape((cells, half)), shape((2, half)), shape((2, half))],
        2 * cells * half * half,
        far=[w_trans],
    )
    trans_all = here.everywhere(trans_pay)
    shortcut, unite_part, short_coef = stage(
        functools.partial(shortcut_kernel, groups),
        "shortcut",
        [scal],
        [*short_all, short_pre, params],
        [shape((cells, half), BF), shape((cells, full)), shape((2, half))],
        2 * cells * half * full,
        far=[w_unite],
    )
    transition, unite_pre, unite_pay, trans_coef = stage(
        functools.partial(unite_kernel, groups),
        "unite",
        [scal],
        [*trans_all, trans_pre, unite_part, params],
        [shape((cells, half), BF), shape((cells, full)), shape((2, full)), shape((2, half))],
        2 * cells * half * full,
        far=[w_unite],
    )
    unite_all = here.everywhere(unite_pay)
    unite_pushed, mine, other, unite_pay, unite_coef = stage(
        functools.partial(turn_kernel, groups, 2 * chips),
        "turn",
        [scal, spots],
        [*unite_all, unite_pre, params],
        [
            shape((cells, full)), shape((width, full), BF), shape((width, full), BF),
            shape((2, full)), shape((2, full)),
        ],
        40 * cells * full,
        far=grad_pieces,
        spill=(1, 2),
    )
    output_rows = (mine, here.swap(other))

    unite_all = here.everywhere(unite_pay)
    grad_unite_pre, unite_sums, trans_pushed, trans_pay = stage(
        functools.partial(back_trans_kernel, groups),
        "back_trans",
        [scal],
        [*unite_all, unite_pushed, unite_pre, unite_coef, params, trans_pre, trans_coef],
        [shape((cells, full), BF), shape((2, full)), shape((cells, half)), shape((2, half))],
        2 * cells * half * full,
        [shape((cells, half))],
        far=[w_unite],
    )
    trans_all = here.everywhere(trans_pay)
    if wide:

        def of_pair(pair):
            mine, other = pair
            return (mine.astype(F32) + here.swap(other).astype(F32)).astype(BF)

        share_unite = of_pair(
            stage(
                share_unite_kernel,
                "share_unite",
                [spot_pair],
                [shortcut, transition, grad_unite_pre],
                [shape((full, full // chips // 2), BF)] * 2,
                2 * cells * full * full // chips,
            )
        )
    short_pushed, short_pay = stage(
        back_short_kernel,
        "back_short",
        [],
        [grad_unite_pre, short_pre, short_coef, params],
        [shape((cells, half)), shape((2, half))],
        2 * cells * half * full,
        [shape((cells, half))],
        far=[w_unite],
    )
    grad_trans_pre, trans_sums, grad_merged, spatial_pushed, spatial_pay = stage(
        functools.partial(back_spatial_kernel, groups),
        "back_spatial",
        [scal],
        [*trans_all, trans_pushed, trans_pre, trans_coef, spatial_pre, spatial_coef, params],
        [
            shape((cells, half), BF), shape((2, half)), shape((cells, half)), shape((cells, half)),
            shape((2, half)),
        ],
        2 * cells * half * half,
        far=[w_trans],
    )
    both_all = here.everywhere(jnp.concatenate([spatial_pay, short_pay], axis=1))
    spatial_all = [b[:, :half] for b in both_all]
    short_all = [b[:, half:] for b in both_all]
    grad_spatial_pre, spatial_sums, inner_pushed, inner_pay = stage(
        functools.partial(back_inner_kernel, groups, width),
        "back_inner",
        [scal],
        [
            *spatial_all, spatial_pushed, spatial_pre, spatial_coef, inner_pre, inner_coef, params,
        ],
        [shape((cells, half), BF), shape((2, half)), shape((cells, half)), shape((2, half))],
        18 * cells * half * half,
        [shape((cells + 2 * width, 3 * half), BF), shape((cells, half))],
        far=[w_spatial.reshape(9 * half, half)],
    )
    inner_all = here.everywhere(inner_pay)
    grad_short_pre, short_sums, sectioned_part = stage(
        functools.partial(settle_short_kernel, groups),
        "settle_short",
        [scal],
        [*short_all, short_pushed, short_pre, short_coef, params],
        [shape((cells, half), BF), shape((2, half)), shape((cells, full))],
        2 * cells * half * full,
        far=[w_short],
    )
    grad_inner_pre, inner_sums, main_pushed, main_pay = stage(
        functools.partial(back_main_kernel, groups),
        "back_main",
        [scal],
        [*inner_all, inner_pushed, inner_pre, inner_coef, grad_merged, main_pre, main_coef, params],
        [shape((cells, half), BF), shape((2, half)), shape((cells, half)), shape((2, half))],
        2 * cells * half * half,
        [shape((cells, half))],
        far=[w_inner],
    )
    if wide:
        lean = half // chips // 2
        share_spatial = of_pair(
            stage(
                functools.partial(share_spatial_kernel, cells),
                "share_spatial",
                [spot_pair],
                [rim, grad_spatial_pre],
                [shape((lean, 9 * half), BF)] * 2,
                18 * cells * half * half // chips,
            )
        )
        share_pack = of_pair(
            stage(
                share_pack_kernel,
                "share_pack",
                [spot_pair],
                [sectioned, grad_short_pre, merged, grad_trans_pre, mainline, grad_inner_pre],
                [shape((lean, 2 * full), BF)] * 2,
                8 * cells * half * half // chips,
            )
        )
    main_all = here.everywhere(main_pay)
    grad_main_pre, main_sums, down_pushed, down_pay = stage(
        functools.partial(back_down_kernel, groups),
        "back_down",
        [scal],
        [
            *main_all, main_pushed, main_pre, main_coef, sectioned_part, down_pre, down_coef, params,
        ],
        [shape((cells, half), BF), shape((2, half)), shape((cells, full)), shape((2, full))],
        2 * cells * half * full,
        [shape((cells, full))],
        far=[w_main],
    )
    down_all = here.everywhere(down_pay)
    spare = width
    if wide:
        grad_cut = stage(
            functools.partial(cut_down_kernel, groups),
            "cut_down",
            [scal, spot_pair],
            [*down_all, down_pushed, down_pre, down_coef, params],
            [shape((cells, full // chips), BF)],
            10 * cells * full // chips,
        )[0]
        cuts = here.plane_hops(grad_cut)
    grad_down_pre, down_sums = stage(
        functools.partial(settle_down_kernel, groups),
        "settle_down",
        [scal],
        [*down_all, down_pushed, down_pre, down_coef, params],
        [shape((cells + spare, full), BF), shape((2, full))],
        10 * cells * full,
    )
    if wide:
        near = pl.pallas_call(
            functools.partial(back_input_kernel, width),
            name="back_input",
            grid=(half // 128,),
            out_shape=shape((4, 2 * width, half)),
            in_specs=[
                SMEM,
                pl.BlockSpec((cells + spare, full), lambda n: (0, 0)),
                pl.BlockSpec((9, 128, full), lambda n: (0, n, 0)),
            ],
            out_specs=pl.BlockSpec((4, 2 * width, 128), lambda n: (0, 0, n)),
            scratch_shapes=[pltpu.VMEM((3 * width, full), BF)] * 2,
            compiler_params=pltpu.CompilerParams(vmem_limit_bytes=16 << 20),
            cost_estimate=pl.CostEstimate(
                flops=36 * width * full * half, bytes_accessed=18 * full * half, transcendentals=0
            ),
        )(spot_pair, grad_down_pre, w_down.reshape(9, half, full))
        share_main = of_pair(
            stage(
                share_main_kernel,
                "share_main",
                [spot_pair],
                [sectioned, grad_main_pre],
                [shape((lean, full), BF)] * 2,
                4 * cells * half * half // chips,
            )
        )
        shares = lax.psum((share_unite, share_pack, share_spatial, share_main), "batch")
        mine, other = here.split(near.reshape(2, 2, 2 * width, half))
        grad_inputs = jnp.stack(here.by_core(mine, here.swap(other)))
        columns = full // chips
        sums_here = [shape((full, 4 * columns)), shape((full, 4 * columns))]
        halves = [shape((9 * half, columns // 2), BF)] * 2

        def share_down(steps, earlier):
            outs = halves if earlier else sums_here
            near = [*(cuts[step] for step in steps), *earlier]
            scratch = [
                pltpu.VMEM((cells + spare, columns), BF),
                pltpu.VMEM((cells, 4 * columns), BF),
                pltpu.VMEM((len(steps), 2 * chips, 2, width, full), BF),
                pltpu.SemaphoreType.DMA((len(steps), 2 * chips)),
            ]
            if earlier:
                scratch = [pltpu.VMEM(a.shape, F32) for a in sums_here] + scratch
            return pl.pallas_call(
                functools.partial(share_down_kernel, steps, chips, width, int(bool(earlier))),
                name="share_down",
                out_shape=tuple(pltpu.VMEM(o.shape, o.dtype) for o in outs),
                in_specs=[SMEM] + [VMEM] * len(near) + [ANY],
                out_specs=(VMEM, VMEM),
                scratch_shapes=scratch,
                compiler_params=pltpu.CompilerParams(vmem_limit_bytes=30 << 20),
                cost_estimate=pl.CostEstimate(
                    flops=18 * len(steps) * cells * half * columns,
                    bytes_accessed=len(steps) * 4 * cells * full,
                    transcendentals=0,
                ),
            )(planes, *map(in_vmem, near), in_hbm(source))

        middle = (groups + 1) // 2
        cuts[:middle] = lax.optimization_barrier((*cuts[:middle], near))[:middle]
        first_sums = share_down(range(middle), ())
        cuts[middle:] = lax.optimization_barrier((*cuts[middle:], *first_sums))[: groups - middle]
        mine, other = share_down(range(middle, groups), first_sums)
        grad_w_down = mine.astype(F32) + here.swap(other).astype(F32)
        early = stage(
            finish_kernel,
            "finish",
            [],
            shares,
            [
                shape((full, 2 * lean)), shape((lean, full)), shape((lean, half)), shape((lean, half)),
                shape((9, lean, half)), shape((lean, full)),
            ],
            0,
            spill=range(6),
        )
        early = [
            early[1].T, early[5].T, early[3].T, jnp.swapaxes(early[4], 1, 2), early[2].T, early[0],
        ]
    else:
        grad_down_pre = grad_down_pre[:cells]
        def share(values, grad):
            columns = grad.shape[1] // chips
            grad = lax.dynamic_slice_in_dim(grad, here.chip * columns, columns, 1)
            part = jnp.concatenate([dot_cells(v, grad) for v in values], axis=0)
            mine, other = here.split(part.reshape(part.shape[0], 2, columns // 2), 1)
            return (mine + here.swap(other.astype(BF)).astype(F32)).astype(BF)

        windows = [rim[i * width : i * width + cells] for i in range(3)]
        early = lax.psum(
            (
                share([sectioned], grad_short_pre),
                share([sectioned], grad_main_pre),
                share([mainline], grad_inner_pre),
                share(windows, grad_spatial_pre),
                share([merged], grad_trans_pre),
                jnp.concatenate([share([shortcut], grad_unite_pre), share([transition], grad_unite_pre)]),
            ),
            "batch",
        )
        early = [e.astype(F32) for e in early]

        mine, other = here.split(view)
        got = here.chip_hops(jnp.stack([mine, here.swap(other)], axis=1))
        source = jnp.zeros((2, here.rows, width, full), BF)
        for step, piece in enumerate(got):
            for side in range(2):
                source = lax.dynamic_update_slice_in_dim(
                    source, piece[:, side : side + 1], spots[2 * step + side], 1
                )
        grad_map = grad_down_pre.reshape(height, width, full)
        columns = full // chips
        grad_cut = lax.dynamic_slice_in_dim(grad_map, here.chip * columns, columns, 2)
        ahead = jnp.pad(grad_cut[:, 1:], ((0, 0), (0, 1), (0, 0)))
        upper = jnp.pad(grad_cut[1:], ((0, 1), (0, 0), (0, 0)))
        both_ahead = jnp.pad(ahead[1:], ((0, 1), (0, 0), (0, 0)))
        even_rows = source[0].reshape(cells, full)
        odd_rows = source[1].reshape(cells, full)

        def taps_of(rows, here_grad, ahead_grad):
            plain = dot_cells(rows, here_grad.reshape(cells, columns))
            before = dot_cells(rows[:, half:], ahead_grad.reshape(cells, columns))
            return [before, plain]

        part = jnp.concatenate(
            taps_of(odd_rows, upper, both_ahead)
            + taps_of(even_rows, grad_cut, ahead)
            + taps_of(odd_rows, grad_cut, ahead),
            axis=0,
        )
        mine, other = here.split(part.reshape(9 * half, 2, columns // 2), 1)
        part = (mine + here.swap(other.astype(BF)).astype(F32)).astype(BF)
        grad_w_down = lax.psum(part, "batch").astype(F32)

        pair_rows = 2 * height_dev
        grad_image = jnp.pad(grad_map, ((0, 1), (0, 0), (0, 0)))
        grad_block = lax.dynamic_slice_in_dim(grad_image, here.chip * pair_rows, pair_rows + 1, 0)
        widened = lax.conv_general_dilated(
            grad_block[None],
            flipped(w_down),
            (1, 1),
            ((1, 0), (1, 2)),
            lhs_dilation=(2, 2),
            dimension_numbers=("NHWC", "HWIO", "NHWC"),
            preferred_element_type=F32,
        )[0]
        mine = lax.dynamic_slice_in_dim(widened, here.core * pair_rows, pair_rows, 0)
        other = lax.dynamic_slice_in_dim(widened, (1 - here.core) * pair_rows, pair_rows, 0)
        grad_inputs = jnp.stack(here.by_core(mine, here.swap(other)))

    output = jnp.stack(here.by_core(*after(output_rows, down_pay))).reshape(grad_output.shape)
    norm_grads = stage(
        functools.partial(norm_sums_kernel, 2),
        "norm_sums",
        [],
        [down_sums, unite_sums, short_sums, main_sums, inner_sums, spatial_sums, trans_sums],
        [shape((2, full)), shape((5, half))] * 2,
        0,
        spill=range(4),
    )
    return (
        output,
        grad_inputs,
        grad_w_down.reshape(3, 3, half, -1),
        early[0],
        early[1],
        early[2],
        early[3].reshape(3, 3, half, -1),
        early[4],
        early[5],
        *norm_grads,
    )


def solution(mesh):
    placed = (P("batch", "rows", None, None),) + (P(),) * 12 + (P("batch", "rows", None, None),)
    return jax.shard_map(
        on_device,
        mesh=mesh,
        in_specs=placed,
        out_specs=(
            P("batch", "rows", None, None),
            P("batch", "rows", None, None),
            P(None, None, None, "rows"),
            P(None, "rows"),
            P(None, "rows"),
            P(None, "rows"),
            P(None, None, None, "rows"),
            P(None, "rows"),
            P(None, "rows"),
            P(),
            P(),
            P(),
            P(),
        ),
        check_vma=False,
    )
```

time: 391 us -> 306 us (0.78)
  local copies, waits for them, and re-layouts: 86.5 us -> 10.7 us
  Pallas kernels: 47.5 us -> 86.3 us
  waiting for transfers between devices: 114 us -> 90 us
  other arithmetic: 30.1 us -> 10.6 us
  matrix products: 17.5 us -> 0 us
  starting transfers between devices: 71.7 us -> 84.2 us
    psum x1, waiting for transfers between devices: 93.8 us -> 30.9 us  [on_device(): lax.psum((share_unite, share_pack, share_spatial, share_main), 'batch')]
    pallas_call x18 -> x27, Pallas kernels: 47.5 us -> 86.3 us  [the longest x23 63.6 us: call(): pl.pallas_call(body if far else kernel, name=name, out_shape=tuple(outs),...]
    unnamed x161 -> x60, local copies, waits for them, and re-layouts: 35.4 us -> 5.29 us
    ppermute x33 -> x36, waiting for transfers between devices: 17 us -> 42 us  [plane_hops(): lax.ppermute(value, 'batch', [(i, i ^ step) for i in range(self.groups)])]
    convert_element_type x14 -> x4, other arithmetic: 18.3 us -> 3.18 us  [of_pair(): return (mine.astype(F32) + here.swap(other).astype(F32)).astype(BF)]
    dynamic_slice x12 -> x0, local copies, waits for them, and re-layouts: 13.6 us -> none  [the longest x2 8.55 us: split(): other = lax.dynamic_index_in_dim(block, 1 - self.core, axis, keepdims=False)]
    dot_general x15 -> x0, matrix products: 11.6 us -> none  [dot_cells(): lax.dot_general(a, b, (((0,), (0,)), ((), ())), preferred_element_type=F32)]
    dynamic_update_slice x8 -> x0, local copies, waits for them, and re-layouts: 8.26 us -> none  [on_device(): lax.dynamic_update_slice_in_dim(source, piece[:, side:side + 1], spots[2...]
  transfers between devices with their start and end apart: 69 -> 72, of which waited for: 24 -> 31; matrix products, arithmetic and copies ran while one was open for 24% -> 4% of each run, Pallas kernels for 11% -> 28%
where the time goes in v3:
time: 306 us; the launch traced here: 305 us
  waiting for transfers between devices  90 us (29%)
  Pallas kernels  86.3 us (28%)
  starting transfers between devices  84.2 us (28%)
  between operations  23.3 us (8%)
  local copies, waits for them, and re-layouts  10.7 us (3%)
  other arithmetic  10.6 us (3%)
    pallas_call x23, Pallas kernels, call(): pl.pallas_call(body if far else kernel, name=name, out_shape=tuple(outs),...  63.6 us
    ppermute x36, starting transfers between devices, plane_hops(): lax.ppermute(value, 'batch', [(i, i ^ step) for i in range(self.groups)])  53.6 us
    ppermute x36, waiting for transfers between devices, plane_hops(): lax.ppermute(value, 'batch', [(i, i ^ step) for i in range(self.groups)])  42 us
    psum x1, waiting for transfers between devices, on_device(): lax.psum((share_unite, share_pack, share_spatial, share_main), 'batch')  30.9 us
    ppermute x12, starting transfers between devices, two_ways(): lax.ppermute(value, 'rows', [(i, i ^ 2 * step) for i in range(self.rows)])  15.4 us
    pallas_call x2, Pallas kernels, share_down(): pl.pallas_call(functools.partial(share_down_kernel, steps, chips, width,...  11.8 us
    ppermute x20, waiting for transfers between devices, swap(): return lax.ppermute(value, 'rows', [(i, i ^ 1) for i in range(self.rows)])  10.1 us
    ppermute x12, waiting for transfers between devices, two_ways(): lax.ppermute(value, 'rows', [(i, i ^ 2 * step) for i in range(self.rows)])  6.95 us
  transfers between devices with their start and end apart: 72, of which 31 were waited for; matrix products, arithmetic and copies ran while one was open for 4% of the time, Pallas kernels for 28%

profile of v3, /device:TPU:0, one launch (start us, length us, event | category | flops | bytes accessed | tf_op | source)
XLA Modules:
  0.0 305.0 jit_solution(17292158620966117285)
XLA Ops:
  8.1 2.0 all_gather_reshape.3
  11.3 2.4 collective-permute-start
  16.0 6.2 %first.1 = (bf16[2,64,1024]{2,1,0:T(8,128)(2,1)S(1)}, f32[32,2,1024]{2,1,0:T(2,128)}) custom-call(f32[3]{0:T(128)S(1)} %pad_maximum_fusion.12.scal, bf16[2,2,64,1024]{3,2,1,0:T(8,128)(2,1)S(1)} %reshape.78.x, bf16[2,64,1024]{2,1,0:T(8,128)(2,1)S(1)} %collective-permute-done.above, bf16[3,1536,1024]{2,1,0:T(8,128)(2,1)} %bitcast.86), custom_call_target="tpu_custom_call" | custom-call | flops 1207959552 | bytes 9437184 | tf_op jit(solution)/shard_map/first/pallas_call | solution.py:841
  22.3 3.7 %collective-permute-start.1 = (bf16[64,1024]{1,0:T(8,128)(2,1)S(1)}, bf16[64,1024]{1,0:T(8,128)(2,1)S(1)}, u32[]{:S(2)}, u32[]{:S(2)}) collective-permute-start(bf16[64,1024]{1,0:T(8,128)(2,1)S(1)} %get-tuple-element.264), channel_id=1, source_target_pairs={{0,4},{4,0},{8,12},{12,8},{16,20},{20,16},{24,28},{28,24},{1,5},{5... | collective-permute-start | bytes 393224 | tf_op jit(solution)/shard_map/ppermute | solution.py:63
  26.7 2.5 collective-permute-start.2
  29.2 6.0 %all-to-all-start = ((f32[32,2,1024]{2,1,0:T(2,128)}), f32[32,2,1024]{2,1,0:T(2,128)S(1)}, u32[]{:S(2)}, u32[]{:S(2)}) async-start(f32[32,2,1024]{2,1,0:T(2,128)} %get-tuple-element.115), calls=%async_computation | async-start | bytes 524288 | tf_op jit(solution)/shard_map/all_to_all | solution.py:918
  35.2 1.8 collective-permute-start.5
  37.4 1.8 collective-permute-start.3
  39.2 1.5 collective-permute-start.6
  40.7 2.6 collective-permute-done.5.refs_11_
  52.6 3.6 %main.1 = (bf16[512,1024]{1,0:T(8,128)(2,1)S(1)}, bf16[512,1024]{1,0:T(8,128)(2,1)S(1)}, f32[512,512]{1,0:T(8,128)S(1)}, f32[2,512]{1,0:T(2,128)S(1)}, f32[2,1024]{1,0:T(2,128)S(1)}) custom-call(f32[18]{0:T(128)S(1)} %stack.150.refs_0_.scal, s32[8]{0:T(128)S(1)} %stack.159.refs_1_, f32[32,2,1024]{2,1,0:T(2,128)S(1)} %all-to-all-done.refs_2_, ...), custom_call_target="tpu_custom_call" | custom-call | flops 536870912 | bytes 5574912 | tf_op jit(solution)/shard_map/main/pallas_call | solution.py:818
  57.5 3.0 collective-permute-start.10
  62.3 3.6 %collective-permute-done.11.refs_4_ = f32[4,512]{1,0:T(4,128)S(1)} collective-permute-done((f32[4,512]{1,0:T(4,128)S(1)}, f32[4,512]{1,0:T(4,128)S(1)}, u32[]{:S(2)}, u32[]{:S(2)}) %collective-permute-start.11) | collective-permute-done | bytes 8224 | tf_op jit(solution)/shard_map/ppermute | solution.py:83
  65.9 2.2 inner.1
  70.4 2.5 collective-permute-start.14
  72.9 1.8 collective-permute-start.15
  74.7 2.7 short.1
  81.6 5.7 %spatial.1 = (bf16[640,1536]{1,0:T(8,128)(2,1)S(1)}, f32[512,512]{1,0:T(8,128)S(1)}, f32[2,512]{1,0:T(2,128)S(1)}, f32[2,512]{1,0:T(2,128)S(1)}) custom-call(f32[18]{0:T(128)S(1)} %stack.150.refs_0_.scal, f32[4,512]{1,0:T(4,128)S(1)} %pad_maximum_fusion.7.refs_1_, f32[4,512]{1,0:T(4,128)S(1)} %collective-permute-done.13.refs_2_, ...), custom_call_target="tpu_custom_call" | custom-call | flops 2415919104 | bytes 8880128 | tf_op jit(solution)/shard_map/spatial/pallas_call | solution.py:818
  87.5 1.9 collective-permute-done.21.refs_14_
  89.4 2.3 collective-permute-done.22.refs_15_
  93.7 3.8 %collective-permute-start.24 = (f32[4,1024]{1,0:T(4,128)S(1)}, f32[4,1024]{1,0:T(4,128)S(1)}, u32[]{:S(2)}, u32[]{:S(2)}) collective-permute-start(f32[4,1024]{1,0:T(4,128)S(1)} %pad_maximum_fusion.1), channel_id=1, source_target_pairs={{0,1},{1,0},{2,3},{3,2},{4,5},{5,4},{6,7},{7,6},{8,9},{9,8},{10,11... | collective-permute-start | bytes 49160 | tf_op jit(solution)/shard_map/ppermute | solution.py:83
  97.4 1.7 collective-permute-done.26
  99.1 1.6 collective-permute-done.24
  100.7 2.2 trans.1
  105.1 1.8 collective-permute-start.29
  106.8 1.8 collective-permute-start.30
  108.7 2.9 shortcut.1
  112.5 3.1 %unite.1 = (bf16[512,512]{1,0:T(8,128)(2,1)S(1)}, f32[512,1024]{1,0:T(8,128)S(1)}, f32[2,1024]{1,0:T(2,128)S(1)}, f32[2,512]{1,0:T(2,128)S(1)}) custom-call(f32[18]{0:T(128)S(1)} %stack.150.refs_0_.scal, f32[4,512]{1,0:T(4,128)S(1)} %pad_maximum_fusion.8.refs_1_, f32[4,512]{1,0:T(4,128)S(1)} %collective-permute-done.28.refs_2_, ...), custom_call_target="tpu_custom_call" | custom-call | flops 536870912 | bytes 7966720 | tf_op jit(solution)/shard_map/unite/pallas_call | solution.py:818
  116.9 2.4 collective-permute-start.33
  119.3 2.0 collective-permute-start.34
  121.3 1.4 collective-permute-done.33.refs_4_
  122.7 2.4 collective-permute-done.34.refs_5_
  125.2 3.8 %turn.1 = (f32[512,1024]{1,0:T(8,128)S(1)}, bf16[64,1024]{1,0:T(8,128)(2,1)S(1)}, bf16[64,1024]{1,0:T(8,128)(2,1)S(1)}, f32[2,1024]{1,0:T(2,128)S(1)}, f32[2,1024]{1,0:T(2,128)S(1)}) custom-call(f32[18]{0:T(128)S(1)} %stack.150.refs_0_.scal, s32[8]{0:T(128)S(1)} %stack.159.refs_1_, f32[4,1024]{1,0:T(4,128)S(1)} %pad_maximum_fusion.3.refs_2_, ...), custom_call_target="tpu_custom_call" | custom-call | flops 20971520 | bytes 5644288 | tf_op jit(solution)/shard_map/turn/pallas_call | solution.py:818
  130.3 2.5 collective-permute-start.38
  132.9 1.8 collective-permute-start.39
  135.2 3.2 %collective-permute-done.39.refs_4_ = f32[4,1024]{1,0:T(4,128)S(1)} collective-permute-done((f32[4,1024]{1,0:T(4,128)S(1)}, f32[4,1024]{1,0:T(4,128)S(1)}, u32[]{:S(2)}, u32[]{:S(2)}) %collective-permute-start.39) | collective-permute-done | bytes 16416 | tf_op jit(solution)/shard_map/ppermute | solution.py:83
  138.4 4.1 %back_trans.1 = (bf16[512,1024]{1,0:T(8,128)(2,1)S(1)}, f32[2,1024]{1,0:T(2,128)S(1)}, f32[512,512]{1,0:T(8,128)S(1)}, f32[2,512]{1,0:T(2,128)S(1)}) custom-call(f32[18]{0:T(128)S(1)} %stack.150.refs_0_.scal, f32[4,1024]{1,0:T(4,128)S(1)} %pad_maximum_fusion.4.refs_1_, f32[4,1024]{1,0:T(4,128)S(1)} %collective-permute-done.37.refs_2_, ...), custom_call_target="tpu_custom_call" | custom-call | flops 536870912 | bytes 9584640 | tf_op jit(solution)/shard_map/back_trans/pallas_call | solution.py:818
  143.8 2.4 collective-permute-start.42
  146.2 2.0 collective-permute-start.43
  148.2 3.6 %back_short.1 = (f32[512,512]{1,0:T(8,128)S(1)}, f32[2,512]{1,0:T(2,128)S(1)}) custom-call(bf16[512,1024]{1,0:T(8,128)(2,1)S(1)} %get-tuple-element.153.refs_0_.grad, f32[512,512]{1,0:T(8,128)S(1)} %get-tuple-element.139.refs_5_.refs_1_.refs_6_, f32[2,512]{1,0:T(2,128)S(1)} %get-tuple-element.154.refs_2_.refs_7_, ...), custom_call_target="tpu_custom_call" | custom-call | flops 536870912 | bytes 5308416 | tf_op jit(solution)/shard_map/back_short/pallas_call | solution.py:818
  151.8 3.3 %back_spatial.1 = (bf16[512,512]{1,0:T(8,128)(2,1)S(1)}, f32[2,512]{1,0:T(2,128)S(1)}, f32[512,512]{1,0:T(8,128)S(1)}, f32[512,512]{1,0:T(8,128)S(1)}, f32[2,512]{1,0:T(2,128)S(1)}) custom-call(f32[18]{0:T(128)S(1)} %stack.150.refs_0_.scal, f32[4,512]{1,0:T(4,128)S(1)} %pad_maximum_fusion.9.refs_1_, f32[4,512]{1,0:T(4,128)S(1)} %collective-permute-done.41.refs_2_, ...), custom_call_target="tpu_custom_call" | custom-call | flops 268435456 | bytes 6397952 | tf_op jit(solution)/shard_map/back_spatial/pallas_call | solution.py:818
  156.4 1.9 collective-permute-start.47
  158.3 2.5 collective-permute-start.45
  163.0 6.7 %back_inner.1 = (bf16[512,512]{1,0:T(8,128)(2,1)S(1)}, f32[2,512]{1,0:T(2,128)S(1)}, f32[512,512]{1,0:T(8,128)S(1)}, f32[2,512]{1,0:T(2,128)S(1)}) custom-call(f32[18]{0:T(128)S(1)} %stack.150.refs_0_.scal, f32[4,512]{1,0:T(4,128)S(1)} %get-tuple-element.275.refs_1_, f32[4,512]{1,0:T(4,128)S(1)} %get-tuple-element.273.refs_2_, ...), custom_call_target="tpu_custom_call" | custom-call | flops 2415919104 | bytes 9543680 | tf_op jit(solution)/shard_map/back_inner/pallas_call | solution.py:818
  171.0 1.7 collective-permute-start.49
  173.6 1.8 collective-permute-start.51
  177.2 1.8 collective-permute-done.51.refs_4_
  179.0 3.3 %back_main.1 = (bf16[512,512]{1,0:T(8,128)(2,1)S(1)}, f32[2,512]{1,0:T(2,128)S(1)}, f32[512,512]{1,0:T(8,128)S(1)}, f32[2,512]{1,0:T(2,128)S(1)}) custom-call(f32[18]{0:T(128)S(1)} %stack.150.refs_0_.scal, f32[4,512]{1,0:T(4,128)S(1)} %pad_maximum_fusion.10.refs_1_, f32[4,512]{1,0:T(4,128)S(1)} %collective-permute-done.49.refs_2_, ...), custom_call_target="tpu_custom_call" | custom-call | flops 268435456 | bytes 6397952 | tf_op jit(solution)/shard_map/back_main/pallas_call | solution.py:818
  183.9 2.4 collective-permute-start.54
  186.3 2.0 collective-permute-start.55
  188.3 2.5 settle_short.1
  191.7 5.2 %back_down.1 = (bf16[512,512]{1,0:T(8,128)(2,1)S(1)}, f32[2,512]{1,0:T(2,128)S(1)}, f32[512,1024]{1,0:T(8,128)S(1)}, f32[2,1024]{1,0:T(2,128)S(1)}) custom-call(f32[18]{0:T(128)S(1)} %stack.150.refs_0_.scal, f32[4,512]{1,0:T(4,128)S(1)} %pad_maximum_fusion.11.refs_1_, f32[4,512]{1,0:T(4,128)S(1)} %collective-permute-done.53.refs_2_, ...), custom_call_target="tpu_custom_call" | custom-call | flops 536870912 | bytes 9027584 | tf_op jit(solution)/shard_map/back_down/pallas_call | solution.py:818
  198.6 2.5 collective-permute-start.58
  201.1 1.8 collective-permute-start.59
  204.6 2.1 collective-permute-done.59.rest_3_
  208.8 4.7 %back_input.1 = f32[4,128,512]{2,1,0:T(8,128)S(1)} custom-call(s32[2]{0:T(128)S(1)} %pad_add_fusion.spots, bf16[576,1024]{1,0:T(8,128)(2,1)S(1)} %get-tuple-element.173.grad, bf16[9,512,1024]{2,1,0:T(8,128)(2,1)S(1)} %bitcast.89), custom_call_target="tpu_custom_call" | custom-call | flops 1207959552 | bytes 9437184 | tf_op jit(solution)/shard_map/back_input/pallas_call | solution.py:1168
  213.4 2.4 collective-permute-start.61
  216.6 2.0 collective-permute-start.62
  221.1 5.2 %share_down.2 = (f32[1024,1024]{1,0:T(8,128)S(1)}, f32[1024,1024]{1,0:T(8,128)S(1)}) custom-call(s32[6]{0:T(128)S(1)} %stack.167.spots, bf16[512,256]{1,0:T(8,128)(2,1)S(1)} %cut_down.1.rest_0_, bf16[512,256]{1,0:T(8,128)(2,1)S(1)} %collective-permute-done.63.rest_1_, bf16[32,2,2,64,1024]{4,3,2,1,0:T(8,128)(2,1)} %all-gather.2.cloned.1.call-done.rest_2_.rest_4_), custom_call_target="tpu_custom_call" | custom-call | flops 2415919104 | bytes 4194304 | tf_op jit(solution)/shard_map/share_down/pallas_call | solution.py:1213
  226.3 19.0 %collective-permute-done.61.rest_0_ = bf16[512,256]{1,0:T(8,128)(2,1)S(1)} collective-permute-done((bf16[512,256]{1,0:T(8,128)(2,1)S(1)}, bf16[512,256]{1,0:T(8,128)(2,1)S(1)}, u32[]{:S(2)}, u32[]{:S(2)}) %collective-permute-start.61) | collective-permute-done | bytes 262176 | tf_op jit(solution)/shard_map/ppermute | solution.py:83
  245.3 6.6 %share_down.3 = (bf16[4608,128]{1,0:T(8,128)(2,1)S(1)}, bf16[4608,128]{1,0:T(8,128)(2,1)}) custom-call(s32[6]{0:T(128)S(1)} %stack.167.spots, bf16[512,256]{1,0:T(8,128)(2,1)S(1)} %collective-permute-done.61.rest_0_, bf16[512,256]{1,0:T(8,128)(2,1)S(1)} %collective-permute-done.62.rest_1_, f32[1024,1024]{1,0:T(8,128)S(1)} %get-tuple-element.177.rest_2_, ...), custom_call_target="tpu_custom_call" | custom-call | flops 2415919104 | bytes 4194304 | tf_op jit(solution)/shard_map/share_down/pallas_call | solution.py:1213
  258.3 30.9 %all-reduce.5.cloned.1.call-done = (bf16[1024,128]{1,0:T(8,128)(2,1)}, bf16[64,2048]{1,0:T(8,128)(2,1)}, bf16[64,4608]{1,0:T(8,128)(2,1)}, bf16[64,1024]{1,0:T(8,128)(2,1)}) async-done(((bf16[1024,128]{1,0:T(8,128)(2,1)}, bf16[64,2048]{1,0:T(8,128)(2,1)}, bf16[64,4608]{1,0:T(8,128)(2,1)}, bf16[64,1024]{1,0:T(8,128)(2,1)}), (bf16[1024,128]{1,0:T(8,128)(2,1)}, bf16[64,2048]{1,0:T(8,128)(2,1)}, ...) | async-done | bytes 1245200 | tf_op jit(solution)/shard_map/psum | solution.py:1195
  293.1 1.6 finish.1
  294.7 2.9 convert_add_fusion
  (220 shorter events, 54.4 us)
Async XLA Ops:
  8.0 213.1 %all-gather.2.cloned.1.call-start = ((), (), s32[]{:S(2)}) async-start(), calls=%async_computation.1 | async-start | bytes 17301504 | tf_op jit(solution)/shard_map/all_gather | solution.py:930
  11.3 4.6 %collective-permute-start = (bf16[2,64,1024]{2,1,0:T(8,128)(2,1)S(1)}, bf16[2,64,1024]{2,1,0:T(8,128)(2,1)S(1)}, u32[]{:S(2)}, u32[]{:S(2)}) collective-permute-start(bf16[2,64,1024]{2,1,0:T(8,128)(2,1)S(1)} %slice_bitcast_fusion), channel_id=1, source_target_pairs={{0,4},{4,8},{8,12},{12,16},{16,20},{20,24},{24,28},{1,5},{5,9},{9,... | collective-permute-start | bytes 786440 | tf_op jit(solution)/shard_map/ppermute | solution.py:912
  22.3 12.9 %collective-permute-start.1 = (bf16[64,1024]{1,0:T(8,128)(2,1)S(1)}, bf16[64,1024]{1,0:T(8,128)(2,1)S(1)}, u32[]{:S(2)}, u32[]{:S(2)}) collective-permute-start(bf16[64,1024]{1,0:T(8,128)(2,1)S(1)} %get-tuple-element.264), channel_id=1, source_target_pairs={{0,4},{4,0},{8,12},{12,8},{16,20},{20,16},{24,28},{28,24},{1,5},{5... | collective-permute-start | bytes 393224 | tf_op jit(solution)/shard_map/ppermute | solution.py:63
  26.7 12.5 %collective-permute-start.2 = (bf16[64,1024]{1,0:T(8,128)(2,1)S(1)}, bf16[64,1024]{1,0:T(8,128)(2,1)S(1)}, u32[]{:S(2)}, u32[]{:S(2)}) collective-permute-start(bf16[64,1024]{1,0:T(8,128)(2,1)S(1)} %get-tuple-element.265.refs_6_), channel_id=1, source_target_pairs={{0,8},{4,12},{8,0},{12,4},{16,24},{20,28},{24,16},{28,20},{1,9},{5... | collective-permute-start | bytes 393224 | tf_op jit(solution)/shard_map/ppermute | solution.py:72
  29.2 21.9 %all-to-all-start = ((f32[32,2,1024]{2,1,0:T(2,128)}), f32[32,2,1024]{2,1,0:T(2,128)S(1)}, u32[]{:S(2)}, u32[]{:S(2)}) async-start(f32[32,2,1024]{2,1,0:T(2,128)} %get-tuple-element.115), calls=%async_computation | async-start | bytes 524288 | tf_op jit(solution)/shard_map/all_to_all | solution.py:918
  35.1 254.1 %all-reduce.5.cloned.1.call-start = ((), (), s32[]{:S(2)}) async-start(), calls=%async_computation.2 | async-start | bytes 2490368 | tf_op jit(solution)/shard_map/psum | solution.py:1195
  35.2 8.1 %collective-permute-start.5 = (bf16[64,1024]{1,0:T(8,128)(2,1)S(1)}, bf16[64,1024]{1,0:T(8,128)(2,1)S(1)}, u32[]{:S(2)}, u32[]{:S(2)}) collective-permute-start(bf16[64,1024]{1,0:T(8,128)(2,1)S(1)} %collective-permute-done.1.refs_7_), channel_id=1, source_target_pairs={{0,16},{4,20},{8,24},{12,28},{16,0},{20,4},{24,8},{28,12},{1,17},{... | collective-permute-start | bytes 393224 | tf_op jit(solution)/shard_map/ppermute | solution.py:72
  37.1 14.1 %collective-permute-start.4 = (bf16[64,1024]{1,0:T(8,128)(2,1)S(1)}, bf16[64,1024]{1,0:T(8,128)(2,1)S(1)}, u32[]{:S(2)}, u32[]{:S(2)}) collective-permute-start(bf16[64,1024]{1,0:T(8,128)(2,1)S(1)} %get-tuple-element.265.refs_6_), channel_id=1, source_target_pairs={{0,16},{4,20},{8,24},{12,28},{16,0},{20,4},{24,8},{28,12},{1,17},{... | collective-permute-start | bytes 393224 | tf_op jit(solution)/shard_map/ppermute | solution.py:72
  37.4 13.8 %collective-permute-start.3 = (bf16[64,1024]{1,0:T(8,128)(2,1)S(1)}, bf16[64,1024]{1,0:T(8,128)(2,1)S(1)}, u32[]{:S(2)}, u32[]{:S(2)}) collective-permute-start(bf16[64,1024]{1,0:T(8,128)(2,1)S(1)} %collective-permute-done.1.refs_7_), channel_id=1, source_target_pairs={{0,8},{4,12},{8,0},{12,4},{16,24},{20,28},{24,16},{28,20},{1,9},{5... | collective-permute-start | bytes 393224 | tf_op jit(solution)/shard_map/ppermute | solution.py:72
  39.2 12.0 %collective-permute-start.6 = (bf16[64,1024]{1,0:T(8,128)(2,1)S(1)}, bf16[64,1024]{1,0:T(8,128)(2,1)S(1)}, u32[]{:S(2)}, u32[]{:S(2)}) collective-permute-start(bf16[64,1024]{1,0:T(8,128)(2,1)S(1)} %collective-permute-done.2.refs_8_), channel_id=1, source_target_pairs={{0,16},{4,20},{8,24},{12,28},{16,0},{20,4},{24,8},{28,12},{1,17},{... | collective-permute-start | bytes 393224 | tf_op jit(solution)/shard_map/ppermute | solution.py:72
  43.3 8.0 %collective-permute-start.7 = (bf16[64,1024]{1,0:T(8,128)(2,1)S(1)}, bf16[64,1024]{1,0:T(8,128)(2,1)S(1)}, u32[]{:S(2)}, u32[]{:S(2)}) collective-permute-start(bf16[64,1024]{1,0:T(8,128)(2,1)S(1)} %collective-permute-done.5.refs_11_), channel_id=1, source_target_pairs={{0,8},{4,12},{8,0},{12,4},{16,24},{20,28},{24,16},{28,20},{1,9},{5... | collective-permute-start | bytes 393224 | tf_op jit(solution)/shard_map/ppermute | solution.py:72
  56.3 13.0 %collective-permute-start.16 = (bf16[64,1024]{1,0:T(8,128)(2,1)S(1)}, bf16[64,1024]{1,0:T(8,128)(2,1)S(1)}, u32[]{:S(2)}, u32[]{:S(2)}) collective-permute-start(bf16[64,1024]{1,0:T(8,128)(2,1)S(1)} %get-tuple-element.131), channel_id=1, source_target_pairs={{0,4},{4,0},{8,12},{12,8},{16,20},{20,16},{24,28},{28,24},{1,5},{5... | collective-permute-start | bytes 393224 | tf_op jit(solution)/shard_map/ppermute | solution.py:63
  57.5 4.8 %collective-permute-start.10 = (f32[4,512]{1,0:T(4,128)S(1)}, f32[4,512]{1,0:T(4,128)S(1)}, u32[]{:S(2)}, u32[]{:S(2)}) collective-permute-start(f32[4,512]{1,0:T(4,128)S(1)} %pad_maximum_fusion.6.refs_1_), channel_id=1, source_target_pairs={{0,2},{1,3},{2,0},{3,1},{4,6},{5,7},{6,4},{7,5},{8,10},{9,11},{10,... | collective-permute-start | bytes 24584 | tf_op jit(solution)/shard_map/ppermute | solution.py:83
  60.4 5.5 %collective-permute-start.11 = (f32[4,512]{1,0:T(4,128)S(1)}, f32[4,512]{1,0:T(4,128)S(1)}, u32[]{:S(2)}, u32[]{:S(2)}) collective-permute-start(f32[4,512]{1,0:T(4,128)S(1)} %pad_maximum_fusion.6.refs_1_), channel_id=1, source_target_pairs={{0,3},{1,2},{2,1},{3,0},{4,7},{5,6},{6,5},{7,4},{8,11},{9,10},{10,... | collective-permute-start | bytes 24584 | tf_op jit(solution)/shard_map/ppermute | solution.py:83
  61.6 4.3 %collective-permute-start.9 = (f32[4,512]{1,0:T(4,128)S(1)}, f32[4,512]{1,0:T(4,128)S(1)}, u32[]{:S(2)}, u32[]{:S(2)}) collective-permute-start(f32[4,512]{1,0:T(4,128)S(1)} %pad_maximum_fusion.6.refs_1_), channel_id=1, source_target_pairs={{0,1},{1,0},{2,3},{3,2},{4,5},{5,4},{6,7},{7,6},{8,9},{9,8},{10,11... | collective-permute-start | bytes 24584 | tf_op jit(solution)/shard_map/ppermute | solution.py:83
  68.2 2.1 collective-permute-start.12
  68.2 11.4 %collective-permute-start.17 = (bf16[64,1024]{1,0:T(8,128)(2,1)S(1)}, bf16[64,1024]{1,0:T(8,128)(2,1)S(1)}, u32[]{:S(2)}, u32[]{:S(2)}) collective-permute-start(bf16[64,1024]{1,0:T(8,128)(2,1)S(1)} %get-tuple-element.129.refs_8_), channel_id=1, source_target_pairs={{0,8},{4,12},{8,0},{12,4},{16,24},{20,28},{24,16},{28,20},{1,9},{5... | collective-permute-start | bytes 393224 | tf_op jit(solution)/shard_map/ppermute | solution.py:72
  69.3 11.7 %collective-permute-start.20 = (bf16[64,1024]{1,0:T(8,128)(2,1)S(1)}, bf16[64,1024]{1,0:T(8,128)(2,1)S(1)}, u32[]{:S(2)}, u32[]{:S(2)}) collective-permute-start(bf16[64,1024]{1,0:T(8,128)(2,1)S(1)} %collective-permute-done.16.refs_9_), channel_id=1, source_target_pairs={{0,16},{4,20},{8,24},{12,28},{16,0},{20,4},{24,8},{28,12},{1,17},{... | collective-permute-start | bytes 393224 | tf_op jit(solution)/shard_map/ppermute | solution.py:72
  70.3 7.2 %collective-permute-start.13 = (f32[4,512]{1,0:T(4,128)S(1)}, f32[4,512]{1,0:T(4,128)S(1)}, u32[]{:S(2)}, u32[]{:S(2)}) collective-permute-start(f32[4,512]{1,0:T(4,128)S(1)} %pad_maximum_fusion.7.refs_1_), channel_id=1, source_target_pairs={{0,1},{1,0},{2,3},{3,2},{4,5},{5,4},{6,7},{7,6},{8,9},{9,8},{10,11... | collective-permute-start | bytes 24584 | tf_op jit(solution)/shard_map/ppermute | solution.py:83
  70.4 8.3 %collective-permute-start.14 = (f32[4,512]{1,0:T(4,128)S(1)}, f32[4,512]{1,0:T(4,128)S(1)}, u32[]{:S(2)}, u32[]{:S(2)}) collective-permute-start(f32[4,512]{1,0:T(4,128)S(1)} %pad_maximum_fusion.7.refs_1_), channel_id=1, source_target_pairs={{0,2},{1,3},{2,0},{3,1},{4,6},{5,7},{6,4},{7,5},{8,10},{9,11},{10,... | collective-permute-start | bytes 24584 | tf_op jit(solution)/shard_map/ppermute | solution.py:83
  72.9 8.7 %collective-permute-start.15 = (f32[4,512]{1,0:T(4,128)S(1)}, f32[4,512]{1,0:T(4,128)S(1)}, u32[]{:S(2)}, u32[]{:S(2)}) collective-permute-start(f32[4,512]{1,0:T(4,128)S(1)} %pad_maximum_fusion.7.refs_1_), channel_id=1, source_target_pairs={{0,3},{1,2},{2,1},{3,0},{4,7},{5,6},{6,5},{7,4},{8,11},{9,10},{10,... | collective-permute-start | bytes 24584 | tf_op jit(solution)/shard_map/ppermute | solution.py:83
  77.5 9.9 %collective-permute-start.19 = (bf16[64,1024]{1,0:T(8,128)(2,1)S(1)}, bf16[64,1024]{1,0:T(8,128)(2,1)S(1)}, u32[]{:S(2)}, u32[]{:S(2)}) collective-permute-start(bf16[64,1024]{1,0:T(8,128)(2,1)S(1)} %get-tuple-element.129.refs_8_), channel_id=1, source_target_pairs={{0,16},{4,20},{8,24},{12,28},{16,0},{20,4},{24,8},{28,12},{1,17},{... | collective-permute-start | bytes 393224 | tf_op jit(solution)/shard_map/ppermute | solution.py:72
  78.6 8.9 %collective-permute-start.18 = (bf16[64,1024]{1,0:T(8,128)(2,1)S(1)}, bf16[64,1024]{1,0:T(8,128)(2,1)S(1)}, u32[]{:S(2)}, u32[]{:S(2)}) collective-permute-start(bf16[64,1024]{1,0:T(8,128)(2,1)S(1)} %collective-permute-done.16.refs_9_), channel_id=1, source_target_pairs={{0,8},{4,12},{8,0},{12,4},{16,24},{20,28},{24,16},{28,20},{1,9},{5... | collective-permute-start | bytes 393224 | tf_op jit(solution)/shard_map/ppermute | solution.py:72
  79.6 9.7 %collective-permute-start.21 = (bf16[64,1024]{1,0:T(8,128)(2,1)S(1)}, bf16[64,1024]{1,0:T(8,128)(2,1)S(1)}, u32[]{:S(2)}, u32[]{:S(2)}) collective-permute-start(bf16[64,1024]{1,0:T(8,128)(2,1)S(1)} %collective-permute-done.17.refs_10_), channel_id=1, source_target_pairs={{0,16},{4,20},{8,24},{12,28},{16,0},{20,4},{24,8},{28,12},{1,17},{... | collective-permute-start | bytes 393224 | tf_op jit(solution)/shard_map/ppermute | solution.py:72
  81.1 10.6 %collective-permute-start.22 = (bf16[64,1024]{1,0:T(8,128)(2,1)S(1)}, bf16[64,1024]{1,0:T(8,128)(2,1)S(1)}, u32[]{:S(2)}, u32[]{:S(2)}) collective-permute-start(bf16[64,1024]{1,0:T(8,128)(2,1)S(1)} %collective-permute-done.20.refs_13_), channel_id=1, source_target_pairs={{0,8},{4,12},{8,0},{12,4},{16,24},{20,28},{24,16},{28,20},{1,9},{5... | collective-permute-start | bytes 393224 | tf_op jit(solution)/shard_map/ppermute | solution.py:72
  93.0 6.1 %collective-permute-start.26 = (f32[4,1024]{1,0:T(4,128)S(1)}, f32[4,1024]{1,0:T(4,128)S(1)}, u32[]{:S(2)}, u32[]{:S(2)}) collective-permute-start(f32[4,1024]{1,0:T(4,128)S(1)} %pad_maximum_fusion.1), channel_id=1, source_target_pairs={{0,3},{1,2},{2,1},{3,0},{4,7},{5,6},{6,5},{7,4},{8,11},{9,10},{10,... | collective-permute-start | bytes 49160 | tf_op jit(solution)/shard_map/ppermute | solution.py:83
  93.7 5.4 %collective-permute-start.25 = (f32[4,1024]{1,0:T(4,128)S(1)}, f32[4,1024]{1,0:T(4,128)S(1)}, u32[]{:S(2)}, u32[]{:S(2)}) collective-permute-start(f32[4,1024]{1,0:T(4,128)S(1)} %pad_maximum_fusion.1), channel_id=1, source_target_pairs={{0,2},{1,3},{2,0},{3,1},{4,6},{5,7},{6,4},{7,5},{8,10},{9,11},{10,... | collective-permute-start | bytes 49160 | tf_op jit(solution)/shard_map/ppermute | solution.py:83
  93.7 7.0 %collective-permute-start.24 = (f32[4,1024]{1,0:T(4,128)S(1)}, f32[4,1024]{1,0:T(4,128)S(1)}, u32[]{:S(2)}, u32[]{:S(2)}) collective-permute-start(f32[4,1024]{1,0:T(4,128)S(1)} %pad_maximum_fusion.1), channel_id=1, source_target_pairs={{0,1},{1,0},{2,3},{3,2},{4,5},{5,4},{6,7},{7,6},{8,9},{9,8},{10,11... | collective-permute-start | bytes 49160 | tf_op jit(solution)/shard_map/ppermute | solution.py:83
  104.2 7.5 %collective-permute-start.28 = (f32[4,512]{1,0:T(4,128)S(1)}, f32[4,512]{1,0:T(4,128)S(1)}, u32[]{:S(2)}, u32[]{:S(2)}) collective-permute-start(f32[4,512]{1,0:T(4,128)S(1)} %pad_maximum_fusion.8.refs_1_), channel_id=1, source_target_pairs={{0,1},{1,0},{2,3},{3,2},{4,5},{5,4},{6,7},{7,6},{8,9},{9,8},{10,11... | collective-permute-start | bytes 24584 | tf_op jit(solution)/shard_map/ppermute | solution.py:83
  105.1 6.6 %collective-permute-start.29 = (f32[4,512]{1,0:T(4,128)S(1)}, f32[4,512]{1,0:T(4,128)S(1)}, u32[]{:S(2)}, u32[]{:S(2)}) collective-permute-start(f32[4,512]{1,0:T(4,128)S(1)} %pad_maximum_fusion.8.refs_1_), channel_id=1, source_target_pairs={{0,2},{1,3},{2,0},{3,1},{4,6},{5,7},{6,4},{7,5},{8,10},{9,11},{10,... | collective-permute-start | bytes 24584 | tf_op jit(solution)/shard_map/ppermute | solution.py:83
  106.8 5.6 %collective-permute-start.30 = (f32[4,512]{1,0:T(4,128)S(1)}, f32[4,512]{1,0:T(4,128)S(1)}, u32[]{:S(2)}, u32[]{:S(2)}) collective-permute-start(f32[4,512]{1,0:T(4,128)S(1)} %pad_maximum_fusion.8.refs_1_), channel_id=1, source_target_pairs={{0,3},{1,2},{2,1},{3,0},{4,7},{5,6},{6,5},{7,4},{8,11},{9,10},{10,... | collective-permute-start | bytes 24584 | tf_op jit(solution)/shard_map/ppermute | solution.py:83
  116.8 4.5 %collective-permute-start.32 = (f32[4,1024]{1,0:T(4,128)S(1)}, f32[4,1024]{1,0:T(4,128)S(1)}, u32[]{:S(2)}, u32[]{:S(2)}) collective-permute-start(f32[4,1024]{1,0:T(4,128)S(1)} %pad_maximum_fusion.3.refs_2_), channel_id=1, source_target_pairs={{0,1},{1,0},{2,3},{3,2},{4,5},{5,4},{6,7},{7,6},{8,9},{9,8},{10,11... | collective-permute-start | bytes 49160 | tf_op jit(solution)/shard_map/ppermute | solution.py:83
  116.9 5.8 %collective-permute-start.33 = (f32[4,1024]{1,0:T(4,128)S(1)}, f32[4,1024]{1,0:T(4,128)S(1)}, u32[]{:S(2)}, u32[]{:S(2)}) collective-permute-start(f32[4,1024]{1,0:T(4,128)S(1)} %pad_maximum_fusion.3.refs_2_), channel_id=1, source_target_pairs={{0,2},{1,3},{2,0},{3,1},{4,6},{5,7},{6,4},{7,5},{8,10},{9,11},{10,... | collective-permute-start | bytes 49160 | tf_op jit(solution)/shard_map/ppermute | solution.py:83
  119.3 5.9 %collective-permute-start.34 = (f32[4,1024]{1,0:T(4,128)S(1)}, f32[4,1024]{1,0:T(4,128)S(1)}, u32[]{:S(2)}, u32[]{:S(2)}) collective-permute-start(f32[4,1024]{1,0:T(4,128)S(1)} %pad_maximum_fusion.3.refs_2_), channel_id=1, source_target_pairs={{0,3},{1,2},{2,1},{3,0},{4,7},{5,6},{6,5},{7,4},{8,11},{9,10},{10,... | collective-permute-start | bytes 49160 | tf_op jit(solution)/shard_map/ppermute | solution.py:83
  130.2 4.5 %collective-permute-start.37 = (f32[4,1024]{1,0:T(4,128)S(1)}, f32[4,1024]{1,0:T(4,128)S(1)}, u32[]{:S(2)}, u32[]{:S(2)}) collective-permute-start(f32[4,1024]{1,0:T(4,128)S(1)} %pad_maximum_fusion.4.refs_1_), channel_id=1, source_target_pairs={{0,1},{1,0},{2,3},{3,2},{4,5},{5,4},{6,7},{7,6},{8,9},{9,8},{10,11... | collective-permute-start | bytes 49160 | tf_op jit(solution)/shard_map/ppermute | solution.py:83
  130.3 4.9 %collective-permute-start.38 = (f32[4,1024]{1,0:T(4,128)S(1)}, f32[4,1024]{1,0:T(4,128)S(1)}, u32[]{:S(2)}, u32[]{:S(2)}) collective-permute-start(f32[4,1024]{1,0:T(4,128)S(1)} %pad_maximum_fusion.4.refs_1_), channel_id=1, source_target_pairs={{0,2},{1,3},{2,0},{3,1},{4,6},{5,7},{6,4},{7,5},{8,10},{9,11},{10,... | collective-permute-start | bytes 49160 | tf_op jit(solution)/shard_map/ppermute | solution.py:83
  132.9 5.5 %collective-permute-start.39 = (f32[4,1024]{1,0:T(4,128)S(1)}, f32[4,1024]{1,0:T(4,128)S(1)}, u32[]{:S(2)}, u32[]{:S(2)}) collective-permute-start(f32[4,1024]{1,0:T(4,128)S(1)} %pad_maximum_fusion.4.refs_1_), channel_id=1, source_target_pairs={{0,3},{1,2},{2,1},{3,0},{4,7},{5,6},{6,5},{7,4},{8,11},{9,10},{10,... | collective-permute-start | bytes 49160 | tf_op jit(solution)/shard_map/ppermute | solution.py:83
  143.8 8.0 %collective-permute-start.41 = (f32[4,512]{1,0:T(4,128)S(1)}, f32[4,512]{1,0:T(4,128)S(1)}, u32[]{:S(2)}, u32[]{:S(2)}) collective-permute-start(f32[4,512]{1,0:T(4,128)S(1)} %pad_maximum_fusion.9.refs_1_), channel_id=1, source_target_pairs={{0,1},{1,0},{2,3},{3,2},{4,5},{5,4},{6,7},{7,6},{8,9},{9,8},{10,11... | collective-permute-start | bytes 24584 | tf_op jit(solution)/shard_map/ppermute | solution.py:83
  143.8 8.0 %collective-permute-start.42 = (f32[4,512]{1,0:T(4,128)S(1)}, f32[4,512]{1,0:T(4,128)S(1)}, u32[]{:S(2)}, u32[]{:S(2)}) collective-permute-start(f32[4,512]{1,0:T(4,128)S(1)} %pad_maximum_fusion.9.refs_1_), channel_id=1, source_target_pairs={{0,2},{1,3},{2,0},{3,1},{4,6},{5,7},{6,4},{7,5},{8,10},{9,11},{10,... | collective-permute-start | bytes 24584 | tf_op jit(solution)/shard_map/ppermute | solution.py:83
  146.2 5.6 %collective-permute-start.43 = (f32[4,512]{1,0:T(4,128)S(1)}, f32[4,512]{1,0:T(4,128)S(1)}, u32[]{:S(2)}, u32[]{:S(2)}) collective-permute-start(f32[4,512]{1,0:T(4,128)S(1)} %pad_maximum_fusion.9.refs_1_), channel_id=1, source_target_pairs={{0,3},{1,2},{2,1},{3,0},{4,7},{5,6},{6,5},{7,4},{8,11},{9,10},{10,... | collective-permute-start | bytes 24584 | tf_op jit(solution)/shard_map/ppermute | solution.py:83
  156.4 5.6 %collective-permute-start.47 = (f32[4,1024]{1,0:T(4,128)S(1)}, f32[4,1024]{1,0:T(4,128)S(1)}, u32[]{:S(2)}, u32[]{:S(2)}) collective-permute-start(f32[4,1024]{1,0:T(4,128)S(1)} %pad_maximum_fusion.2), channel_id=1, source_target_pairs={{0,3},{1,2},{2,1},{3,0},{4,7},{5,6},{6,5},{7,4},{8,11},{9,10},{10,... | collective-permute-start | bytes 49160 | tf_op jit(solution)/shard_map/ppermute | solution.py:83
  158.3 4.6 %collective-permute-start.46 = (f32[4,1024]{1,0:T(4,128)S(1)}, f32[4,1024]{1,0:T(4,128)S(1)}, u32[]{:S(2)}, u32[]{:S(2)}) collective-permute-start(f32[4,1024]{1,0:T(4,128)S(1)} %pad_maximum_fusion.2), channel_id=1, source_target_pairs={{0,2},{1,3},{2,0},{3,1},{4,6},{5,7},{6,4},{7,5},{8,10},{9,11},{10,... | collective-permute-start | bytes 49160 | tf_op jit(solution)/shard_map/ppermute | solution.py:83
  158.3 4.6 %collective-permute-start.45 = (f32[4,1024]{1,0:T(4,128)S(1)}, f32[4,1024]{1,0:T(4,128)S(1)}, u32[]{:S(2)}, u32[]{:S(2)}) collective-permute-start(f32[4,1024]{1,0:T(4,128)S(1)} %pad_maximum_fusion.2), channel_id=1, source_target_pairs={{0,1},{1,0},{2,3},{3,2},{4,5},{5,4},{6,7},{7,6},{8,9},{9,8},{10,11... | collective-permute-start | bytes 49160 | tf_op jit(solution)/shard_map/ppermute | solution.py:83
  171.0 5.6 %collective-permute-start.49 = (f32[4,512]{1,0:T(4,128)S(1)}, f32[4,512]{1,0:T(4,128)S(1)}, u32[]{:S(2)}, u32[]{:S(2)}) collective-permute-start(f32[4,512]{1,0:T(4,128)S(1)} %pad_maximum_fusion.10.refs_1_), channel_id=1, source_target_pairs={{0,1},{1,0},{2,3},{3,2},{4,5},{5,4},{6,7},{7,6},{8,9},{9,8},{10,11... | collective-permute-start | bytes 24584 | tf_op jit(solution)/shard_map/ppermute | solution.py:83
  172.7 4.5 %collective-permute-start.50 = (f32[4,512]{1,0:T(4,128)S(1)}, f32[4,512]{1,0:T(4,128)S(1)}, u32[]{:S(2)}, u32[]{:S(2)}) collective-permute-start(f32[4,512]{1,0:T(4,128)S(1)} %pad_maximum_fusion.10.refs_1_), channel_id=1, source_target_pairs={{0,2},{1,3},{2,0},{3,1},{4,6},{5,7},{6,4},{7,5},{8,10},{9,11},{10,... | collective-permute-start | bytes 24584 | tf_op jit(solution)/shard_map/ppermute | solution.py:83
  173.6 5.4 %collective-permute-start.51 = (f32[4,512]{1,0:T(4,128)S(1)}, f32[4,512]{1,0:T(4,128)S(1)}, u32[]{:S(2)}, u32[]{:S(2)}) collective-permute-start(f32[4,512]{1,0:T(4,128)S(1)} %pad_maximum_fusion.10.refs_1_), channel_id=1, source_target_pairs={{0,3},{1,2},{2,1},{3,0},{4,7},{5,6},{6,5},{7,4},{8,11},{9,10},{10,... | collective-permute-start | bytes 24584 | tf_op jit(solution)/shard_map/ppermute | solution.py:83
  176.5 40.1 %collective-permute-start.65 = (bf16[1024,128]{1,0:T(8,128)(2,1)S(1)}, bf16[1024,128]{1,0:T(8,128)(2,1)S(1)}, u32[]{:S(2)}, u32[]{:S(2)}) collective-permute-start(bf16[1024,128]{1,0:T(8,128)(2,1)S(1)} %get-tuple-element.186), channel_id=1, source_target_pairs={{0,4},{4,0},{8,12},{12,8},{16,20},{20,16},{24,28},{28,24},{1,5},{5... | collective-permute-start | bytes 786440 | tf_op jit(solution)/shard_map/ppermute | solution.py:63
  182.3 1.5 collective-permute-start.52
  183.8 7.0 %collective-permute-start.53 = (f32[4,512]{1,0:T(4,128)S(1)}, f32[4,512]{1,0:T(4,128)S(1)}, u32[]{:S(2)}, u32[]{:S(2)}) collective-permute-start(f32[4,512]{1,0:T(4,128)S(1)} %pad_maximum_fusion.11.refs_1_), channel_id=1, source_target_pairs={{0,1},{1,0},{2,3},{3,2},{4,5},{5,4},{6,7},{7,6},{8,9},{9,8},{10,11... | collective-permute-start | bytes 24584 | tf_op jit(solution)/shard_map/ppermute | solution.py:83
  183.9 6.9 %collective-permute-start.54 = (f32[4,512]{1,0:T(4,128)S(1)}, f32[4,512]{1,0:T(4,128)S(1)}, u32[]{:S(2)}, u32[]{:S(2)}) collective-permute-start(f32[4,512]{1,0:T(4,128)S(1)} %pad_maximum_fusion.11.refs_1_), channel_id=1, source_target_pairs={{0,2},{1,3},{2,0},{3,1},{4,6},{5,7},{6,4},{7,5},{8,10},{9,11},{10,... | collective-permute-start | bytes 24584 | tf_op jit(solution)/shard_map/ppermute | solution.py:83
  186.3 5.4 %collective-permute-start.55 = (f32[4,512]{1,0:T(4,128)S(1)}, f32[4,512]{1,0:T(4,128)S(1)}, u32[]{:S(2)}, u32[]{:S(2)}) collective-permute-start(f32[4,512]{1,0:T(4,128)S(1)} %pad_maximum_fusion.11.refs_1_), channel_id=1, source_target_pairs={{0,3},{1,2},{2,1},{3,0},{4,7},{5,6},{6,5},{7,4},{8,11},{9,10},{10,... | collective-permute-start | bytes 24584 | tf_op jit(solution)/shard_map/ppermute | solution.py:83
  197.0 1.5 collective-permute-start.56
  197.9 15.5 %collective-permute-start.68 = (bf16[64,1024]{1,0:T(8,128)(2,1)S(1)}, bf16[64,1024]{1,0:T(8,128)(2,1)S(1)}, u32[]{:S(2)}, u32[]{:S(2)}) collective-permute-start(bf16[64,1024]{1,0:T(8,128)(2,1)S(1)} %get-tuple-element.199), channel_id=1, source_target_pairs={{0,4},{4,0},{8,12},{12,8},{16,20},{20,16},{24,28},{28,24},{1,5},{5... | collective-permute-start | bytes 393224 | tf_op jit(solution)/shard_map/ppermute | solution.py:63
  198.5 5.5 %collective-permute-start.57 = (f32[4,1024]{1,0:T(4,128)S(1)}, f32[4,1024]{1,0:T(4,128)S(1)}, u32[]{:S(2)}, u32[]{:S(2)}) collective-permute-start(f32[4,1024]{1,0:T(4,128)S(1)} %pad_maximum_fusion.5.rest_0_), channel_id=1, source_target_pairs={{0,1},{1,0},{2,3},{3,2},{4,5},{5,4},{6,7},{7,6},{8,9},{9,8},{10,11... | collective-permute-start | bytes 49160 | tf_op jit(solution)/shard_map/ppermute | solution.py:83
  198.6 5.5 %collective-permute-start.58 = (f32[4,1024]{1,0:T(4,128)S(1)}, f32[4,1024]{1,0:T(4,128)S(1)}, u32[]{:S(2)}, u32[]{:S(2)}) collective-permute-start(f32[4,1024]{1,0:T(4,128)S(1)} %pad_maximum_fusion.5.rest_0_), channel_id=1, source_target_pairs={{0,2},{1,3},{2,0},{3,1},{4,6},{5,7},{6,4},{7,5},{8,10},{9,11},{10,... | collective-permute-start | bytes 49160 | tf_op jit(solution)/shard_map/ppermute | solution.py:83
  201.1 5.5 %collective-permute-start.59 = (f32[4,1024]{1,0:T(4,128)S(1)}, f32[4,1024]{1,0:T(4,128)S(1)}, u32[]{:S(2)}, u32[]{:S(2)}) collective-permute-start(f32[4,1024]{1,0:T(4,128)S(1)} %pad_maximum_fusion.5.rest_0_), channel_id=1, source_target_pairs={{0,3},{1,2},{2,1},{3,0},{4,7},{5,6},{6,5},{7,4},{8,11},{9,10},{10,... | collective-permute-start | bytes 49160 | tf_op jit(solution)/shard_map/ppermute | solution.py:83
  204.0 16.1 %collective-permute-start.67 = (bf16[64,4608]{1,0:T(8,128)(2,1)S(1)}, bf16[64,4608]{1,0:T(8,128)(2,1)S(1)}, u32[]{:S(2)}, u32[]{:S(2)}) collective-permute-start(bf16[64,4608]{1,0:T(8,128)(2,1)S(1)} %get-tuple-element.196), channel_id=1, source_target_pairs={{0,4},{4,0},{8,12},{12,8},{16,20},{20,16},{24,28},{28,24},{1,5},{5... | collective-permute-start | bytes 1769480 | tf_op jit(solution)/shard_map/ppermute | solution.py:63
  204.1 15.3 %collective-permute-start.66 = (bf16[64,2048]{1,0:T(8,128)(2,1)S(1)}, bf16[64,2048]{1,0:T(8,128)(2,1)S(1)}, u32[]{:S(2)}, u32[]{:S(2)}) collective-permute-start(bf16[64,2048]{1,0:T(8,128)(2,1)S(1)} %get-tuple-element.192), channel_id=1, source_target_pairs={{0,4},{4,0},{8,12},{12,8},{16,20},{20,16},{24,28},{28,24},{1,5},{5... | collective-permute-start | bytes 786440 | tf_op jit(solution)/shard_map/ppermute | solution.py:63
  207.5 12.7 %collective-permute-start.63 = (bf16[512,256]{1,0:T(8,128)(2,1)S(1)}, bf16[512,256]{1,0:T(8,128)(2,1)S(1)}, u32[]{:S(2)}, u32[]{:S(2)}) collective-permute-start(bf16[512,256]{1,0:T(8,128)(2,1)S(1)} %cut_down.1.rest_0_), channel_id=1, source_target_pairs={{0,1},{1,0},{2,3},{3,2},{4,5},{5,4},{6,7},{7,6},{8,9},{9,8},{10,11... | collective-permute-start | bytes 786440 | tf_op jit(solution)/shard_map/ppermute | solution.py:83
  213.4 31.9 %collective-permute-start.61 = (bf16[512,256]{1,0:T(8,128)(2,1)S(1)}, bf16[512,256]{1,0:T(8,128)(2,1)S(1)}, u32[]{:S(2)}, u32[]{:S(2)}) collective-permute-start(bf16[512,256]{1,0:T(8,128)(2,1)S(1)} %cut_down.1.rest_0_), channel_id=1, source_target_pairs={{0,2},{1,3},{2,0},{3,1},{4,6},{5,7},{6,4},{7,5},{8,10},{9,11},{10,... | collective-permute-start | bytes 786440 | tf_op jit(solution)/shard_map/ppermute | solution.py:83
  216.6 28.7 %collective-permute-start.62 = (bf16[512,256]{1,0:T(8,128)(2,1)S(1)}, bf16[512,256]{1,0:T(8,128)(2,1)S(1)}, u32[]{:S(2)}, u32[]{:S(2)}) collective-permute-start(bf16[512,256]{1,0:T(8,128)(2,1)S(1)} %cut_down.1.rest_0_), channel_id=1, source_target_pairs={{0,3},{1,2},{2,1},{3,0},{4,7},{5,6},{6,5},{7,4},{8,11},{9,10},{10,... | collective-permute-start | bytes 786440 | tf_op jit(solution)/shard_map/ppermute | solution.py:83
  251.9 42.7 %collective-permute-start.64 = (bf16[4608,128]{1,0:T(8,128)(2,1)}, bf16[4608,128]{1,0:T(8,128)(2,1)}, u32[]{:S(2)}, u32[]{:S(2)}) collective-permute-start(bf16[4608,128]{1,0:T(8,128)(2,1)} %get-tuple-element.182), channel_id=1, source_target_pairs={{0,4},{4,0},{8,12},{12,8},{16,20},{20,16},{24,28},{28,24},{1,5},{5... | collective-permute-start | bytes 3538952 | tf_op jit(solution)/shard_map/ppermute | solution.py:63
  252.9 3.3 %collective-permute-start.60 = (f32[2,128,512]{2,1,0:T(8,128)}, f32[2,128,512]{2,1,0:T(8,128)}, u32[]{:S(2)}, u32[]{:S(2)}) collective-permute-start(f32[2,128,512]{2,1,0:T(8,128)} %dynamic-slice_bitcast_fusion), channel_id=1, source_target_pairs={{0,4},{4,0},{8,12},{12,8},{16,20},{20,16},{24,28},{28,24},{1,5},{5... | collective-permute-start | bytes 1572872 | tf_op jit(solution)/shard_map/ppermute | solution.py:63
  253.3 1.9 collective-permute-start.35
  (37 other events, 398.9 us)
Sparse Core Ops, SparseCore 0:
  12.4 124.2 all-gather.1
Sparse Core Ops, SparseCore 1:
  221.2 68.0 all-reduce.4

commit v4 on v3

--- a/solution.py
+++ b/solution.py
@@ -68,15 +68,8 @@
             for step in range(1, self.chips)
         ]
 
-    def two_ways(self, first, second):
-        hop = lambda value, step: lax.ppermute(
-            value, "rows", [(i, i ^ (2 * step)) for i in range(self.rows)]
-        )
-        first_near, second_near = hop(first, 1), hop(second, 2)
-        return first_near, second_near, lambda: (
-            [first, first_near, hop(first, 2), hop(first_near, 2)],
-            [second, hop(second, 1), second_near, hop(second_near, 1)],
-        )
+    def chip_hop(self, value, step):
+        return lax.ppermute(value, "rows", [(i, i ^ (2 * step)) for i in range(self.rows)])
 
     def plane_hops(self, value):
         return [value] + [
@@ -93,13 +86,19 @@
         other = lax.dynamic_index_in_dim(block, 1 - self.core, axis, keepdims=False)
         return mine, other
 
-    def row_pieces(self, mine, other):
-        got = self.swap(other)
-        if self.chips == 4:
-            firsts, seconds = self.two_ways(mine, got)[2]()
-        else:
-            firsts, seconds = self.chip_hops(mine), self.chip_hops(got)
-        return [piece for pair in zip(firsts, seconds) for piece in pair]
+    def pieces(self, mine, other):
+        return self.chip_hops(jnp.concatenate([mine, self.swap(other)], axis=0))
+
+    def plane_steps(self, value):
+        found = {0: value}
+        step = self.groups // 2
+        while step:
+            found |= {far + step: self.plane_hop(v, step) for far, v in found.items()}
+            step //= 2
+        return [found[k] for k in range(self.groups)]
+
+    def plane_hop(self, value, step):
+        return lax.ppermute(value, "batch", [(i, i ^ step) for i in range(self.groups)])
 
     def everywhere(self, pay):
         return self.plane_hops(jnp.concatenate([pay, self.swap(pay)], axis=0))
@@ -133,6 +132,7 @@
 
 
 def finish_moments(scal, refs, cols=slice(None)):
+    scal = [scal[k : k + 1, 0 : refs[0].shape[1]] for k in range(2 + 4 * len(refs))]
     pixels = scal[1]
     center = tree_sum([r[0:1, cols] + r[2:3, cols] for r in refs]) / pixels
     terms = []
@@ -153,14 +153,15 @@
     )
 
 
-def put_moments(values, pay, cols, weight):
+def put_moments(values, pay, cols, scal):
+    weight = scal[0:1, cols]
     total = jnp.sum(values, axis=0, keepdims=True)
     off = values - total * (1.0 / values.shape[0])
     pay[0:1, cols] = total * weight
     pay[1:2, cols] = jnp.sum(off * off, axis=0, keepdims=True) * weight
 
 
-def project(left, weights, pre, pay, weight, add=None):
+def project(left, weights, pre, pay, scal, add=None):
     weights = weights.ready() if isinstance(weights, Far) else weights
     for start in range(0, pre.shape[1], COLS):
         cols = slice(start, start + COLS)
@@ -168,7 +169,7 @@
         if add is not None:
             out = out + add[:, cols]
         pre[:, cols] = out
-        put_moments(out, pay, cols, weight)
+        put_moments(out, pay, cols, scal)
 
 
 def fold(values):
@@ -192,9 +193,10 @@
     first, second = finish_sums(refs)
     sums[0:1, :] = first
     sums[1:2, :] = second
-    over = 1.0 / scal[1]
+    width = pre.shape[1]
+    over = 1.0 / scal[1:2, 0:width]
     center, rstd = coef[0:1, :], coef[1:2, :]
-    scale = gain * rstd * scal[0]
+    scale = gain * rstd * scal[0:1, 0:width]
     level, tilt = first * over, second * over * rstd
 
     def body(rows, _):
@@ -202,6 +204,38 @@
         out[rows, :] = (scale * (pushed[rows, :] - level - x * tilt)).astype(BF)
 
     rows_loop(pre.shape[0], body)
+
+
+def own_core():
+    return lax.rem(lax.axis_index("rows"), 2)
+
+
+def own_chip():
+    return lax.div(lax.axis_index("rows"), 2)
+
+
+def image_row(step, side):
+    return 2 * (own_chip() ^ step) + (own_core() ^ side)
+
+
+def put_scalars(cells, counts, scal):
+    groups = counts.shape[0]
+    core, batch = own_core(), lax.axis_index("batch")
+    total = counts[0]
+    for k in range(1, groups):
+        total = total + counts[k]
+
+    def put(k, value):
+        scal[k : k + 1, :] = jnp.full((1, scal.shape[1]), value, F32)
+
+    put(0, (core < counts[batch]).astype(F32))
+    put(1, total.astype(F32) * cells)
+    for step in range(groups):
+        own = counts[batch ^ step]
+        for side, slot in enumerate((core, 1 - core)):
+            valid = (slot < own).astype(F32)
+            put(2 + 4 * step + 2 * side, valid * cells)
+            put(3 + 4 * step + 2 * side, valid * (1.0 / cells) + (1.0 - valid))
 
 
 def shifted_row(both):
@@ -212,70 +246,98 @@
     return jnp.concatenate([before, both], axis=1)
 
 
-def first_kernel(scal, x, above, w, rows, pay, held, semaphores):
-    slots, cells = above.shape[0], above.shape[1]
-    count, _, _, wide = held.shape
+def row_of_slots(values):
+    return jnp.concatenate([shifted_row(values[slot]) for slot in range(values.shape[0])], axis=0)
+
+
+def streamed(w, rows, held, semaphores):
+    count, wide = held.shape[0], held.shape[-1]
     copies = [
-        pltpu.make_async_copy(w.at[:, :, n * wide : (n + 1) * wide], held.at[n], semaphores.at[n])
+        pltpu.make_async_copy(w.at[rows, :, n * wide : (n + 1) * wide], held.at[n], semaphores.at[n])
         for n in range(count)
     ]
-    for copy in copies:
+    for copy in copies[:2]:
         copy.start()
-    sources = [above[...]] + [x[:, row] for row in range(2)]
-    lefts = [
-        jnp.concatenate([shifted_row(source[slot]) for slot in range(slots)], axis=0)
-        for source in sources
-    ]
-    for n, copy in enumerate(copies):
-        cols = slice(n * wide, (n + 1) * wide)
-        copy.wait()
-        out = sum(dot(left, held[n, tap]) for tap, left in enumerate(lefts))
-        for slot in range(slots):
+    for n in range(count):
+        copies[n].wait()
+        if n + 2 < count:
+            copies[n + 2].start()
+        yield slice(n * wide, (n + 1) * wide), held.at[n]
+
+
+def own_kernel(x, w, part, held, semaphores):
+    blocks = streamed(w, slice(1, 3), held, semaphores)
+    cols, block = next(blocks)
+    lefts = [row_of_slots(x[:, row]) for row in range(2)]
+    while cols is not None:
+        part[:, cols] = dot(lefts[0], block[0]) + dot(lefts[1], block[1])
+        cols, block = next(blocks, (None, None))
+
+
+def above_kernel(above, part, w, rows, held, semaphores):
+    cells = above.shape[1]
+    blocks = streamed(w, slice(0, 1), held, semaphores)
+    cols, block = next(blocks)
+    left = row_of_slots(above[...])
+    while cols is not None:
+        out = part[:, cols] + dot(left, block[0])
+        for slot in range(above.shape[0]):
             rows[slot, :, cols] = out[slot * cells : (slot + 1) * cells].astype(BF)
-        total = sum(
-            jnp.sum(out[slot * cells : (slot + 1) * cells], axis=0, keepdims=True) * scal[slot]
-            for slot in range(slots)
-        )
-        mean = total * scal[slots]
-        spread = 0.0
-        for slot in range(slots):
-            off = out[slot * cells : (slot + 1) * cells] - mean
-            spread += jnp.sum(off * off, axis=0, keepdims=True) * scal[slot]
-        both = jnp.concatenate([total, spread], axis=0)
-        pay[:, :, cols] = jnp.broadcast_to(both[None], (pay.shape[0],) + both.shape)
-
-
-def main_kernel(pieces, scal, spots, got, counts, over, params, *rest):
-    parts = rest[:pieces]
-    w_main, down_pre, sectioned, main_pre, pay, coef = rest[pieces:]
-    pixels = scal[1]
-    firsts, seconds = got[:, 0, :], got[:, 1, :]
-    center = jnp.sum(firsts, axis=0, keepdims=True) / pixels
-    gap = firsts * over[...] - center
-    total = jnp.sum(seconds + gap * gap * counts[...], axis=0, keepdims=True)
-    rstd = lax.rsqrt(total / pixels + EPSILON)
+        cols, block = next(blocks, (None, None))
+
+
+def whole_kernel(counts, *rest):
+    parts, (down_pre, keep, pay, scal, semaphore) = rest[:-5], rest[-5:]
+    put_scalars(down_pre.shape[0], counts, scal)
+    total = jnp.zeros((8, down_pre.shape[1]), F32)
+    for k, part in enumerate(parts):
+        width = part.shape[0] // 2
+        for side in range(2):
+            start = image_row(k, side) * width
+
+            def body(index, total, part=part, side=side, start=start, width=width):
+                src = pl.ds(pl.multiple_of(side * width + index * CHUNK, CHUNK), CHUNK)
+                dst = pl.ds(pl.multiple_of(start + index * CHUNK, CHUNK), CHUNK)
+                down_pre[dst, :] = part[src, :]
+                return total + fold(part[src, :].astype(F32))
+
+            total = lax.fori_loop(0, width // CHUNK, body, total)
+    copy = pltpu.make_async_copy(down_pre, keep, semaphore)
+    copy.start()
+    total = jnp.sum(total, axis=0, keepdims=True)
+    mean = total * (1.0 / down_pre.shape[0])
+
+    def spread(rows, squares):
+        off = down_pre[rows, :].astype(F32) - mean
+        return squares + fold(off * off)
+
+    squares = rows_loop(down_pre.shape[0], spread, jnp.zeros((8, down_pre.shape[1]), F32))
+    pay[0:1, :] = total * scal[0:1, :]
+    pay[1:2, :] = jnp.sum(squares, axis=0, keepdims=True) * scal[0:1, :]
+    copy.wait()
+
+
+def main_kernel(groups, scal, *rest):
+    refs = rest[:groups]
+    down_pre, params, w_main, sectioned, main_pre, main_keep, pay, coef, semaphore = rest[groups:]
+    center, rstd = finish_moments(scal, refs)
     coef[0:1, :] = center
     coef[1:2, :] = rstd
     scale, offset = rstd * row_of(params, GAIN_WIDE, 0), row_of(params, SHIFT_WIDE, 0)
-    for k, part in enumerate(parts):
-        part = part.ready()
-        width = part.shape[0]
-        start = spots[k] * width
-
-        def body(index, _, part=part, start=start):
-            src = pl.ds(pl.multiple_of(index * CHUNK, CHUNK), CHUNK)
-            dst = pl.ds(pl.multiple_of(start + index * CHUNK, CHUNK), CHUNK)
-            x = part[src, :]
-            down_pre[dst, :] = x
-            value = (x.astype(F32) - center) * scale + offset
-            sectioned[dst, :] = mish(value).astype(BF)
-
-        lax.fori_loop(0, width // CHUNK, body, None)
-    project(sectioned, w_main, main_pre, pay, scal[0])
+
+    def body(rows, _):
+        value = (down_pre[rows, :].astype(F32) - center) * scale + offset
+        sectioned[rows, :] = mish(value).astype(BF)
+
+    rows_loop(down_pre.shape[0], body)
+    project(sectioned, w_main, main_pre, pay, scal)
+    copy = pltpu.make_async_copy(main_pre, main_keep, semaphore)
+    copy.start()
+    copy.wait()
 
 
 def short_kernel(scal, sectioned, w_short, short_pre, pay):
-    project(sectioned, w_short, short_pre, pay, scal[0])
+    project(sectioned, w_short, short_pre, pay, scal)
 
 
 def inner_kernel(groups, scal, *rest):
@@ -291,7 +353,7 @@
         mainline[rows, :] = mish((pre[rows, :] - center) * scale + offset).astype(BF)
 
     rows_loop(pre.shape[0], body)
-    project(mainline, w_inner, inner_pre, pay, scal[0])
+    project(mainline, w_inner, inner_pre, pay, scal)
 
 
 def three_shifts(values, rim, start, forward):
@@ -335,7 +397,7 @@
             for i in range(3)
         )
         spatial_pre[:, cols] = out
-        put_moments(out, pay, cols, scal[0])
+        put_moments(out, pay, cols, scal)
 
 
 def trans_kernel(groups, scal, *rest):
@@ -352,7 +414,7 @@
         merged[rows, :] = (mainline[rows, :].astype(F32) + act).astype(BF)
 
     rows_loop(pre.shape[0], body)
-    project(merged, w_trans, trans_pre, pay, scal[0])
+    project(merged, w_trans, trans_pre, pay, scal)
 
 
 def shortcut_kernel(groups, scal, *rest):
@@ -387,10 +449,10 @@
         transition[rows, :] = mish((pre[rows, :] - center) * scale + offset).astype(BF)
 
     rows_loop(pre.shape[0], body)
-    project(transition, w_unite.ready().at[half:, :], unite_pre, pay, scal[0], part)
-
-
-def turn_kernel(groups, pieces, scal, spots, *rest):
+    project(transition, w_unite.ready().at[half:, :], unite_pre, pay, scal, part)
+
+
+def turn_kernel(groups, pieces, scal, *rest):
     refs = rest[:groups]
     pre, params = rest[groups : groups + 2]
     parts = rest[groups + 2 : groups + 2 + pieces]
@@ -398,30 +460,32 @@
     center, rstd = finish_moments(scal, refs)
     coef[0:1, :] = center
     coef[1:2, :] = rstd
-    gain, offset, weight = row_of(params, GAIN_WIDE, 1), row_of(params, SHIFT_WIDE, 1), scal[0]
+    gain, offset, weight = row_of(params, GAIN_WIDE, 1), row_of(params, SHIFT_WIDE, 1), scal[0:1, 0 : pre.shape[1]]
     sums = (jnp.zeros((8, pre.shape[1]), F32),) * 2
     for k, part in enumerate(parts):
         part = part.ready()
-        width = part.shape[0]
-        start = spots[k] * width
-
-        def body(index, sums, k=k, part=part, start=start):
-            src = pl.ds(pl.multiple_of(index * 16, 16), 16)
-            dst = pl.ds(pl.multiple_of(start + index * 16, 16), 16)
-            unit = (pre[dst, :] - center) * rstd
-            value = unit * gain + offset
-            grown = jnp.exp(jnp.minimum(value, FAR))
-            wide = grown * (grown + 2.0)
-            share = 1.0 / (wide + 2.0)
-            level = wide * share
-            if k < 2:
-                outputs[k][src, :] = (value * level * weight).astype(BF)
-            slope = level + 4.0 * value * (grown * (grown + 1.0) * share) * share
-            out = part[src, :].astype(F32) * weight * slope
-            pushed[dst, :] = out
-            return sums[0] + fold(out), sums[1] + fold(out * unit)
-
-        sums = lax.fori_loop(0, width // 16, body, sums)
+        width = part.shape[0] // 2
+        for side in range(2):
+            start = image_row(k, side) * width
+
+            def body(index, sums, k=k, part=part, side=side, start=start, width=width):
+                src = pl.ds(pl.multiple_of(side * width + index * 16, 16), 16)
+                dst = pl.ds(pl.multiple_of(start + index * 16, 16), 16)
+                unit = (pre[dst, :] - center) * rstd
+                value = unit * gain + offset
+                grown = jnp.exp(jnp.minimum(value, FAR))
+                wide = grown * (grown + 2.0)
+                share = 1.0 / (wide + 2.0)
+                level = wide * share
+                if k == 0:
+                    rows = pl.ds(pl.multiple_of(index * 16, 16), 16)
+                    outputs[side][rows, :] = (value * level * weight).astype(BF)
+                slope = level + 4.0 * value * (grown * (grown + 1.0) * share) * share
+                out = part[src, :].astype(F32) * weight * slope
+                pushed[dst, :] = out
+                return sums[0] + fold(out), sums[1] + fold(out * unit)
+
+            sums = lax.fori_loop(0, width // 16, body, sums)
     pay[0:1, :] = jnp.sum(sums[0], axis=0, keepdims=True)
     pay[1:2, :] = jnp.sum(sums[1], axis=0, keepdims=True)
 
@@ -535,29 +599,30 @@
 
 def settle_short_kernel(groups, scal, *rest):
     refs = rest[:groups]
-    pushed, pre, coef, params, w_short, grad_short, sums, part = rest[groups:]
+    pushed, pre, coef, params, grad_short, sums = rest[groups:]
     half = pre.shape[1]
     settle(scal, refs, pushed, pre, coef, row_of(params, GAIN, 0, half), grad_short, sums)
-    w_short = w_short.ready()
-    for start in range(0, part.shape[1], COLS):
-        part[:, start : start + COLS] = dot_back(grad_short[...], w_short[start : start + COLS, :])
 
 
 def back_down_kernel(groups, scal, *rest):
     refs = rest[:groups]
     (
-        main_pushed, main_pre, main_coef, part, down_pre, down_coef, params, w_main,
+        main_coef, down_coef, params, main_pushed, main_pre, w_main, grad_short, w_short, down_pre,
         grad_main, sums, pushed, pay, scratch,
     ) = rest[groups:]
+    main_pushed, main_pre = main_pushed.ready(), main_pre.ready()
     half = main_pre.shape[1]
     settle(scal, refs, main_pushed, main_pre, main_coef, row_of(params, GAIN, 1, half), grad_main, sums)
-    w_main = w_main.ready()
-    for start in range(0, part.shape[1], COLS):
+    w_main, grad_short, w_short = w_main.ready(), grad_short.ready(), w_short.ready()
+    for start in range(0, pushed.shape[1], COLS):
         cols = slice(start, start + COLS)
-        scratch[:, cols] = part[:, cols] + dot_back(grad_main[...], w_main[cols, :])
+        scratch[:, cols] = dot_back(grad_short[...], w_short[cols, :]) + dot_back(
+            grad_main[...], w_main[cols, :]
+        )
     push(
         lambda rows: scratch[rows, :],
-        down_pre, down_coef[0:1, :], down_coef[1:2, :], row_of(params, GAIN_WIDE, 0), row_of(params, SHIFT_WIDE, 0),
+        down_pre.ready(), down_coef[0:1, :], down_coef[1:2, :],
+        row_of(params, GAIN_WIDE, 0), row_of(params, SHIFT_WIDE, 0),
         pushed, pay,
     )
 
@@ -570,15 +635,15 @@
     grad_down[cells:, :] = jnp.zeros((grad_down.shape[0] - cells, pre.shape[1]), BF)
 
 
-def cut_down_kernel(groups, scal, spots, *rest):
+def cut_down_kernel(groups, scal, *rest):
     refs = rest[:groups]
     pushed, pre, coef, params, cut = rest[groups:]
     width = cut.shape[1]
-    cols = pl.ds(pl.multiple_of(spots[1] * width, width), width)
+    cols = pl.ds(pl.multiple_of(own_chip() * width, width), width)
     first, second = finish_sums(refs, cols)
-    over = 1.0 / scal[1]
+    over = 1.0 / scal[1:2, 0:width]
     center, rstd = coef[0:1, cols], coef[1:2, cols]
-    scale = params[GAIN_WIDE : GAIN_WIDE + 1, cols] * rstd * scal[0]
+    scale = params[GAIN_WIDE : GAIN_WIDE + 1, cols] * rstd * scal[0:1, 0:width]
     level, tilt = first * over, second * over * rstd
 
     def body(rows, _):
@@ -588,61 +653,69 @@
     rows_loop(pre.shape[0], body)
 
 
-def by_place(spots, first, second):
-    low = spots[0] == 0
+def by_place(first, second):
+    low = own_core() == 0
     return jnp.where(low, first, second), jnp.where(low, second, first)
 
 
-def share_unite_kernel(spots, shortcut, transition, grad, mine, other):
+def share_unite_kernel(shortcut, transition, grad, mine, other):
     width = 2 * mine.shape[1]
-    cut = grad[:, pl.ds(pl.multiple_of(spots[1] * width, width), width)]
+    cut = grad[:, pl.ds(pl.multiple_of(own_chip() * width, width), width)]
     half = shortcut.shape[1]
     for k, values in enumerate((shortcut, transition)):
         out = dot_cells(values[...], cut)
-        near, far = by_place(spots, out[:, : width // 2], out[:, width // 2 :])
+        near, far = by_place(out[:, : width // 2], out[:, width // 2 :])
         mine[k * half : (k + 1) * half, :] = near.astype(BF)
         other[k * half : (k + 1) * half, :] = far.astype(BF)
 
 
-def put_halves(spots, cut, values, start, mine, other):
+def put_halves(cut, values, start, mine, other):
     out = dot_cells(cut, values)
     rows, cols = mine.shape[0], slice(start, start + out.shape[1])
-    near, far = by_place(spots, out[:rows], out[rows:])
+    near, far = by_place(out[:rows], out[rows:])
     mine[:, cols] = near.astype(BF)
     other[:, cols] = far.astype(BF)
 
 
-def chip_columns(spots, mine):
+def chip_columns(mine):
     width = 2 * mine.shape[0]
-    return pl.ds(pl.multiple_of(spots[1] * width, width), width)
-
-
-def share_pack_kernel(spots, sectioned, grad_short, merged, grad_trans, mainline, grad_inner, mine, other):
-    cols = chip_columns(spots, mine)
+    return pl.ds(pl.multiple_of(own_chip() * width, width), width)
+
+
+def share_pack_kernel(*rest):
+    pairs, (mine, other) = rest[:-2], rest[-2:]
+    cols = chip_columns(mine)
     start = 0
-    for values, grad in ((sectioned, grad_short), (merged, grad_trans), (mainline, grad_inner)):
-        put_halves(spots, grad[:, cols], values[...], start, mine, other)
+    for values, grad in zip(pairs[::2], pairs[1::2]):
+        put_halves(grad[:, cols], values[...], start, mine, other)
         start += values.shape[1]
 
 
-def share_spatial_kernel(cells, spots, rim, grad, mine, other):
-    cut = grad[:, chip_columns(spots, mine)]
+def share_spatial_kernel(cells, rim, grad, mine, other):
+    cut = grad[:, chip_columns(mine)]
     line, side = (rim.shape[0] - cells) // 2, rim.shape[1]
     for row in range(3):
-        put_halves(spots, cut, rim[row * line : row * line + cells, :], row * side, mine, other)
-
-
-def share_main_kernel(spots, sectioned, grad, mine, other):
-    put_halves(spots, grad[:, chip_columns(spots, mine)], sectioned[...], 0, mine, other)
-
-
-def finish_kernel(unite, pack, taps, main, w_unite, w_short, w_trans, w_inner, w_spatial, w_main):
+        put_halves(cut, rim[row * line : row * line + cells, :], row * side, mine, other)
+
+
+def share_main_kernel(grad, grad_inner, sectioned, mainline, mine, other):
+    cols = chip_columns(mine)
+    sectioned, mainline = sectioned.ready(), mainline.ready()
+    put_halves(grad[:, cols], sectioned[...], 0, mine, other)
+    put_halves(grad_inner[:, cols], mainline[...], sectioned.shape[1], mine, other)
+
+
+def finish_kernel(unite, pack, taps, *rest):
+    mains, (w_unite, w_short, w_trans, w_inner, w_spatial, w_main) = rest[:-6], rest[-6:]
     w_unite[...] = unite[...].astype(F32)
-    w_main[...] = main[...].astype(F32)
-    start = 0
-    for out in (w_short, w_trans, w_inner):
-        out[...] = pack[:, start : start + out.shape[1]].astype(F32)
-        start += out.shape[1]
+    for outs, values in (
+        ((w_short, w_trans), pack[...].astype(F32)),
+        ((w_main, w_inner), tree_sum([main[...].astype(F32) for main in mains])),
+    ):
+        start = 0
+        for out in outs:
+            out[...] = values[:, start : start + out.shape[1]]
+            start += out.shape[1]
     half = w_trans.shape[1]
     for tap in range(w_spatial.shape[0]):
         w_spatial[tap] = taps[:, tap * half : (tap + 1) * half].astype(F32)
@@ -656,7 +729,7 @@
             out[index : index + 1, :] = pair[row : row + 1, :]
 
 
-def share_down_kernel(steps, chips, width, last_call, spots, *rest):
+def share_down_kernel(steps, chips, width, last_call, *rest):
     grads = rest[: len(steps)]
     earlier = rest[len(steps) : len(steps) + 2 * last_call]
     rest = rest[len(steps) + 2 * last_call :]
@@ -672,11 +745,11 @@
     planes = source.shape[0] // (2 * chips)
     copies = []
     for k, step in enumerate(steps):
-        plane = spots[2 + step]
+        plane = lax.axis_index("batch") ^ step
         copies.append(
             [
                 pltpu.make_async_copy(
-                    source.at[row * planes + plane, spots[0]], held.at[k, row], semaphores.at[k, row]
+                    source.at[row * planes + plane, own_core()], held.at[k, row], semaphores.at[k, row]
                 )
                 for row in range(2 * chips)
             ]
@@ -729,12 +802,12 @@
     )
     for tap, (acc, side, block) in enumerate(places):
         values = acc[side * half : (side + 1) * half, block * columns : (block + 1) * columns]
-        near, far = by_place(spots, values[:, : columns // 2], values[:, columns // 2 :])
+        near, far = by_place(values[:, : columns // 2], values[:, columns // 2 :])
         mine[tap * half : (tap + 1) * half, :] = near.astype(BF)
         other[tap * half : (tap + 1) * half, :] = far.astype(BF)
 
 
-def back_input_kernel(width, spots, grad, w, out, near, far):
+def back_input_kernel(width, grad, w, out, near, far):
     cells = 2 * width
     full = grad.shape[1]
 
@@ -742,7 +815,7 @@
     def _():
         last = lax.broadcasted_iota(jnp.int32, (width, full), 0) == width - 1
         for block in range(3):
-            start = pl.multiple_of(spots[1] * cells + block * width, width)
+            start = pl.multiple_of(own_chip() * cells + block * width, width)
             values = grad[pl.ds(start, width), :]
             rows = slice(block * width, (block + 1) * width)
             near[rows, :] = values
@@ -795,15 +868,20 @@
     return pltpu.with_memory_space_constraint(value, pltpu.HBM)
 
 
-def call(kernel, name, scalars, near, outs, flops, scratch=(), far=(), pin=False, spill=()):
+LIGHT = pl.CostEstimate(flops=0, bytes_accessed=0, transcendentals=0)
+
+
+def call(kernel, name, scalars, near, outs, flops, scratch=(), far=(), pin=False, spill=(), light=False, out=(), late=False):
     moved = sum(nbytes(a.shape, a.dtype) for a in (*near, *far, *outs))
-    held = moved + sum(nbytes(s.shape, s.dtype) for s in scratch)
+    scratch = [s if hasattr(s, "memory_space") or not hasattr(s, "shape") else pltpu.VMEM(s.shape, s.dtype) for s in scratch]
+    held = moved + sum(nbytes(s.shape, s.dtype) for s in scratch if hasattr(s, "shape"))
     if pin:
         held -= moved - sum(nbytes(a.shape, a.dtype) for a in far)
         held += sum(nbytes(outs[k].shape, outs[k].dtype) for k in spill)
         near, far = [in_vmem(a) for a in near], [in_hbm(a) for a in far]
         outs = [
-            o if k in spill else pltpu.VMEM(o.shape, o.dtype) for k, o in enumerate(outs)
+            o if k in spill else (pltpu.HBM if k in out else pltpu.VMEM)(o.shape, o.dtype)
+            for k, o in enumerate(outs)
         ]
     before, after_far, last = len(scalars) + len(near), len(far), len(outs) + len(scratch)
 
@@ -820,16 +898,16 @@
         name=name,
         out_shape=tuple(outs),
         in_specs=[SMEM] * len(scalars) + [VMEM] * len(near) + [ANY] * len(far),
-        out_specs=tuple([VMEM] * len(outs)),
-        scratch_shapes=[pltpu.VMEM(s.shape, s.dtype) for s in scratch]
+        out_specs=tuple(ANY if k in out and not late else VMEM for k in range(len(outs))),
+        scratch_shapes=scratch
         + [pltpu.VMEM(a.shape, a.dtype) for a in far]
         + ([pltpu.SemaphoreType.DMA((len(far),))] if far else []),
         compiler_params=pltpu.CompilerParams(vmem_limit_bytes=held + (8 << 20)),
-        cost_estimate=pl.CostEstimate(flops=flops, bytes_accessed=moved, transcendentals=0),
+        cost_estimate=LIGHT if light else pl.CostEstimate(flops=flops, bytes_accessed=moved, transcendentals=0),
     )(*scalars, *near, *far)
 
 
-def first_conv(scal, view, above, w_down, devices, pin):
+def first_conv(view, above, w_down, pin):
     slots, _, cells, both = view.shape
     half = both // 2
     full = w_down.shape[-1]
@@ -838,20 +916,28 @@
         view, above, taps = in_vmem(view), in_vmem(above), in_hbm(taps)
     wide = 256
     count = full // wide
-    return pl.pallas_call(
-        first_kernel,
-        name="first",
-        out_shape=(shape((slots, cells, full), BF), shape((devices, 2, full))),
-        in_specs=[SMEM, VMEM, VMEM, ANY],
-        out_specs=(VMEM, VMEM),
-        scratch_shapes=[
-            pltpu.VMEM((count, 3, 3 * half, wide), BF), pltpu.SemaphoreType.DMA((count,))
-        ],
-        compiler_params=pltpu.CompilerParams(vmem_limit_bytes=32 << 20),
-        cost_estimate=pl.CostEstimate(
-            flops=18 * slots * cells * half * full, bytes_accessed=18 * half * full, transcendentals=0
-        ),
-    )(scal, view, above, taps)
+
+    def run(kernel, name, rows, values, out):
+        return pl.pallas_call(
+            kernel,
+            name=name,
+            out_shape=(pltpu.VMEM if pin else shape)(out.shape, out.dtype),
+            in_specs=[VMEM] * len(values) + [ANY],
+            out_specs=VMEM,
+            scratch_shapes=[
+                pltpu.VMEM((count, rows, 3 * half, wide), BF), pltpu.SemaphoreType.DMA((count,))
+            ],
+            compiler_params=pltpu.CompilerParams(vmem_limit_bytes=24 << 20),
+            cost_estimate=pl.CostEstimate(
+                flops=6 * rows * slots * cells * half * full,
+                bytes_accessed=6 * rows * half * full,
+                transcendentals=0,
+            ),
+        )(*values, taps)
+
+    part = run(own_kernel, "own", 2, [view], shape((slots * cells, full)))
+    part = in_vmem(part) if pin else part
+    return run(above_kernel, "above", 1, [above, part], shape((slots, cells, full), BF))
 
 
 def flipped(kernel):
@@ -884,29 +970,6 @@
     height = here.rows * height_dev
     cells = height * width
     batch = lax.axis_index("batch")
-    counts = image_counts.astype(F32)
-    own_count = image_counts[batch]
-    pixels = jnp.sum(counts) * cells
-    weight = (here.core < own_count).astype(F32)
-
-    scal = [weight, pixels]
-    for step in range(groups):
-        plane = batch ^ step
-        for slot in (here.core, 1 - here.core):
-            count = (slot < image_counts[plane]).astype(F32) * cells
-            scal += [count, 1.0 / jnp.maximum(count, 1.0)]
-    scal = jnp.stack(scal)
-    spots = jnp.stack(
-        [2 * (here.chip ^ step) + (here.core ^ side) for step in range(chips) for side in range(2)]
-    ).astype(jnp.int32)
-    slot_scal = jnp.concatenate(
-        [
-            (jnp.arange(slots) < own_count).astype(F32),
-            (1.0 / (own_count.astype(F32) * height_dev * width))[None],
-        ]
-    )
-    device_counts = jnp.tile(counts * (height_dev * width), here.rows).reshape(-1, 1)
-
     view = inputs.reshape(slots, 2, width, 2 * half)
     below = [(i, i + 1) for i in range(here.rows - 1)]
     above = lax.ppermute(view[:, 1], "rows", below)
@@ -914,41 +977,56 @@
         [gains_wide, shifts_wide]
         + [jnp.pad(p, ((0, 0), (0, half))) for p in (gains_narrow, shifts_narrow)]
     )
-    down_rows, sums = first_conv(slot_scal, view, above, w_down, here.rows * groups, wide)
-    gathered = lax.all_to_all(sums, ("rows", "batch"), 0, 0, tiled=True)
-    down_pieces = here.row_pieces(*here.split(down_rows))
+    down_rows = first_conv(view, above, w_down, wide)
+    down_pieces = here.pieces(*here.split(down_rows))
     grad_mine, grad_other = here.split(grad_output.reshape(slots, width, full))
-    spot_pair = jnp.stack([here.core, here.chip]).astype(jnp.int32)
-    planes = jnp.stack([here.core, here.chip] + [batch ^ step for step in range(groups)]).astype(jnp.int32)
-    over_counts = 1.0 / device_counts
-    gathered, scal, spots, spot_pair, planes, device_counts, over_counts, params, grad_mine, grad_other = (
-        lax.optimization_barrier(
-            (gathered, scal, spots, spot_pair, planes, device_counts, over_counts, params, grad_mine, grad_other)
-        )
+    down_pieces[1], params, grad_mine, grad_other = lax.optimization_barrier(
+        (down_pieces[1], params, grad_mine, grad_other)
+    )
+    down_pre, down_keep, down_pay, scal = stage(
+        whole_kernel,
+        "whole",
+        [image_counts],
+        down_pieces,
+        [
+            shape((cells, full), BF), shape((cells, full), BF), shape((2, full)),
+            shape((2 + 4 * groups, full)),
+        ],
+        10 * cells * full,
+        out=(1,),
+        scratch=[pltpu.SemaphoreType.DMA],
     )
     if wide:
-        source = lax.all_gather(view, ("rows", "batch"))
-    down_pre, sectioned, main_pre, main_pay, down_coef = stage(
-        functools.partial(main_kernel, 2 * chips),
+        flat = after(view, down_pay).reshape(slots * 2 * width, 2 * half)
+        source = lax.all_gather(flat, ("rows", "batch")).reshape(-1, *view.shape)
+        grad_piece = jnp.concatenate([grad_mine, here.swap(after(grad_other, down_pay))], axis=0)
+        grad_pieces = [grad_piece, here.chip_hop(grad_piece, 1), here.chip_hop(grad_piece, 2)]
+        grad_pieces.append(here.chip_hop(grad_pieces[1], 2))
+    else:
+        grad_pieces = here.pieces(grad_mine, grad_other)
+    sectioned, main_pre, main_keep, main_pay, down_coef = stage(
+        functools.partial(main_kernel, groups),
         "main",
-        [scal, spots],
-        [gathered, device_counts, over_counts, params],
+        [],
+        [scal, *here.everywhere(down_pay), down_pre, params],
         [
-            shape((cells, full), BF), shape((cells, full), BF), shape((cells, half)),
+            shape((cells, full), BF), shape((cells, half)), shape((cells, half)),
             shape((2, half)), shape((2, full)),
         ],
         2 * cells * full * half,
-        far=[*down_pieces, w_main],
-    )
-
-    grad_pieces = here.row_pieces(after(grad_mine, main_pay), after(grad_other, main_pay))
-
+        far=[w_main],
+        out=(2,),
+        scratch=[pltpu.SemaphoreType.DMA],
+    )
+
+    if wide:
+        main_pay = after(main_pay, *grad_pieces[:3])
     main_all = here.everywhere(main_pay)
     short_pre, short_pay = stage(
         short_kernel,
         "short",
-        [scal],
-        [sectioned],
+        [],
+        [scal, sectioned],
         [shape((cells, half)), shape((2, half))],
         2 * cells * full * half,
         far=[w_short],
@@ -956,8 +1034,8 @@
     mainline, inner_pre, inner_pay, main_coef = stage(
         functools.partial(inner_kernel, groups),
         "inner",
-        [scal],
-        [*main_all, main_pre, params],
+        [],
+        [scal, *main_all, main_pre, params],
         [shape((cells, half), BF), shape((cells, half)), shape((2, half)), shape((2, half))],
         2 * cells * half * half,
         far=[w_inner],
@@ -966,8 +1044,8 @@
     rim, spatial_pre, spatial_pay, inner_coef = stage(
         functools.partial(spatial_kernel, groups, width),
         "spatial",
-        [scal],
-        [*inner_all, inner_pre, params],
+        [],
+        [scal, *inner_all, inner_pre, params],
         [
             shape((cells + 2 * width, 3 * half), BF), shape((cells, half)),
             shape((2, half)), shape((2, half)),
@@ -976,15 +1054,15 @@
         far=[w_spatial.reshape(9 * half, half)],
     )
     if wide:
-        spatial_pay = after(spatial_pay, *grad_pieces)
+        spatial_pay = after(spatial_pay, grad_pieces[3])
     both_all = here.everywhere(jnp.concatenate([spatial_pay, short_pay], axis=1))
     spatial_all = [b[:, :half] for b in both_all]
     short_all = [b[:, half:] for b in both_all]
     merged, trans_pre, trans_pay, spatial_coef = stage(
         functools.partial(trans_kernel, groups),
         "trans",
-        [scal],
-        [*spatial_all, spatial_pre, mainline, params],
+        [],
+        [scal, *spatial_all, spatial_pre, mainline, params],
         [shape((cells, half), BF), shape((cells, half)), shape((2, half)), shape((2, half))],
         2 * cells * half * half,
         far=[w_trans],
@@ -993,8 +1071,8 @@
     shortcut, unite_part, short_coef = stage(
         functools.partial(shortcut_kernel, groups),
         "shortcut",
-        [scal],
-        [*short_all, short_pre, params],
+        [],
+        [scal, *short_all, short_pre, params],
         [shape((cells, half), BF), shape((cells, full)), shape((2, half))],
         2 * cells * half * full,
         far=[w_unite],
@@ -1002,18 +1080,18 @@
     transition, unite_pre, unite_pay, trans_coef = stage(
         functools.partial(unite_kernel, groups),
         "unite",
-        [scal],
-        [*trans_all, trans_pre, unite_part, params],
+        [],
+        [scal, *trans_all, trans_pre, unite_part, params],
         [shape((cells, half), BF), shape((cells, full)), shape((2, full)), shape((2, half))],
         2 * cells * half * full,
         far=[w_unite],
     )
     unite_all = here.everywhere(unite_pay)
     unite_pushed, mine, other, unite_pay, unite_coef = stage(
-        functools.partial(turn_kernel, groups, 2 * chips),
+        functools.partial(turn_kernel, groups, chips),
         "turn",
-        [scal, spots],
-        [*unite_all, unite_pre, params],
+        [],
+        [scal, *unite_all, unite_pre, params],
         [
             shape((cells, full)), shape((width, full), BF), shape((width, full), BF),
             shape((2, full)), shape((2, full)),
@@ -1028,8 +1106,8 @@
     grad_unite_pre, unite_sums, trans_pushed, trans_pay = stage(
         functools.partial(back_trans_kernel, groups),
         "back_trans",
-        [scal],
-        [*unite_all, unite_pushed, unite_pre, unite_coef, params, trans_pre, trans_coef],
+        [],
+        [scal, *unite_all, unite_pushed, unite_pre, unite_coef, params, trans_pre, trans_coef],
         [shape((cells, full), BF), shape((2, full)), shape((cells, half)), shape((2, half))],
         2 * cells * half * full,
         [shape((cells, half))],
@@ -1046,7 +1124,7 @@
             stage(
                 share_unite_kernel,
                 "share_unite",
-                [spot_pair],
+                [],
                 [shortcut, transition, grad_unite_pre],
                 [shape((full, full // chips // 2), BF)] * 2,
                 2 * cells * full * full // chips,
@@ -1065,8 +1143,8 @@
     grad_trans_pre, trans_sums, grad_merged, spatial_pushed, spatial_pay = stage(
         functools.partial(back_spatial_kernel, groups),
         "back_spatial",
-        [scal],
-        [*trans_all, trans_pushed, trans_pre, trans_coef, spatial_pre, spatial_coef, params],
+        [],
+        [scal, *trans_all, trans_pushed, trans_pre, trans_coef, spatial_pre, spatial_coef, params],
         [
             shape((cells, half), BF), shape((2, half)), shape((cells, half)), shape((cells, half)),
             shape((2, half)),
@@ -1080,8 +1158,8 @@
     grad_spatial_pre, spatial_sums, inner_pushed, inner_pay = stage(
         functools.partial(back_inner_kernel, groups, width),
         "back_inner",
-        [scal],
-        [
+        [],
+        [scal,
             *spatial_all, spatial_pushed, spatial_pre, spatial_coef, inner_pre, inner_coef, params,
         ],
         [shape((cells, half), BF), shape((2, half)), shape((cells, half)), shape((2, half))],
@@ -1090,24 +1168,13 @@
         far=[w_spatial.reshape(9 * half, half)],
     )
     inner_all = here.everywhere(inner_pay)
-    grad_short_pre, short_sums, sectioned_part = stage(
+    grad_short_pre, short_sums = stage(
         functools.partial(settle_short_kernel, groups),
         "settle_short",
-        [scal],
-        [*short_all, short_pushed, short_pre, short_coef, params],
-        [shape((cells, half), BF), shape((2, half)), shape((cells, full))],
-        2 * cells * half * full,
-        far=[w_short],
-    )
-    grad_inner_pre, inner_sums, main_pushed, main_pay = stage(
-        functools.partial(back_main_kernel, groups),
-        "back_main",
-        [scal],
-        [*inner_all, inner_pushed, inner_pre, inner_coef, grad_merged, main_pre, main_coef, params],
-        [shape((cells, half), BF), shape((2, half)), shape((cells, half)), shape((2, half))],
-        2 * cells * half * half,
-        [shape((cells, half))],
-        far=[w_inner],
+        [],
+        [scal, *short_all, short_pushed, short_pre, short_coef, params],
+        [shape((cells, half), BF), shape((2, half))],
+        10 * cells * half,
     )
     if wide:
         lean = half // chips // 2
@@ -1115,7 +1182,7 @@
             stage(
                 functools.partial(share_spatial_kernel, cells),
                 "share_spatial",
-                [spot_pair],
+                [],
                 [rim, grad_spatial_pre],
                 [shape((lean, 9 * half), BF)] * 2,
                 18 * cells * half * half // chips,
@@ -1125,45 +1192,65 @@
             stage(
                 share_pack_kernel,
                 "share_pack",
-                [spot_pair],
-                [sectioned, grad_short_pre, merged, grad_trans_pre, mainline, grad_inner_pre],
-                [shape((lean, 2 * full), BF)] * 2,
-                8 * cells * half * half // chips,
+                [],
+                [sectioned, grad_short_pre, merged, grad_trans_pre],
+                [shape((lean, full + half), BF)] * 2,
+                6 * cells * half * half // chips,
             )
         )
+        inner_all[0], source, *shares = lax.optimization_barrier(
+            (inner_all[0], source, share_unite, share_pack, share_spatial)
+        )
+        shares = lax.psum(tuple(shares), "batch")
+    grad_inner_pre, inner_sums, main_pushed, main_pay = stage(
+        functools.partial(back_main_kernel, groups),
+        "back_main",
+        [],
+        [scal, *inner_all, inner_pushed, inner_pre, inner_coef, grad_merged, main_pre, main_coef, params],
+        [shape((cells, half), BF), shape((2, half)), shape((cells, half)), shape((2, half))],
+        2 * cells * half * half,
+        [shape((cells, half))],
+        far=[w_inner],
+        out=(2,),
+        late=True,
+    )
     main_all = here.everywhere(main_pay)
     grad_main_pre, main_sums, down_pushed, down_pay = stage(
         functools.partial(back_down_kernel, groups),
         "back_down",
-        [scal],
-        [
-            *main_all, main_pushed, main_pre, main_coef, sectioned_part, down_pre, down_coef, params,
-        ],
+        [],
+        [scal, *main_all, main_coef, down_coef, params],
         [shape((cells, half), BF), shape((2, half)), shape((cells, full)), shape((2, full))],
-        2 * cells * half * full,
+        4 * cells * half * full,
         [shape((cells, full))],
-        far=[w_main],
-    )
+        far=[main_pushed, main_keep, w_main, grad_short_pre, w_short, down_keep], light=True)
     down_all = here.everywhere(down_pay)
     spare = width
     if wide:
         grad_cut = stage(
             functools.partial(cut_down_kernel, groups),
             "cut_down",
-            [scal, spot_pair],
-            [*down_all, down_pushed, down_pre, down_coef, params],
+            [],
+            [scal, *down_all, down_pushed, down_pre, down_coef, params],
             [shape((cells, full // chips), BF)],
-            10 * cells * full // chips,
-        )[0]
+            10 * cells * full // chips, light=True)[0]
         cuts = here.plane_hops(grad_cut)
     grad_down_pre, down_sums = stage(
         functools.partial(settle_down_kernel, groups),
         "settle_down",
-        [scal],
-        [*down_all, down_pushed, down_pre, down_coef, params],
+        [],
+        [scal, *down_all, down_pushed, down_pre, down_coef, params],
         [shape((cells + spare, full), BF), shape((2, full))],
-        10 * cells * full,
-    )
+        10 * cells * full, light=True)
+    output = jnp.stack(here.by_core(*after(output_rows, down_pay))).reshape(grad_output.shape)
+    norm_grads = stage(
+        functools.partial(norm_sums_kernel, 2),
+        "norm_sums",
+        [],
+        [down_sums, unite_sums, short_sums, main_sums, inner_sums, spatial_sums, trans_sums],
+        [shape((2, full)), shape((5, half))] * 2,
+        0,
+        spill=range(4), light=True)
     if wide:
         near = pl.pallas_call(
             functools.partial(back_input_kernel, width),
@@ -1171,28 +1258,26 @@
             grid=(half // 128,),
             out_shape=shape((4, 2 * width, half)),
             in_specs=[
-                SMEM,
                 pl.BlockSpec((cells + spare, full), lambda n: (0, 0)),
                 pl.BlockSpec((9, 128, full), lambda n: (0, n, 0)),
             ],
             out_specs=pl.BlockSpec((4, 2 * width, 128), lambda n: (0, 0, n)),
             scratch_shapes=[pltpu.VMEM((3 * width, full), BF)] * 2,
             compiler_params=pltpu.CompilerParams(vmem_limit_bytes=16 << 20),
-            cost_estimate=pl.CostEstimate(
-                flops=36 * width * full * half, bytes_accessed=18 * full * half, transcendentals=0
-            ),
-        )(spot_pair, grad_down_pre, w_down.reshape(9, half, full))
+            cost_estimate=LIGHT,
+        )(grad_down_pre, in_hbm(w_down.reshape(9, half, full)))
         share_main = of_pair(
             stage(
                 share_main_kernel,
                 "share_main",
-                [spot_pair],
-                [sectioned, grad_main_pre],
-                [shape((lean, full), BF)] * 2,
-                4 * cells * half * half // chips,
+                [],
+                [grad_main_pre, grad_inner_pre],
+                [shape((lean, full + half), BF)] * 2,
+                6 * cells * half * half // chips,
+                far=[sectioned, mainline],
+                light=True,
             )
         )
-        shares = lax.psum((share_unite, share_pack, share_spatial, share_main), "batch")
         mine, other = here.split(near.reshape(2, 2, 2 * width, half))
         grad_inputs = jnp.stack(here.by_core(mine, here.swap(other)))
         columns = full // chips
@@ -1214,35 +1299,33 @@
                 functools.partial(share_down_kernel, steps, chips, width, int(bool(earlier))),
                 name="share_down",
                 out_shape=tuple(pltpu.VMEM(o.shape, o.dtype) for o in outs),
-                in_specs=[SMEM] + [VMEM] * len(near) + [ANY],
-                out_specs=(VMEM, VMEM),
+                in_specs=[VMEM] * len(near) + [ANY],
+                out_specs=(VMEM,) * len(outs),
                 scratch_shapes=scratch,
                 compiler_params=pltpu.CompilerParams(vmem_limit_bytes=30 << 20),
-                cost_estimate=pl.CostEstimate(
-                    flops=18 * len(steps) * cells * half * columns,
-                    bytes_accessed=len(steps) * 4 * cells * full,
-                    transcendentals=0,
-                ),
-            )(planes, *map(in_vmem, near), in_hbm(source))
+                cost_estimate=LIGHT,
+            )(*map(in_vmem, near), in_hbm(source))
 
         middle = (groups + 1) // 2
-        cuts[:middle] = lax.optimization_barrier((*cuts[:middle], near))[:middle]
+        cuts[:middle], near = lax.optimization_barrier((cuts[:middle], near))
         first_sums = share_down(range(middle), ())
-        cuts[middle:] = lax.optimization_barrier((*cuts[middle:], *first_sums))[: groups - middle]
+        mains = here.plane_hops(after(share_main, grad_cut))
+        cuts[middle:], first_sums = lax.optimization_barrier((cuts[middle:], first_sums))
         mine, other = share_down(range(middle, groups), first_sums)
+        other, *tied = lax.optimization_barrier((other, *shares, *mains))
+        shares, mains = tied[: len(shares)], tied[len(shares) :]
         grad_w_down = mine.astype(F32) + here.swap(other).astype(F32)
         early = stage(
             finish_kernel,
             "finish",
             [],
-            shares,
+            [*shares, *mains],
             [
                 shape((full, 2 * lean)), shape((lean, full)), shape((lean, half)), shape((lean, half)),
                 shape((9, lean, half)), shape((lean, full)),
             ],
             0,
-            spill=range(6),
-        )
+            spill=range(6), light=True)
         early = [
             early[1].T, early[5].T, early[3].T, jnp.swapaxes(early[4], 1, 2), early[2].T, early[0],
         ]
@@ -1275,7 +1358,7 @@
         for step, piece in enumerate(got):
             for side in range(2):
                 source = lax.dynamic_update_slice_in_dim(
-                    source, piece[:, side : side + 1], spots[2 * step + side], 1
+                    source, piece[:, side : side + 1], 2 * (here.chip ^ step) + (here.core ^ side), 1
                 )
         grad_map = grad_down_pre.reshape(height, width, full)
         columns = full // chips
@@ -1317,16 +1400,6 @@
         other = lax.dynamic_slice_in_dim(widened, (1 - here.core) * pair_rows, pair_rows, 0)
         grad_inputs = jnp.stack(here.by_core(mine, here.swap(other)))
 
-    output = jnp.stack(here.by_core(*after(output_rows, down_pay))).reshape(grad_output.shape)
-    norm_grads = stage(
-        functools.partial(norm_sums_kernel, 2),
-        "norm_sums",
-        [],
-        [down_sums, unite_sums, short_sums, main_sums, inner_sums, spatial_sums, trans_sums],
-        [shape((2, full)), shape((5, half))] * 2,
-        0,
-        spill=range(4),
-    )
     return (
         output,
         grad_inputs,

time: 306 us -> 278 us (0.908)
  waiting for transfers between devices: 90 us -> 78.8 us
  between operations: 23.3 us -> 15 us
  Pallas kernels: 86.3 us -> 80.8 us
  local copies, waits for them, and re-layouts: 10.7 us -> 6.99 us
    psum x1, waiting for transfers between devices: 30.9 us -> 0.01 us  [on_device(): shares = lax.psum(tuple(shares), 'batch')]
    ppermute x36 -> x42, starting transfers between devices: 53.6 us -> 68.7 us  [plane_hops(): lax.ppermute(value, 'batch', [(i, i ^ step) for i in range(self.groups)])]
    ppermute x36 -> x42, waiting for transfers between devices: 42 us -> 51 us  [plane_hops(): lax.ppermute(value, 'batch', [(i, i ^ step) for i in range(self.groups)])]
    ppermute x12 -> x6, starting transfers between devices: 15.4 us -> 6.96 us  [the longest x3 4.36 us: chip_hops(): lax.ppermute(value, 'rows', [(i, i ^ 2 * step) for i in range(self.rows)])]
    pallas_call x23 -> x24, Pallas kernels: 63.6 us -> 57.5 us  [call(): pl.pallas_call(body if far else kernel, name=name, out_shape=tuple(outs),...]
    all_to_all x1 -> x0, starting transfers between devices: 5.95 us -> none  [on_device(): gathered = lax.all_to_all(sums, ('rows', 'batch'), 0, 0, tiled=True)]
    ppermute x20 -> x21, waiting for transfers between devices: 10.1 us -> 16 us  [swap(): return lax.ppermute(value, 'rows', [(i, i ^ 1) for i in range(self.rows)])]
    ppermute x12 -> x6, waiting for transfers between devices: 6.95 us -> 11.8 us  [the longest x3 11.8 us: chip_hops(): lax.ppermute(value, 'rows', [(i, i ^ 2 * step) for i in range(self.rows)])]
  transfers between devices with their start and end apart: 72 -> 72, of which waited for: 31 -> 42; matrix products, arithmetic and copies ran while one was open for 4% -> 3% of each run, Pallas kernels for 28% -> 28%
where the time goes in v4:
time: 278 us; the launch traced here: 275 us
  starting transfers between devices  84 us (30%)
  Pallas kernels  80.8 us (29%)
  waiting for transfers between devices  78.8 us (28%)
  between operations  15 us (5%)
  other arithmetic  9.59 us (3%)
  local copies, waits for them, and re-layouts  6.99 us (3%)
    ppermute x42, starting transfers between devices, plane_hops(): lax.ppermute(value, 'batch', [(i, i ^ step) for i in range(self.groups)])  68.7 us
    pallas_call x24, Pallas kernels, call(): pl.pallas_call(body if far else kernel, name=name, out_shape=tuple(outs),...  57.5 us
    ppermute x42, waiting for transfers between devices, plane_hops(): lax.ppermute(value, 'batch', [(i, i ^ step) for i in range(self.groups)])  51 us
    ppermute x21, waiting for transfers between devices, swap(): return lax.ppermute(value, 'rows', [(i, i ^ 1) for i in range(self.rows)])  16 us
    ppermute x3, waiting for transfers between devices, chip_hops(): lax.ppermute(value, 'rows', [(i, i ^ 2 * step) for i in range(self.rows)])  11.8 us
    pallas_call x2, Pallas kernels, share_down(): pl.pallas_call(functools.partial(share_down_kernel, steps, chips, width,...  9.79 us
    pallas_call x2, Pallas kernels, run(): pl.pallas_call(kernel, name=name, out_shape=(pltpu.VMEM if pin else shape...  7.15 us
    pallas_call x1, Pallas kernels, on_device(): pl.pallas_call(functools.partial(back_input_kernel, width), name='back_in...  6.33 us
  transfers between devices with their start and end apart: 72, of which 42 were waited for; matrix products, arithmetic and copies ran while one was open for 3% of the time, Pallas kernels for 28%

profile of v4, /device:TPU:0, one launch (start us, length us, event | category | flops | bytes accessed | tf_op | source)
XLA Modules:
  0.0 275.2 jit_solution(15541835419518137607)
XLA Ops:
  8.5 2.4 collective-permute-start
  10.9 4.1 %own.1.part = f32[128,1024]{1,0:T(8,128)S(1)} custom-call(bf16[2,2,64,1024]{3,2,1,0:T(8,128)(2,1)S(1)} %reshape.68.x, bf16[3,1536,1024]{2,1,0:T(8,128)(2,1)} %bitcast.49), custom_call_target="tpu_custom_call" | custom-call | flops 805306368 | bytes 6291456 | tf_op jit(solution)/shard_map/own/pallas_call | solution.py:921
  15.0 3.1 %above.1 = bf16[2,64,1024]{2,1,0:T(8,128)(2,1)S(1)} custom-call(bf16[2,64,1024]{2,1,0:T(8,128)(2,1)S(1)} %collective-permute-done.above, f32[128,1024]{1,0:T(8,128)S(1)} %own.1.part, bf16[3,1536,1024]{2,1,0:T(8,128)(2,1)} %bitcast.50), custom_call_target="tpu_custom_call" | custom-call | flops 402653184 | bytes 3145728 | tf_op jit(solution)/shard_map/above/pallas_call | solution.py:921
  18.2 2.7 collective-permute-start.1
  21.8 2.0 collective-permute-start.2
  26.3 4.7 %collective-permute-done.2.rest_1_ = bf16[128,1024]{1,0:T(8,128)(2,1)S(1)} collective-permute-done((bf16[128,1024]{1,0:T(8,128)(2,1)S(1)}, bf16[128,1024]{1,0:T(8,128)(2,1)S(1)}, u32[]{:S(2)}, u32[]{:S(2)}) %collective-permute-start.2) | collective-permute-done | bytes 262176 | tf_op jit(solution)/shard_map/ppermute | solution.py:67
  31.0 5.5 %collective-permute-done.3.rest_2_ = bf16[128,1024]{1,0:T(8,128)(2,1)S(1)} collective-permute-done((bf16[128,1024]{1,0:T(8,128)(2,1)S(1)}, bf16[128,1024]{1,0:T(8,128)(2,1)S(1)}, u32[]{:S(2)}, u32[]{:S(2)}) %collective-permute-start.3) | collective-permute-done | bytes 262176 | tf_op jit(solution)/shard_map/ppermute | solution.py:67
  36.5 1.6 collective-permute-done.4.rest_3_
  38.1 1.8 whole.1
  43.1 1.7 collective-permute-start.11
  46.0 1.6 collective-permute-start.6
  47.7 2.6 collective-permute-start.7
  50.5 1.9 collective-permute-done.7.refs_3_
  52.4 3.4 %collective-permute-done.8.refs_4_ = f32[4,1024]{1,0:T(4,128)S(1)} collective-permute-done((f32[4,1024]{1,0:T(4,128)S(1)}, f32[4,1024]{1,0:T(4,128)S(1)}, u32[]{:S(2)}, u32[]{:S(2)}) %collective-permute-start.8) | collective-permute-done | bytes 16416 | tf_op jit(solution)/shard_map/ppermute | solution.py:76
  55.8 3.0 %main.1 = (bf16[512,1024]{1,0:T(8,128)(2,1)S(1)}, f32[512,512]{1,0:T(8,128)S(1)}, f32[512,512]{1,0:T(8,128)}, f32[2,512]{1,0:T(2,128)S(1)}, f32[2,1024]{1,0:T(2,128)S(1)}) custom-call(f32[18,1024]{1,0:T(8,128)S(1)} %get-tuple-element.128.refs_0_.scal, f32[4,1024]{1,0:T(4,128)S(1)} %pad_maximum_fusion.4.refs_1_, ...), custom_call_target="tpu_custom_call" | custom-call | flops 536870912 | bytes 5451776 | tf_op jit(solution)/shard_map/main/pallas_call | solution.py:896
  61.4 3.2 %collective-permute-start.15 = (f32[4,512]{1,0:T(4,128)S(1)}, f32[4,512]{1,0:T(4,128)S(1)}, u32[]{:S(2)}, u32[]{:S(2)}) collective-permute-start(f32[4,512]{1,0:T(4,128)S(1)} %pad_maximum_fusion.8.refs_1_), channel_id=1, source_target_pairs={{0,3},{1,2},{2,1},{3,0},{4,7},{5,6},{6,5},{7,4},{8,11},{9,10},{10,... | collective-permute-start | bytes 24584 | tf_op jit(solution)/shard_map/ppermute | solution.py:76
  64.8 2.1 collective-permute-done.15.refs_4_
  66.9 1.7 inner.1
  69.9 3.6 %collective-permute-start.18 = (f32[4,512]{1,0:T(4,128)S(1)}, f32[4,512]{1,0:T(4,128)S(1)}, u32[]{:S(2)}, u32[]{:S(2)}) collective-permute-start(f32[4,512]{1,0:T(4,128)S(1)} %pad_maximum_fusion.9.refs_1_), channel_id=1, source_target_pairs={{0,2},{1,3},{2,0},{3,1},{4,6},{5,7},{6,4},{7,5},{8,10},{9,11},{10,... | collective-permute-start | bytes 24584 | tf_op jit(solution)/shard_map/ppermute | solution.py:76
  74.3 2.2 short.1
  76.5 2.7 collective-permute-done.19.refs_4_
  79.2 5.2 %spatial.1 = (bf16[640,1536]{1,0:T(8,128)(2,1)S(1)}, f32[512,512]{1,0:T(8,128)S(1)}, f32[2,512]{1,0:T(2,128)S(1)}, f32[2,512]{1,0:T(2,128)S(1)}) custom-call(f32[18,1024]{1,0:T(8,128)S(1)} %get-tuple-element.128.refs_0_.scal, f32[4,512]{1,0:T(4,128)S(1)} %pad_maximum_fusion.9.refs_1_, f32[4,512]{1,0:T(4,128)S(1)} %collective-permute-done.17.refs_2_, ...), custom_call_target="tpu_custom_call" | custom-call | flops 2415919104 | bytes 8953856 | tf_op jit(solution)/shard_map/spatial/pallas_call | solution.py:896
  86.5 3.7 %collective-permute-start.22 = (f32[4,1024]{1,0:T(4,128)S(1)}, f32[4,1024]{1,0:T(4,128)S(1)}, u32[]{:S(2)}, u32[]{:S(2)}) collective-permute-start(f32[4,1024]{1,0:T(4,128)S(1)} %pad_maximum_fusion.2), channel_id=1, source_target_pairs={{0,1},{1,0},{2,3},{3,2},{4,5},{5,4},{6,7},{7,6},{8,9},{9,8},{10,11... | collective-permute-start | bytes 49160 | tf_op jit(solution)/shard_map/ppermute | solution.py:76
  92.6 1.7 trans.1
  95.6 1.7 collective-permute-start.26
  98.5 1.6 collective-permute-start.28
  100.1 2.3 shortcut.1
  103.9 3.2 %unite.1 = (bf16[512,512]{1,0:T(8,128)(2,1)S(1)}, f32[512,1024]{1,0:T(8,128)S(1)}, f32[2,1024]{1,0:T(2,128)S(1)}, f32[2,512]{1,0:T(2,128)S(1)}) custom-call(f32[18,1024]{1,0:T(8,128)S(1)} %get-tuple-element.128.refs_0_.scal, f32[4,512]{1,0:T(4,128)S(1)} %pad_maximum_fusion.10.refs_1_, f32[4,512]{1,0:T(4,128)S(1)} %collective-permute-done.26.refs_2_, ...), custom_call_target="tpu_custom_call" | custom-call | flops 536870912 | bytes 8040448 | tf_op jit(solution)/shard_map/unite/pallas_call | solution.py:896
  110.0 2.9 %collective-permute-start.32 = (f32[4,1024]{1,0:T(4,128)S(1)}, f32[4,1024]{1,0:T(4,128)S(1)}, u32[]{:S(2)}, u32[]{:S(2)}) collective-permute-start(f32[4,1024]{1,0:T(4,128)S(1)} %pad_maximum_fusion.5.refs_1_), channel_id=1, source_target_pairs={{0,3},{1,2},{2,1},{3,0},{4,7},{5,6},{6,5},{7,4},{8,11},{9,10},{10,... | collective-permute-start | bytes 49160 | tf_op jit(solution)/shard_map/ppermute | solution.py:76
  112.8 2.3 collective-permute-done.31.refs_3_
  115.8 3.3 %turn.1 = (f32[512,1024]{1,0:T(8,128)S(1)}, bf16[64,1024]{1,0:T(8,128)(2,1)S(1)}, bf16[64,1024]{1,0:T(8,128)(2,1)S(1)}, f32[2,1024]{1,0:T(2,128)S(1)}, f32[2,1024]{1,0:T(2,128)S(1)}) custom-call(f32[18,1024]{1,0:T(8,128)S(1)} %get-tuple-element.128.refs_0_.scal, f32[4,1024]{1,0:T(4,128)S(1)} %pad_maximum_fusion.5.refs_1_, ...), custom_call_target="tpu_custom_call" | custom-call | flops 20971520 | bytes 5718016 | tf_op jit(solution)/shard_map/turn/pallas_call | solution.py:896
  121.2 2.7 collective-permute-start.36
  124.9 2.3 collective-permute-done.36.refs_3_
  127.2 2.6 collective-permute-done.37.refs_4_
  129.8 3.6 %back_trans.1 = (bf16[512,1024]{1,0:T(8,128)(2,1)S(1)}, f32[2,1024]{1,0:T(2,128)S(1)}, f32[512,512]{1,0:T(8,128)S(1)}, f32[2,512]{1,0:T(2,128)S(1)}) custom-call(f32[18,1024]{1,0:T(8,128)S(1)} %get-tuple-element.128.refs_0_.scal, f32[4,1024]{1,0:T(4,128)S(1)} %pad_maximum_fusion.6.refs_1_, f32[4,1024]{1,0:T(4,128)S(1)} %collective-permute-done.35.refs_2_, ...), custom_call_target="tpu_custom_call" | custom-call | flops 536870912 | bytes 9658368 | tf_op jit(solution)/shard_map/back_trans/pallas_call | solution.py:896
  134.7 2.2 collective-permute-start.40
  136.9 2.2 collective-permute-start.41
  139.1 3.6 %back_short.1 = (f32[512,512]{1,0:T(8,128)S(1)}, f32[2,512]{1,0:T(2,128)S(1)}) custom-call(bf16[512,1024]{1,0:T(8,128)(2,1)S(1)} %get-tuple-element.162.refs_0_.grad, f32[512,512]{1,0:T(8,128)S(1)} %get-tuple-element.148.refs_5_.refs_1_.rest_5_, f32[2,512]{1,0:T(2,128)S(1)} %get-tuple-element.163.refs_2_.rest_6_, ...), custom_call_target="tpu_custom_call" | custom-call | flops 536870912 | bytes 5308416 | tf_op jit(solution)/shard_map/back_short/pallas_call | solution.py:896
  142.7 2.8 %back_spatial.1 = (bf16[512,512]{1,0:T(8,128)(2,1)S(1)}, f32[2,512]{1,0:T(2,128)S(1)}, f32[512,512]{1,0:T(8,128)S(1)}, f32[512,512]{1,0:T(8,128)S(1)}, f32[2,512]{1,0:T(2,128)S(1)}) custom-call(f32[18,1024]{1,0:T(8,128)S(1)} %get-tuple-element.128.refs_0_.scal, f32[4,512]{1,0:T(4,128)S(1)} %pad_maximum_fusion.11.refs_1_, ...), custom_call_target="tpu_custom_call" | custom-call | flops 268435456 | bytes 6471680 | tf_op jit(solution)/shard_map/back_spatial/pallas_call | solution.py:896
  146.7 2.1 collective-permute-start.45
  148.9 2.2 collective-permute-start.43
  151.2 1.5 collective-permute-done.45
  152.7 2.3 collective-permute-done.44
  156.2 6.4 %back_inner.1 = (bf16[512,512]{1,0:T(8,128)(2,1)S(1)}, f32[2,512]{1,0:T(2,128)S(1)}, f32[512,512]{1,0:T(8,128)S(1)}, f32[2,512]{1,0:T(2,128)S(1)}) custom-call(f32[18,1024]{1,0:T(8,128)S(1)} %get-tuple-element.128.refs_0_.scal, f32[4,512]{1,0:T(4,128)S(1)} %get-tuple-element.298.refs_1_, f32[4,512]{1,0:T(4,128)S(1)} %get-tuple-element.296.refs_2_, ...), custom_call_target="tpu_custom_call" | custom-call | flops 2415919104 | bytes 9617408 | tf_op jit(solution)/shard_map/back_inner/pallas_call | solution.py:896
  167.3 1.6 collective-permute-start.51
  168.9 2.8 %collective-permute-start.52 = (f32[4,512]{1,0:T(4,128)S(1)}, f32[4,512]{1,0:T(4,128)S(1)}, u32[]{:S(2)}, u32[]{:S(2)}) collective-permute-start(f32[4,512]{1,0:T(4,128)S(1)} %pad_maximum_fusion.12.refs_1_), channel_id=1, source_target_pairs={{0,3},{1,2},{2,1},{3,0},{4,7},{5,6},{6,5},{7,4},{8,11},{9,10},{10,... | collective-permute-start | bytes 24584 | tf_op jit(solution)/shard_map/ppermute | solution.py:76
  171.9 2.6 collective-permute-done.52.refs_4_
  177.0 3.7 %back_main.1 = (bf16[512,512]{1,0:T(8,128)(2,1)S(1)}, f32[2,512]{1,0:T(2,128)S(1)}, f32[512,512]{1,0:T(8,128)}, f32[2,512]{1,0:T(2,128)S(1)}) custom-call(f32[18,1024]{1,0:T(8,128)S(1)} %get-tuple-element.128.refs_0_.scal, f32[4,512]{1,0:T(4,128)S(1)} %pad_maximum_fusion.12.refs_1_, f32[4,512]{1,0:T(4,128)S(1)} %collective-permute-done.50.refs_2_, ...), custom_call_target="tpu_custom_call" | custom-call | flops 268435456 | bytes 6471680 | tf_op jit(solution)/shard_map/back_main/pallas_call | solution.py:896
  182.0 3.4 %collective-permute-start.55 = (f32[4,512]{1,0:T(4,128)S(1)}, f32[4,512]{1,0:T(4,128)S(1)}, u32[]{:S(2)}, u32[]{:S(2)}) collective-permute-start(f32[4,512]{1,0:T(4,128)S(1)} %pad_maximum_fusion.13.refs_1_), channel_id=1, source_target_pairs={{0,2},{1,3},{2,0},{3,1},{4,6},{5,7},{6,4},{7,5},{8,10},{9,11},{10,... | collective-permute-start | bytes 24584 | tf_op jit(solution)/shard_map/ppermute | solution.py:76
  187.5 3.7 %collective-permute-done.56.refs_4_ = f32[4,512]{1,0:T(4,128)S(1)} collective-permute-done((f32[4,512]{1,0:T(4,128)S(1)}, f32[4,512]{1,0:T(4,128)S(1)}, u32[]{:S(2)}, u32[]{:S(2)}) %collective-permute-start.56) | collective-permute-done | bytes 8224 | tf_op jit(solution)/shard_map/ppermute | solution.py:76
  191.2 6.1 %back_down.1 = (bf16[512,512]{1,0:T(8,128)(2,1)S(1)}, f32[2,512]{1,0:T(2,128)S(1)}, f32[512,1024]{1,0:T(8,128)S(1)}, f32[2,1024]{1,0:T(2,128)S(1)}) custom-call(f32[18,1024]{1,0:T(8,128)S(1)} %get-tuple-element.128.refs_0_.scal, f32[4,512]{1,0:T(4,128)S(1)} %pad_maximum_fusion.13.refs_1_, f32[4,512]{1,0:T(4,128)S(1)} %collective-permute-done.54.refs_2_, ...), custom_call_target="tpu_custom_call" | custom-call | tf_op jit(solution)/shard_map/back_down/pallas_call | solution.py:896
  197.4 1.8 share_main.1
  202.3 2.9 %collective-permute-start.60 = (f32[4,1024]{1,0:T(4,128)S(1)}, f32[4,1024]{1,0:T(4,128)S(1)}, u32[]{:S(2)}, u32[]{:S(2)}) collective-permute-start(f32[4,1024]{1,0:T(4,128)S(1)} %pad_maximum_fusion.7.rest_0_), channel_id=1, source_target_pairs={{0,3},{1,2},{2,1},{3,0},{4,7},{5,6},{6,5},{7,4},{8,11},{9,10},{10,... | collective-permute-start | bytes 49160 | tf_op jit(solution)/shard_map/ppermute | solution.py:76
  205.5 1.6 collective-permute-done.59.rest_2_
  209.5 2.5 collective-permute-start.62
  213.1 3.4 %collective-permute-start.67 = (bf16[64,1536]{1,0:T(8,128)(2,1)S(1)}, bf16[64,1536]{1,0:T(8,128)(2,1)S(1)}, u32[]{:S(2)}, u32[]{:S(2)}) collective-permute-start(bf16[64,1536]{1,0:T(8,128)(2,1)S(1)} %add_convert_fusion.2.rest_0_), channel_id=1, source_target_pairs={{0,2},{1,3},{2,0},{3,1},{4,6},{5,7},{6,4},{7,5},{8,10},{9,11},{10,... | collective-permute-start | bytes 589832 | tf_op jit(solution)/shard_map/ppermute | solution.py:76
  216.6 13.7 %collective-permute-done.64.rest_1_ = bf16[512,256]{1,0:T(8,128)(2,1)S(1)} collective-permute-done((bf16[512,256]{1,0:T(8,128)(2,1)S(1)}, bf16[512,256]{1,0:T(8,128)(2,1)S(1)}, u32[]{:S(2)}, u32[]{:S(2)}) %collective-permute-start.64) | collective-permute-done | bytes 262176 | tf_op jit(solution)/shard_map/ppermute | solution.py:76
  230.3 7.2 %collective-permute-start.68 = (bf16[64,1536]{1,0:T(8,128)(2,1)S(1)}, bf16[64,1536]{1,0:T(8,128)(2,1)S(1)}, u32[]{:S(2)}, u32[]{:S(2)}) collective-permute-start(bf16[64,1536]{1,0:T(8,128)(2,1)S(1)} %add_convert_fusion.2.rest_0_), channel_id=1, source_target_pairs={{0,3},{1,2},{2,1},{3,0},{4,7},{5,6},{6,5},{7,4},{8,11},{9,10},{10,... | collective-permute-start | bytes 589832 | tf_op jit(solution)/shard_map/ppermute | solution.py:76
  238.1 6.3 %back_input.1 = f32[4,128,512]{2,1,0:T(8,128)S(1)} custom-call(bf16[576,1024]{1,0:T(8,128)(2,1)S(1)} %get-tuple-element.196.grad, bf16[9,512,1024]{2,1,0:T(8,128)(2,1)} %bitcast.51), custom_call_target="tpu_custom_call" | custom-call | tf_op jit(solution)/shard_map/back_input/pallas_call | solution.py:1255
  244.5 4.7 %share_down.2 = (f32[1024,1024]{1,0:T(8,128)S(1)}, f32[1024,1024]{1,0:T(8,128)S(1)}) custom-call(bf16[512,256]{1,0:T(8,128)(2,1)S(1)} %cut_down.1.rest_0_, bf16[512,256]{1,0:T(8,128)(2,1)S(1)} %collective-permute-done.64.rest_1_, bf16[32,2,2,64,1024]{4,3,2,1,0:T(8,128)(2,1)} %bitcast.52), custom_call_target="tpu_custom_call" | custom-call | tf_op jit(solution)/shard_map/share_down/pallas_call | solution.py:1298
  249.2 5.1 %share_down.3 = (bf16[4608,128]{1,0:T(8,128)(2,1)S(1)}, bf16[4608,128]{1,0:T(8,128)(2,1)S(1)}) custom-call(bf16[512,256]{1,0:T(8,128)(2,1)S(1)} %collective-permute-done.62.rest_0_, bf16[512,256]{1,0:T(8,128)(2,1)S(1)} %collective-permute-done.63.rest_1_, f32[1024,1024]{1,0:T(8,128)S(1)} %get-tuple-element.204.rest_2_, ...), custom_call_target="tpu_custom_call" | custom-call | tf_op jit(solution)/shard_map/share_down/pallas_call | solution.py:1298
  257.3 2.0 collective-permute-done.33
  263.9 1.6 finish.1
  265.5 2.9 %convert_add_fusion = f32[4608,128]{1,0:T(8,128)} fusion(bf16[4608,128]{1,0:T(8,128)(2,1)} %collective-permute-done.69, bf16[4608,128]{1,0:T(8,128)(2,1)S(1)} %get-tuple-element.206), kind=kLoop, calls=%fused_computation | loop fusion | flops 1769472 | bytes 4718592 | tf_op jit(solution)/shard_map/add | solution.py:1317
  (205 shorter events, 58.7 us)
Async XLA Ops:
  7.2 160.0 %all-gather.2.cloned.1.call-start = ((), (), s32[]{:S(2)}) async-start(), calls=%async_computation | async-start | bytes 17301504 | tf_op jit(solution)/shard_map/all_gather | solution.py:1001
  8.5 6.5 %collective-permute-start = (bf16[2,64,1024]{2,1,0:T(8,128)(2,1)S(1)}, bf16[2,64,1024]{2,1,0:T(8,128)(2,1)S(1)}, u32[]{:S(2)}, u32[]{:S(2)}) collective-permute-start(bf16[2,64,1024]{2,1,0:T(8,128)(2,1)S(1)} %slice_bitcast_fusion), channel_id=1, source_target_pairs={{0,4},{4,8},{8,12},{12,16},{16,20},{20,24},{24,28},{1,5},{5,9},{9,... | collective-permute-start | bytes 786440 | tf_op jit(solution)/shard_map/ppermute | solution.py:975
  18.2 3.6 %collective-permute-start.1 = (bf16[64,1024]{1,0:T(8,128)(2,1)S(1)}, bf16[64,1024]{1,0:T(8,128)(2,1)S(1)}, u32[]{:S(2)}, u32[]{:S(2)}) collective-permute-start(bf16[64,1024]{1,0:T(8,128)(2,1)S(1)} %get-tuple-element.290), channel_id=1, source_target_pairs={{0,4},{4,0},{8,12},{12,8},{16,20},{20,16},{24,28},{28,24},{1,5},{5... | collective-permute-start | bytes 393224 | tf_op jit(solution)/shard_map/ppermute | solution.py:63
  21.8 9.2 %collective-permute-start.2 = (bf16[128,1024]{1,0:T(8,128)(2,1)S(1)}, bf16[128,1024]{1,0:T(8,128)(2,1)S(1)}, u32[]{:S(2)}, u32[]{:S(2)}) collective-permute-start(bf16[128,1024]{1,0:T(8,128)(2,1)S(1)} %pad_maximum_fusion.1.rest_0_), channel_id=1, source_target_pairs={{0,8},{4,12},{8,0},{12,4},{16,24},{20,28},{24,16},{28,20},{1,9},{5... | collective-permute-start | bytes 786440 | tf_op jit(solution)/shard_map/ppermute | solution.py:67
  23.8 12.7 %collective-permute-start.3 = (bf16[128,1024]{1,0:T(8,128)(2,1)S(1)}, bf16[128,1024]{1,0:T(8,128)(2,1)S(1)}, u32[]{:S(2)}, u32[]{:S(2)}) collective-permute-start(bf16[128,1024]{1,0:T(8,128)(2,1)S(1)} %pad_maximum_fusion.1.rest_0_), channel_id=1, source_target_pairs={{0,16},{4,20},{8,24},{12,28},{16,0},{20,4},{24,8},{28,12},{1,17},{... | collective-permute-start | bytes 786440 | tf_op jit(solution)/shard_map/ppermute | solution.py:67
  25.3 12.8 %collective-permute-start.4 = (bf16[128,1024]{1,0:T(8,128)(2,1)S(1)}, bf16[128,1024]{1,0:T(8,128)(2,1)S(1)}, u32[]{:S(2)}, u32[]{:S(2)}) collective-permute-start(bf16[128,1024]{1,0:T(8,128)(2,1)S(1)} %pad_maximum_fusion.1.rest_0_), channel_id=1, source_target_pairs={{0,24},{4,28},{8,16},{12,20},{16,8},{20,12},{24,0},{28,4},{1,25},{... | collective-permute-start | bytes 786440 | tf_op jit(solution)/shard_map/ppermute | solution.py:67
  40.8 215.2 %all-reduce.5.cloned.1.call-start = ((), (), s32[]{:S(2)}) async-start(), calls=%async_computation.1 | async-start | bytes 2097152 | tf_op jit(solution)/shard_map/psum | solution.py:1204
  41.0 1.4 collective-permute-start.9
  42.4 16.3 %collective-permute-start.10 = (bf16[128,1024]{1,0:T(8,128)(2,1)S(1)}, bf16[128,1024]{1,0:T(8,128)(2,1)S(1)}, u32[]{:S(2)}, u32[]{:S(2)}) collective-permute-start(bf16[128,1024]{1,0:T(8,128)(2,1)S(1)} %constant_dynamic-update-slice_fusion.refs_7_), channel_id=1, source_target_pairs={{0,8},{4,12},{8,0},{12,4},{16,24},{20,28},{24,16},{28,20},{1,9},{5... | collective-permute-start | bytes 786440 | tf_op jit(solution)/shard_map/ppermute | solution.py:72
  43.1 15.7 %collective-permute-start.11 = (bf16[128,1024]{1,0:T(8,128)(2,1)S(1)}, bf16[128,1024]{1,0:T(8,128)(2,1)S(1)}, u32[]{:S(2)}, u32[]{:S(2)}) collective-permute-start(bf16[128,1024]{1,0:T(8,128)(2,1)S(1)} %constant_dynamic-update-slice_fusion.refs_7_), channel_id=1, source_target_pairs={{0,16},{4,20},{8,24},{12,28},{16,0},{20,4},{24,8},{28,12},{1,17},{... | collective-permute-start | bytes 786440 | tf_op jit(solution)/shard_map/ppermute | solution.py:72
  46.0 4.5 %collective-permute-start.6 = (f32[4,1024]{1,0:T(4,128)S(1)}, f32[4,1024]{1,0:T(4,128)S(1)}, u32[]{:S(2)}, u32[]{:S(2)}) collective-permute-start(f32[4,1024]{1,0:T(4,128)S(1)} %pad_maximum_fusion.4.refs_1_), channel_id=1, source_target_pairs={{0,1},{1,0},{2,3},{3,2},{4,5},{5,4},{6,7},{7,6},{8,9},{9,8},{10,11... | collective-permute-start | bytes 49160 | tf_op jit(solution)/shard_map/ppermute | solution.py:76
  47.7 4.7 %collective-permute-start.7 = (f32[4,1024]{1,0:T(4,128)S(1)}, f32[4,1024]{1,0:T(4,128)S(1)}, u32[]{:S(2)}, u32[]{:S(2)}) collective-permute-start(f32[4,1024]{1,0:T(4,128)S(1)} %pad_maximum_fusion.4.refs_1_), channel_id=1, source_target_pairs={{0,2},{1,3},{2,0},{3,1},{4,6},{5,7},{6,4},{7,5},{8,10},{9,11},{10,... | collective-permute-start | bytes 49160 | tf_op jit(solution)/shard_map/ppermute | solution.py:76
  50.2 5.6 %collective-permute-start.8 = (f32[4,1024]{1,0:T(4,128)S(1)}, f32[4,1024]{1,0:T(4,128)S(1)}, u32[]{:S(2)}, u32[]{:S(2)}) collective-permute-start(f32[4,1024]{1,0:T(4,128)S(1)} %pad_maximum_fusion.4.refs_1_), channel_id=1, source_target_pairs={{0,3},{1,2},{2,1},{3,0},{4,7},{5,6},{6,5},{7,4},{8,11},{9,10},{10,... | collective-permute-start | bytes 49160 | tf_op jit(solution)/shard_map/ppermute | solution.py:76
  60.1 4.5 %collective-permute-start.13 = (f32[4,512]{1,0:T(4,128)S(1)}, f32[4,512]{1,0:T(4,128)S(1)}, u32[]{:S(2)}, u32[]{:S(2)}) collective-permute-start(f32[4,512]{1,0:T(4,128)S(1)} %pad_maximum_fusion.8.refs_1_), channel_id=1, source_target_pairs={{0,1},{1,0},{2,3},{3,2},{4,5},{5,4},{6,7},{7,6},{8,9},{9,8},{10,11... | collective-permute-start | bytes 24584 | tf_op jit(solution)/shard_map/ppermute | solution.py:76
  60.2 4.7 %collective-permute-start.14 = (f32[4,512]{1,0:T(4,128)S(1)}, f32[4,512]{1,0:T(4,128)S(1)}, u32[]{:S(2)}, u32[]{:S(2)}) collective-permute-start(f32[4,512]{1,0:T(4,128)S(1)} %pad_maximum_fusion.8.refs_1_), channel_id=1, source_target_pairs={{0,2},{1,3},{2,0},{3,1},{4,6},{5,7},{6,4},{7,5},{8,10},{9,11},{10,... | collective-permute-start | bytes 24584 | tf_op jit(solution)/shard_map/ppermute | solution.py:76
  61.4 5.5 %collective-permute-start.15 = (f32[4,512]{1,0:T(4,128)S(1)}, f32[4,512]{1,0:T(4,128)S(1)}, u32[]{:S(2)}, u32[]{:S(2)}) collective-permute-start(f32[4,512]{1,0:T(4,128)S(1)} %pad_maximum_fusion.8.refs_1_), channel_id=1, source_target_pairs={{0,3},{1,2},{2,1},{3,0},{4,7},{5,6},{6,5},{7,4},{8,11},{9,10},{10,... | collective-permute-start | bytes 24584 | tf_op jit(solution)/shard_map/ppermute | solution.py:76
  68.7 15.7 %collective-permute-start.20 = (bf16[128,1024]{1,0:T(8,128)(2,1)S(1)}, bf16[128,1024]{1,0:T(8,128)(2,1)S(1)}, u32[]{:S(2)}, u32[]{:S(2)}) collective-permute-start(bf16[128,1024]{1,0:T(8,128)(2,1)S(1)} %collective-permute-done.10.refs_8_), channel_id=1, source_target_pairs={{0,16},{4,20},{8,24},{12,28},{16,0},{20,4},{24,8},{28,12},{1,17},{... | collective-permute-start | bytes 786440 | tf_op jit(solution)/shard_map/ppermute | solution.py:72
  69.9 6.6 %collective-permute-start.17 = (f32[4,512]{1,0:T(4,128)S(1)}, f32[4,512]{1,0:T(4,128)S(1)}, u32[]{:S(2)}, u32[]{:S(2)}) collective-permute-start(f32[4,512]{1,0:T(4,128)S(1)} %pad_maximum_fusion.9.refs_1_), channel_id=1, source_target_pairs={{0,1},{1,0},{2,3},{3,2},{4,5},{5,4},{6,7},{7,6},{8,9},{9,8},{10,11... | collective-permute-start | bytes 24584 | tf_op jit(solution)/shard_map/ppermute | solution.py:76
  69.9 6.6 %collective-permute-start.18 = (f32[4,512]{1,0:T(4,128)S(1)}, f32[4,512]{1,0:T(4,128)S(1)}, u32[]{:S(2)}, u32[]{:S(2)}) collective-permute-start(f32[4,512]{1,0:T(4,128)S(1)} %pad_maximum_fusion.9.refs_1_), channel_id=1, source_target_pairs={{0,2},{1,3},{2,0},{3,1},{4,6},{5,7},{6,4},{7,5},{8,10},{9,11},{10,... | collective-permute-start | bytes 24584 | tf_op jit(solution)/shard_map/ppermute | solution.py:76
  73.6 5.6 %collective-permute-start.19 = (f32[4,512]{1,0:T(4,128)S(1)}, f32[4,512]{1,0:T(4,128)S(1)}, u32[]{:S(2)}, u32[]{:S(2)}) collective-permute-start(f32[4,512]{1,0:T(4,128)S(1)} %pad_maximum_fusion.9.refs_1_), channel_id=1, source_target_pairs={{0,3},{1,2},{2,1},{3,0},{4,7},{5,6},{6,5},{7,4},{8,11},{9,10},{10,... | collective-permute-start | bytes 24584 | tf_op jit(solution)/shard_map/ppermute | solution.py:76
  84.5 1.2 collective-permute-start.21
  85.7 5.9 %collective-permute-start.24 = (f32[4,1024]{1,0:T(4,128)S(1)}, f32[4,1024]{1,0:T(4,128)S(1)}, u32[]{:S(2)}, u32[]{:S(2)}) collective-permute-start(f32[4,1024]{1,0:T(4,128)S(1)} %pad_maximum_fusion.2), channel_id=1, source_target_pairs={{0,3},{1,2},{2,1},{3,0},{4,7},{5,6},{6,5},{7,4},{8,11},{9,10},{10,... | collective-permute-start | bytes 49160 | tf_op jit(solution)/shard_map/ppermute | solution.py:76
  86.5 5.1 %collective-permute-start.23 = (f32[4,1024]{1,0:T(4,128)S(1)}, f32[4,1024]{1,0:T(4,128)S(1)}, u32[]{:S(2)}, u32[]{:S(2)}) collective-permute-start(f32[4,1024]{1,0:T(4,128)S(1)} %pad_maximum_fusion.2), channel_id=1, source_target_pairs={{0,2},{1,3},{2,0},{3,1},{4,6},{5,7},{6,4},{7,5},{8,10},{9,11},{10,... | collective-permute-start | bytes 49160 | tf_op jit(solution)/shard_map/ppermute | solution.py:76
  86.5 6.1 %collective-permute-start.22 = (f32[4,1024]{1,0:T(4,128)S(1)}, f32[4,1024]{1,0:T(4,128)S(1)}, u32[]{:S(2)}, u32[]{:S(2)}) collective-permute-start(f32[4,1024]{1,0:T(4,128)S(1)} %pad_maximum_fusion.2), channel_id=1, source_target_pairs={{0,1},{1,0},{2,3},{3,2},{4,5},{5,4},{6,7},{7,6},{8,9},{9,8},{10,11... | collective-permute-start | bytes 49160 | tf_op jit(solution)/shard_map/ppermute | solution.py:76
  95.6 6.8 %collective-permute-start.26 = (f32[4,512]{1,0:T(4,128)S(1)}, f32[4,512]{1,0:T(4,128)S(1)}, u32[]{:S(2)}, u32[]{:S(2)}) collective-permute-start(f32[4,512]{1,0:T(4,128)S(1)} %pad_maximum_fusion.10.refs_1_), channel_id=1, source_target_pairs={{0,1},{1,0},{2,3},{3,2},{4,5},{5,4},{6,7},{7,6},{8,9},{9,8},{10,11... | collective-permute-start | bytes 24584 | tf_op jit(solution)/shard_map/ppermute | solution.py:76
  97.3 5.1 %collective-permute-start.27 = (f32[4,512]{1,0:T(4,128)S(1)}, f32[4,512]{1,0:T(4,128)S(1)}, u32[]{:S(2)}, u32[]{:S(2)}) collective-permute-start(f32[4,512]{1,0:T(4,128)S(1)} %pad_maximum_fusion.10.refs_1_), channel_id=1, source_target_pairs={{0,2},{1,3},{2,0},{3,1},{4,6},{5,7},{6,4},{7,5},{8,10},{9,11},{10,... | collective-permute-start | bytes 24584 | tf_op jit(solution)/shard_map/ppermute | solution.py:76
  98.5 5.4 %collective-permute-start.28 = (f32[4,512]{1,0:T(4,128)S(1)}, f32[4,512]{1,0:T(4,128)S(1)}, u32[]{:S(2)}, u32[]{:S(2)}) collective-permute-start(f32[4,512]{1,0:T(4,128)S(1)} %pad_maximum_fusion.10.refs_1_), channel_id=1, source_target_pairs={{0,3},{1,2},{2,1},{3,0},{4,7},{5,6},{6,5},{7,4},{8,11},{9,10},{10,... | collective-permute-start | bytes 24584 | tf_op jit(solution)/shard_map/ppermute | solution.py:76
  107.1 1.2 collective-permute-start.29
  108.4 4.5 %collective-permute-start.30 = (f32[4,1024]{1,0:T(4,128)S(1)}, f32[4,1024]{1,0:T(4,128)S(1)}, u32[]{:S(2)}, u32[]{:S(2)}) collective-permute-start(f32[4,1024]{1,0:T(4,128)S(1)} %pad_maximum_fusion.5.refs_1_), channel_id=1, source_target_pairs={{0,1},{1,0},{2,3},{3,2},{4,5},{5,4},{6,7},{7,6},{8,9},{9,8},{10,11... | collective-permute-start | bytes 49160 | tf_op jit(solution)/shard_map/ppermute | solution.py:76
  108.5 6.7 %collective-permute-start.31 = (f32[4,1024]{1,0:T(4,128)S(1)}, f32[4,1024]{1,0:T(4,128)S(1)}, u32[]{:S(2)}, u32[]{:S(2)}) collective-permute-start(f32[4,1024]{1,0:T(4,128)S(1)} %pad_maximum_fusion.5.refs_1_), channel_id=1, source_target_pairs={{0,2},{1,3},{2,0},{3,1},{4,6},{5,7},{6,4},{7,5},{8,10},{9,11},{10,... | collective-permute-start | bytes 49160 | tf_op jit(solution)/shard_map/ppermute | solution.py:76
  110.0 5.9 %collective-permute-start.32 = (f32[4,1024]{1,0:T(4,128)S(1)}, f32[4,1024]{1,0:T(4,128)S(1)}, u32[]{:S(2)}, u32[]{:S(2)}) collective-permute-start(f32[4,1024]{1,0:T(4,128)S(1)} %pad_maximum_fusion.5.refs_1_), channel_id=1, source_target_pairs={{0,3},{1,2},{2,1},{3,0},{4,7},{5,6},{6,5},{7,4},{8,11},{9,10},{10,... | collective-permute-start | bytes 49160 | tf_op jit(solution)/shard_map/ppermute | solution.py:76
  120.4 4.5 %collective-permute-start.35 = (f32[4,1024]{1,0:T(4,128)S(1)}, f32[4,1024]{1,0:T(4,128)S(1)}, u32[]{:S(2)}, u32[]{:S(2)}) collective-permute-start(f32[4,1024]{1,0:T(4,128)S(1)} %pad_maximum_fusion.6.refs_1_), channel_id=1, source_target_pairs={{0,1},{1,0},{2,3},{3,2},{4,5},{5,4},{6,7},{7,6},{8,9},{9,8},{10,11... | collective-permute-start | bytes 49160 | tf_op jit(solution)/shard_map/ppermute | solution.py:76
  121.2 6.0 %collective-permute-start.36 = (f32[4,1024]{1,0:T(4,128)S(1)}, f32[4,1024]{1,0:T(4,128)S(1)}, u32[]{:S(2)}, u32[]{:S(2)}) collective-permute-start(f32[4,1024]{1,0:T(4,128)S(1)} %pad_maximum_fusion.6.refs_1_), channel_id=1, source_target_pairs={{0,2},{1,3},{2,0},{3,1},{4,6},{5,7},{6,4},{7,5},{8,10},{9,11},{10,... | collective-permute-start | bytes 49160 | tf_op jit(solution)/shard_map/ppermute | solution.py:76
  123.9 5.9 %collective-permute-start.37 = (f32[4,1024]{1,0:T(4,128)S(1)}, f32[4,1024]{1,0:T(4,128)S(1)}, u32[]{:S(2)}, u32[]{:S(2)}) collective-permute-start(f32[4,1024]{1,0:T(4,128)S(1)} %pad_maximum_fusion.6.refs_1_), channel_id=1, source_target_pairs={{0,3},{1,2},{2,1},{3,0},{4,7},{5,6},{6,5},{7,4},{8,11},{9,10},{10,... | collective-permute-start | bytes 49160 | tf_op jit(solution)/shard_map/ppermute | solution.py:76
  134.6 8.0 %collective-permute-start.39 = (f32[4,512]{1,0:T(4,128)S(1)}, f32[4,512]{1,0:T(4,128)S(1)}, u32[]{:S(2)}, u32[]{:S(2)}) collective-permute-start(f32[4,512]{1,0:T(4,128)S(1)} %pad_maximum_fusion.11.refs_1_), channel_id=1, source_target_pairs={{0,1},{1,0},{2,3},{3,2},{4,5},{5,4},{6,7},{7,6},{8,9},{9,8},{10,11... | collective-permute-start | bytes 24584 | tf_op jit(solution)/shard_map/ppermute | solution.py:76
  134.7 8.0 %collective-permute-start.40 = (f32[4,512]{1,0:T(4,128)S(1)}, f32[4,512]{1,0:T(4,128)S(1)}, u32[]{:S(2)}, u32[]{:S(2)}) collective-permute-start(f32[4,512]{1,0:T(4,128)S(1)} %pad_maximum_fusion.11.refs_1_), channel_id=1, source_target_pairs={{0,2},{1,3},{2,0},{3,1},{4,6},{5,7},{6,4},{7,5},{8,10},{9,11},{10,... | collective-permute-start | bytes 24584 | tf_op jit(solution)/shard_map/ppermute | solution.py:76
  136.9 5.8 %collective-permute-start.41 = (f32[4,512]{1,0:T(4,128)S(1)}, f32[4,512]{1,0:T(4,128)S(1)}, u32[]{:S(2)}, u32[]{:S(2)}) collective-permute-start(f32[4,512]{1,0:T(4,128)S(1)} %pad_maximum_fusion.11.refs_1_), channel_id=1, source_target_pairs={{0,3},{1,2},{2,1},{3,0},{4,7},{5,6},{6,5},{7,4},{8,11},{9,10},{10,... | collective-permute-start | bytes 24584 | tf_op jit(solution)/shard_map/ppermute | solution.py:76
  146.1 18.9 %collective-permute-start.47 = (bf16[1024,128]{1,0:T(8,128)(2,1)S(1)}, bf16[1024,128]{1,0:T(8,128)(2,1)S(1)}, u32[]{:S(2)}, u32[]{:S(2)}) collective-permute-start(bf16[1024,128]{1,0:T(8,128)(2,1)S(1)} %get-tuple-element.172), channel_id=1, source_target_pairs={{0,4},{4,0},{8,12},{12,8},{16,20},{20,16},{24,28},{28,24},{1,5},{5... | collective-permute-start | bytes 786440 | tf_op jit(solution)/shard_map/ppermute | solution.py:63
  146.7 6.0 %collective-permute-start.45 = (f32[4,1024]{1,0:T(4,128)S(1)}, f32[4,1024]{1,0:T(4,128)S(1)}, u32[]{:S(2)}, u32[]{:S(2)}) collective-permute-start(f32[4,1024]{1,0:T(4,128)S(1)} %pad_maximum_fusion.3), channel_id=1, source_target_pairs={{0,3},{1,2},{2,1},{3,0},{4,7},{5,6},{6,5},{7,4},{8,11},{9,10},{10,... | collective-permute-start | bytes 49160 | tf_op jit(solution)/shard_map/ppermute | solution.py:76
  148.8 6.2 %collective-permute-start.44 = (f32[4,1024]{1,0:T(4,128)S(1)}, f32[4,1024]{1,0:T(4,128)S(1)}, u32[]{:S(2)}, u32[]{:S(2)}) collective-permute-start(f32[4,1024]{1,0:T(4,128)S(1)} %pad_maximum_fusion.3), channel_id=1, source_target_pairs={{0,2},{1,3},{2,0},{3,1},{4,6},{5,7},{6,4},{7,5},{8,10},{9,11},{10,... | collective-permute-start | bytes 49160 | tf_op jit(solution)/shard_map/ppermute | solution.py:76
  148.9 6.1 %collective-permute-start.43 = (f32[4,1024]{1,0:T(4,128)S(1)}, f32[4,1024]{1,0:T(4,128)S(1)}, u32[]{:S(2)}, u32[]{:S(2)}) collective-permute-start(f32[4,1024]{1,0:T(4,128)S(1)} %pad_maximum_fusion.3), channel_id=1, source_target_pairs={{0,1},{1,0},{2,3},{3,2},{4,5},{5,4},{6,7},{7,6},{8,9},{9,8},{10,11... | collective-permute-start | bytes 49160 | tf_op jit(solution)/shard_map/ppermute | solution.py:76
  156.2 8.0 %collective-permute-start.48 = (bf16[64,1536]{1,0:T(8,128)(2,1)S(1)}, bf16[64,1536]{1,0:T(8,128)(2,1)S(1)}, u32[]{:S(2)}, u32[]{:S(2)}) collective-permute-start(bf16[64,1536]{1,0:T(8,128)(2,1)S(1)} %get-tuple-element.178), channel_id=1, source_target_pairs={{0,4},{4,0},{8,12},{12,8},{16,20},{20,16},{24,28},{28,24},{1,5},{5... | collective-permute-start | bytes 589832 | tf_op jit(solution)/shard_map/ppermute | solution.py:63
  162.7 1.6 collective-permute-start.46
  164.1 2.1 collective-permute-start.49
  167.2 4.5 %collective-permute-start.50 = (f32[4,512]{1,0:T(4,128)S(1)}, f32[4,512]{1,0:T(4,128)S(1)}, u32[]{:S(2)}, u32[]{:S(2)}) collective-permute-start(f32[4,512]{1,0:T(4,128)S(1)} %pad_maximum_fusion.12.refs_1_), channel_id=1, source_target_pairs={{0,1},{1,0},{2,3},{3,2},{4,5},{5,4},{6,7},{7,6},{8,9},{9,8},{10,11... | collective-permute-start | bytes 24584 | tf_op jit(solution)/shard_map/ppermute | solution.py:76
  167.3 4.6 %collective-permute-start.51 = (f32[4,512]{1,0:T(4,128)S(1)}, f32[4,512]{1,0:T(4,128)S(1)}, u32[]{:S(2)}, u32[]{:S(2)}) collective-permute-start(f32[4,512]{1,0:T(4,128)S(1)} %pad_maximum_fusion.12.refs_1_), channel_id=1, source_target_pairs={{0,2},{1,3},{2,0},{3,1},{4,6},{5,7},{6,4},{7,5},{8,10},{9,11},{10,... | collective-permute-start | bytes 24584 | tf_op jit(solution)/shard_map/ppermute | solution.py:76
  168.9 5.6 %collective-permute-start.52 = (f32[4,512]{1,0:T(4,128)S(1)}, f32[4,512]{1,0:T(4,128)S(1)}, u32[]{:S(2)}, u32[]{:S(2)}) collective-permute-start(f32[4,512]{1,0:T(4,128)S(1)} %pad_maximum_fusion.12.refs_1_), channel_id=1, source_target_pairs={{0,3},{1,2},{2,1},{3,0},{4,7},{5,6},{6,5},{7,4},{8,11},{9,10},{10,... | collective-permute-start | bytes 24584 | tf_op jit(solution)/shard_map/ppermute | solution.py:76
  182.0 4.7 %collective-permute-start.54 = (f32[4,512]{1,0:T(4,128)S(1)}, f32[4,512]{1,0:T(4,128)S(1)}, u32[]{:S(2)}, u32[]{:S(2)}) collective-permute-start(f32[4,512]{1,0:T(4,128)S(1)} %pad_maximum_fusion.13.refs_1_), channel_id=1, source_target_pairs={{0,1},{1,0},{2,3},{3,2},{4,5},{5,4},{6,7},{7,6},{8,9},{9,8},{10,11... | collective-permute-start | bytes 24584 | tf_op jit(solution)/shard_map/ppermute | solution.py:76
  182.0 5.4 %collective-permute-start.55 = (f32[4,512]{1,0:T(4,128)S(1)}, f32[4,512]{1,0:T(4,128)S(1)}, u32[]{:S(2)}, u32[]{:S(2)}) collective-permute-start(f32[4,512]{1,0:T(4,128)S(1)} %pad_maximum_fusion.13.refs_1_), channel_id=1, source_target_pairs={{0,2},{1,3},{2,0},{3,1},{4,6},{5,7},{6,4},{7,5},{8,10},{9,11},{10,... | collective-permute-start | bytes 24584 | tf_op jit(solution)/shard_map/ppermute | solution.py:76
  185.4 5.8 %collective-permute-start.56 = (f32[4,512]{1,0:T(4,128)S(1)}, f32[4,512]{1,0:T(4,128)S(1)}, u32[]{:S(2)}, u32[]{:S(2)}) collective-permute-start(f32[4,512]{1,0:T(4,128)S(1)} %pad_maximum_fusion.13.refs_1_), channel_id=1, source_target_pairs={{0,3},{1,2},{2,1},{3,0},{4,7},{5,6},{6,5},{7,4},{8,11},{9,10},{10,... | collective-permute-start | bytes 24584 | tf_op jit(solution)/shard_map/ppermute | solution.py:76
  199.2 13.7 %collective-permute-start.65 = (bf16[64,1536]{1,0:T(8,128)(2,1)S(1)}, bf16[64,1536]{1,0:T(8,128)(2,1)S(1)}, u32[]{:S(2)}, u32[]{:S(2)}) collective-permute-start(bf16[64,1536]{1,0:T(8,128)(2,1)S(1)} %get-tuple-element.214), channel_id=1, source_target_pairs={{0,4},{4,0},{8,12},{12,8},{16,20},{20,16},{24,28},{28,24},{1,5},{5... | collective-permute-start | bytes 589832 | tf_op jit(solution)/shard_map/ppermute | solution.py:63
  199.3 1.4 collective-permute-start.57
  200.8 4.8 %collective-permute-start.58 = (f32[4,1024]{1,0:T(4,128)S(1)}, f32[4,1024]{1,0:T(4,128)S(1)}, u32[]{:S(2)}, u32[]{:S(2)}) collective-permute-start(f32[4,1024]{1,0:T(4,128)S(1)} %pad_maximum_fusion.7.rest_0_), channel_id=1, source_target_pairs={{0,1},{1,0},{2,3},{3,2},{4,5},{5,4},{6,7},{7,6},{8,9},{9,8},{10,11... | collective-permute-start | bytes 49160 | tf_op jit(solution)/shard_map/ppermute | solution.py:76
  200.8 6.3 %collective-permute-start.59 = (f32[4,1024]{1,0:T(4,128)S(1)}, f32[4,1024]{1,0:T(4,128)S(1)}, u32[]{:S(2)}, u32[]{:S(2)}) collective-permute-start(f32[4,1024]{1,0:T(4,128)S(1)} %pad_maximum_fusion.7.rest_0_), channel_id=1, source_target_pairs={{0,2},{1,3},{2,0},{3,1},{4,6},{5,7},{6,4},{7,5},{8,10},{9,11},{10,... | collective-permute-start | bytes 49160 | tf_op jit(solution)/shard_map/ppermute | solution.py:76
  202.3 5.9 %collective-permute-start.60 = (f32[4,1024]{1,0:T(4,128)S(1)}, f32[4,1024]{1,0:T(4,128)S(1)}, u32[]{:S(2)}, u32[]{:S(2)}) collective-permute-start(f32[4,1024]{1,0:T(4,128)S(1)} %pad_maximum_fusion.7.rest_0_), channel_id=1, source_target_pairs={{0,3},{1,2},{2,1},{3,0},{4,7},{5,6},{6,5},{7,4},{8,11},{9,10},{10,... | collective-permute-start | bytes 49160 | tf_op jit(solution)/shard_map/ppermute | solution.py:76
  208.4 21.8 %collective-permute-start.64 = (bf16[512,256]{1,0:T(8,128)(2,1)S(1)}, bf16[512,256]{1,0:T(8,128)(2,1)S(1)}, u32[]{:S(2)}, u32[]{:S(2)}) collective-permute-start(bf16[512,256]{1,0:T(8,128)(2,1)S(1)} %cut_down.1.rest_0_), channel_id=1, source_target_pairs={{0,1},{1,0},{2,3},{3,2},{4,5},{5,4},{6,7},{7,6},{8,9},{9,8},{10,11... | collective-permute-start | bytes 786440 | tf_op jit(solution)/shard_map/ppermute | solution.py:76
  209.5 39.7 %collective-permute-start.62 = (bf16[512,256]{1,0:T(8,128)(2,1)S(1)}, bf16[512,256]{1,0:T(8,128)(2,1)S(1)}, u32[]{:S(2)}, u32[]{:S(2)}) collective-permute-start(bf16[512,256]{1,0:T(8,128)(2,1)S(1)} %cut_down.1.rest_0_), channel_id=1, source_target_pairs={{0,2},{1,3},{2,0},{3,1},{4,6},{5,7},{6,4},{7,5},{8,10},{9,11},{10,... | collective-permute-start | bytes 786440 | tf_op jit(solution)/shard_map/ppermute | solution.py:76
  212.1 37.1 %collective-permute-start.63 = (bf16[512,256]{1,0:T(8,128)(2,1)S(1)}, bf16[512,256]{1,0:T(8,128)(2,1)S(1)}, u32[]{:S(2)}, u32[]{:S(2)}) collective-permute-start(bf16[512,256]{1,0:T(8,128)(2,1)S(1)} %cut_down.1.rest_0_), channel_id=1, source_target_pairs={{0,3},{1,2},{2,1},{3,0},{4,7},{5,6},{6,5},{7,4},{8,11},{9,10},{10,... | collective-permute-start | bytes 786440 | tf_op jit(solution)/shard_map/ppermute | solution.py:76
  213.0 42.4 %collective-permute-start.66 = (bf16[64,1536]{1,0:T(8,128)(2,1)S(1)}, bf16[64,1536]{1,0:T(8,128)(2,1)S(1)}, u32[]{:S(2)}, u32[]{:S(2)}) collective-permute-start(bf16[64,1536]{1,0:T(8,128)(2,1)S(1)} %add_convert_fusion.2.rest_0_), channel_id=1, source_target_pairs={{0,1},{1,0},{2,3},{3,2},{4,5},{5,4},{6,7},{7,6},{8,9},{9,8},{10,11... | collective-permute-start | bytes 589832 | tf_op jit(solution)/shard_map/ppermute | solution.py:76
  213.1 42.8 %collective-permute-start.67 = (bf16[64,1536]{1,0:T(8,128)(2,1)S(1)}, bf16[64,1536]{1,0:T(8,128)(2,1)S(1)}, u32[]{:S(2)}, u32[]{:S(2)}) collective-permute-start(bf16[64,1536]{1,0:T(8,128)(2,1)S(1)} %add_convert_fusion.2.rest_0_), channel_id=1, source_target_pairs={{0,2},{1,3},{2,0},{3,1},{4,6},{5,7},{6,4},{7,5},{8,10},{9,11},{10,... | collective-permute-start | bytes 589832 | tf_op jit(solution)/shard_map/ppermute | solution.py:76
  230.3 25.7 %collective-permute-start.68 = (bf16[64,1536]{1,0:T(8,128)(2,1)S(1)}, bf16[64,1536]{1,0:T(8,128)(2,1)S(1)}, u32[]{:S(2)}, u32[]{:S(2)}) collective-permute-start(bf16[64,1536]{1,0:T(8,128)(2,1)S(1)} %add_convert_fusion.2.rest_0_), channel_id=1, source_target_pairs={{0,3},{1,2},{2,1},{3,0},{4,7},{5,6},{6,5},{7,4},{8,11},{9,10},{10,... | collective-permute-start | bytes 589832 | tf_op jit(solution)/shard_map/ppermute | solution.py:76
  255.9 9.6 %collective-permute-start.69 = (bf16[4608,128]{1,0:T(8,128)(2,1)}, bf16[4608,128]{1,0:T(8,128)(2,1)}, u32[]{:S(2)}, u32[]{:S(2)}) collective-permute-start(bf16[4608,128]{1,0:T(8,128)(2,1)} %copy-done.13), channel_id=1, source_target_pairs={{0,4},{4,0},{8,12},{12,8},{16,20},{20,16},{24,28},{28,24},{1,5},{5... | collective-permute-start | bytes 3538952 | tf_op jit(solution)/shard_map/ppermute | solution.py:63
  256.8 4.8 %collective-permute-start.61 = (f32[2,128,512]{2,1,0:T(8,128)}, f32[2,128,512]{2,1,0:T(8,128)}, u32[]{:S(2)}, u32[]{:S(2)}) collective-permute-start(f32[2,128,512]{2,1,0:T(8,128)} %dynamic-slice_bitcast_fusion), channel_id=1, source_target_pairs={{0,4},{4,0},{8,12},{12,8},{16,20},{20,16},{24,28},{28,24},{1,5},{5... | collective-permute-start | bytes 1572872 | tf_op jit(solution)/shard_map/ppermute | solution.py:63
  257.3 2.0 collective-permute-start.33
  (33 other events, 437.7 us)
Sparse Core Ops, SparseCore 0:
  40.9 118.6 all-gather.1
  167.3 60.8 all-reduce.4

commit v5 on v4

--- a/solution.py
+++ b/solution.py
@@ -9,7 +9,7 @@
 
 EPSILON = 1e-05
 FAR = 20.0
-CHUNK = 32
+CHUNK = 64
 COLS = 256
 BF = jnp.bfloat16
 F32 = jnp.float32
@@ -121,7 +121,7 @@
     def turn(index, state):
         return body(pl.ds(pl.multiple_of(index * step, step), step), state)
 
-    return lax.fori_loop(0, total // step, turn, carry)
+    return lax.fori_loop(0, total // step, turn, carry, unroll=2)
 
 
 GAIN_WIDE, SHIFT_WIDE, GAIN, SHIFT = 0, 2, 4, 9
@@ -184,7 +184,7 @@
         return sums[0] + fold(out), sums[1] + fold(out * unit)
 
     zero = jnp.zeros((8, pre.shape[1]), F32)
-    first, second = rows_loop(pre.shape[0], body, (zero, zero), 16)
+    first, second = rows_loop(pre.shape[0], body, (zero, zero), 32)
     pay[0:1, :] = jnp.sum(first, axis=0, keepdims=True)
     pay[1:2, :] = jnp.sum(second, axis=0, keepdims=True)
 
@@ -433,7 +433,7 @@
     w_unite = w_unite.ready()
     for start in range(0, part.shape[1], COLS):
         cols = slice(start, start + COLS)
-        part[:, cols] = dot(shortcut[...], w_unite[0:half, cols])
+        part[:, cols] = dot(shortcut[...], w_unite[:, cols])
 
 
 def unite_kernel(groups, scal, *rest):
@@ -449,7 +449,7 @@
         transition[rows, :] = mish((pre[rows, :] - center) * scale + offset).astype(BF)
 
     rows_loop(pre.shape[0], body)
-    project(transition, w_unite.ready().at[half:, :], unite_pre, pay, scal, part)
+    project(transition, w_unite.ready(), unite_pre, pay, scal, part)
 
 
 def turn_kernel(groups, pieces, scal, *rest):
@@ -501,7 +501,7 @@
     w_unite = w_unite.ready()
     for start in range(0, half, COLS):
         scratch[:, start : start + COLS] = dot_back(
-            grad_unite[...], w_unite[half + start : half + start + COLS, :]
+            grad_unite[...], w_unite[start : start + COLS, :]
         )
     push(
         lambda rows: scratch[rows, :],
@@ -607,10 +607,10 @@
 def back_down_kernel(groups, scal, *rest):
     refs = rest[:groups]
     (
-        main_coef, down_coef, params, main_pushed, main_pre, w_main, grad_short, w_short, down_pre,
+        main_pushed, main_coef, down_coef, params, main_pre, w_main, grad_short, w_short, down_pre,
         grad_main, sums, pushed, pay, scratch,
     ) = rest[groups:]
-    main_pushed, main_pre = main_pushed.ready(), main_pre.ready()
+    main_pre = main_pre.ready()
     half = main_pre.shape[1]
     settle(scal, refs, main_pushed, main_pre, main_coef, row_of(params, GAIN, 1, half), grad_main, sums)
     w_main, grad_short, w_short = w_main.ready(), grad_short.ready(), w_short.ready()
@@ -705,8 +705,18 @@
     put_halves(grad_inner[:, cols], mainline[...], sectioned.shape[1], mine, other)
 
 
-def finish_kernel(unite, pack, taps, *rest):
-    mains, (w_unite, w_short, w_trans, w_inner, w_spatial, w_main) = rest[:-6], rest[-6:]
+def finish_kernel(planes, unite, pack, taps, *rest):
+    mains, (mine, got, near, far) = rest[:planes], rest[planes : planes + 4]
+    w_unite, w_short, w_trans, w_inner, w_spatial, w_main, output, grad_inputs, semaphores = rest[planes + 4 :]
+    core = own_core()
+    copies = [
+        pltpu.make_async_copy(mine, output.at[core, 0], semaphores.at[0]),
+        pltpu.make_async_copy(got, output.at[1 - core, 0], semaphores.at[1]),
+        pltpu.make_async_copy(near.at[0], grad_inputs.at[core], semaphores.at[2]),
+        pltpu.make_async_copy(far.at[1], grad_inputs.at[1 - core], semaphores.at[3]),
+    ]
+    for copy in copies:
+        copy.start()
     w_unite[...] = unite[...].astype(F32)
     for outs, values in (
         ((w_short, w_trans), pack[...].astype(F32)),
@@ -719,6 +729,8 @@
     half = w_trans.shape[1]
     for tap in range(w_spatial.shape[0]):
         w_spatial[tap] = taps[:, tap * half : (tap + 1) * half].astype(F32)
+    for copy in copies:
+        copy.wait()
 
 
 def norm_sums_kernel(wide_count, *refs):
@@ -830,7 +842,7 @@
 
     def put(parity, column, values):
         for row in range(2):
-            out[2 * row + parity, pl.ds(column, width, stride=2), :] = values[
+            out[row ^ own_core(), parity, pl.ds(column, width, stride=2), :] = values[
                 row * width : (row + 1) * width
             ]
 
@@ -872,6 +884,11 @@
 
 
 def call(kernel, name, scalars, near, outs, flops, scratch=(), far=(), pin=False, spill=(), light=False, out=(), late=False):
+    cuts = [one[1] if isinstance(one, tuple) else None for one in far]
+    far = [one[0] if isinstance(one, tuple) else one for one in far]
+    held_far = [
+        shape((cut.stop - cut.start,) + a.shape[1:], a.dtype) if cut else a for a, cut in zip(far, cuts)
+    ]
     moved = sum(nbytes(a.shape, a.dtype) for a in (*near, *far, *outs))
     scratch = [s if hasattr(s, "memory_space") or not hasattr(s, "shape") else pltpu.VMEM(s.shape, s.dtype) for s in scratch]
     held = moved + sum(nbytes(s.shape, s.dtype) for s in scratch if hasattr(s, "shape"))
@@ -888,7 +905,10 @@
     def body(*refs):
         sources, rest = refs[before : before + after_far], refs[before + after_far :]
         targets = rest[last : last + after_far]
-        fars = [Far(a, b, rest[-1].at[k]) for k, (a, b) in enumerate(zip(sources, targets))]
+        fars = [
+            Far(a.at[cut] if cut else a, b, rest[-1].at[k])
+            for k, (a, b, cut) in enumerate(zip(sources, targets, cuts))
+        ]
         kernel(*refs[:before], *fars, *rest[:last])
         for one in fars:
             one.ready()
@@ -900,7 +920,7 @@
         in_specs=[SMEM] * len(scalars) + [VMEM] * len(near) + [ANY] * len(far),
         out_specs=tuple(ANY if k in out and not late else VMEM for k in range(len(outs))),
         scratch_shapes=scratch
-        + [pltpu.VMEM(a.shape, a.dtype) for a in far]
+        + [pltpu.VMEM(a.shape, a.dtype) for a in held_far]
         + ([pltpu.SemaphoreType.DMA((len(far),))] if far else []),
         compiler_params=pltpu.CompilerParams(vmem_limit_bytes=held + (8 << 20)),
         cost_estimate=LIGHT if light else pl.CostEstimate(flops=flops, bytes_accessed=moved, transcendentals=0),
@@ -1075,7 +1095,7 @@
         [scal, *short_all, short_pre, params],
         [shape((cells, half), BF), shape((cells, full)), shape((2, half))],
         2 * cells * half * full,
-        far=[w_unite],
+        far=[(w_unite, slice(0, half))],
     )
     transition, unite_pre, unite_pay, trans_coef = stage(
         functools.partial(unite_kernel, groups),
@@ -1084,7 +1104,7 @@
         [scal, *trans_all, trans_pre, unite_part, params],
         [shape((cells, half), BF), shape((cells, full)), shape((2, full)), shape((2, half))],
         2 * cells * half * full,
-        far=[w_unite],
+        far=[(w_unite, slice(half, full))],
     )
     unite_all = here.everywhere(unite_pay)
     unite_pushed, mine, other, unite_pay, unite_coef = stage(
@@ -1111,7 +1131,7 @@
         [shape((cells, full), BF), shape((2, full)), shape((cells, half)), shape((2, half))],
         2 * cells * half * full,
         [shape((cells, half))],
-        far=[w_unite],
+        far=[(w_unite, slice(half, full))],
     )
     trans_all = here.everywhere(trans_pay)
     if wide:
@@ -1138,7 +1158,7 @@
         [shape((cells, half)), shape((2, half))],
         2 * cells * half * full,
         [shape((cells, half))],
-        far=[w_unite],
+        far=[(w_unite, slice(0, half))],
     )
     grad_trans_pre, trans_sums, grad_merged, spatial_pushed, spatial_pay = stage(
         functools.partial(back_spatial_kernel, groups),
@@ -1211,19 +1231,17 @@
         2 * cells * half * half,
         [shape((cells, half))],
         far=[w_inner],
-        out=(2,),
-        late=True,
     )
     main_all = here.everywhere(main_pay)
     grad_main_pre, main_sums, down_pushed, down_pay = stage(
         functools.partial(back_down_kernel, groups),
         "back_down",
         [],
-        [scal, *main_all, main_coef, down_coef, params],
+        [scal, *main_all, main_pushed, main_coef, down_coef, params],
         [shape((cells, half), BF), shape((2, half)), shape((cells, full)), shape((2, full))],
         4 * cells * half * full,
         [shape((cells, full))],
-        far=[main_pushed, main_keep, w_main, grad_short_pre, w_short, down_keep], light=True)
+        far=[main_keep, w_main, grad_short_pre, w_short, down_keep], light=True)
     down_all = here.everywhere(down_pay)
     spare = width
     if wide:
@@ -1242,7 +1260,8 @@
         [scal, *down_all, down_pushed, down_pre, down_coef, params],
         [shape((cells + spare, full), BF), shape((2, full))],
         10 * cells * full, light=True)
-    output = jnp.stack(here.by_core(*after(output_rows, down_pay))).reshape(grad_output.shape)
+    if not wide:
+        output = jnp.stack(here.by_core(*output_rows)).reshape(grad_output.shape)
     norm_grads = stage(
         functools.partial(norm_sums_kernel, 2),
         "norm_sums",
@@ -1256,12 +1275,12 @@
             functools.partial(back_input_kernel, width),
             name="back_input",
             grid=(half // 128,),
-            out_shape=shape((4, 2 * width, half)),
+            out_shape=shape((2, 2, 2 * width, half)),
             in_specs=[
                 pl.BlockSpec((cells + spare, full), lambda n: (0, 0)),
                 pl.BlockSpec((9, 128, full), lambda n: (0, n, 0)),
             ],
-            out_specs=pl.BlockSpec((4, 2 * width, 128), lambda n: (0, 0, n)),
+            out_specs=pl.BlockSpec((2, 2, 2 * width, 128), lambda n: (0, 0, 0, n)),
             scratch_shapes=[pltpu.VMEM((3 * width, full), BF)] * 2,
             compiler_params=pltpu.CompilerParams(vmem_limit_bytes=16 << 20),
             cost_estimate=LIGHT,
@@ -1278,8 +1297,6 @@
                 light=True,
             )
         )
-        mine, other = here.split(near.reshape(2, 2, 2 * width, half))
-        grad_inputs = jnp.stack(here.by_core(mine, here.swap(other)))
         columns = full // chips
         sums_here = [shape((full, 4 * columns)), shape((full, 4 * columns))]
         halves = [shape((9 * half, columns // 2), BF)] * 2
@@ -1315,17 +1332,23 @@
         other, *tied = lax.optimization_barrier((other, *shares, *mains))
         shares, mains = tied[: len(shares)], tied[len(shares) :]
         grad_w_down = mine.astype(F32) + here.swap(other).astype(F32)
-        early = stage(
-            finish_kernel,
-            "finish",
-            [],
-            [*shares, *mains],
-            [
-                shape((full, 2 * lean)), shape((lean, full)), shape((lean, half)), shape((lean, half)),
-                shape((9, lean, half)), shape((lean, full)),
-            ],
-            0,
-            spill=range(6), light=True)
+        outs = [
+            shape((full, 2 * lean)), shape((lean, full)), shape((lean, half)), shape((lean, half)),
+            shape((9, lean, half)), shape((lean, full)),
+            shape(grad_output.shape, BF), shape(inputs.shape),
+        ]
+        placed = [*output_rows, near, here.swap(near)]
+        early = pl.pallas_call(
+            functools.partial(finish_kernel, groups),
+            name="finish",
+            out_shape=tuple(outs),
+            in_specs=[VMEM] * (3 + groups) + [ANY] * 4,
+            out_specs=(VMEM,) * 6 + (ANY,) * 2,
+            scratch_shapes=[pltpu.SemaphoreType.DMA((4,))],
+            compiler_params=pltpu.CompilerParams(vmem_limit_bytes=24 << 20),
+            cost_estimate=LIGHT,
+        )(*shares, *mains, *placed)
+        output, grad_inputs = early[6:]
         early = [
             early[1].T, early[5].T, early[3].T, jnp.swapaxes(early[4], 1, 2), early[2].T, early[0],
         ]

time: 278 us -> 275 us (0.989)
  waiting for transfers between devices: 78.8 us -> 85.1 us
  other arithmetic: 9.59 us -> 4.36 us
  Pallas kernels: 80.8 us -> 76.3 us
    pallas_call x24 -> x23, Pallas kernels: 57.5 us -> 50.4 us  [call(): pl.pallas_call(body if far else kernel, name=name, out_shape=tuple(outs),...]
    ppermute x42, waiting for transfers between devices: 51 us -> 55.9 us  [plane_hops(): lax.ppermute(value, 'batch', [(i, i ^ step) for i in range(self.groups)])]
    another operation x3 -> x0, other arithmetic: 3.26 us -> none  [the longest x2 2.33 us: on_device(): grad_inputs = jnp.stack(here.by_core(mine, here.swap(other)))]
  transfers between devices with their start and end apart: 72 -> 72, of which waited for: 42 -> 45; matrix products, arithmetic and copies ran while one was open for 3% -> 1% of each run, Pallas kernels for 28% -> 26%
where the time goes in v5:
time: 275 us; the launch traced here: 272 us
  waiting for transfers between devices  85.1 us (31%)
  starting transfers between devices  83.4 us (30%)
  Pallas kernels  76.3 us (28%)
  between operations  15 us (5%)
  local copies, waits for them, and re-layouts  8.05 us (3%)
  other arithmetic  4.36 us (2%)
    ppermute x42, starting transfers between devices, plane_hops(): lax.ppermute(value, 'batch', [(i, i ^ step) for i in range(self.groups)])  68.3 us
    ppermute x42, waiting for transfers between devices, plane_hops(): lax.ppermute(value, 'batch', [(i, i ^ step) for i in range(self.groups)])  55.9 us
    pallas_call x23, Pallas kernels, call(): pl.pallas_call(body if far else kernel, name=name, out_shape=tuple(outs),...  50.4 us
    ppermute x21, waiting for transfers between devices, swap(): return lax.ppermute(value, 'rows', [(i, i ^ 1) for i in range(self.rows)])  17.4 us
    ppermute x3, waiting for transfers between devices, chip_hops(): lax.ppermute(value, 'rows', [(i, i ^ 2 * step) for i in range(self.rows)])  11.8 us
    pallas_call x2, Pallas kernels, share_down(): pl.pallas_call(functools.partial(share_down_kernel, steps, chips, width,...  9.79 us
    pallas_call x2, Pallas kernels, run(): pl.pallas_call(kernel, name=name, out_shape=(pltpu.VMEM if pin else shape...  7.15 us
    pallas_call x1, Pallas kernels, on_device(): pl.pallas_call(functools.partial(back_input_kernel, width), name='back_in...  6.37 us
  transfers between devices with their start and end apart: 72, of which 45 were waited for; matrix products, arithmetic and copies ran while one was open for 1% of the time, Pallas kernels for 26%

profile of v5, /device:TPU:0, one launch (start us, length us, event | category | flops | bytes accessed | tf_op | source)
XLA Modules:
  0.0 272.3 jit_solution(6493954482714429428)
XLA Ops:
  8.5 2.4 collective-permute-start
  10.9 4.1 %own.1.part = f32[128,1024]{1,0:T(8,128)S(1)} custom-call(bf16[2,2,64,1024]{3,2,1,0:T(8,128)(2,1)S(1)} %reshape.60.x, bf16[3,1536,1024]{2,1,0:T(8,128)(2,1)} %bitcast.25), custom_call_target="tpu_custom_call" | custom-call | flops 805306368 | bytes 6291456 | tf_op jit(solution)/shard_map/own/pallas_call | solution.py:941
  15.0 3.1 %above.1 = bf16[2,64,1024]{2,1,0:T(8,128)(2,1)S(1)} custom-call(bf16[2,64,1024]{2,1,0:T(8,128)(2,1)S(1)} %collective-permute-done.above, f32[128,1024]{1,0:T(8,128)S(1)} %own.1.part, bf16[3,1536,1024]{2,1,0:T(8,128)(2,1)} %bitcast.26), custom_call_target="tpu_custom_call" | custom-call | flops 402653184 | bytes 3145728 | tf_op jit(solution)/shard_map/above/pallas_call | solution.py:941
  18.2 2.7 collective-permute-start.1
  21.8 2.0 collective-permute-start.2
  26.3 4.7 %collective-permute-done.2.rest_1_ = bf16[128,1024]{1,0:T(8,128)(2,1)S(1)} collective-permute-done((bf16[128,1024]{1,0:T(8,128)(2,1)S(1)}, bf16[128,1024]{1,0:T(8,128)(2,1)S(1)}, u32[]{:S(2)}, u32[]{:S(2)}) %collective-permute-start.2) | collective-permute-done | bytes 262176 | tf_op jit(solution)/shard_map/ppermute | solution.py:67
  31.0 5.5 %collective-permute-done.3.rest_2_ = bf16[128,1024]{1,0:T(8,128)(2,1)S(1)} collective-permute-done((bf16[128,1024]{1,0:T(8,128)(2,1)S(1)}, bf16[128,1024]{1,0:T(8,128)(2,1)S(1)}, u32[]{:S(2)}, u32[]{:S(2)}) %collective-permute-start.3) | collective-permute-done | bytes 262176 | tf_op jit(solution)/shard_map/ppermute | solution.py:67
  38.1 1.7 whole.1
  42.8 1.7 collective-permute-start.11
  47.3 2.6 collective-permute-start.7
  50.2 1.9 collective-permute-done.7.refs_3_
  52.1 3.6 %collective-permute-done.8.refs_4_ = f32[4,1024]{1,0:T(4,128)S(1)} collective-permute-done((f32[4,1024]{1,0:T(4,128)S(1)}, f32[4,1024]{1,0:T(4,128)S(1)}, u32[]{:S(2)}, u32[]{:S(2)}) %collective-permute-start.8) | collective-permute-done | bytes 16416 | tf_op jit(solution)/shard_map/ppermute | solution.py:76
  55.6 2.9 %main.1 = (bf16[512,1024]{1,0:T(8,128)(2,1)S(1)}, f32[512,512]{1,0:T(8,128)S(1)}, f32[512,512]{1,0:T(8,128)}, f32[2,512]{1,0:T(2,128)S(1)}, f32[2,1024]{1,0:T(2,128)S(1)}) custom-call(f32[18,1024]{1,0:T(8,128)S(1)} %get-tuple-element.129.refs_0_.scal, f32[4,1024]{1,0:T(4,128)S(1)} %pad_maximum_fusion.3.refs_1_, ...), custom_call_target="tpu_custom_call" | custom-call | flops 536870912 | bytes 5451776 | tf_op jit(solution)/shard_map/main/pallas_call | solution.py:916
  61.1 3.2 %collective-permute-start.15 = (f32[4,512]{1,0:T(4,128)S(1)}, f32[4,512]{1,0:T(4,128)S(1)}, u32[]{:S(2)}, u32[]{:S(2)}) collective-permute-start(f32[4,512]{1,0:T(4,128)S(1)} %pad_maximum_fusion.7.refs_1_), channel_id=1, source_target_pairs={{0,3},{1,2},{2,1},{3,0},{4,7},{5,6},{6,5},{7,4},{8,11},{9,10},{10,... | collective-permute-start | bytes 24584 | tf_op jit(solution)/shard_map/ppermute | solution.py:76
  64.8 1.9 collective-permute-done.15.refs_4_
  66.7 1.7 inner.1
  69.7 3.7 %collective-permute-start.18 = (f32[4,512]{1,0:T(4,128)S(1)}, f32[4,512]{1,0:T(4,128)S(1)}, u32[]{:S(2)}, u32[]{:S(2)}) collective-permute-start(f32[4,512]{1,0:T(4,128)S(1)} %pad_maximum_fusion.8.refs_1_), channel_id=1, source_target_pairs={{0,2},{1,3},{2,0},{3,1},{4,6},{5,7},{6,4},{7,5},{8,10},{9,11},{10,... | collective-permute-start | bytes 24584 | tf_op jit(solution)/shard_map/ppermute | solution.py:76
  74.1 2.2 short.1
  76.3 2.7 collective-permute-done.19.refs_4_
  79.0 5.2 %spatial.1 = (bf16[640,1536]{1,0:T(8,128)(2,1)S(1)}, f32[512,512]{1,0:T(8,128)S(1)}, f32[2,512]{1,0:T(2,128)S(1)}, f32[2,512]{1,0:T(2,128)S(1)}) custom-call(f32[18,1024]{1,0:T(8,128)S(1)} %get-tuple-element.129.refs_0_.scal, f32[4,512]{1,0:T(4,128)S(1)} %pad_maximum_fusion.8.refs_1_, f32[4,512]{1,0:T(4,128)S(1)} %collective-permute-done.17.refs_2_, ...), custom_call_target="tpu_custom_call" | custom-call | flops 2415919104 | bytes 8953856 | tf_op jit(solution)/shard_map/spatial/pallas_call | solution.py:916
  86.3 3.7 %collective-permute-start.22 = (f32[4,1024]{1,0:T(4,128)S(1)}, f32[4,1024]{1,0:T(4,128)S(1)}, u32[]{:S(2)}, u32[]{:S(2)}) collective-permute-start(f32[4,1024]{1,0:T(4,128)S(1)} %pad_maximum_fusion.1), channel_id=1, source_target_pairs={{0,1},{1,0},{2,3},{3,2},{4,5},{5,4},{6,7},{7,6},{8,9},{9,8},{10,11... | collective-permute-start | bytes 49160 | tf_op jit(solution)/shard_map/ppermute | solution.py:76
  92.7 1.7 trans.1
  98.4 1.7 collective-permute-start.28
  100.1 1.9 shortcut.1
  102.1 1.7 collective-permute-done.28.refs_4_
  103.8 2.5 unite.1
  107.7 1.9 collective-permute-start.31
  109.7 2.4 collective-permute-start.32
  112.6 2.4 collective-permute-done.31.refs_3_
  115.5 3.3 %turn.1 = (f32[512,1024]{1,0:T(8,128)S(1)}, bf16[64,1024]{1,0:T(8,128)(2,1)S(1)}, bf16[64,1024]{1,0:T(8,128)(2,1)S(1)}, f32[2,1024]{1,0:T(2,128)S(1)}, f32[2,1024]{1,0:T(2,128)S(1)}) custom-call(f32[18,1024]{1,0:T(8,128)S(1)} %get-tuple-element.129.refs_0_.scal, f32[4,1024]{1,0:T(4,128)S(1)} %pad_maximum_fusion.4.refs_1_, ...), custom_call_target="tpu_custom_call" | custom-call | flops 20971520 | bytes 5718016 | tf_op jit(solution)/shard_map/turn/pallas_call | solution.py:916
  120.9 2.3 collective-permute-start.35
  125.0 2.2 collective-permute-done.35.refs_3_
  127.2 1.8 collective-permute-done.36.refs_4_
  129.0 3.0 %back_trans.1 = (bf16[512,1024]{1,0:T(8,128)(2,1)S(1)}, f32[2,1024]{1,0:T(2,128)S(1)}, f32[512,512]{1,0:T(8,128)S(1)}, f32[2,512]{1,0:T(2,128)S(1)}) custom-call(f32[18,1024]{1,0:T(8,128)S(1)} %get-tuple-element.129.refs_0_.scal, f32[4,1024]{1,0:T(4,128)S(1)} %pad_maximum_fusion.5.refs_1_, f32[4,1024]{1,0:T(4,128)S(1)} %collective-permute-done.34.refs_2_, ...), custom_call_target="tpu_custom_call" | custom-call | flops 536870912 | bytes 9658368 | tf_op jit(solution)/shard_map/back_trans/pallas_call | solution.py:916
  133.3 1.9 collective-permute-start.39
  135.2 2.5 collective-permute-start.40
  137.7 2.9 %back_short.1 = (f32[512,512]{1,0:T(8,128)S(1)}, f32[2,512]{1,0:T(2,128)S(1)}) custom-call(bf16[512,1024]{1,0:T(8,128)(2,1)S(1)} %get-tuple-element.161.refs_0_.grad, f32[512,512]{1,0:T(8,128)S(1)} %get-tuple-element.149.refs_5_.refs_1_.rest_5_, f32[2,512]{1,0:T(2,128)S(1)} %get-tuple-element.162.refs_2_.rest_6_, ...), custom_call_target="tpu_custom_call" | custom-call | flops 536870912 | bytes 5308416 | tf_op jit(solution)/shard_map/back_short/pallas_call | solution.py:916
  140.7 2.5 back_spatial.1
  144.5 2.6 collective-permute-start.44
  147.1 1.8 collective-permute-start.42
  150.5 1.6 collective-permute-done.43
  153.9 5.9 %back_inner.1 = (bf16[512,512]{1,0:T(8,128)(2,1)S(1)}, f32[2,512]{1,0:T(2,128)S(1)}, f32[512,512]{1,0:T(8,128)S(1)}, f32[2,512]{1,0:T(2,128)S(1)}) custom-call(f32[18,1024]{1,0:T(8,128)S(1)} %get-tuple-element.129.refs_0_.scal, f32[4,512]{1,0:T(4,128)S(1)} %get-tuple-element.257.refs_1_, f32[4,512]{1,0:T(4,128)S(1)} %get-tuple-element.255.refs_2_, ...), custom_call_target="tpu_custom_call" | custom-call | flops 2415919104 | bytes 9617408 | tf_op jit(solution)/shard_map/back_inner/pallas_call | solution.py:916
  165.1 2.0 collective-permute-start.50
  167.1 1.8 collective-permute-start.51
  169.6 3.0 %collective-permute-done.51.refs_4_ = f32[4,512]{1,0:T(4,128)S(1)} collective-permute-done((f32[4,512]{1,0:T(4,128)S(1)}, f32[4,512]{1,0:T(4,128)S(1)}, u32[]{:S(2)}, u32[]{:S(2)}) %collective-permute-start.51) | collective-permute-done | bytes 8224 | tf_op jit(solution)/shard_map/ppermute | solution.py:76
  175.1 2.5 back_main.1
  178.9 2.4 collective-permute-start.54
  181.3 2.0 collective-permute-start.55
  183.9 3.3 %collective-permute-done.55.refs_4_ = f32[4,512]{1,0:T(4,128)S(1)} collective-permute-done((f32[4,512]{1,0:T(4,128)S(1)}, f32[4,512]{1,0:T(4,128)S(1)}, u32[]{:S(2)}, u32[]{:S(2)}) %collective-permute-start.55) | collective-permute-done | bytes 8224 | tf_op jit(solution)/shard_map/ppermute | solution.py:76
  187.1 5.2 %back_down.1 = (bf16[512,512]{1,0:T(8,128)(2,1)S(1)}, f32[2,512]{1,0:T(2,128)S(1)}, f32[512,1024]{1,0:T(8,128)S(1)}, f32[2,1024]{1,0:T(2,128)S(1)}) custom-call(f32[18,1024]{1,0:T(8,128)S(1)} %get-tuple-element.129.refs_0_.scal, f32[4,512]{1,0:T(4,128)S(1)} %pad_maximum_fusion.12.refs_1_, f32[4,512]{1,0:T(4,128)S(1)} %collective-permute-done.53.refs_2_, ...), custom_call_target="tpu_custom_call" | custom-call | tf_op jit(solution)/shard_map/back_down/pallas_call | solution.py:916
  192.4 1.8 share_main.1
  195.8 2.5 collective-permute-start.58
  198.3 1.9 collective-permute-start.59
  201.5 2.6 collective-permute-done.59.rest_3_
  204.4 2.5 collective-permute-start.60
  206.9 1.9 collective-permute-start.61
  208.9 2.5 collective-permute-start.65
  211.4 16.1 %collective-permute-done.62.rest_1_ = bf16[512,256]{1,0:T(8,128)(2,1)S(1)} collective-permute-done((bf16[512,256]{1,0:T(8,128)(2,1)S(1)}, bf16[512,256]{1,0:T(8,128)(2,1)S(1)}, u32[]{:S(2)}, u32[]{:S(2)}) %collective-permute-start.62) | collective-permute-done | bytes 262176 | tf_op jit(solution)/shard_map/ppermute | solution.py:76
  227.5 7.9 %collective-permute-start.66 = (bf16[64,1536]{1,0:T(8,128)(2,1)S(1)}, bf16[64,1536]{1,0:T(8,128)(2,1)S(1)}, u32[]{:S(2)}, u32[]{:S(2)}) collective-permute-start(bf16[64,1536]{1,0:T(8,128)(2,1)S(1)} %add_convert_fusion.2.rest_0_), channel_id=1, source_target_pairs={{0,3},{1,2},{2,1},{3,0},{4,7},{5,6},{6,5},{7,4},{8,11},{9,10},{10,... | collective-permute-start | bytes 589832 | tf_op jit(solution)/shard_map/ppermute | solution.py:76
  236.0 6.4 %back_input.1.rest_6_ = f32[2,2,128,512]{3,2,1,0:T(8,128)S(1)} custom-call(bf16[576,1024]{1,0:T(8,128)(2,1)S(1)} %get-tuple-element.193.grad, bf16[9,512,1024]{2,1,0:T(8,128)(2,1)} %bitcast.27), custom_call_target="tpu_custom_call" | custom-call | tf_op jit(solution)/shard_map/back_input/pallas_call | solution.py:1274
  242.3 4.7 %share_down.2 = (f32[1024,1024]{1,0:T(8,128)S(1)}, f32[1024,1024]{1,0:T(8,128)S(1)}) custom-call(bf16[512,256]{1,0:T(8,128)(2,1)S(1)} %cut_down.1.rest_0_, bf16[512,256]{1,0:T(8,128)(2,1)S(1)} %collective-permute-done.62.rest_1_, bf16[32,2,2,64,1024]{4,3,2,1,0:T(8,128)(2,1)} %bitcast.28), custom_call_target="tpu_custom_call" | custom-call | tf_op jit(solution)/shard_map/share_down/pallas_call | solution.py:1315
  247.1 5.1 %share_down.3 = (bf16[4608,128]{1,0:T(8,128)(2,1)S(1)}, bf16[4608,128]{1,0:T(8,128)(2,1)S(1)}) custom-call(bf16[512,256]{1,0:T(8,128)(2,1)S(1)} %collective-permute-done.60.rest_0_, bf16[512,256]{1,0:T(8,128)(2,1)S(1)} %collective-permute-done.61.rest_1_, f32[1024,1024]{1,0:T(8,128)S(1)} %get-tuple-element.201.rest_2_, ...), custom_call_target="tpu_custom_call" | custom-call | tf_op jit(solution)/shard_map/share_down/pallas_call | solution.py:1315
  255.0 3.3 %collective-permute-done.67.rest_5_ = bf16[64,1024]{1,0:T(8,128)(2,1)S(1)} collective-permute-done((bf16[64,1024]{1,0:T(8,128)(2,1)S(1)}, bf16[64,1024]{1,0:T(8,128)(2,1)S(1)}, u32[]{:S(2)}, u32[]{:S(2)}) %collective-permute-start.67) | collective-permute-done | bytes 131104 | tf_op jit(solution)/shard_map/ppermute | solution.py:63
  261.2 2.5 finish.1
  (200 shorter events, 59.8 us)
Async XLA Ops:
  7.2 157.2 %all-gather.2.cloned.1.call-start = ((), (), s32[]{:S(2)}) async-start(), calls=%async_computation | async-start | bytes 17301504 | tf_op jit(solution)/shard_map/all_gather | solution.py:1021
  8.5 6.5 %collective-permute-start = (bf16[2,64,1024]{2,1,0:T(8,128)(2,1)S(1)}, bf16[2,64,1024]{2,1,0:T(8,128)(2,1)S(1)}, u32[]{:S(2)}, u32[]{:S(2)}) collective-permute-start(bf16[2,64,1024]{2,1,0:T(8,128)(2,1)S(1)} %slice_bitcast_fusion), channel_id=1, source_target_pairs={{0,4},{4,8},{8,12},{12,16},{16,20},{20,24},{24,28},{1,5},{5,9},{9,... | collective-permute-start | bytes 786440 | tf_op jit(solution)/shard_map/ppermute | solution.py:995
  18.2 3.6 %collective-permute-start.1 = (bf16[64,1024]{1,0:T(8,128)(2,1)S(1)}, bf16[64,1024]{1,0:T(8,128)(2,1)S(1)}, u32[]{:S(2)}, u32[]{:S(2)}) collective-permute-start(bf16[64,1024]{1,0:T(8,128)(2,1)S(1)} %get-tuple-element.249), channel_id=1, source_target_pairs={{0,4},{4,0},{8,12},{12,8},{16,20},{20,16},{24,28},{28,24},{1,5},{5... | collective-permute-start | bytes 393224 | tf_op jit(solution)/shard_map/ppermute | solution.py:63
  21.8 9.2 %collective-permute-start.2 = (bf16[128,1024]{1,0:T(8,128)(2,1)S(1)}, bf16[128,1024]{1,0:T(8,128)(2,1)S(1)}, u32[]{:S(2)}, u32[]{:S(2)}) collective-permute-start(bf16[128,1024]{1,0:T(8,128)(2,1)S(1)} %pad_maximum_fusion.rest_0_), channel_id=1, source_target_pairs={{0,8},{4,12},{8,0},{12,4},{16,24},{20,28},{24,16},{28,20},{1,9},{5... | collective-permute-start | bytes 786440 | tf_op jit(solution)/shard_map/ppermute | solution.py:67
  23.8 12.7 %collective-permute-start.3 = (bf16[128,1024]{1,0:T(8,128)(2,1)S(1)}, bf16[128,1024]{1,0:T(8,128)(2,1)S(1)}, u32[]{:S(2)}, u32[]{:S(2)}) collective-permute-start(bf16[128,1024]{1,0:T(8,128)(2,1)S(1)} %pad_maximum_fusion.rest_0_), channel_id=1, source_target_pairs={{0,16},{4,20},{8,24},{12,28},{16,0},{20,4},{24,8},{28,12},{1,17},{... | collective-permute-start | bytes 786440 | tf_op jit(solution)/shard_map/ppermute | solution.py:67
  25.3 12.8 %collective-permute-start.4 = (bf16[128,1024]{1,0:T(8,128)(2,1)S(1)}, bf16[128,1024]{1,0:T(8,128)(2,1)S(1)}, u32[]{:S(2)}, u32[]{:S(2)}) collective-permute-start(bf16[128,1024]{1,0:T(8,128)(2,1)S(1)} %pad_maximum_fusion.rest_0_), channel_id=1, source_target_pairs={{0,24},{4,28},{8,16},{12,20},{16,8},{20,12},{24,0},{28,4},{1,25},{... | collective-permute-start | bytes 786440 | tf_op jit(solution)/shard_map/ppermute | solution.py:67
  40.6 213.0 %all-reduce.5.cloned.1.call-start = ((), (), s32[]{:S(2)}) async-start(), calls=%async_computation.1 | async-start | bytes 2097152 | tf_op jit(solution)/shard_map/psum | solution.py:1224
  40.7 1.4 collective-permute-start.9
  42.1 16.5 %collective-permute-start.10 = (bf16[128,1024]{1,0:T(8,128)(2,1)S(1)}, bf16[128,1024]{1,0:T(8,128)(2,1)S(1)}, u32[]{:S(2)}, u32[]{:S(2)}) collective-permute-start(bf16[128,1024]{1,0:T(8,128)(2,1)S(1)} %constant_dynamic-update-slice_fusion.refs_7_), channel_id=1, source_target_pairs={{0,8},{4,12},{8,0},{12,4},{16,24},{20,28},{24,16},{28,20},{1,9},{5... | collective-permute-start | bytes 786440 | tf_op jit(solution)/shard_map/ppermute | solution.py:72
  42.8 15.8 %collective-permute-start.11 = (bf16[128,1024]{1,0:T(8,128)(2,1)S(1)}, bf16[128,1024]{1,0:T(8,128)(2,1)S(1)}, u32[]{:S(2)}, u32[]{:S(2)}) collective-permute-start(bf16[128,1024]{1,0:T(8,128)(2,1)S(1)} %constant_dynamic-update-slice_fusion.refs_7_), channel_id=1, source_target_pairs={{0,16},{4,20},{8,24},{12,28},{16,0},{20,4},{24,8},{28,12},{1,17},{... | collective-permute-start | bytes 786440 | tf_op jit(solution)/shard_map/ppermute | solution.py:72
  45.7 4.5 %collective-permute-start.6 = (f32[4,1024]{1,0:T(4,128)S(1)}, f32[4,1024]{1,0:T(4,128)S(1)}, u32[]{:S(2)}, u32[]{:S(2)}) collective-permute-start(f32[4,1024]{1,0:T(4,128)S(1)} %pad_maximum_fusion.3.refs_1_), channel_id=1, source_target_pairs={{0,1},{1,0},{2,3},{3,2},{4,5},{5,4},{6,7},{7,6},{8,9},{9,8},{10,11... | collective-permute-start | bytes 49160 | tf_op jit(solution)/shard_map/ppermute | solution.py:76
  47.3 4.7 %collective-permute-start.7 = (f32[4,1024]{1,0:T(4,128)S(1)}, f32[4,1024]{1,0:T(4,128)S(1)}, u32[]{:S(2)}, u32[]{:S(2)}) collective-permute-start(f32[4,1024]{1,0:T(4,128)S(1)} %pad_maximum_fusion.3.refs_1_), channel_id=1, source_target_pairs={{0,2},{1,3},{2,0},{3,1},{4,6},{5,7},{6,4},{7,5},{8,10},{9,11},{10,... | collective-permute-start | bytes 49160 | tf_op jit(solution)/shard_map/ppermute | solution.py:76
  49.9 5.7 %collective-permute-start.8 = (f32[4,1024]{1,0:T(4,128)S(1)}, f32[4,1024]{1,0:T(4,128)S(1)}, u32[]{:S(2)}, u32[]{:S(2)}) collective-permute-start(f32[4,1024]{1,0:T(4,128)S(1)} %pad_maximum_fusion.3.refs_1_), channel_id=1, source_target_pairs={{0,3},{1,2},{2,1},{3,0},{4,7},{5,6},{6,5},{7,4},{8,11},{9,10},{10,... | collective-permute-start | bytes 49160 | tf_op jit(solution)/shard_map/ppermute | solution.py:76
  59.9 4.5 %collective-permute-start.13 = (f32[4,512]{1,0:T(4,128)S(1)}, f32[4,512]{1,0:T(4,128)S(1)}, u32[]{:S(2)}, u32[]{:S(2)}) collective-permute-start(f32[4,512]{1,0:T(4,128)S(1)} %pad_maximum_fusion.7.refs_1_), channel_id=1, source_target_pairs={{0,1},{1,0},{2,3},{3,2},{4,5},{5,4},{6,7},{7,6},{8,9},{9,8},{10,11... | collective-permute-start | bytes 24584 | tf_op jit(solution)/shard_map/ppermute | solution.py:76
  59.9 4.8 %collective-permute-start.14 = (f32[4,512]{1,0:T(4,128)S(1)}, f32[4,512]{1,0:T(4,128)S(1)}, u32[]{:S(2)}, u32[]{:S(2)}) collective-permute-start(f32[4,512]{1,0:T(4,128)S(1)} %pad_maximum_fusion.7.refs_1_), channel_id=1, source_target_pairs={{0,2},{1,3},{2,0},{3,1},{4,6},{5,7},{6,4},{7,5},{8,10},{9,11},{10,... | collective-permute-start | bytes 24584 | tf_op jit(solution)/shard_map/ppermute | solution.py:76
  61.1 5.5 %collective-permute-start.15 = (f32[4,512]{1,0:T(4,128)S(1)}, f32[4,512]{1,0:T(4,128)S(1)}, u32[]{:S(2)}, u32[]{:S(2)}) collective-permute-start(f32[4,512]{1,0:T(4,128)S(1)} %pad_maximum_fusion.7.refs_1_), channel_id=1, source_target_pairs={{0,3},{1,2},{2,1},{3,0},{4,7},{5,6},{6,5},{7,4},{8,11},{9,10},{10,... | collective-permute-start | bytes 24584 | tf_op jit(solution)/shard_map/ppermute | solution.py:76
  68.5 15.7 %collective-permute-start.20 = (bf16[128,1024]{1,0:T(8,128)(2,1)S(1)}, bf16[128,1024]{1,0:T(8,128)(2,1)S(1)}, u32[]{:S(2)}, u32[]{:S(2)}) collective-permute-start(bf16[128,1024]{1,0:T(8,128)(2,1)S(1)} %collective-permute-done.10.refs_8_), channel_id=1, source_target_pairs={{0,16},{4,20},{8,24},{12,28},{16,0},{20,4},{24,8},{28,12},{1,17},{... | collective-permute-start | bytes 786440 | tf_op jit(solution)/shard_map/ppermute | solution.py:72
  69.6 6.6 %collective-permute-start.17 = (f32[4,512]{1,0:T(4,128)S(1)}, f32[4,512]{1,0:T(4,128)S(1)}, u32[]{:S(2)}, u32[]{:S(2)}) collective-permute-start(f32[4,512]{1,0:T(4,128)S(1)} %pad_maximum_fusion.8.refs_1_), channel_id=1, source_target_pairs={{0,1},{1,0},{2,3},{3,2},{4,5},{5,4},{6,7},{7,6},{8,9},{9,8},{10,11... | collective-permute-start | bytes 24584 | tf_op jit(solution)/shard_map/ppermute | solution.py:76
  69.7 6.6 %collective-permute-start.18 = (f32[4,512]{1,0:T(4,128)S(1)}, f32[4,512]{1,0:T(4,128)S(1)}, u32[]{:S(2)}, u32[]{:S(2)}) collective-permute-start(f32[4,512]{1,0:T(4,128)S(1)} %pad_maximum_fusion.8.refs_1_), channel_id=1, source_target_pairs={{0,2},{1,3},{2,0},{3,1},{4,6},{5,7},{6,4},{7,5},{8,10},{9,11},{10,... | collective-permute-start | bytes 24584 | tf_op jit(solution)/shard_map/ppermute | solution.py:76
  73.4 5.6 %collective-permute-start.19 = (f32[4,512]{1,0:T(4,128)S(1)}, f32[4,512]{1,0:T(4,128)S(1)}, u32[]{:S(2)}, u32[]{:S(2)}) collective-permute-start(f32[4,512]{1,0:T(4,128)S(1)} %pad_maximum_fusion.8.refs_1_), channel_id=1, source_target_pairs={{0,3},{1,2},{2,1},{3,0},{4,7},{5,6},{6,5},{7,4},{8,11},{9,10},{10,... | collective-permute-start | bytes 24584 | tf_op jit(solution)/shard_map/ppermute | solution.py:76
  84.2 1.2 collective-permute-start.21
  85.5 5.9 %collective-permute-start.24 = (f32[4,1024]{1,0:T(4,128)S(1)}, f32[4,1024]{1,0:T(4,128)S(1)}, u32[]{:S(2)}, u32[]{:S(2)}) collective-permute-start(f32[4,1024]{1,0:T(4,128)S(1)} %pad_maximum_fusion.1), channel_id=1, source_target_pairs={{0,3},{1,2},{2,1},{3,0},{4,7},{5,6},{6,5},{7,4},{8,11},{9,10},{10,... | collective-permute-start | bytes 49160 | tf_op jit(solution)/shard_map/ppermute | solution.py:76
  86.3 5.1 %collective-permute-start.23 = (f32[4,1024]{1,0:T(4,128)S(1)}, f32[4,1024]{1,0:T(4,128)S(1)}, u32[]{:S(2)}, u32[]{:S(2)}) collective-permute-start(f32[4,1024]{1,0:T(4,128)S(1)} %pad_maximum_fusion.1), channel_id=1, source_target_pairs={{0,2},{1,3},{2,0},{3,1},{4,6},{5,7},{6,4},{7,5},{8,10},{9,11},{10,... | collective-permute-start | bytes 49160 | tf_op jit(solution)/shard_map/ppermute | solution.py:76
  86.3 6.4 %collective-permute-start.22 = (f32[4,1024]{1,0:T(4,128)S(1)}, f32[4,1024]{1,0:T(4,128)S(1)}, u32[]{:S(2)}, u32[]{:S(2)}) collective-permute-start(f32[4,1024]{1,0:T(4,128)S(1)} %pad_maximum_fusion.1), channel_id=1, source_target_pairs={{0,1},{1,0},{2,3},{3,2},{4,5},{5,4},{6,7},{7,6},{8,9},{9,8},{10,11... | collective-permute-start | bytes 49160 | tf_op jit(solution)/shard_map/ppermute | solution.py:76
  95.6 6.4 %collective-permute-start.26 = (f32[4,512]{1,0:T(4,128)S(1)}, f32[4,512]{1,0:T(4,128)S(1)}, u32[]{:S(2)}, u32[]{:S(2)}) collective-permute-start(f32[4,512]{1,0:T(4,128)S(1)} %pad_maximum_fusion.9.refs_1_), channel_id=1, source_target_pairs={{0,1},{1,0},{2,3},{3,2},{4,5},{5,4},{6,7},{7,6},{8,9},{9,8},{10,11... | collective-permute-start | bytes 24584 | tf_op jit(solution)/shard_map/ppermute | solution.py:76
  97.0 5.0 %collective-permute-start.27 = (f32[4,512]{1,0:T(4,128)S(1)}, f32[4,512]{1,0:T(4,128)S(1)}, u32[]{:S(2)}, u32[]{:S(2)}) collective-permute-start(f32[4,512]{1,0:T(4,128)S(1)} %pad_maximum_fusion.9.refs_1_), channel_id=1, source_target_pairs={{0,2},{1,3},{2,0},{3,1},{4,6},{5,7},{6,4},{7,5},{8,10},{9,11},{10,... | collective-permute-start | bytes 24584 | tf_op jit(solution)/shard_map/ppermute | solution.py:76
  98.4 5.4 %collective-permute-start.28 = (f32[4,512]{1,0:T(4,128)S(1)}, f32[4,512]{1,0:T(4,128)S(1)}, u32[]{:S(2)}, u32[]{:S(2)}) collective-permute-start(f32[4,512]{1,0:T(4,128)S(1)} %pad_maximum_fusion.9.refs_1_), channel_id=1, source_target_pairs={{0,3},{1,2},{2,1},{3,0},{4,7},{5,6},{6,5},{7,4},{8,11},{9,10},{10,... | collective-permute-start | bytes 24584 | tf_op jit(solution)/shard_map/ppermute | solution.py:76
  106.4 1.2 collective-permute-start.29
  107.6 5.0 %collective-permute-start.30 = (f32[4,1024]{1,0:T(4,128)S(1)}, f32[4,1024]{1,0:T(4,128)S(1)}, u32[]{:S(2)}, u32[]{:S(2)}) collective-permute-start(f32[4,1024]{1,0:T(4,128)S(1)} %pad_maximum_fusion.4.refs_1_), channel_id=1, source_target_pairs={{0,1},{1,0},{2,3},{3,2},{4,5},{5,4},{6,7},{7,6},{8,9},{9,8},{10,11... | collective-permute-start | bytes 49160 | tf_op jit(solution)/shard_map/ppermute | solution.py:76
  107.7 7.3 %collective-permute-start.31 = (f32[4,1024]{1,0:T(4,128)S(1)}, f32[4,1024]{1,0:T(4,128)S(1)}, u32[]{:S(2)}, u32[]{:S(2)}) collective-permute-start(f32[4,1024]{1,0:T(4,128)S(1)} %pad_maximum_fusion.4.refs_1_), channel_id=1, source_target_pairs={{0,2},{1,3},{2,0},{3,1},{4,6},{5,7},{6,4},{7,5},{8,10},{9,11},{10,... | collective-permute-start | bytes 49160 | tf_op jit(solution)/shard_map/ppermute | solution.py:76
  109.7 5.9 %collective-permute-start.32 = (f32[4,1024]{1,0:T(4,128)S(1)}, f32[4,1024]{1,0:T(4,128)S(1)}, u32[]{:S(2)}, u32[]{:S(2)}) collective-permute-start(f32[4,1024]{1,0:T(4,128)S(1)} %pad_maximum_fusion.4.refs_1_), channel_id=1, source_target_pairs={{0,3},{1,2},{2,1},{3,0},{4,7},{5,6},{6,5},{7,4},{8,11},{9,10},{10,... | collective-permute-start | bytes 49160 | tf_op jit(solution)/shard_map/ppermute | solution.py:76
  120.1 4.9 %collective-permute-start.34 = (f32[4,1024]{1,0:T(4,128)S(1)}, f32[4,1024]{1,0:T(4,128)S(1)}, u32[]{:S(2)}, u32[]{:S(2)}) collective-permute-start(f32[4,1024]{1,0:T(4,128)S(1)} %pad_maximum_fusion.5.refs_1_), channel_id=1, source_target_pairs={{0,1},{1,0},{2,3},{3,2},{4,5},{5,4},{6,7},{7,6},{8,9},{9,8},{10,11... | collective-permute-start | bytes 49160 | tf_op jit(solution)/shard_map/ppermute | solution.py:76
  120.9 6.3 %collective-permute-start.35 = (f32[4,1024]{1,0:T(4,128)S(1)}, f32[4,1024]{1,0:T(4,128)S(1)}, u32[]{:S(2)}, u32[]{:S(2)}) collective-permute-start(f32[4,1024]{1,0:T(4,128)S(1)} %pad_maximum_fusion.5.refs_1_), channel_id=1, source_target_pairs={{0,2},{1,3},{2,0},{3,1},{4,6},{5,7},{6,4},{7,5},{8,10},{9,11},{10,... | collective-permute-start | bytes 49160 | tf_op jit(solution)/shard_map/ppermute | solution.py:76
  123.1 5.9 %collective-permute-start.36 = (f32[4,1024]{1,0:T(4,128)S(1)}, f32[4,1024]{1,0:T(4,128)S(1)}, u32[]{:S(2)}, u32[]{:S(2)}) collective-permute-start(f32[4,1024]{1,0:T(4,128)S(1)} %pad_maximum_fusion.5.refs_1_), channel_id=1, source_target_pairs={{0,3},{1,2},{2,1},{3,0},{4,7},{5,6},{6,5},{7,4},{8,11},{9,10},{10,... | collective-permute-start | bytes 49160 | tf_op jit(solution)/shard_map/ppermute | solution.py:76
  133.2 7.4 %collective-permute-start.38 = (f32[4,512]{1,0:T(4,128)S(1)}, f32[4,512]{1,0:T(4,128)S(1)}, u32[]{:S(2)}, u32[]{:S(2)}) collective-permute-start(f32[4,512]{1,0:T(4,128)S(1)} %pad_maximum_fusion.10.refs_1_), channel_id=1, source_target_pairs={{0,1},{1,0},{2,3},{3,2},{4,5},{5,4},{6,7},{7,6},{8,9},{9,8},{10,11... | collective-permute-start | bytes 24584 | tf_op jit(solution)/shard_map/ppermute | solution.py:76
  133.3 7.3 %collective-permute-start.39 = (f32[4,512]{1,0:T(4,128)S(1)}, f32[4,512]{1,0:T(4,128)S(1)}, u32[]{:S(2)}, u32[]{:S(2)}) collective-permute-start(f32[4,512]{1,0:T(4,128)S(1)} %pad_maximum_fusion.10.refs_1_), channel_id=1, source_target_pairs={{0,2},{1,3},{2,0},{3,1},{4,6},{5,7},{6,4},{7,5},{8,10},{9,11},{10,... | collective-permute-start | bytes 24584 | tf_op jit(solution)/shard_map/ppermute | solution.py:76
  135.2 5.5 %collective-permute-start.40 = (f32[4,512]{1,0:T(4,128)S(1)}, f32[4,512]{1,0:T(4,128)S(1)}, u32[]{:S(2)}, u32[]{:S(2)}) collective-permute-start(f32[4,512]{1,0:T(4,128)S(1)} %pad_maximum_fusion.10.refs_1_), channel_id=1, source_target_pairs={{0,3},{1,2},{2,1},{3,0},{4,7},{5,6},{6,5},{7,4},{8,11},{9,10},{10,... | collective-permute-start | bytes 24584 | tf_op jit(solution)/shard_map/ppermute | solution.py:76
  143.8 18.4 %collective-permute-start.46 = (bf16[1024,128]{1,0:T(8,128)(2,1)S(1)}, bf16[1024,128]{1,0:T(8,128)(2,1)S(1)}, u32[]{:S(2)}, u32[]{:S(2)}) collective-permute-start(bf16[1024,128]{1,0:T(8,128)(2,1)S(1)} %get-tuple-element.171), channel_id=1, source_target_pairs={{0,4},{4,0},{8,12},{12,8},{16,20},{20,16},{24,28},{28,24},{1,5},{5... | collective-permute-start | bytes 786440 | tf_op jit(solution)/shard_map/ppermute | solution.py:63
  144.5 6.0 %collective-permute-start.44 = (f32[4,1024]{1,0:T(4,128)S(1)}, f32[4,1024]{1,0:T(4,128)S(1)}, u32[]{:S(2)}, u32[]{:S(2)}) collective-permute-start(f32[4,1024]{1,0:T(4,128)S(1)} %pad_maximum_fusion.2), channel_id=1, source_target_pairs={{0,3},{1,2},{2,1},{3,0},{4,7},{5,6},{6,5},{7,4},{8,11},{9,10},{10,... | collective-permute-start | bytes 49160 | tf_op jit(solution)/shard_map/ppermute | solution.py:76
  147.1 5.0 %collective-permute-start.43 = (f32[4,1024]{1,0:T(4,128)S(1)}, f32[4,1024]{1,0:T(4,128)S(1)}, u32[]{:S(2)}, u32[]{:S(2)}) collective-permute-start(f32[4,1024]{1,0:T(4,128)S(1)} %pad_maximum_fusion.2), channel_id=1, source_target_pairs={{0,2},{1,3},{2,0},{3,1},{4,6},{5,7},{6,4},{7,5},{8,10},{9,11},{10,... | collective-permute-start | bytes 49160 | tf_op jit(solution)/shard_map/ppermute | solution.py:76
  147.1 5.5 %collective-permute-start.42 = (f32[4,1024]{1,0:T(4,128)S(1)}, f32[4,1024]{1,0:T(4,128)S(1)}, u32[]{:S(2)}, u32[]{:S(2)}) collective-permute-start(f32[4,1024]{1,0:T(4,128)S(1)} %pad_maximum_fusion.2), channel_id=1, source_target_pairs={{0,1},{1,0},{2,3},{3,2},{4,5},{5,4},{6,7},{7,6},{8,9},{9,8},{10,11... | collective-permute-start | bytes 49160 | tf_op jit(solution)/shard_map/ppermute | solution.py:76
  153.9 7.5 %collective-permute-start.47 = (bf16[64,1536]{1,0:T(8,128)(2,1)S(1)}, bf16[64,1536]{1,0:T(8,128)(2,1)S(1)}, u32[]{:S(2)}, u32[]{:S(2)}) collective-permute-start(bf16[64,1536]{1,0:T(8,128)(2,1)S(1)} %get-tuple-element.177), channel_id=1, source_target_pairs={{0,4},{4,0},{8,12},{12,8},{16,20},{20,16},{24,28},{28,24},{1,5},{5... | collective-permute-start | bytes 589832 | tf_op jit(solution)/shard_map/ppermute | solution.py:63
  159.9 1.5 collective-permute-start.45
  161.3 2.1 collective-permute-start.48
  164.4 4.5 %collective-permute-start.49 = (f32[4,512]{1,0:T(4,128)S(1)}, f32[4,512]{1,0:T(4,128)S(1)}, u32[]{:S(2)}, u32[]{:S(2)}) collective-permute-start(f32[4,512]{1,0:T(4,128)S(1)} %pad_maximum_fusion.11.refs_1_), channel_id=1, source_target_pairs={{0,1},{1,0},{2,3},{3,2},{4,5},{5,4},{6,7},{7,6},{8,9},{9,8},{10,11... | collective-permute-start | bytes 24584 | tf_op jit(solution)/shard_map/ppermute | solution.py:76
  165.1 4.5 %collective-permute-start.50 = (f32[4,512]{1,0:T(4,128)S(1)}, f32[4,512]{1,0:T(4,128)S(1)}, u32[]{:S(2)}, u32[]{:S(2)}) collective-permute-start(f32[4,512]{1,0:T(4,128)S(1)} %pad_maximum_fusion.11.refs_1_), channel_id=1, source_target_pairs={{0,2},{1,3},{2,0},{3,1},{4,6},{5,7},{6,4},{7,5},{8,10},{9,11},{10,... | collective-permute-start | bytes 24584 | tf_op jit(solution)/shard_map/ppermute | solution.py:76
  167.1 5.6 %collective-permute-start.51 = (f32[4,512]{1,0:T(4,128)S(1)}, f32[4,512]{1,0:T(4,128)S(1)}, u32[]{:S(2)}, u32[]{:S(2)}) collective-permute-start(f32[4,512]{1,0:T(4,128)S(1)} %pad_maximum_fusion.11.refs_1_), channel_id=1, source_target_pairs={{0,3},{1,2},{2,1},{3,0},{4,7},{5,6},{6,5},{7,4},{8,11},{9,10},{10,... | collective-permute-start | bytes 24584 | tf_op jit(solution)/shard_map/ppermute | solution.py:76
  178.8 4.5 %collective-permute-start.53 = (f32[4,512]{1,0:T(4,128)S(1)}, f32[4,512]{1,0:T(4,128)S(1)}, u32[]{:S(2)}, u32[]{:S(2)}) collective-permute-start(f32[4,512]{1,0:T(4,128)S(1)} %pad_maximum_fusion.12.refs_1_), channel_id=1, source_target_pairs={{0,1},{1,0},{2,3},{3,2},{4,5},{5,4},{6,7},{7,6},{8,9},{9,8},{10,11... | collective-permute-start | bytes 24584 | tf_op jit(solution)/shard_map/ppermute | solution.py:76
  178.9 4.9 %collective-permute-start.54 = (f32[4,512]{1,0:T(4,128)S(1)}, f32[4,512]{1,0:T(4,128)S(1)}, u32[]{:S(2)}, u32[]{:S(2)}) collective-permute-start(f32[4,512]{1,0:T(4,128)S(1)} %pad_maximum_fusion.12.refs_1_), channel_id=1, source_target_pairs={{0,2},{1,3},{2,0},{3,1},{4,6},{5,7},{6,4},{7,5},{8,10},{9,11},{10,... | collective-permute-start | bytes 24584 | tf_op jit(solution)/shard_map/ppermute | solution.py:76
  181.3 5.8 %collective-permute-start.55 = (f32[4,512]{1,0:T(4,128)S(1)}, f32[4,512]{1,0:T(4,128)S(1)}, u32[]{:S(2)}, u32[]{:S(2)}) collective-permute-start(f32[4,512]{1,0:T(4,128)S(1)} %pad_maximum_fusion.12.refs_1_), channel_id=1, source_target_pairs={{0,3},{1,2},{2,1},{3,0},{4,7},{5,6},{6,5},{7,4},{8,11},{9,10},{10,... | collective-permute-start | bytes 24584 | tf_op jit(solution)/shard_map/ppermute | solution.py:76
  194.2 14.6 %collective-permute-start.63 = (bf16[64,1536]{1,0:T(8,128)(2,1)S(1)}, bf16[64,1536]{1,0:T(8,128)(2,1)S(1)}, u32[]{:S(2)}, u32[]{:S(2)}) collective-permute-start(bf16[64,1536]{1,0:T(8,128)(2,1)S(1)} %get-tuple-element.210), channel_id=1, source_target_pairs={{0,4},{4,0},{8,12},{12,8},{16,20},{20,16},{24,28},{28,24},{1,5},{5... | collective-permute-start | bytes 589832 | tf_op jit(solution)/shard_map/ppermute | solution.py:63
  194.3 1.4 collective-permute-start.56
  195.7 4.6 %collective-permute-start.57 = (f32[4,1024]{1,0:T(4,128)S(1)}, f32[4,1024]{1,0:T(4,128)S(1)}, u32[]{:S(2)}, u32[]{:S(2)}) collective-permute-start(f32[4,1024]{1,0:T(4,128)S(1)} %pad_maximum_fusion.6.rest_0_), channel_id=1, source_target_pairs={{0,1},{1,0},{2,3},{3,2},{4,5},{5,4},{6,7},{7,6},{8,9},{9,8},{10,11... | collective-permute-start | bytes 49160 | tf_op jit(solution)/shard_map/ppermute | solution.py:76
  195.8 5.7 %collective-permute-start.58 = (f32[4,1024]{1,0:T(4,128)S(1)}, f32[4,1024]{1,0:T(4,128)S(1)}, u32[]{:S(2)}, u32[]{:S(2)}) collective-permute-start(f32[4,1024]{1,0:T(4,128)S(1)} %pad_maximum_fusion.6.rest_0_), channel_id=1, source_target_pairs={{0,2},{1,3},{2,0},{3,1},{4,6},{5,7},{6,4},{7,5},{8,10},{9,11},{10,... | collective-permute-start | bytes 49160 | tf_op jit(solution)/shard_map/ppermute | solution.py:76
  198.3 5.9 %collective-permute-start.59 = (f32[4,1024]{1,0:T(4,128)S(1)}, f32[4,1024]{1,0:T(4,128)S(1)}, u32[]{:S(2)}, u32[]{:S(2)}) collective-permute-start(f32[4,1024]{1,0:T(4,128)S(1)} %pad_maximum_fusion.6.rest_0_), channel_id=1, source_target_pairs={{0,3},{1,2},{2,1},{3,0},{4,7},{5,6},{6,5},{7,4},{8,11},{9,10},{10,... | collective-permute-start | bytes 49160 | tf_op jit(solution)/shard_map/ppermute | solution.py:76
  204.3 23.2 %collective-permute-start.62 = (bf16[512,256]{1,0:T(8,128)(2,1)S(1)}, bf16[512,256]{1,0:T(8,128)(2,1)S(1)}, u32[]{:S(2)}, u32[]{:S(2)}) collective-permute-start(bf16[512,256]{1,0:T(8,128)(2,1)S(1)} %cut_down.1.rest_0_), channel_id=1, source_target_pairs={{0,1},{1,0},{2,3},{3,2},{4,5},{5,4},{6,7},{7,6},{8,9},{9,8},{10,11... | collective-permute-start | bytes 786440 | tf_op jit(solution)/shard_map/ppermute | solution.py:76
  204.4 42.6 %collective-permute-start.60 = (bf16[512,256]{1,0:T(8,128)(2,1)S(1)}, bf16[512,256]{1,0:T(8,128)(2,1)S(1)}, u32[]{:S(2)}, u32[]{:S(2)}) collective-permute-start(bf16[512,256]{1,0:T(8,128)(2,1)S(1)} %cut_down.1.rest_0_), channel_id=1, source_target_pairs={{0,2},{1,3},{2,0},{3,1},{4,6},{5,7},{6,4},{7,5},{8,10},{9,11},{10,... | collective-permute-start | bytes 786440 | tf_op jit(solution)/shard_map/ppermute | solution.py:76
  206.9 40.1 %collective-permute-start.61 = (bf16[512,256]{1,0:T(8,128)(2,1)S(1)}, bf16[512,256]{1,0:T(8,128)(2,1)S(1)}, u32[]{:S(2)}, u32[]{:S(2)}) collective-permute-start(bf16[512,256]{1,0:T(8,128)(2,1)S(1)} %cut_down.1.rest_0_), channel_id=1, source_target_pairs={{0,3},{1,2},{2,1},{3,0},{4,7},{5,6},{6,5},{7,4},{8,11},{9,10},{10,... | collective-permute-start | bytes 786440 | tf_op jit(solution)/shard_map/ppermute | solution.py:76
  208.8 43.4 %collective-permute-start.64 = (bf16[64,1536]{1,0:T(8,128)(2,1)S(1)}, bf16[64,1536]{1,0:T(8,128)(2,1)S(1)}, u32[]{:S(2)}, u32[]{:S(2)}) collective-permute-start(bf16[64,1536]{1,0:T(8,128)(2,1)S(1)} %add_convert_fusion.2.rest_0_), channel_id=1, source_target_pairs={{0,1},{1,0},{2,3},{3,2},{4,5},{5,4},{6,7},{7,6},{8,9},{9,8},{10,11... | collective-permute-start | bytes 589832 | tf_op jit(solution)/shard_map/ppermute | solution.py:76
  208.9 44.8 %collective-permute-start.65 = (bf16[64,1536]{1,0:T(8,128)(2,1)S(1)}, bf16[64,1536]{1,0:T(8,128)(2,1)S(1)}, u32[]{:S(2)}, u32[]{:S(2)}) collective-permute-start(bf16[64,1536]{1,0:T(8,128)(2,1)S(1)} %add_convert_fusion.2.rest_0_), channel_id=1, source_target_pairs={{0,2},{1,3},{2,0},{3,1},{4,6},{5,7},{6,4},{7,5},{8,10},{9,11},{10,... | collective-permute-start | bytes 589832 | tf_op jit(solution)/shard_map/ppermute | solution.py:76
  227.5 26.1 %collective-permute-start.66 = (bf16[64,1536]{1,0:T(8,128)(2,1)S(1)}, bf16[64,1536]{1,0:T(8,128)(2,1)S(1)}, u32[]{:S(2)}, u32[]{:S(2)}) collective-permute-start(bf16[64,1536]{1,0:T(8,128)(2,1)S(1)} %add_convert_fusion.2.rest_0_), channel_id=1, source_target_pairs={{0,3},{1,2},{2,1},{3,0},{4,7},{5,6},{6,5},{7,4},{8,11},{9,10},{10,... | collective-permute-start | bytes 589832 | tf_op jit(solution)/shard_map/ppermute | solution.py:76
  253.7 10.1 %collective-permute-start.69 = (bf16[4608,128]{1,0:T(8,128)(2,1)}, bf16[4608,128]{1,0:T(8,128)(2,1)S(1)}, u32[]{:S(2)}, u32[]{:S(2)}) collective-permute-start(bf16[4608,128]{1,0:T(8,128)(2,1)} %copy-done.13), channel_id=1, source_target_pairs={{0,4},{4,0},{8,12},{12,8},{16,20},{20,16},{24,28},{28,24},{1,5},{5... | collective-permute-start | bytes 3538952 | tf_op jit(solution)/shard_map/ppermute | solution.py:63
  253.8 4.5 %collective-permute-start.68 = (f32[2,2,128,512]{3,2,1,0:T(8,128)S(1)}, f32[2,2,128,512]{3,2,1,0:T(8,128)S(1)}, u32[]{:S(2)}, u32[]{:S(2)}) collective-permute-start(f32[2,2,128,512]{3,2,1,0:T(8,128)S(1)} %back_input.1.rest_6_), channel_id=1, source_target_pairs={{0,4},{4,0},{8,12},{12,8},{16,20},{20,16},{24,28},{28,24},{1,5},{5... | collective-permute-start | bytes 3145736 | tf_op jit(solution)/shard_map/ppermute | solution.py:63
  254.3 4.0 %collective-permute-start.67 = (bf16[64,1024]{1,0:T(8,128)(2,1)S(1)}, bf16[64,1024]{1,0:T(8,128)(2,1)S(1)}, u32[]{:S(2)}, u32[]{:S(2)}) collective-permute-start(bf16[64,1024]{1,0:T(8,128)(2,1)S(1)} %copy-done.15), channel_id=1, source_target_pairs={{0,4},{4,0},{8,12},{12,8},{16,20},{20,16},{24,28},{28,24},{1,5},{5... | collective-permute-start | bytes 393224 | tf_op jit(solution)/shard_map/ppermute | solution.py:63
  (33 other events, 429.1 us)
Sparse Core Ops, SparseCore 0:
  40.8 118.6 all-gather.1
  164.5 64.9 all-reduce.4

commit v6 on v5

--- a/solution.py
+++ b/solution.py
@@ -707,7 +707,10 @@
 
 def finish_kernel(planes, unite, pack, taps, *rest):
     mains, (mine, got, near, far) = rest[:planes], rest[planes : planes + 4]
-    w_unite, w_short, w_trans, w_inner, w_spatial, w_main, output, grad_inputs, semaphores = rest[planes + 4 :]
+    rest = rest[planes + 4 :]
+    w_unite, w_short, w_trans, w_inner, w_spatial, w_main, output, grad_inputs = rest[:8]
+    *held, semaphores = rest[8:]
+    sums = [Far(a, b, semaphores.at[4 + k]) for k, (a, b) in enumerate(zip((unite, pack, taps), held))]
     core = own_core()
     copies = [
         pltpu.make_async_copy(mine, output.at[core, 0], semaphores.at[0]),
@@ -717,6 +720,7 @@
     ]
     for copy in copies:
         copy.start()
+    unite, pack, taps = (one.ready() for one in sums)
     w_unite[...] = unite[...].astype(F32)
     for outs, values in (
         ((w_short, w_trans), pack[...].astype(F32)),
@@ -1342,12 +1346,13 @@
             functools.partial(finish_kernel, groups),
             name="finish",
             out_shape=tuple(outs),
-            in_specs=[VMEM] * (3 + groups) + [ANY] * 4,
+            in_specs=[ANY] * 3 + [VMEM] * groups + [ANY] * 4,
             out_specs=(VMEM,) * 6 + (ANY,) * 2,
-            scratch_shapes=[pltpu.SemaphoreType.DMA((4,))],
+            scratch_shapes=[pltpu.VMEM(one.shape, one.dtype) for one in shares]
+            + [pltpu.SemaphoreType.DMA((7,))],
             compiler_params=pltpu.CompilerParams(vmem_limit_bytes=24 << 20),
             cost_estimate=LIGHT,
-        )(*shares, *mains, *placed)
+        )(*map(in_hbm, shares), *mains, *placed)
         output, grad_inputs = early[6:]
         early = [
             early[1].T, early[5].T, early[3].T, jnp.swapaxes(early[4], 1, 2), early[2].T, early[0],

time: 275 us -> 273 us (level)
  local copies, waits for them, and re-layouts: 8.05 us -> 5.11 us
    unnamed x53 -> x47, local copies, waits for them, and re-layouts: 5.87 us -> 2.93 us
  transfers between devices with their start and end apart: 72 -> 72, of which waited for: 45 -> 45; matrix products, arithmetic and copies ran while one was open for 1% -> 1% of each run, Pallas kernels for 26% -> 27%
where the time goes in v6:
time: 273 us; the launch traced here: 270 us
  waiting for transfers between devices  85.1 us (31%)
  starting transfers between devices  83.4 us (31%)
  Pallas kernels  77.2 us (28%)
  between operations  15 us (5%)
  local copies, waits for them, and re-layouts  5.11 us (2%)
  other arithmetic  4.35 us (2%)
    ppermute x42, starting transfers between devices, plane_hops(): lax.ppermute(value, 'batch', [(i, i ^ step) for i in range(self.groups)])  68.3 us
    ppermute x42, waiting for transfers between devices, plane_hops(): lax.ppermute(value, 'batch', [(i, i ^ step) for i in range(self.groups)])  55.9 us
    pallas_call x23, Pallas kernels, call(): pl.pallas_call(body if far else kernel, name=name, out_shape=tuple(outs),...  50.4 us
    ppermute x21, waiting for transfers between devices, swap(): return lax.ppermute(value, 'rows', [(i, i ^ 1) for i in range(self.rows)])  17.4 us
    ppermute x3, waiting for transfers between devices, chip_hops(): lax.ppermute(value, 'rows', [(i, i ^ 2 * step) for i in range(self.rows)])  11.8 us
    pallas_call x2, Pallas kernels, share_down(): pl.pallas_call(functools.partial(share_down_kernel, steps, chips, width,...  9.79 us
    pallas_call x2, Pallas kernels, run(): pl.pallas_call(kernel, name=name, out_shape=(pltpu.VMEM if pin else shape...  7.15 us
    pallas_call x1, Pallas kernels, on_device(): pl.pallas_call(functools.partial(back_input_kernel, width), name='back_in...  6.38 us
  transfers between devices with their start and end apart: 72, of which 45 were waited for; matrix products, arithmetic and copies ran while one was open for 1% of the time, Pallas kernels for 27%

profile of v6, /device:TPU:0, one launch (start us, length us, event | category | flops | bytes accessed | tf_op | source)
XLA Modules:
  0.0 270.2 jit_solution(9259241258577536823)
XLA Ops:
  8.5 2.4 collective-permute-start
  10.9 4.1 %own.1.part = f32[128,1024]{1,0:T(8,128)S(1)} custom-call(bf16[2,2,64,1024]{3,2,1,0:T(8,128)(2,1)S(1)} %reshape.60.x, bf16[3,1536,1024]{2,1,0:T(8,128)(2,1)} %bitcast.25), custom_call_target="tpu_custom_call" | custom-call | flops 805306368 | bytes 6291456 | tf_op jit(solution)/shard_map/own/pallas_call | solution.py:945
  15.0 3.1 %above.1 = bf16[2,64,1024]{2,1,0:T(8,128)(2,1)S(1)} custom-call(bf16[2,64,1024]{2,1,0:T(8,128)(2,1)S(1)} %collective-permute-done.above, f32[128,1024]{1,0:T(8,128)S(1)} %own.1.part, bf16[3,1536,1024]{2,1,0:T(8,128)(2,1)} %bitcast.26), custom_call_target="tpu_custom_call" | custom-call | flops 402653184 | bytes 3145728 | tf_op jit(solution)/shard_map/above/pallas_call | solution.py:945
  18.2 2.7 collective-permute-start.1
  21.8 2.0 collective-permute-start.2
  26.3 4.7 %collective-permute-done.2.rest_1_ = bf16[128,1024]{1,0:T(8,128)(2,1)S(1)} collective-permute-done((bf16[128,1024]{1,0:T(8,128)(2,1)S(1)}, bf16[128,1024]{1,0:T(8,128)(2,1)S(1)}, u32[]{:S(2)}, u32[]{:S(2)}) %collective-permute-start.2) | collective-permute-done | bytes 262176 | tf_op jit(solution)/shard_map/ppermute | solution.py:67
  31.0 5.5 %collective-permute-done.3.rest_2_ = bf16[128,1024]{1,0:T(8,128)(2,1)S(1)} collective-permute-done((bf16[128,1024]{1,0:T(8,128)(2,1)S(1)}, bf16[128,1024]{1,0:T(8,128)(2,1)S(1)}, u32[]{:S(2)}, u32[]{:S(2)}) %collective-permute-start.3) | collective-permute-done | bytes 262176 | tf_op jit(solution)/shard_map/ppermute | solution.py:67
  38.1 1.7 whole.1
  42.8 1.7 collective-permute-start.11
  45.7 1.6 collective-permute-start.6
  47.3 2.6 collective-permute-start.7
  50.1 1.9 collective-permute-done.7.refs_3_
  52.1 3.6 %collective-permute-done.8.refs_4_ = f32[4,1024]{1,0:T(4,128)S(1)} collective-permute-done((f32[4,1024]{1,0:T(4,128)S(1)}, f32[4,1024]{1,0:T(4,128)S(1)}, u32[]{:S(2)}, u32[]{:S(2)}) %collective-permute-start.8) | collective-permute-done | bytes 16416 | tf_op jit(solution)/shard_map/ppermute | solution.py:76
  55.6 2.9 %main.1 = (bf16[512,1024]{1,0:T(8,128)(2,1)S(1)}, f32[512,512]{1,0:T(8,128)S(1)}, f32[512,512]{1,0:T(8,128)}, f32[2,512]{1,0:T(2,128)S(1)}, f32[2,1024]{1,0:T(2,128)S(1)}) custom-call(f32[18,1024]{1,0:T(8,128)S(1)} %get-tuple-element.129.refs_0_.scal, f32[4,1024]{1,0:T(4,128)S(1)} %pad_maximum_fusion.3.refs_1_, ...), custom_call_target="tpu_custom_call" | custom-call | flops 536870912 | bytes 5451776 | tf_op jit(solution)/shard_map/main/pallas_call | solution.py:920
  61.1 3.2 %collective-permute-start.15 = (f32[4,512]{1,0:T(4,128)S(1)}, f32[4,512]{1,0:T(4,128)S(1)}, u32[]{:S(2)}, u32[]{:S(2)}) collective-permute-start(f32[4,512]{1,0:T(4,128)S(1)} %pad_maximum_fusion.7.refs_1_), channel_id=1, source_target_pairs={{0,3},{1,2},{2,1},{3,0},{4,7},{5,6},{6,5},{7,4},{8,11},{9,10},{10,... | collective-permute-start | bytes 24584 | tf_op jit(solution)/shard_map/ppermute | solution.py:76
  64.8 1.9 collective-permute-done.15.refs_4_
  66.7 1.7 inner.1
  69.7 3.7 %collective-permute-start.18 = (f32[4,512]{1,0:T(4,128)S(1)}, f32[4,512]{1,0:T(4,128)S(1)}, u32[]{:S(2)}, u32[]{:S(2)}) collective-permute-start(f32[4,512]{1,0:T(4,128)S(1)} %pad_maximum_fusion.8.refs_1_), channel_id=1, source_target_pairs={{0,2},{1,3},{2,0},{3,1},{4,6},{5,7},{6,4},{7,5},{8,10},{9,11},{10,... | collective-permute-start | bytes 24584 | tf_op jit(solution)/shard_map/ppermute | solution.py:76
  74.1 2.2 short.1
  76.3 2.7 %collective-permute-done.19.refs_4_ = f32[4,512]{1,0:T(4,128)S(1)} collective-permute-done((f32[4,512]{1,0:T(4,128)S(1)}, f32[4,512]{1,0:T(4,128)S(1)}, u32[]{:S(2)}, u32[]{:S(2)}) %collective-permute-start.19) | collective-permute-done | bytes 8224 | tf_op jit(solution)/shard_map/ppermute | solution.py:76
  79.0 5.2 %spatial.1 = (bf16[640,1536]{1,0:T(8,128)(2,1)S(1)}, f32[512,512]{1,0:T(8,128)S(1)}, f32[2,512]{1,0:T(2,128)S(1)}, f32[2,512]{1,0:T(2,128)S(1)}) custom-call(f32[18,1024]{1,0:T(8,128)S(1)} %get-tuple-element.129.refs_0_.scal, f32[4,512]{1,0:T(4,128)S(1)} %pad_maximum_fusion.8.refs_1_, f32[4,512]{1,0:T(4,128)S(1)} %collective-permute-done.17.refs_2_, ...), custom_call_target="tpu_custom_call" | custom-call | flops 2415919104 | bytes 8953856 | tf_op jit(solution)/shard_map/spatial/pallas_call | solution.py:920
  86.3 3.7 %collective-permute-start.22 = (f32[4,1024]{1,0:T(4,128)S(1)}, f32[4,1024]{1,0:T(4,128)S(1)}, u32[]{:S(2)}, u32[]{:S(2)}) collective-permute-start(f32[4,1024]{1,0:T(4,128)S(1)} %pad_maximum_fusion.1), channel_id=1, source_target_pairs={{0,1},{1,0},{2,3},{3,2},{4,5},{5,4},{6,7},{7,6},{8,9},{9,8},{10,11... | collective-permute-start | bytes 49160 | tf_op jit(solution)/shard_map/ppermute | solution.py:76
  92.7 1.7 trans.1
  98.4 1.7 collective-permute-start.28
  100.1 1.9 shortcut.1
  102.1 1.7 collective-permute-done.28.refs_4_
  103.8 2.5 unite.1
  107.7 2.0 collective-permute-start.31
  109.7 2.4 collective-permute-start.32
  112.6 2.4 collective-permute-done.31.refs_3_
  115.5 3.3 %turn.1 = (f32[512,1024]{1,0:T(8,128)S(1)}, bf16[64,1024]{1,0:T(8,128)(2,1)S(1)}, bf16[64,1024]{1,0:T(8,128)(2,1)S(1)}, f32[2,1024]{1,0:T(2,128)S(1)}, f32[2,1024]{1,0:T(2,128)S(1)}) custom-call(f32[18,1024]{1,0:T(8,128)S(1)} %get-tuple-element.129.refs_0_.scal, f32[4,1024]{1,0:T(4,128)S(1)} %pad_maximum_fusion.4.refs_1_, ...), custom_call_target="tpu_custom_call" | custom-call | flops 20971520 | bytes 5718016 | tf_op jit(solution)/shard_map/turn/pallas_call | solution.py:920
  120.9 2.3 collective-permute-start.35
  125.0 2.2 collective-permute-done.35.refs_3_
  127.2 1.8 collective-permute-done.36.refs_4_
  129.0 3.0 %back_trans.1 = (bf16[512,1024]{1,0:T(8,128)(2,1)S(1)}, f32[2,1024]{1,0:T(2,128)S(1)}, f32[512,512]{1,0:T(8,128)S(1)}, f32[2,512]{1,0:T(2,128)S(1)}) custom-call(f32[18,1024]{1,0:T(8,128)S(1)} %get-tuple-element.129.refs_0_.scal, f32[4,1024]{1,0:T(4,128)S(1)} %pad_maximum_fusion.5.refs_1_, f32[4,1024]{1,0:T(4,128)S(1)} %collective-permute-done.34.refs_2_, ...), custom_call_target="tpu_custom_call" | custom-call | flops 536870912 | bytes 9658368 | tf_op jit(solution)/shard_map/back_trans/pallas_call | solution.py:920
  133.3 1.9 collective-permute-start.39
  135.2 2.5 collective-permute-start.40
  137.7 2.9 %back_short.1 = (f32[512,512]{1,0:T(8,128)S(1)}, f32[2,512]{1,0:T(2,128)S(1)}) custom-call(bf16[512,1024]{1,0:T(8,128)(2,1)S(1)} %get-tuple-element.161.refs_0_.grad, f32[512,512]{1,0:T(8,128)S(1)} %get-tuple-element.149.refs_5_.refs_1_.rest_5_, f32[2,512]{1,0:T(2,128)S(1)} %get-tuple-element.162.refs_2_.rest_6_, ...), custom_call_target="tpu_custom_call" | custom-call | flops 536870912 | bytes 5308416 | tf_op jit(solution)/shard_map/back_short/pallas_call | solution.py:920
  140.7 2.5 back_spatial.1
  144.5 2.6 collective-permute-start.44
  147.1 1.8 collective-permute-start.42
  153.9 5.9 %back_inner.1 = (bf16[512,512]{1,0:T(8,128)(2,1)S(1)}, f32[2,512]{1,0:T(2,128)S(1)}, f32[512,512]{1,0:T(8,128)S(1)}, f32[2,512]{1,0:T(2,128)S(1)}) custom-call(f32[18,1024]{1,0:T(8,128)S(1)} %get-tuple-element.129.refs_0_.scal, f32[4,512]{1,0:T(4,128)S(1)} %get-tuple-element.257.refs_1_, f32[4,512]{1,0:T(4,128)S(1)} %get-tuple-element.255.refs_2_, ...), custom_call_target="tpu_custom_call" | custom-call | flops 2415919104 | bytes 9617408 | tf_op jit(solution)/shard_map/back_inner/pallas_call | solution.py:920
  165.1 2.0 collective-permute-start.50
  167.1 1.8 collective-permute-start.51
  169.6 3.0 %collective-permute-done.51.refs_4_ = f32[4,512]{1,0:T(4,128)S(1)} collective-permute-done((f32[4,512]{1,0:T(4,128)S(1)}, f32[4,512]{1,0:T(4,128)S(1)}, u32[]{:S(2)}, u32[]{:S(2)}) %collective-permute-start.51) | collective-permute-done | bytes 8224 | tf_op jit(solution)/shard_map/ppermute | solution.py:76
  175.1 2.5 back_main.1
  178.9 2.4 collective-permute-start.54
  181.3 2.0 collective-permute-start.55
  183.9 3.2 %collective-permute-done.55.refs_4_ = f32[4,512]{1,0:T(4,128)S(1)} collective-permute-done((f32[4,512]{1,0:T(4,128)S(1)}, f32[4,512]{1,0:T(4,128)S(1)}, u32[]{:S(2)}, u32[]{:S(2)}) %collective-permute-start.55) | collective-permute-done | bytes 8224 | tf_op jit(solution)/shard_map/ppermute | solution.py:76
  187.1 5.2 %back_down.1 = (bf16[512,512]{1,0:T(8,128)(2,1)S(1)}, f32[2,512]{1,0:T(2,128)S(1)}, f32[512,1024]{1,0:T(8,128)S(1)}, f32[2,1024]{1,0:T(2,128)S(1)}) custom-call(f32[18,1024]{1,0:T(8,128)S(1)} %get-tuple-element.129.refs_0_.scal, f32[4,512]{1,0:T(4,128)S(1)} %pad_maximum_fusion.12.refs_1_, f32[4,512]{1,0:T(4,128)S(1)} %collective-permute-done.53.refs_2_, ...), custom_call_target="tpu_custom_call" | custom-call | tf_op jit(solution)/shard_map/back_down/pallas_call | solution.py:920
  192.4 1.8 share_main.1
  195.8 2.5 collective-permute-start.58
  198.3 1.9 collective-permute-start.59
  201.5 2.6 collective-permute-done.59.rest_3_
  204.4 2.5 collective-permute-start.60
  206.9 1.9 collective-permute-start.61
  208.9 2.5 collective-permute-start.65
  211.4 16.2 %collective-permute-done.62.rest_1_ = bf16[512,256]{1,0:T(8,128)(2,1)S(1)} collective-permute-done((bf16[512,256]{1,0:T(8,128)(2,1)S(1)}, bf16[512,256]{1,0:T(8,128)(2,1)S(1)}, u32[]{:S(2)}, u32[]{:S(2)}) %collective-permute-start.62) | collective-permute-done | bytes 262176 | tf_op jit(solution)/shard_map/ppermute | solution.py:76
  227.6 7.9 %collective-permute-start.66 = (bf16[64,1536]{1,0:T(8,128)(2,1)S(1)}, bf16[64,1536]{1,0:T(8,128)(2,1)S(1)}, u32[]{:S(2)}, u32[]{:S(2)}) collective-permute-start(bf16[64,1536]{1,0:T(8,128)(2,1)S(1)} %add_convert_fusion.2.rest_0_), channel_id=1, source_target_pairs={{0,3},{1,2},{2,1},{3,0},{4,7},{5,6},{6,5},{7,4},{8,11},{9,10},{10,... | collective-permute-start | bytes 589832 | tf_op jit(solution)/shard_map/ppermute | solution.py:76
  236.0 6.4 %back_input.1.rest_6_ = f32[2,2,128,512]{3,2,1,0:T(8,128)S(1)} custom-call(bf16[576,1024]{1,0:T(8,128)(2,1)S(1)} %get-tuple-element.193.grad, bf16[9,512,1024]{2,1,0:T(8,128)(2,1)} %bitcast.27), custom_call_target="tpu_custom_call" | custom-call | tf_op jit(solution)/shard_map/back_input/pallas_call | solution.py:1278
  242.4 4.7 %share_down.2 = (f32[1024,1024]{1,0:T(8,128)S(1)}, f32[1024,1024]{1,0:T(8,128)S(1)}) custom-call(bf16[512,256]{1,0:T(8,128)(2,1)S(1)} %cut_down.1.rest_0_, bf16[512,256]{1,0:T(8,128)(2,1)S(1)} %collective-permute-done.62.rest_1_, bf16[32,2,2,64,1024]{4,3,2,1,0:T(8,128)(2,1)} %bitcast.28), custom_call_target="tpu_custom_call" | custom-call | tf_op jit(solution)/shard_map/share_down/pallas_call | solution.py:1319
  247.1 5.1 %share_down.3 = (bf16[4608,128]{1,0:T(8,128)(2,1)S(1)}, bf16[4608,128]{1,0:T(8,128)(2,1)S(1)}) custom-call(bf16[512,256]{1,0:T(8,128)(2,1)S(1)} %collective-permute-done.60.rest_0_, bf16[512,256]{1,0:T(8,128)(2,1)S(1)} %collective-permute-done.61.rest_1_, f32[1024,1024]{1,0:T(8,128)S(1)} %get-tuple-element.201.rest_2_, ...), custom_call_target="tpu_custom_call" | custom-call | tf_op jit(solution)/shard_map/share_down/pallas_call | solution.py:1319
  254.9 3.3 %collective-permute-done.67.rest_5_ = bf16[64,1024]{1,0:T(8,128)(2,1)S(1)} collective-permute-done((bf16[64,1024]{1,0:T(8,128)(2,1)S(1)}, bf16[64,1024]{1,0:T(8,128)(2,1)S(1)}, u32[]{:S(2)}, u32[]{:S(2)}) %collective-permute-start.67) | collective-permute-done | bytes 131104 | tf_op jit(solution)/shard_map/ppermute | solution.py:63
  258.3 3.4 %finish.1 = (f32[1024,128]{1,0:T(8,128)}, f32[64,1024]{1,0:T(8,128)}, f32[64,512]{1,0:T(8,128)}, f32[64,512]{1,0:T(8,128)}, f32[9,64,512]{2,1,0:T(8,128)}, /*ind...) custom-call(bf16[1024,128]{1,0:T(8,128)(2,1)} %get-tuple-element.212.unite, ...), custom_call_target="tpu_custom_call" | custom-call | tf_op jit(solution)/shard_map/finish/pallas_call | solution.py:1345
  (194 shorter events, 56.8 us)
Async XLA Ops:
  7.2 157.2 %all-gather.2.cloned.1.call-start = ((), (), s32[]{:S(2)}) async-start(), calls=%async_computation | async-start | bytes 17301504 | tf_op jit(solution)/shard_map/all_gather | solution.py:1025
  8.5 6.5 %collective-permute-start = (bf16[2,64,1024]{2,1,0:T(8,128)(2,1)S(1)}, bf16[2,64,1024]{2,1,0:T(8,128)(2,1)S(1)}, u32[]{:S(2)}, u32[]{:S(2)}) collective-permute-start(bf16[2,64,1024]{2,1,0:T(8,128)(2,1)S(1)} %slice_bitcast_fusion), channel_id=1, source_target_pairs={{0,4},{4,8},{8,12},{12,16},{16,20},{20,24},{24,28},{1,5},{5,9},{9,... | collective-permute-start | bytes 786440 | tf_op jit(solution)/shard_map/ppermute | solution.py:999
  18.2 3.6 %collective-permute-start.1 = (bf16[64,1024]{1,0:T(8,128)(2,1)S(1)}, bf16[64,1024]{1,0:T(8,128)(2,1)S(1)}, u32[]{:S(2)}, u32[]{:S(2)}) collective-permute-start(bf16[64,1024]{1,0:T(8,128)(2,1)S(1)} %get-tuple-element.249), channel_id=1, source_target_pairs={{0,4},{4,0},{8,12},{12,8},{16,20},{20,16},{24,28},{28,24},{1,5},{5... | collective-permute-start | bytes 393224 | tf_op jit(solution)/shard_map/ppermute | solution.py:63
  21.8 9.2 %collective-permute-start.2 = (bf16[128,1024]{1,0:T(8,128)(2,1)S(1)}, bf16[128,1024]{1,0:T(8,128)(2,1)S(1)}, u32[]{:S(2)}, u32[]{:S(2)}) collective-permute-start(bf16[128,1024]{1,0:T(8,128)(2,1)S(1)} %pad_maximum_fusion.rest_0_), channel_id=1, source_target_pairs={{0,8},{4,12},{8,0},{12,4},{16,24},{20,28},{24,16},{28,20},{1,9},{5... | collective-permute-start | bytes 786440 | tf_op jit(solution)/shard_map/ppermute | solution.py:67
  23.8 12.7 %collective-permute-start.3 = (bf16[128,1024]{1,0:T(8,128)(2,1)S(1)}, bf16[128,1024]{1,0:T(8,128)(2,1)S(1)}, u32[]{:S(2)}, u32[]{:S(2)}) collective-permute-start(bf16[128,1024]{1,0:T(8,128)(2,1)S(1)} %pad_maximum_fusion.rest_0_), channel_id=1, source_target_pairs={{0,16},{4,20},{8,24},{12,28},{16,0},{20,4},{24,8},{28,12},{1,17},{... | collective-permute-start | bytes 786440 | tf_op jit(solution)/shard_map/ppermute | solution.py:67
  25.3 12.8 %collective-permute-start.4 = (bf16[128,1024]{1,0:T(8,128)(2,1)S(1)}, bf16[128,1024]{1,0:T(8,128)(2,1)S(1)}, u32[]{:S(2)}, u32[]{:S(2)}) collective-permute-start(bf16[128,1024]{1,0:T(8,128)(2,1)S(1)} %pad_maximum_fusion.rest_0_), channel_id=1, source_target_pairs={{0,24},{4,28},{8,16},{12,20},{16,8},{20,12},{24,0},{28,4},{1,25},{... | collective-permute-start | bytes 786440 | tf_op jit(solution)/shard_map/ppermute | solution.py:67
  40.6 213.0 %all-reduce.5.cloned.1.call-start = ((), (), s32[]{:S(2)}) async-start(), calls=%async_computation.1 | async-start | bytes 2097152 | tf_op jit(solution)/shard_map/psum | solution.py:1228
  40.7 1.4 collective-permute-start.9
  42.1 16.5 %collective-permute-start.10 = (bf16[128,1024]{1,0:T(8,128)(2,1)S(1)}, bf16[128,1024]{1,0:T(8,128)(2,1)S(1)}, u32[]{:S(2)}, u32[]{:S(2)}) collective-permute-start(bf16[128,1024]{1,0:T(8,128)(2,1)S(1)} %constant_dynamic-update-slice_fusion.refs_7_), channel_id=1, source_target_pairs={{0,8},{4,12},{8,0},{12,4},{16,24},{20,28},{24,16},{28,20},{1,9},{5... | collective-permute-start | bytes 786440 | tf_op jit(solution)/shard_map/ppermute | solution.py:72
  42.8 15.8 %collective-permute-start.11 = (bf16[128,1024]{1,0:T(8,128)(2,1)S(1)}, bf16[128,1024]{1,0:T(8,128)(2,1)S(1)}, u32[]{:S(2)}, u32[]{:S(2)}) collective-permute-start(bf16[128,1024]{1,0:T(8,128)(2,1)S(1)} %constant_dynamic-update-slice_fusion.refs_7_), channel_id=1, source_target_pairs={{0,16},{4,20},{8,24},{12,28},{16,0},{20,4},{24,8},{28,12},{1,17},{... | collective-permute-start | bytes 786440 | tf_op jit(solution)/shard_map/ppermute | solution.py:72
  45.7 4.5 %collective-permute-start.6 = (f32[4,1024]{1,0:T(4,128)S(1)}, f32[4,1024]{1,0:T(4,128)S(1)}, u32[]{:S(2)}, u32[]{:S(2)}) collective-permute-start(f32[4,1024]{1,0:T(4,128)S(1)} %pad_maximum_fusion.3.refs_1_), channel_id=1, source_target_pairs={{0,1},{1,0},{2,3},{3,2},{4,5},{5,4},{6,7},{7,6},{8,9},{9,8},{10,11... | collective-permute-start | bytes 49160 | tf_op jit(solution)/shard_map/ppermute | solution.py:76
  47.3 4.7 %collective-permute-start.7 = (f32[4,1024]{1,0:T(4,128)S(1)}, f32[4,1024]{1,0:T(4,128)S(1)}, u32[]{:S(2)}, u32[]{:S(2)}) collective-permute-start(f32[4,1024]{1,0:T(4,128)S(1)} %pad_maximum_fusion.3.refs_1_), channel_id=1, source_target_pairs={{0,2},{1,3},{2,0},{3,1},{4,6},{5,7},{6,4},{7,5},{8,10},{9,11},{10,... | collective-permute-start | bytes 49160 | tf_op jit(solution)/shard_map/ppermute | solution.py:76
  49.9 5.7 %collective-permute-start.8 = (f32[4,1024]{1,0:T(4,128)S(1)}, f32[4,1024]{1,0:T(4,128)S(1)}, u32[]{:S(2)}, u32[]{:S(2)}) collective-permute-start(f32[4,1024]{1,0:T(4,128)S(1)} %pad_maximum_fusion.3.refs_1_), channel_id=1, source_target_pairs={{0,3},{1,2},{2,1},{3,0},{4,7},{5,6},{6,5},{7,4},{8,11},{9,10},{10,... | collective-permute-start | bytes 49160 | tf_op jit(solution)/shard_map/ppermute | solution.py:76
  59.9 4.5 %collective-permute-start.13 = (f32[4,512]{1,0:T(4,128)S(1)}, f32[4,512]{1,0:T(4,128)S(1)}, u32[]{:S(2)}, u32[]{:S(2)}) collective-permute-start(f32[4,512]{1,0:T(4,128)S(1)} %pad_maximum_fusion.7.refs_1_), channel_id=1, source_target_pairs={{0,1},{1,0},{2,3},{3,2},{4,5},{5,4},{6,7},{7,6},{8,9},{9,8},{10,11... | collective-permute-start | bytes 24584 | tf_op jit(solution)/shard_map/ppermute | solution.py:76
  59.9 4.8 %collective-permute-start.14 = (f32[4,512]{1,0:T(4,128)S(1)}, f32[4,512]{1,0:T(4,128)S(1)}, u32[]{:S(2)}, u32[]{:S(2)}) collective-permute-start(f32[4,512]{1,0:T(4,128)S(1)} %pad_maximum_fusion.7.refs_1_), channel_id=1, source_target_pairs={{0,2},{1,3},{2,0},{3,1},{4,6},{5,7},{6,4},{7,5},{8,10},{9,11},{10,... | collective-permute-start | bytes 24584 | tf_op jit(solution)/shard_map/ppermute | solution.py:76
  61.1 5.5 %collective-permute-start.15 = (f32[4,512]{1,0:T(4,128)S(1)}, f32[4,512]{1,0:T(4,128)S(1)}, u32[]{:S(2)}, u32[]{:S(2)}) collective-permute-start(f32[4,512]{1,0:T(4,128)S(1)} %pad_maximum_fusion.7.refs_1_), channel_id=1, source_target_pairs={{0,3},{1,2},{2,1},{3,0},{4,7},{5,6},{6,5},{7,4},{8,11},{9,10},{10,... | collective-permute-start | bytes 24584 | tf_op jit(solution)/shard_map/ppermute | solution.py:76
  68.5 15.7 %collective-permute-start.20 = (bf16[128,1024]{1,0:T(8,128)(2,1)S(1)}, bf16[128,1024]{1,0:T(8,128)(2,1)S(1)}, u32[]{:S(2)}, u32[]{:S(2)}) collective-permute-start(bf16[128,1024]{1,0:T(8,128)(2,1)S(1)} %collective-permute-done.10.refs_8_), channel_id=1, source_target_pairs={{0,16},{4,20},{8,24},{12,28},{16,0},{20,4},{24,8},{28,12},{1,17},{... | collective-permute-start | bytes 786440 | tf_op jit(solution)/shard_map/ppermute | solution.py:72
  69.6 6.6 %collective-permute-start.17 = (f32[4,512]{1,0:T(4,128)S(1)}, f32[4,512]{1,0:T(4,128)S(1)}, u32[]{:S(2)}, u32[]{:S(2)}) collective-permute-start(f32[4,512]{1,0:T(4,128)S(1)} %pad_maximum_fusion.8.refs_1_), channel_id=1, source_target_pairs={{0,1},{1,0},{2,3},{3,2},{4,5},{5,4},{6,7},{7,6},{8,9},{9,8},{10,11... | collective-permute-start | bytes 24584 | tf_op jit(solution)/shard_map/ppermute | solution.py:76
  69.7 6.6 %collective-permute-start.18 = (f32[4,512]{1,0:T(4,128)S(1)}, f32[4,512]{1,0:T(4,128)S(1)}, u32[]{:S(2)}, u32[]{:S(2)}) collective-permute-start(f32[4,512]{1,0:T(4,128)S(1)} %pad_maximum_fusion.8.refs_1_), channel_id=1, source_target_pairs={{0,2},{1,3},{2,0},{3,1},{4,6},{5,7},{6,4},{7,5},{8,10},{9,11},{10,... | collective-permute-start | bytes 24584 | tf_op jit(solution)/shard_map/ppermute | solution.py:76
  73.4 5.6 %collective-permute-start.19 = (f32[4,512]{1,0:T(4,128)S(1)}, f32[4,512]{1,0:T(4,128)S(1)}, u32[]{:S(2)}, u32[]{:S(2)}) collective-permute-start(f32[4,512]{1,0:T(4,128)S(1)} %pad_maximum_fusion.8.refs_1_), channel_id=1, source_target_pairs={{0,3},{1,2},{2,1},{3,0},{4,7},{5,6},{6,5},{7,4},{8,11},{9,10},{10,... | collective-permute-start | bytes 24584 | tf_op jit(solution)/shard_map/ppermute | solution.py:76
  84.2 1.2 collective-permute-start.21
  85.5 5.9 %collective-permute-start.24 = (f32[4,1024]{1,0:T(4,128)S(1)}, f32[4,1024]{1,0:T(4,128)S(1)}, u32[]{:S(2)}, u32[]{:S(2)}) collective-permute-start(f32[4,1024]{1,0:T(4,128)S(1)} %pad_maximum_fusion.1), channel_id=1, source_target_pairs={{0,3},{1,2},{2,1},{3,0},{4,7},{5,6},{6,5},{7,4},{8,11},{9,10},{10,... | collective-permute-start | bytes 49160 | tf_op jit(solution)/shard_map/ppermute | solution.py:76
  86.3 5.1 %collective-permute-start.23 = (f32[4,1024]{1,0:T(4,128)S(1)}, f32[4,1024]{1,0:T(4,128)S(1)}, u32[]{:S(2)}, u32[]{:S(2)}) collective-permute-start(f32[4,1024]{1,0:T(4,128)S(1)} %pad_maximum_fusion.1), channel_id=1, source_target_pairs={{0,2},{1,3},{2,0},{3,1},{4,6},{5,7},{6,4},{7,5},{8,10},{9,11},{10,... | collective-permute-start | bytes 49160 | tf_op jit(solution)/shard_map/ppermute | solution.py:76
  86.3 6.4 %collective-permute-start.22 = (f32[4,1024]{1,0:T(4,128)S(1)}, f32[4,1024]{1,0:T(4,128)S(1)}, u32[]{:S(2)}, u32[]{:S(2)}) collective-permute-start(f32[4,1024]{1,0:T(4,128)S(1)} %pad_maximum_fusion.1), channel_id=1, source_target_pairs={{0,1},{1,0},{2,3},{3,2},{4,5},{5,4},{6,7},{7,6},{8,9},{9,8},{10,11... | collective-permute-start | bytes 49160 | tf_op jit(solution)/shard_map/ppermute | solution.py:76
  95.6 6.4 %collective-permute-start.26 = (f32[4,512]{1,0:T(4,128)S(1)}, f32[4,512]{1,0:T(4,128)S(1)}, u32[]{:S(2)}, u32[]{:S(2)}) collective-permute-start(f32[4,512]{1,0:T(4,128)S(1)} %pad_maximum_fusion.9.refs_1_), channel_id=1, source_target_pairs={{0,1},{1,0},{2,3},{3,2},{4,5},{5,4},{6,7},{7,6},{8,9},{9,8},{10,11... | collective-permute-start | bytes 24584 | tf_op jit(solution)/shard_map/ppermute | solution.py:76
  97.0 5.0 %collective-permute-start.27 = (f32[4,512]{1,0:T(4,128)S(1)}, f32[4,512]{1,0:T(4,128)S(1)}, u32[]{:S(2)}, u32[]{:S(2)}) collective-permute-start(f32[4,512]{1,0:T(4,128)S(1)} %pad_maximum_fusion.9.refs_1_), channel_id=1, source_target_pairs={{0,2},{1,3},{2,0},{3,1},{4,6},{5,7},{6,4},{7,5},{8,10},{9,11},{10,... | collective-permute-start | bytes 24584 | tf_op jit(solution)/shard_map/ppermute | solution.py:76
  98.4 5.4 %collective-permute-start.28 = (f32[4,512]{1,0:T(4,128)S(1)}, f32[4,512]{1,0:T(4,128)S(1)}, u32[]{:S(2)}, u32[]{:S(2)}) collective-permute-start(f32[4,512]{1,0:T(4,128)S(1)} %pad_maximum_fusion.9.refs_1_), channel_id=1, source_target_pairs={{0,3},{1,2},{2,1},{3,0},{4,7},{5,6},{6,5},{7,4},{8,11},{9,10},{10,... | collective-permute-start | bytes 24584 | tf_op jit(solution)/shard_map/ppermute | solution.py:76
  106.4 1.2 collective-permute-start.29
  107.6 5.0 %collective-permute-start.30 = (f32[4,1024]{1,0:T(4,128)S(1)}, f32[4,1024]{1,0:T(4,128)S(1)}, u32[]{:S(2)}, u32[]{:S(2)}) collective-permute-start(f32[4,1024]{1,0:T(4,128)S(1)} %pad_maximum_fusion.4.refs_1_), channel_id=1, source_target_pairs={{0,1},{1,0},{2,3},{3,2},{4,5},{5,4},{6,7},{7,6},{8,9},{9,8},{10,11... | collective-permute-start | bytes 49160 | tf_op jit(solution)/shard_map/ppermute | solution.py:76
  107.7 7.3 %collective-permute-start.31 = (f32[4,1024]{1,0:T(4,128)S(1)}, f32[4,1024]{1,0:T(4,128)S(1)}, u32[]{:S(2)}, u32[]{:S(2)}) collective-permute-start(f32[4,1024]{1,0:T(4,128)S(1)} %pad_maximum_fusion.4.refs_1_), channel_id=1, source_target_pairs={{0,2},{1,3},{2,0},{3,1},{4,6},{5,7},{6,4},{7,5},{8,10},{9,11},{10,... | collective-permute-start | bytes 49160 | tf_op jit(solution)/shard_map/ppermute | solution.py:76
  109.7 5.9 %collective-permute-start.32 = (f32[4,1024]{1,0:T(4,128)S(1)}, f32[4,1024]{1,0:T(4,128)S(1)}, u32[]{:S(2)}, u32[]{:S(2)}) collective-permute-start(f32[4,1024]{1,0:T(4,128)S(1)} %pad_maximum_fusion.4.refs_1_), channel_id=1, source_target_pairs={{0,3},{1,2},{2,1},{3,0},{4,7},{5,6},{6,5},{7,4},{8,11},{9,10},{10,... | collective-permute-start | bytes 49160 | tf_op jit(solution)/shard_map/ppermute | solution.py:76
  120.1 4.9 %collective-permute-start.34 = (f32[4,1024]{1,0:T(4,128)S(1)}, f32[4,1024]{1,0:T(4,128)S(1)}, u32[]{:S(2)}, u32[]{:S(2)}) collective-permute-start(f32[4,1024]{1,0:T(4,128)S(1)} %pad_maximum_fusion.5.refs_1_), channel_id=1, source_target_pairs={{0,1},{1,0},{2,3},{3,2},{4,5},{5,4},{6,7},{7,6},{8,9},{9,8},{10,11... | collective-permute-start | bytes 49160 | tf_op jit(solution)/shard_map/ppermute | solution.py:76
  120.9 6.3 %collective-permute-start.35 = (f32[4,1024]{1,0:T(4,128)S(1)}, f32[4,1024]{1,0:T(4,128)S(1)}, u32[]{:S(2)}, u32[]{:S(2)}) collective-permute-start(f32[4,1024]{1,0:T(4,128)S(1)} %pad_maximum_fusion.5.refs_1_), channel_id=1, source_target_pairs={{0,2},{1,3},{2,0},{3,1},{4,6},{5,7},{6,4},{7,5},{8,10},{9,11},{10,... | collective-permute-start | bytes 49160 | tf_op jit(solution)/shard_map/ppermute | solution.py:76
  123.1 5.9 %collective-permute-start.36 = (f32[4,1024]{1,0:T(4,128)S(1)}, f32[4,1024]{1,0:T(4,128)S(1)}, u32[]{:S(2)}, u32[]{:S(2)}) collective-permute-start(f32[4,1024]{1,0:T(4,128)S(1)} %pad_maximum_fusion.5.refs_1_), channel_id=1, source_target_pairs={{0,3},{1,2},{2,1},{3,0},{4,7},{5,6},{6,5},{7,4},{8,11},{9,10},{10,... | collective-permute-start | bytes 49160 | tf_op jit(solution)/shard_map/ppermute | solution.py:76
  133.2 7.4 %collective-permute-start.38 = (f32[4,512]{1,0:T(4,128)S(1)}, f32[4,512]{1,0:T(4,128)S(1)}, u32[]{:S(2)}, u32[]{:S(2)}) collective-permute-start(f32[4,512]{1,0:T(4,128)S(1)} %pad_maximum_fusion.10.refs_1_), channel_id=1, source_target_pairs={{0,1},{1,0},{2,3},{3,2},{4,5},{5,4},{6,7},{7,6},{8,9},{9,8},{10,11... | collective-permute-start | bytes 24584 | tf_op jit(solution)/shard_map/ppermute | solution.py:76
  133.3 7.3 %collective-permute-start.39 = (f32[4,512]{1,0:T(4,128)S(1)}, f32[4,512]{1,0:T(4,128)S(1)}, u32[]{:S(2)}, u32[]{:S(2)}) collective-permute-start(f32[4,512]{1,0:T(4,128)S(1)} %pad_maximum_fusion.10.refs_1_), channel_id=1, source_target_pairs={{0,2},{1,3},{2,0},{3,1},{4,6},{5,7},{6,4},{7,5},{8,10},{9,11},{10,... | collective-permute-start | bytes 24584 | tf_op jit(solution)/shard_map/ppermute | solution.py:76
  135.2 5.5 %collective-permute-start.40 = (f32[4,512]{1,0:T(4,128)S(1)}, f32[4,512]{1,0:T(4,128)S(1)}, u32[]{:S(2)}, u32[]{:S(2)}) collective-permute-start(f32[4,512]{1,0:T(4,128)S(1)} %pad_maximum_fusion.10.refs_1_), channel_id=1, source_target_pairs={{0,3},{1,2},{2,1},{3,0},{4,7},{5,6},{6,5},{7,4},{8,11},{9,10},{10,... | collective-permute-start | bytes 24584 | tf_op jit(solution)/shard_map/ppermute | solution.py:76
  143.8 18.4 %collective-permute-start.46 = (bf16[1024,128]{1,0:T(8,128)(2,1)S(1)}, bf16[1024,128]{1,0:T(8,128)(2,1)S(1)}, u32[]{:S(2)}, u32[]{:S(2)}) collective-permute-start(bf16[1024,128]{1,0:T(8,128)(2,1)S(1)} %get-tuple-element.171), channel_id=1, source_target_pairs={{0,4},{4,0},{8,12},{12,8},{16,20},{20,16},{24,28},{28,24},{1,5},{5... | collective-permute-start | bytes 786440 | tf_op jit(solution)/shard_map/ppermute | solution.py:63
  144.5 6.0 %collective-permute-start.44 = (f32[4,1024]{1,0:T(4,128)S(1)}, f32[4,1024]{1,0:T(4,128)S(1)}, u32[]{:S(2)}, u32[]{:S(2)}) collective-permute-start(f32[4,1024]{1,0:T(4,128)S(1)} %pad_maximum_fusion.2), channel_id=1, source_target_pairs={{0,3},{1,2},{2,1},{3,0},{4,7},{5,6},{6,5},{7,4},{8,11},{9,10},{10,... | collective-permute-start | bytes 49160 | tf_op jit(solution)/shard_map/ppermute | solution.py:76
  147.1 5.0 %collective-permute-start.43 = (f32[4,1024]{1,0:T(4,128)S(1)}, f32[4,1024]{1,0:T(4,128)S(1)}, u32[]{:S(2)}, u32[]{:S(2)}) collective-permute-start(f32[4,1024]{1,0:T(4,128)S(1)} %pad_maximum_fusion.2), channel_id=1, source_target_pairs={{0,2},{1,3},{2,0},{3,1},{4,6},{5,7},{6,4},{7,5},{8,10},{9,11},{10,... | collective-permute-start | bytes 49160 | tf_op jit(solution)/shard_map/ppermute | solution.py:76
  147.1 5.5 %collective-permute-start.42 = (f32[4,1024]{1,0:T(4,128)S(1)}, f32[4,1024]{1,0:T(4,128)S(1)}, u32[]{:S(2)}, u32[]{:S(2)}) collective-permute-start(f32[4,1024]{1,0:T(4,128)S(1)} %pad_maximum_fusion.2), channel_id=1, source_target_pairs={{0,1},{1,0},{2,3},{3,2},{4,5},{5,4},{6,7},{7,6},{8,9},{9,8},{10,11... | collective-permute-start | bytes 49160 | tf_op jit(solution)/shard_map/ppermute | solution.py:76
  153.9 7.5 %collective-permute-start.47 = (bf16[64,1536]{1,0:T(8,128)(2,1)S(1)}, bf16[64,1536]{1,0:T(8,128)(2,1)S(1)}, u32[]{:S(2)}, u32[]{:S(2)}) collective-permute-start(bf16[64,1536]{1,0:T(8,128)(2,1)S(1)} %get-tuple-element.177), channel_id=1, source_target_pairs={{0,4},{4,0},{8,12},{12,8},{16,20},{20,16},{24,28},{28,24},{1,5},{5... | collective-permute-start | bytes 589832 | tf_op jit(solution)/shard_map/ppermute | solution.py:63
  159.9 1.5 collective-permute-start.45
  161.3 2.1 collective-permute-start.48
  164.4 4.5 %collective-permute-start.49 = (f32[4,512]{1,0:T(4,128)S(1)}, f32[4,512]{1,0:T(4,128)S(1)}, u32[]{:S(2)}, u32[]{:S(2)}) collective-permute-start(f32[4,512]{1,0:T(4,128)S(1)} %pad_maximum_fusion.11.refs_1_), channel_id=1, source_target_pairs={{0,1},{1,0},{2,3},{3,2},{4,5},{5,4},{6,7},{7,6},{8,9},{9,8},{10,11... | collective-permute-start | bytes 24584 | tf_op jit(solution)/shard_map/ppermute | solution.py:76
  165.1 4.5 %collective-permute-start.50 = (f32[4,512]{1,0:T(4,128)S(1)}, f32[4,512]{1,0:T(4,128)S(1)}, u32[]{:S(2)}, u32[]{:S(2)}) collective-permute-start(f32[4,512]{1,0:T(4,128)S(1)} %pad_maximum_fusion.11.refs_1_), channel_id=1, source_target_pairs={{0,2},{1,3},{2,0},{3,1},{4,6},{5,7},{6,4},{7,5},{8,10},{9,11},{10,... | collective-permute-start | bytes 24584 | tf_op jit(solution)/shard_map/ppermute | solution.py:76
  167.1 5.6 %collective-permute-start.51 = (f32[4,512]{1,0:T(4,128)S(1)}, f32[4,512]{1,0:T(4,128)S(1)}, u32[]{:S(2)}, u32[]{:S(2)}) collective-permute-start(f32[4,512]{1,0:T(4,128)S(1)} %pad_maximum_fusion.11.refs_1_), channel_id=1, source_target_pairs={{0,3},{1,2},{2,1},{3,0},{4,7},{5,6},{6,5},{7,4},{8,11},{9,10},{10,... | collective-permute-start | bytes 24584 | tf_op jit(solution)/shard_map/ppermute | solution.py:76
  178.8 4.5 %collective-permute-start.53 = (f32[4,512]{1,0:T(4,128)S(1)}, f32[4,512]{1,0:T(4,128)S(1)}, u32[]{:S(2)}, u32[]{:S(2)}) collective-permute-start(f32[4,512]{1,0:T(4,128)S(1)} %pad_maximum_fusion.12.refs_1_), channel_id=1, source_target_pairs={{0,1},{1,0},{2,3},{3,2},{4,5},{5,4},{6,7},{7,6},{8,9},{9,8},{10,11... | collective-permute-start | bytes 24584 | tf_op jit(solution)/shard_map/ppermute | solution.py:76
  178.9 5.0 %collective-permute-start.54 = (f32[4,512]{1,0:T(4,128)S(1)}, f32[4,512]{1,0:T(4,128)S(1)}, u32[]{:S(2)}, u32[]{:S(2)}) collective-permute-start(f32[4,512]{1,0:T(4,128)S(1)} %pad_maximum_fusion.12.refs_1_), channel_id=1, source_target_pairs={{0,2},{1,3},{2,0},{3,1},{4,6},{5,7},{6,4},{7,5},{8,10},{9,11},{10,... | collective-permute-start | bytes 24584 | tf_op jit(solution)/shard_map/ppermute | solution.py:76
  181.3 5.8 %collective-permute-start.55 = (f32[4,512]{1,0:T(4,128)S(1)}, f32[4,512]{1,0:T(4,128)S(1)}, u32[]{:S(2)}, u32[]{:S(2)}) collective-permute-start(f32[4,512]{1,0:T(4,128)S(1)} %pad_maximum_fusion.12.refs_1_), channel_id=1, source_target_pairs={{0,3},{1,2},{2,1},{3,0},{4,7},{5,6},{6,5},{7,4},{8,11},{9,10},{10,... | collective-permute-start | bytes 24584 | tf_op jit(solution)/shard_map/ppermute | solution.py:76
  194.2 14.6 %collective-permute-start.63 = (bf16[64,1536]{1,0:T(8,128)(2,1)S(1)}, bf16[64,1536]{1,0:T(8,128)(2,1)S(1)}, u32[]{:S(2)}, u32[]{:S(2)}) collective-permute-start(bf16[64,1536]{1,0:T(8,128)(2,1)S(1)} %get-tuple-element.210), channel_id=1, source_target_pairs={{0,4},{4,0},{8,12},{12,8},{16,20},{20,16},{24,28},{28,24},{1,5},{5... | collective-permute-start | bytes 589832 | tf_op jit(solution)/shard_map/ppermute | solution.py:63
  194.2 1.4 collective-permute-start.56
  195.7 4.6 %collective-permute-start.57 = (f32[4,1024]{1,0:T(4,128)S(1)}, f32[4,1024]{1,0:T(4,128)S(1)}, u32[]{:S(2)}, u32[]{:S(2)}) collective-permute-start(f32[4,1024]{1,0:T(4,128)S(1)} %pad_maximum_fusion.6.rest_0_), channel_id=1, source_target_pairs={{0,1},{1,0},{2,3},{3,2},{4,5},{5,4},{6,7},{7,6},{8,9},{9,8},{10,11... | collective-permute-start | bytes 49160 | tf_op jit(solution)/shard_map/ppermute | solution.py:76
  195.8 5.8 %collective-permute-start.58 = (f32[4,1024]{1,0:T(4,128)S(1)}, f32[4,1024]{1,0:T(4,128)S(1)}, u32[]{:S(2)}, u32[]{:S(2)}) collective-permute-start(f32[4,1024]{1,0:T(4,128)S(1)} %pad_maximum_fusion.6.rest_0_), channel_id=1, source_target_pairs={{0,2},{1,3},{2,0},{3,1},{4,6},{5,7},{6,4},{7,5},{8,10},{9,11},{10,... | collective-permute-start | bytes 49160 | tf_op jit(solution)/shard_map/ppermute | solution.py:76
  198.3 5.9 %collective-permute-start.59 = (f32[4,1024]{1,0:T(4,128)S(1)}, f32[4,1024]{1,0:T(4,128)S(1)}, u32[]{:S(2)}, u32[]{:S(2)}) collective-permute-start(f32[4,1024]{1,0:T(4,128)S(1)} %pad_maximum_fusion.6.rest_0_), channel_id=1, source_target_pairs={{0,3},{1,2},{2,1},{3,0},{4,7},{5,6},{6,5},{7,4},{8,11},{9,10},{10,... | collective-permute-start | bytes 49160 | tf_op jit(solution)/shard_map/ppermute | solution.py:76
  204.3 23.2 %collective-permute-start.62 = (bf16[512,256]{1,0:T(8,128)(2,1)S(1)}, bf16[512,256]{1,0:T(8,128)(2,1)S(1)}, u32[]{:S(2)}, u32[]{:S(2)}) collective-permute-start(bf16[512,256]{1,0:T(8,128)(2,1)S(1)} %cut_down.1.rest_0_), channel_id=1, source_target_pairs={{0,1},{1,0},{2,3},{3,2},{4,5},{5,4},{6,7},{7,6},{8,9},{9,8},{10,11... | collective-permute-start | bytes 786440 | tf_op jit(solution)/shard_map/ppermute | solution.py:76
  204.4 42.7 %collective-permute-start.60 = (bf16[512,256]{1,0:T(8,128)(2,1)S(1)}, bf16[512,256]{1,0:T(8,128)(2,1)S(1)}, u32[]{:S(2)}, u32[]{:S(2)}) collective-permute-start(bf16[512,256]{1,0:T(8,128)(2,1)S(1)} %cut_down.1.rest_0_), channel_id=1, source_target_pairs={{0,2},{1,3},{2,0},{3,1},{4,6},{5,7},{6,4},{7,5},{8,10},{9,11},{10,... | collective-permute-start | bytes 786440 | tf_op jit(solution)/shard_map/ppermute | solution.py:76
  206.9 40.2 %collective-permute-start.61 = (bf16[512,256]{1,0:T(8,128)(2,1)S(1)}, bf16[512,256]{1,0:T(8,128)(2,1)S(1)}, u32[]{:S(2)}, u32[]{:S(2)}) collective-permute-start(bf16[512,256]{1,0:T(8,128)(2,1)S(1)} %cut_down.1.rest_0_), channel_id=1, source_target_pairs={{0,3},{1,2},{2,1},{3,0},{4,7},{5,6},{6,5},{7,4},{8,11},{9,10},{10,... | collective-permute-start | bytes 786440 | tf_op jit(solution)/shard_map/ppermute | solution.py:76
  208.8 43.4 %collective-permute-start.64 = (bf16[64,1536]{1,0:T(8,128)(2,1)S(1)}, bf16[64,1536]{1,0:T(8,128)(2,1)S(1)}, u32[]{:S(2)}, u32[]{:S(2)}) collective-permute-start(bf16[64,1536]{1,0:T(8,128)(2,1)S(1)} %add_convert_fusion.2.rest_0_), channel_id=1, source_target_pairs={{0,1},{1,0},{2,3},{3,2},{4,5},{5,4},{6,7},{7,6},{8,9},{9,8},{10,11... | collective-permute-start | bytes 589832 | tf_op jit(solution)/shard_map/ppermute | solution.py:76
  208.9 44.7 %collective-permute-start.65 = (bf16[64,1536]{1,0:T(8,128)(2,1)S(1)}, bf16[64,1536]{1,0:T(8,128)(2,1)S(1)}, u32[]{:S(2)}, u32[]{:S(2)}) collective-permute-start(bf16[64,1536]{1,0:T(8,128)(2,1)S(1)} %add_convert_fusion.2.rest_0_), channel_id=1, source_target_pairs={{0,2},{1,3},{2,0},{3,1},{4,6},{5,7},{6,4},{7,5},{8,10},{9,11},{10,... | collective-permute-start | bytes 589832 | tf_op jit(solution)/shard_map/ppermute | solution.py:76
  227.6 26.1 %collective-permute-start.66 = (bf16[64,1536]{1,0:T(8,128)(2,1)S(1)}, bf16[64,1536]{1,0:T(8,128)(2,1)S(1)}, u32[]{:S(2)}, u32[]{:S(2)}) collective-permute-start(bf16[64,1536]{1,0:T(8,128)(2,1)S(1)} %add_convert_fusion.2.rest_0_), channel_id=1, source_target_pairs={{0,3},{1,2},{2,1},{3,0},{4,7},{5,6},{6,5},{7,4},{8,11},{9,10},{10,... | collective-permute-start | bytes 589832 | tf_op jit(solution)/shard_map/ppermute | solution.py:76
  253.7 8.0 %collective-permute-start.69 = (bf16[4608,128]{1,0:T(8,128)(2,1)}, bf16[4608,128]{1,0:T(8,128)(2,1)S(1)}, u32[]{:S(2)}, u32[]{:S(2)}) collective-permute-start(bf16[4608,128]{1,0:T(8,128)(2,1)} %copy-done.10), channel_id=1, source_target_pairs={{0,4},{4,0},{8,12},{12,8},{16,20},{20,16},{24,28},{28,24},{1,5},{5... | collective-permute-start | bytes 3538952 | tf_op jit(solution)/shard_map/ppermute | solution.py:63
  253.7 4.5 %collective-permute-start.68 = (f32[2,2,128,512]{3,2,1,0:T(8,128)S(1)}, f32[2,2,128,512]{3,2,1,0:T(8,128)S(1)}, u32[]{:S(2)}, u32[]{:S(2)}) collective-permute-start(f32[2,2,128,512]{3,2,1,0:T(8,128)S(1)} %back_input.1.rest_6_), channel_id=1, source_target_pairs={{0,4},{4,0},{8,12},{12,8},{16,20},{20,16},{24,28},{28,24},{1,5},{5... | collective-permute-start | bytes 3145736 | tf_op jit(solution)/shard_map/ppermute | solution.py:63
  254.2 4.0 %collective-permute-start.67 = (bf16[64,1024]{1,0:T(8,128)(2,1)S(1)}, bf16[64,1024]{1,0:T(8,128)(2,1)S(1)}, u32[]{:S(2)}, u32[]{:S(2)}) collective-permute-start(bf16[64,1024]{1,0:T(8,128)(2,1)S(1)} %copy-done.12), channel_id=1, source_target_pairs={{0,4},{4,0},{8,12},{12,8},{16,20},{20,16},{24,28},{28,24},{1,5},{5... | collective-permute-start | bytes 393224 | tf_op jit(solution)/shard_map/ppermute | solution.py:63
  (30 other events, 426.0 us)
Sparse Core Ops, SparseCore 0:
  40.8 118.6 all-gather.1
  164.5 64.8 all-reduce.4

commit v7 on v6

--- a/solution.py
+++ b/solution.py
@@ -469,8 +469,8 @@
             start = image_row(k, side) * width
 
             def body(index, sums, k=k, part=part, side=side, start=start, width=width):
-                src = pl.ds(pl.multiple_of(side * width + index * 16, 16), 16)
-                dst = pl.ds(pl.multiple_of(start + index * 16, 16), 16)
+                src = pl.ds(pl.multiple_of(side * width + index * (CHUNK // 2), CHUNK // 2), CHUNK // 2)
+                dst = pl.ds(pl.multiple_of(start + index * (CHUNK // 2), CHUNK // 2), CHUNK // 2)
                 unit = (pre[dst, :] - center) * rstd
                 value = unit * gain + offset
                 grown = jnp.exp(jnp.minimum(value, FAR))
@@ -478,14 +478,14 @@
                 share = 1.0 / (wide + 2.0)
                 level = wide * share
                 if k == 0:
-                    rows = pl.ds(pl.multiple_of(index * 16, 16), 16)
+                    rows = pl.ds(pl.multiple_of(index * (CHUNK // 2), CHUNK // 2), CHUNK // 2)
                     outputs[side][rows, :] = (value * level * weight).astype(BF)
                 slope = level + 4.0 * value * (grown * (grown + 1.0) * share) * share
                 out = part[src, :].astype(F32) * weight * slope
                 pushed[dst, :] = out
                 return sums[0] + fold(out), sums[1] + fold(out * unit)
 
-            sums = lax.fori_loop(0, width // 16, body, sums)
+            sums = lax.fori_loop(0, width // (CHUNK // 2), body, sums)
     pay[0:1, :] = jnp.sum(sums[0], axis=0, keepdims=True)
     pay[1:2, :] = jnp.sum(sums[1], axis=0, keepdims=True)
 

time: 273 us -> 272 us (level)
  transfers between devices with their start and end apart: 72 -> 72, of which waited for: 45 -> 44; matrix products, arithmetic and copies ran while one was open for 1% -> 1% of each run, Pallas kernels for 27% -> 27%
where the time goes in v7:
time: 272 us; the launch traced here: 270 us
  waiting for transfers between devices  84.5 us (31%)
  starting transfers between devices  84 us (31%)
  Pallas kernels  76.9 us (28%)
  between operations  15 us (6%)
  local copies, waits for them, and re-layouts  5.11 us (2%)
  other arithmetic  4.35 us (2%)
    ppermute x42, starting transfers between devices, plane_hops(): lax.ppermute(value, 'batch', [(i, i ^ step) for i in range(self.groups)])  68.4 us
    ppermute x42, waiting for transfers between devices, plane_hops(): lax.ppermute(value, 'batch', [(i, i ^ step) for i in range(self.groups)])  55.4 us
    pallas_call x23, Pallas kernels, call(): pl.pallas_call(body if far else kernel, name=name, out_shape=tuple(outs),...  50.2 us
    ppermute x21, waiting for transfers between devices, swap(): return lax.ppermute(value, 'rows', [(i, i ^ 1) for i in range(self.rows)])  17.3 us
    ppermute x3, waiting for transfers between devices, chip_hops(): lax.ppermute(value, 'rows', [(i, i ^ 2 * step) for i in range(self.rows)])  11.8 us
    pallas_call x2, Pallas kernels, share_down(): pl.pallas_call(functools.partial(share_down_kernel, steps, chips, width,...  9.79 us
    pallas_call x2, Pallas kernels, run(): pl.pallas_call(kernel, name=name, out_shape=(pltpu.VMEM if pin else shape...  7.15 us
    pallas_call x1, Pallas kernels, on_device(): pl.pallas_call(functools.partial(back_input_kernel, width), name='back_in...  6.39 us
  transfers between devices with their start and end apart: 72, of which 44 were waited for; matrix products, arithmetic and copies ran while one was open for 1% of the time, Pallas kernels for 27%

profile of v7, /device:TPU:0, one launch (start us, length us, event | category | flops | bytes accessed | tf_op | source)
XLA Modules:
  0.0 269.9 jit_solution(16418223061456271704)
XLA Ops:
  8.5 2.4 collective-permute-start
  10.9 4.1 %own.1.part = f32[128,1024]{1,0:T(8,128)S(1)} custom-call(bf16[2,2,64,1024]{3,2,1,0:T(8,128)(2,1)S(1)} %reshape.60.x, bf16[3,1536,1024]{2,1,0:T(8,128)(2,1)} %bitcast.25), custom_call_target="tpu_custom_call" | custom-call | flops 805306368 | bytes 6291456 | tf_op jit(solution)/shard_map/own/pallas_call | solution.py:945
  15.0 3.1 %above.1 = bf16[2,64,1024]{2,1,0:T(8,128)(2,1)S(1)} custom-call(bf16[2,64,1024]{2,1,0:T(8,128)(2,1)S(1)} %collective-permute-done.above, f32[128,1024]{1,0:T(8,128)S(1)} %own.1.part, bf16[3,1536,1024]{2,1,0:T(8,128)(2,1)} %bitcast.26), custom_call_target="tpu_custom_call" | custom-call | flops 402653184 | bytes 3145728 | tf_op jit(solution)/shard_map/above/pallas_call | solution.py:945
  18.2 2.7 collective-permute-start.1
  21.8 2.0 collective-permute-start.2
  26.3 4.7 %collective-permute-done.2.rest_1_ = bf16[128,1024]{1,0:T(8,128)(2,1)S(1)} collective-permute-done((bf16[128,1024]{1,0:T(8,128)(2,1)S(1)}, bf16[128,1024]{1,0:T(8,128)(2,1)S(1)}, u32[]{:S(2)}, u32[]{:S(2)}) %collective-permute-start.2) | collective-permute-done | bytes 262176 | tf_op jit(solution)/shard_map/ppermute | solution.py:67
  31.0 5.5 %collective-permute-done.3.rest_2_ = bf16[128,1024]{1,0:T(8,128)(2,1)S(1)} collective-permute-done((bf16[128,1024]{1,0:T(8,128)(2,1)S(1)}, bf16[128,1024]{1,0:T(8,128)(2,1)S(1)}, u32[]{:S(2)}, u32[]{:S(2)}) %collective-permute-start.3) | collective-permute-done | bytes 262176 | tf_op jit(solution)/shard_map/ppermute | solution.py:67
  38.1 1.7 whole.1
  43.0 1.7 collective-permute-start.11
  45.9 1.6 collective-permute-start.6
  47.5 2.6 collective-permute-start.7
  50.3 1.9 collective-permute-done.7.refs_3_
  52.2 3.4 %collective-permute-done.8.refs_4_ = f32[4,1024]{1,0:T(4,128)S(1)} collective-permute-done((f32[4,1024]{1,0:T(4,128)S(1)}, f32[4,1024]{1,0:T(4,128)S(1)}, u32[]{:S(2)}, u32[]{:S(2)}) %collective-permute-start.8) | collective-permute-done | bytes 16416 | tf_op jit(solution)/shard_map/ppermute | solution.py:76
  55.7 2.9 %main.1 = (bf16[512,1024]{1,0:T(8,128)(2,1)S(1)}, f32[512,512]{1,0:T(8,128)S(1)}, f32[512,512]{1,0:T(8,128)}, f32[2,512]{1,0:T(2,128)S(1)}, f32[2,1024]{1,0:T(2,128)S(1)}) custom-call(f32[18,1024]{1,0:T(8,128)S(1)} %get-tuple-element.129.refs_0_.scal, f32[4,1024]{1,0:T(4,128)S(1)} %pad_maximum_fusion.3.refs_1_, ...), custom_call_target="tpu_custom_call" | custom-call | flops 536870912 | bytes 5451776 | tf_op jit(solution)/shard_map/main/pallas_call | solution.py:920
  61.2 3.2 %collective-permute-start.15 = (f32[4,512]{1,0:T(4,128)S(1)}, f32[4,512]{1,0:T(4,128)S(1)}, u32[]{:S(2)}, u32[]{:S(2)}) collective-permute-start(f32[4,512]{1,0:T(4,128)S(1)} %pad_maximum_fusion.7.refs_1_), channel_id=1, source_target_pairs={{0,3},{1,2},{2,1},{3,0},{4,7},{5,6},{6,5},{7,4},{8,11},{9,10},{10,... | collective-permute-start | bytes 24584 | tf_op jit(solution)/shard_map/ppermute | solution.py:76
  64.7 2.0 collective-permute-done.15.refs_4_
  66.7 1.7 inner.1
  69.8 3.7 %collective-permute-start.18 = (f32[4,512]{1,0:T(4,128)S(1)}, f32[4,512]{1,0:T(4,128)S(1)}, u32[]{:S(2)}, u32[]{:S(2)}) collective-permute-start(f32[4,512]{1,0:T(4,128)S(1)} %pad_maximum_fusion.8.refs_1_), channel_id=1, source_target_pairs={{0,2},{1,3},{2,0},{3,1},{4,6},{5,7},{6,4},{7,5},{8,10},{9,11},{10,... | collective-permute-start | bytes 24584 | tf_op jit(solution)/shard_map/ppermute | solution.py:76
  74.1 2.2 short.1
  76.3 2.7 %collective-permute-done.19.refs_4_ = f32[4,512]{1,0:T(4,128)S(1)} collective-permute-done((f32[4,512]{1,0:T(4,128)S(1)}, f32[4,512]{1,0:T(4,128)S(1)}, u32[]{:S(2)}, u32[]{:S(2)}) %collective-permute-start.19) | collective-permute-done | bytes 8224 | tf_op jit(solution)/shard_map/ppermute | solution.py:76
  79.0 5.2 %spatial.1 = (bf16[640,1536]{1,0:T(8,128)(2,1)S(1)}, f32[512,512]{1,0:T(8,128)S(1)}, f32[2,512]{1,0:T(2,128)S(1)}, f32[2,512]{1,0:T(2,128)S(1)}) custom-call(f32[18,1024]{1,0:T(8,128)S(1)} %get-tuple-element.129.refs_0_.scal, f32[4,512]{1,0:T(4,128)S(1)} %pad_maximum_fusion.8.refs_1_, f32[4,512]{1,0:T(4,128)S(1)} %collective-permute-done.17.refs_2_, ...), custom_call_target="tpu_custom_call" | custom-call | flops 2415919104 | bytes 8953856 | tf_op jit(solution)/shard_map/spatial/pallas_call | solution.py:920
  86.3 3.7 %collective-permute-start.22 = (f32[4,1024]{1,0:T(4,128)S(1)}, f32[4,1024]{1,0:T(4,128)S(1)}, u32[]{:S(2)}, u32[]{:S(2)}) collective-permute-start(f32[4,1024]{1,0:T(4,128)S(1)} %pad_maximum_fusion.1), channel_id=1, source_target_pairs={{0,1},{1,0},{2,3},{3,2},{4,5},{5,4},{6,7},{7,6},{8,9},{9,8},{10,11... | collective-permute-start | bytes 49160 | tf_op jit(solution)/shard_map/ppermute | solution.py:76
  92.6 1.7 trans.1
  98.3 1.7 collective-permute-start.28
  100.0 1.9 shortcut.1
  102.0 1.7 collective-permute-done.28.refs_4_
  103.7 2.5 unite.1
  107.6 2.0 collective-permute-start.31
  109.6 2.4 collective-permute-start.32
  112.6 2.4 collective-permute-done.31.refs_3_
  115.5 3.1 %turn.1 = (f32[512,1024]{1,0:T(8,128)S(1)}, bf16[64,1024]{1,0:T(8,128)(2,1)S(1)}, bf16[64,1024]{1,0:T(8,128)(2,1)S(1)}, f32[2,1024]{1,0:T(2,128)S(1)}, f32[2,1024]{1,0:T(2,128)S(1)}) custom-call(f32[18,1024]{1,0:T(8,128)S(1)} %get-tuple-element.129.refs_0_.scal, f32[4,1024]{1,0:T(4,128)S(1)} %pad_maximum_fusion.4.refs_1_, ...), custom_call_target="tpu_custom_call" | custom-call | flops 20971520 | bytes 5718016 | tf_op jit(solution)/shard_map/turn/pallas_call | solution.py:920
  120.6 2.2 collective-permute-start.35
  125.0 2.4 collective-permute-done.35.refs_3_
  128.7 2.9 %back_trans.1 = (bf16[512,1024]{1,0:T(8,128)(2,1)S(1)}, f32[2,1024]{1,0:T(2,128)S(1)}, f32[512,512]{1,0:T(8,128)S(1)}, f32[2,512]{1,0:T(2,128)S(1)}) custom-call(f32[18,1024]{1,0:T(8,128)S(1)} %get-tuple-element.129.refs_0_.scal, f32[4,1024]{1,0:T(4,128)S(1)} %pad_maximum_fusion.5.refs_1_, f32[4,1024]{1,0:T(4,128)S(1)} %collective-permute-done.34.refs_2_, ...), custom_call_target="tpu_custom_call" | custom-call | flops 536870912 | bytes 9658368 | tf_op jit(solution)/shard_map/back_trans/pallas_call | solution.py:920
  133.0 2.0 collective-permute-start.39
  134.9 2.4 collective-permute-start.40
  137.3 3.0 %back_short.1 = (f32[512,512]{1,0:T(8,128)S(1)}, f32[2,512]{1,0:T(2,128)S(1)}) custom-call(bf16[512,1024]{1,0:T(8,128)(2,1)S(1)} %get-tuple-element.161.refs_0_.grad, f32[512,512]{1,0:T(8,128)S(1)} %get-tuple-element.149.refs_5_.refs_1_.rest_5_, f32[2,512]{1,0:T(2,128)S(1)} %get-tuple-element.162.refs_2_.rest_6_, ...), custom_call_target="tpu_custom_call" | custom-call | flops 536870912 | bytes 5308416 | tf_op jit(solution)/shard_map/back_short/pallas_call | solution.py:920
  140.5 2.7 back_spatial.1
  144.5 2.4 collective-permute-start.44
  146.9 2.0 collective-permute-start.42
  153.6 5.9 %back_inner.1 = (bf16[512,512]{1,0:T(8,128)(2,1)S(1)}, f32[2,512]{1,0:T(2,128)S(1)}, f32[512,512]{1,0:T(8,128)S(1)}, f32[2,512]{1,0:T(2,128)S(1)}) custom-call(f32[18,1024]{1,0:T(8,128)S(1)} %get-tuple-element.129.refs_0_.scal, f32[4,512]{1,0:T(4,128)S(1)} %get-tuple-element.257.refs_1_, f32[4,512]{1,0:T(4,128)S(1)} %get-tuple-element.255.refs_2_, ...), custom_call_target="tpu_custom_call" | custom-call | flops 2415919104 | bytes 9617408 | tf_op jit(solution)/shard_map/back_inner/pallas_call | solution.py:920
  164.9 2.1 collective-permute-start.50
  167.0 1.6 collective-permute-start.51
  169.5 3.1 %collective-permute-done.51.refs_4_ = f32[4,512]{1,0:T(4,128)S(1)} collective-permute-done((f32[4,512]{1,0:T(4,128)S(1)}, f32[4,512]{1,0:T(4,128)S(1)}, u32[]{:S(2)}, u32[]{:S(2)}) %collective-permute-start.51) | collective-permute-done | bytes 8224 | tf_op jit(solution)/shard_map/ppermute | solution.py:76
  175.0 2.5 back_main.1
  178.8 2.3 collective-permute-start.54
  181.0 2.1 collective-permute-start.55
  183.7 3.2 %collective-permute-done.55.refs_4_ = f32[4,512]{1,0:T(4,128)S(1)} collective-permute-done((f32[4,512]{1,0:T(4,128)S(1)}, f32[4,512]{1,0:T(4,128)S(1)}, u32[]{:S(2)}, u32[]{:S(2)}) %collective-permute-start.55) | collective-permute-done | bytes 8224 | tf_op jit(solution)/shard_map/ppermute | solution.py:76
  186.9 5.2 %back_down.1 = (bf16[512,512]{1,0:T(8,128)(2,1)S(1)}, f32[2,512]{1,0:T(2,128)S(1)}, f32[512,1024]{1,0:T(8,128)S(1)}, f32[2,1024]{1,0:T(2,128)S(1)}) custom-call(f32[18,1024]{1,0:T(8,128)S(1)} %get-tuple-element.129.refs_0_.scal, f32[4,512]{1,0:T(4,128)S(1)} %pad_maximum_fusion.12.refs_1_, f32[4,512]{1,0:T(4,128)S(1)} %collective-permute-done.53.refs_2_, ...), custom_call_target="tpu_custom_call" | custom-call | tf_op jit(solution)/shard_map/back_down/pallas_call | solution.py:920
  192.2 1.8 share_main.1
  195.6 2.7 collective-permute-start.58
  198.3 1.7 collective-permute-start.59
  201.2 2.9 %collective-permute-done.59.rest_3_ = f32[4,1024]{1,0:T(4,128)S(1)} collective-permute-done((f32[4,1024]{1,0:T(4,128)S(1)}, f32[4,1024]{1,0:T(4,128)S(1)}, u32[]{:S(2)}, u32[]{:S(2)}) %collective-permute-start.59) | collective-permute-done | bytes 16416 | tf_op jit(solution)/shard_map/ppermute | solution.py:76
  204.4 2.3 collective-permute-start.60
  206.7 2.0 collective-permute-start.61
  208.9 2.3 collective-permute-start.65
  211.2 16.0 %collective-permute-done.62.rest_1_ = bf16[512,256]{1,0:T(8,128)(2,1)S(1)} collective-permute-done((bf16[512,256]{1,0:T(8,128)(2,1)S(1)}, bf16[512,256]{1,0:T(8,128)(2,1)S(1)}, u32[]{:S(2)}, u32[]{:S(2)}) %collective-permute-start.62) | collective-permute-done | bytes 262176 | tf_op jit(solution)/shard_map/ppermute | solution.py:76
  227.2 8.2 %collective-permute-start.66 = (bf16[64,1536]{1,0:T(8,128)(2,1)S(1)}, bf16[64,1536]{1,0:T(8,128)(2,1)S(1)}, u32[]{:S(2)}, u32[]{:S(2)}) collective-permute-start(bf16[64,1536]{1,0:T(8,128)(2,1)S(1)} %add_convert_fusion.2.rest_0_), channel_id=1, source_target_pairs={{0,3},{1,2},{2,1},{3,0},{4,7},{5,6},{6,5},{7,4},{8,11},{9,10},{10,... | collective-permute-start | bytes 589832 | tf_op jit(solution)/shard_map/ppermute | solution.py:76
  235.9 6.4 %back_input.1.rest_6_ = f32[2,2,128,512]{3,2,1,0:T(8,128)S(1)} custom-call(bf16[576,1024]{1,0:T(8,128)(2,1)S(1)} %get-tuple-element.193.grad, bf16[9,512,1024]{2,1,0:T(8,128)(2,1)} %bitcast.27), custom_call_target="tpu_custom_call" | custom-call | tf_op jit(solution)/shard_map/back_input/pallas_call | solution.py:1278
  242.3 4.7 %share_down.2 = (f32[1024,1024]{1,0:T(8,128)S(1)}, f32[1024,1024]{1,0:T(8,128)S(1)}) custom-call(bf16[512,256]{1,0:T(8,128)(2,1)S(1)} %cut_down.1.rest_0_, bf16[512,256]{1,0:T(8,128)(2,1)S(1)} %collective-permute-done.62.rest_1_, bf16[32,2,2,64,1024]{4,3,2,1,0:T(8,128)(2,1)} %bitcast.28), custom_call_target="tpu_custom_call" | custom-call | tf_op jit(solution)/shard_map/share_down/pallas_call | solution.py:1319
  247.0 5.1 %share_down.3 = (bf16[4608,128]{1,0:T(8,128)(2,1)S(1)}, bf16[4608,128]{1,0:T(8,128)(2,1)S(1)}) custom-call(bf16[512,256]{1,0:T(8,128)(2,1)S(1)} %collective-permute-done.60.rest_0_, bf16[512,256]{1,0:T(8,128)(2,1)S(1)} %collective-permute-done.61.rest_1_, f32[1024,1024]{1,0:T(8,128)S(1)} %get-tuple-element.201.rest_2_, ...), custom_call_target="tpu_custom_call" | custom-call | tf_op jit(solution)/shard_map/share_down/pallas_call | solution.py:1319
  254.6 3.3 %collective-permute-done.67.rest_5_ = bf16[64,1024]{1,0:T(8,128)(2,1)S(1)} collective-permute-done((bf16[64,1024]{1,0:T(8,128)(2,1)S(1)}, bf16[64,1024]{1,0:T(8,128)(2,1)S(1)}, u32[]{:S(2)}, u32[]{:S(2)}) %collective-permute-start.67) | collective-permute-done | bytes 131104 | tf_op jit(solution)/shard_map/ppermute | solution.py:63
  258.0 3.4 %finish.1 = (f32[1024,128]{1,0:T(8,128)}, f32[64,1024]{1,0:T(8,128)}, f32[64,512]{1,0:T(8,128)}, f32[64,512]{1,0:T(8,128)}, f32[9,64,512]{2,1,0:T(8,128)}, /*ind...) custom-call(bf16[1024,128]{1,0:T(8,128)(2,1)} %get-tuple-element.212.unite, ...), custom_call_target="tpu_custom_call" | custom-call | tf_op jit(solution)/shard_map/finish/pallas_call | solution.py:1345
  261.4 1.6 convert_add_fusion
  (194 shorter events, 56.5 us)
Async XLA Ops:
  7.2 157.0 %all-gather.2.cloned.1.call-start = ((), (), s32[]{:S(2)}) async-start(), calls=%async_computation | async-start | bytes 17301504 | tf_op jit(solution)/shard_map/all_gather | solution.py:1025
  8.5 6.5 %collective-permute-start = (bf16[2,64,1024]{2,1,0:T(8,128)(2,1)S(1)}, bf16[2,64,1024]{2,1,0:T(8,128)(2,1)S(1)}, u32[]{:S(2)}, u32[]{:S(2)}) collective-permute-start(bf16[2,64,1024]{2,1,0:T(8,128)(2,1)S(1)} %slice_bitcast_fusion), channel_id=1, source_target_pairs={{0,4},{4,8},{8,12},{12,16},{16,20},{20,24},{24,28},{1,5},{5,9},{9,... | collective-permute-start | bytes 786440 | tf_op jit(solution)/shard_map/ppermute | solution.py:999
  18.2 3.6 %collective-permute-start.1 = (bf16[64,1024]{1,0:T(8,128)(2,1)S(1)}, bf16[64,1024]{1,0:T(8,128)(2,1)S(1)}, u32[]{:S(2)}, u32[]{:S(2)}) collective-permute-start(bf16[64,1024]{1,0:T(8,128)(2,1)S(1)} %get-tuple-element.249), channel_id=1, source_target_pairs={{0,4},{4,0},{8,12},{12,8},{16,20},{20,16},{24,28},{28,24},{1,5},{5... | collective-permute-start | bytes 393224 | tf_op jit(solution)/shard_map/ppermute | solution.py:63
  21.8 9.2 %collective-permute-start.2 = (bf16[128,1024]{1,0:T(8,128)(2,1)S(1)}, bf16[128,1024]{1,0:T(8,128)(2,1)S(1)}, u32[]{:S(2)}, u32[]{:S(2)}) collective-permute-start(bf16[128,1024]{1,0:T(8,128)(2,1)S(1)} %pad_maximum_fusion.rest_0_), channel_id=1, source_target_pairs={{0,8},{4,12},{8,0},{12,4},{16,24},{20,28},{24,16},{28,20},{1,9},{5... | collective-permute-start | bytes 786440 | tf_op jit(solution)/shard_map/ppermute | solution.py:67
  23.8 12.7 %collective-permute-start.3 = (bf16[128,1024]{1,0:T(8,128)(2,1)S(1)}, bf16[128,1024]{1,0:T(8,128)(2,1)S(1)}, u32[]{:S(2)}, u32[]{:S(2)}) collective-permute-start(bf16[128,1024]{1,0:T(8,128)(2,1)S(1)} %pad_maximum_fusion.rest_0_), channel_id=1, source_target_pairs={{0,16},{4,20},{8,24},{12,28},{16,0},{20,4},{24,8},{28,12},{1,17},{... | collective-permute-start | bytes 786440 | tf_op jit(solution)/shard_map/ppermute | solution.py:67
  25.3 12.8 %collective-permute-start.4 = (bf16[128,1024]{1,0:T(8,128)(2,1)S(1)}, bf16[128,1024]{1,0:T(8,128)(2,1)S(1)}, u32[]{:S(2)}, u32[]{:S(2)}) collective-permute-start(bf16[128,1024]{1,0:T(8,128)(2,1)S(1)} %pad_maximum_fusion.rest_0_), channel_id=1, source_target_pairs={{0,24},{4,28},{8,16},{12,20},{16,8},{20,12},{24,0},{28,4},{1,25},{... | collective-permute-start | bytes 786440 | tf_op jit(solution)/shard_map/ppermute | solution.py:67
  40.6 212.7 %all-reduce.5.cloned.1.call-start = ((), (), s32[]{:S(2)}) async-start(), calls=%async_computation.1 | async-start | bytes 2097152 | tf_op jit(solution)/shard_map/psum | solution.py:1228
  40.9 1.4 collective-permute-start.9
  42.3 16.3 %collective-permute-start.10 = (bf16[128,1024]{1,0:T(8,128)(2,1)S(1)}, bf16[128,1024]{1,0:T(8,128)(2,1)S(1)}, u32[]{:S(2)}, u32[]{:S(2)}) collective-permute-start(bf16[128,1024]{1,0:T(8,128)(2,1)S(1)} %constant_dynamic-update-slice_fusion.refs_7_), channel_id=1, source_target_pairs={{0,8},{4,12},{8,0},{12,4},{16,24},{20,28},{24,16},{28,20},{1,9},{5... | collective-permute-start | bytes 786440 | tf_op jit(solution)/shard_map/ppermute | solution.py:72
  43.0 15.7 %collective-permute-start.11 = (bf16[128,1024]{1,0:T(8,128)(2,1)S(1)}, bf16[128,1024]{1,0:T(8,128)(2,1)S(1)}, u32[]{:S(2)}, u32[]{:S(2)}) collective-permute-start(bf16[128,1024]{1,0:T(8,128)(2,1)S(1)} %constant_dynamic-update-slice_fusion.refs_7_), channel_id=1, source_target_pairs={{0,16},{4,20},{8,24},{12,28},{16,0},{20,4},{24,8},{28,12},{1,17},{... | collective-permute-start | bytes 786440 | tf_op jit(solution)/shard_map/ppermute | solution.py:72
  45.9 4.5 %collective-permute-start.6 = (f32[4,1024]{1,0:T(4,128)S(1)}, f32[4,1024]{1,0:T(4,128)S(1)}, u32[]{:S(2)}, u32[]{:S(2)}) collective-permute-start(f32[4,1024]{1,0:T(4,128)S(1)} %pad_maximum_fusion.3.refs_1_), channel_id=1, source_target_pairs={{0,1},{1,0},{2,3},{3,2},{4,5},{5,4},{6,7},{7,6},{8,9},{9,8},{10,11... | collective-permute-start | bytes 49160 | tf_op jit(solution)/shard_map/ppermute | solution.py:76
  47.5 4.7 %collective-permute-start.7 = (f32[4,1024]{1,0:T(4,128)S(1)}, f32[4,1024]{1,0:T(4,128)S(1)}, u32[]{:S(2)}, u32[]{:S(2)}) collective-permute-start(f32[4,1024]{1,0:T(4,128)S(1)} %pad_maximum_fusion.3.refs_1_), channel_id=1, source_target_pairs={{0,2},{1,3},{2,0},{3,1},{4,6},{5,7},{6,4},{7,5},{8,10},{9,11},{10,... | collective-permute-start | bytes 49160 | tf_op jit(solution)/shard_map/ppermute | solution.py:76
  50.1 5.6 %collective-permute-start.8 = (f32[4,1024]{1,0:T(4,128)S(1)}, f32[4,1024]{1,0:T(4,128)S(1)}, u32[]{:S(2)}, u32[]{:S(2)}) collective-permute-start(f32[4,1024]{1,0:T(4,128)S(1)} %pad_maximum_fusion.3.refs_1_), channel_id=1, source_target_pairs={{0,3},{1,2},{2,1},{3,0},{4,7},{5,6},{6,5},{7,4},{8,11},{9,10},{10,... | collective-permute-start | bytes 49160 | tf_op jit(solution)/shard_map/ppermute | solution.py:76
  59.9 4.5 %collective-permute-start.13 = (f32[4,512]{1,0:T(4,128)S(1)}, f32[4,512]{1,0:T(4,128)S(1)}, u32[]{:S(2)}, u32[]{:S(2)}) collective-permute-start(f32[4,512]{1,0:T(4,128)S(1)} %pad_maximum_fusion.7.refs_1_), channel_id=1, source_target_pairs={{0,1},{1,0},{2,3},{3,2},{4,5},{5,4},{6,7},{7,6},{8,9},{9,8},{10,11... | collective-permute-start | bytes 24584 | tf_op jit(solution)/shard_map/ppermute | solution.py:76
  60.0 4.7 %collective-permute-start.14 = (f32[4,512]{1,0:T(4,128)S(1)}, f32[4,512]{1,0:T(4,128)S(1)}, u32[]{:S(2)}, u32[]{:S(2)}) collective-permute-start(f32[4,512]{1,0:T(4,128)S(1)} %pad_maximum_fusion.7.refs_1_), channel_id=1, source_target_pairs={{0,2},{1,3},{2,0},{3,1},{4,6},{5,7},{6,4},{7,5},{8,10},{9,11},{10,... | collective-permute-start | bytes 24584 | tf_op jit(solution)/shard_map/ppermute | solution.py:76
  61.2 5.5 %collective-permute-start.15 = (f32[4,512]{1,0:T(4,128)S(1)}, f32[4,512]{1,0:T(4,128)S(1)}, u32[]{:S(2)}, u32[]{:S(2)}) collective-permute-start(f32[4,512]{1,0:T(4,128)S(1)} %pad_maximum_fusion.7.refs_1_), channel_id=1, source_target_pairs={{0,3},{1,2},{2,1},{3,0},{4,7},{5,6},{6,5},{7,4},{8,11},{9,10},{10,... | collective-permute-start | bytes 24584 | tf_op jit(solution)/shard_map/ppermute | solution.py:76
  68.5 15.7 %collective-permute-start.20 = (bf16[128,1024]{1,0:T(8,128)(2,1)S(1)}, bf16[128,1024]{1,0:T(8,128)(2,1)S(1)}, u32[]{:S(2)}, u32[]{:S(2)}) collective-permute-start(bf16[128,1024]{1,0:T(8,128)(2,1)S(1)} %collective-permute-done.10.refs_8_), channel_id=1, source_target_pairs={{0,16},{4,20},{8,24},{12,28},{16,0},{20,4},{24,8},{28,12},{1,17},{... | collective-permute-start | bytes 786440 | tf_op jit(solution)/shard_map/ppermute | solution.py:72
  69.7 6.6 %collective-permute-start.17 = (f32[4,512]{1,0:T(4,128)S(1)}, f32[4,512]{1,0:T(4,128)S(1)}, u32[]{:S(2)}, u32[]{:S(2)}) collective-permute-start(f32[4,512]{1,0:T(4,128)S(1)} %pad_maximum_fusion.8.refs_1_), channel_id=1, source_target_pairs={{0,1},{1,0},{2,3},{3,2},{4,5},{5,4},{6,7},{7,6},{8,9},{9,8},{10,11... | collective-permute-start | bytes 24584 | tf_op jit(solution)/shard_map/ppermute | solution.py:76
  69.8 6.6 %collective-permute-start.18 = (f32[4,512]{1,0:T(4,128)S(1)}, f32[4,512]{1,0:T(4,128)S(1)}, u32[]{:S(2)}, u32[]{:S(2)}) collective-permute-start(f32[4,512]{1,0:T(4,128)S(1)} %pad_maximum_fusion.8.refs_1_), channel_id=1, source_target_pairs={{0,2},{1,3},{2,0},{3,1},{4,6},{5,7},{6,4},{7,5},{8,10},{9,11},{10,... | collective-permute-start | bytes 24584 | tf_op jit(solution)/shard_map/ppermute | solution.py:76
  73.4 5.6 %collective-permute-start.19 = (f32[4,512]{1,0:T(4,128)S(1)}, f32[4,512]{1,0:T(4,128)S(1)}, u32[]{:S(2)}, u32[]{:S(2)}) collective-permute-start(f32[4,512]{1,0:T(4,128)S(1)} %pad_maximum_fusion.8.refs_1_), channel_id=1, source_target_pairs={{0,3},{1,2},{2,1},{3,0},{4,7},{5,6},{6,5},{7,4},{8,11},{9,10},{10,... | collective-permute-start | bytes 24584 | tf_op jit(solution)/shard_map/ppermute | solution.py:76
  84.3 1.2 collective-permute-start.21
  85.5 5.9 %collective-permute-start.24 = (f32[4,1024]{1,0:T(4,128)S(1)}, f32[4,1024]{1,0:T(4,128)S(1)}, u32[]{:S(2)}, u32[]{:S(2)}) collective-permute-start(f32[4,1024]{1,0:T(4,128)S(1)} %pad_maximum_fusion.1), channel_id=1, source_target_pairs={{0,3},{1,2},{2,1},{3,0},{4,7},{5,6},{6,5},{7,4},{8,11},{9,10},{10,... | collective-permute-start | bytes 49160 | tf_op jit(solution)/shard_map/ppermute | solution.py:76
  86.3 5.1 %collective-permute-start.23 = (f32[4,1024]{1,0:T(4,128)S(1)}, f32[4,1024]{1,0:T(4,128)S(1)}, u32[]{:S(2)}, u32[]{:S(2)}) collective-permute-start(f32[4,1024]{1,0:T(4,128)S(1)} %pad_maximum_fusion.1), channel_id=1, source_target_pairs={{0,2},{1,3},{2,0},{3,1},{4,6},{5,7},{6,4},{7,5},{8,10},{9,11},{10,... | collective-permute-start | bytes 49160 | tf_op jit(solution)/shard_map/ppermute | solution.py:76
  86.3 6.3 %collective-permute-start.22 = (f32[4,1024]{1,0:T(4,128)S(1)}, f32[4,1024]{1,0:T(4,128)S(1)}, u32[]{:S(2)}, u32[]{:S(2)}) collective-permute-start(f32[4,1024]{1,0:T(4,128)S(1)} %pad_maximum_fusion.1), channel_id=1, source_target_pairs={{0,1},{1,0},{2,3},{3,2},{4,5},{5,4},{6,7},{7,6},{8,9},{9,8},{10,11... | collective-permute-start | bytes 49160 | tf_op jit(solution)/shard_map/ppermute | solution.py:76
  95.6 6.4 %collective-permute-start.26 = (f32[4,512]{1,0:T(4,128)S(1)}, f32[4,512]{1,0:T(4,128)S(1)}, u32[]{:S(2)}, u32[]{:S(2)}) collective-permute-start(f32[4,512]{1,0:T(4,128)S(1)} %pad_maximum_fusion.9.refs_1_), channel_id=1, source_target_pairs={{0,1},{1,0},{2,3},{3,2},{4,5},{5,4},{6,7},{7,6},{8,9},{9,8},{10,11... | collective-permute-start | bytes 24584 | tf_op jit(solution)/shard_map/ppermute | solution.py:76
  97.1 4.9 %collective-permute-start.27 = (f32[4,512]{1,0:T(4,128)S(1)}, f32[4,512]{1,0:T(4,128)S(1)}, u32[]{:S(2)}, u32[]{:S(2)}) collective-permute-start(f32[4,512]{1,0:T(4,128)S(1)} %pad_maximum_fusion.9.refs_1_), channel_id=1, source_target_pairs={{0,2},{1,3},{2,0},{3,1},{4,6},{5,7},{6,4},{7,5},{8,10},{9,11},{10,... | collective-permute-start | bytes 24584 | tf_op jit(solution)/shard_map/ppermute | solution.py:76
  98.3 5.4 %collective-permute-start.28 = (f32[4,512]{1,0:T(4,128)S(1)}, f32[4,512]{1,0:T(4,128)S(1)}, u32[]{:S(2)}, u32[]{:S(2)}) collective-permute-start(f32[4,512]{1,0:T(4,128)S(1)} %pad_maximum_fusion.9.refs_1_), channel_id=1, source_target_pairs={{0,3},{1,2},{2,1},{3,0},{4,7},{5,6},{6,5},{7,4},{8,11},{9,10},{10,... | collective-permute-start | bytes 24584 | tf_op jit(solution)/shard_map/ppermute | solution.py:76
  106.3 1.2 collective-permute-start.29
  107.5 5.0 %collective-permute-start.30 = (f32[4,1024]{1,0:T(4,128)S(1)}, f32[4,1024]{1,0:T(4,128)S(1)}, u32[]{:S(2)}, u32[]{:S(2)}) collective-permute-start(f32[4,1024]{1,0:T(4,128)S(1)} %pad_maximum_fusion.4.refs_1_), channel_id=1, source_target_pairs={{0,1},{1,0},{2,3},{3,2},{4,5},{5,4},{6,7},{7,6},{8,9},{9,8},{10,11... | collective-permute-start | bytes 49160 | tf_op jit(solution)/shard_map/ppermute | solution.py:76
  107.6 7.3 %collective-permute-start.31 = (f32[4,1024]{1,0:T(4,128)S(1)}, f32[4,1024]{1,0:T(4,128)S(1)}, u32[]{:S(2)}, u32[]{:S(2)}) collective-permute-start(f32[4,1024]{1,0:T(4,128)S(1)} %pad_maximum_fusion.4.refs_1_), channel_id=1, source_target_pairs={{0,2},{1,3},{2,0},{3,1},{4,6},{5,7},{6,4},{7,5},{8,10},{9,11},{10,... | collective-permute-start | bytes 49160 | tf_op jit(solution)/shard_map/ppermute | solution.py:76
  109.6 5.9 %collective-permute-start.32 = (f32[4,1024]{1,0:T(4,128)S(1)}, f32[4,1024]{1,0:T(4,128)S(1)}, u32[]{:S(2)}, u32[]{:S(2)}) collective-permute-start(f32[4,1024]{1,0:T(4,128)S(1)} %pad_maximum_fusion.4.refs_1_), channel_id=1, source_target_pairs={{0,3},{1,2},{2,1},{3,0},{4,7},{5,6},{6,5},{7,4},{8,11},{9,10},{10,... | collective-permute-start | bytes 49160 | tf_op jit(solution)/shard_map/ppermute | solution.py:76
  119.8 5.2 %collective-permute-start.34 = (f32[4,1024]{1,0:T(4,128)S(1)}, f32[4,1024]{1,0:T(4,128)S(1)}, u32[]{:S(2)}, u32[]{:S(2)}) collective-permute-start(f32[4,1024]{1,0:T(4,128)S(1)} %pad_maximum_fusion.5.refs_1_), channel_id=1, source_target_pairs={{0,1},{1,0},{2,3},{3,2},{4,5},{5,4},{6,7},{7,6},{8,9},{9,8},{10,11... | collective-permute-start | bytes 49160 | tf_op jit(solution)/shard_map/ppermute | solution.py:76
  120.6 6.8 %collective-permute-start.35 = (f32[4,1024]{1,0:T(4,128)S(1)}, f32[4,1024]{1,0:T(4,128)S(1)}, u32[]{:S(2)}, u32[]{:S(2)}) collective-permute-start(f32[4,1024]{1,0:T(4,128)S(1)} %pad_maximum_fusion.5.refs_1_), channel_id=1, source_target_pairs={{0,2},{1,3},{2,0},{3,1},{4,6},{5,7},{6,4},{7,5},{8,10},{9,11},{10,... | collective-permute-start | bytes 49160 | tf_op jit(solution)/shard_map/ppermute | solution.py:76
  122.8 5.9 %collective-permute-start.36 = (f32[4,1024]{1,0:T(4,128)S(1)}, f32[4,1024]{1,0:T(4,128)S(1)}, u32[]{:S(2)}, u32[]{:S(2)}) collective-permute-start(f32[4,1024]{1,0:T(4,128)S(1)} %pad_maximum_fusion.5.refs_1_), channel_id=1, source_target_pairs={{0,3},{1,2},{2,1},{3,0},{4,7},{5,6},{6,5},{7,4},{8,11},{9,10},{10,... | collective-permute-start | bytes 49160 | tf_op jit(solution)/shard_map/ppermute | solution.py:76
  132.9 7.4 %collective-permute-start.38 = (f32[4,512]{1,0:T(4,128)S(1)}, f32[4,512]{1,0:T(4,128)S(1)}, u32[]{:S(2)}, u32[]{:S(2)}) collective-permute-start(f32[4,512]{1,0:T(4,128)S(1)} %pad_maximum_fusion.10.refs_1_), channel_id=1, source_target_pairs={{0,1},{1,0},{2,3},{3,2},{4,5},{5,4},{6,7},{7,6},{8,9},{9,8},{10,11... | collective-permute-start | bytes 24584 | tf_op jit(solution)/shard_map/ppermute | solution.py:76
  133.0 7.4 %collective-permute-start.39 = (f32[4,512]{1,0:T(4,128)S(1)}, f32[4,512]{1,0:T(4,128)S(1)}, u32[]{:S(2)}, u32[]{:S(2)}) collective-permute-start(f32[4,512]{1,0:T(4,128)S(1)} %pad_maximum_fusion.10.refs_1_), channel_id=1, source_target_pairs={{0,2},{1,3},{2,0},{3,1},{4,6},{5,7},{6,4},{7,5},{8,10},{9,11},{10,... | collective-permute-start | bytes 24584 | tf_op jit(solution)/shard_map/ppermute | solution.py:76
  134.9 5.6 %collective-permute-start.40 = (f32[4,512]{1,0:T(4,128)S(1)}, f32[4,512]{1,0:T(4,128)S(1)}, u32[]{:S(2)}, u32[]{:S(2)}) collective-permute-start(f32[4,512]{1,0:T(4,128)S(1)} %pad_maximum_fusion.10.refs_1_), channel_id=1, source_target_pairs={{0,3},{1,2},{2,1},{3,0},{4,7},{5,6},{6,5},{7,4},{8,11},{9,10},{10,... | collective-permute-start | bytes 24584 | tf_op jit(solution)/shard_map/ppermute | solution.py:76
  143.8 18.1 %collective-permute-start.46 = (bf16[1024,128]{1,0:T(8,128)(2,1)S(1)}, bf16[1024,128]{1,0:T(8,128)(2,1)S(1)}, u32[]{:S(2)}, u32[]{:S(2)}) collective-permute-start(bf16[1024,128]{1,0:T(8,128)(2,1)S(1)} %get-tuple-element.171), channel_id=1, source_target_pairs={{0,4},{4,0},{8,12},{12,8},{16,20},{20,16},{24,28},{28,24},{1,5},{5... | collective-permute-start | bytes 786440 | tf_op jit(solution)/shard_map/ppermute | solution.py:63
  144.5 6.0 %collective-permute-start.44 = (f32[4,1024]{1,0:T(4,128)S(1)}, f32[4,1024]{1,0:T(4,128)S(1)}, u32[]{:S(2)}, u32[]{:S(2)}) collective-permute-start(f32[4,1024]{1,0:T(4,128)S(1)} %pad_maximum_fusion.2), channel_id=1, source_target_pairs={{0,3},{1,2},{2,1},{3,0},{4,7},{5,6},{6,5},{7,4},{8,11},{9,10},{10,... | collective-permute-start | bytes 49160 | tf_op jit(solution)/shard_map/ppermute | solution.py:76
  146.9 5.0 %collective-permute-start.43 = (f32[4,1024]{1,0:T(4,128)S(1)}, f32[4,1024]{1,0:T(4,128)S(1)}, u32[]{:S(2)}, u32[]{:S(2)}) collective-permute-start(f32[4,1024]{1,0:T(4,128)S(1)} %pad_maximum_fusion.2), channel_id=1, source_target_pairs={{0,2},{1,3},{2,0},{3,1},{4,6},{5,7},{6,4},{7,5},{8,10},{9,11},{10,... | collective-permute-start | bytes 49160 | tf_op jit(solution)/shard_map/ppermute | solution.py:76
  146.9 5.5 %collective-permute-start.42 = (f32[4,1024]{1,0:T(4,128)S(1)}, f32[4,1024]{1,0:T(4,128)S(1)}, u32[]{:S(2)}, u32[]{:S(2)}) collective-permute-start(f32[4,1024]{1,0:T(4,128)S(1)} %pad_maximum_fusion.2), channel_id=1, source_target_pairs={{0,1},{1,0},{2,3},{3,2},{4,5},{5,4},{6,7},{7,6},{8,9},{9,8},{10,11... | collective-permute-start | bytes 49160 | tf_op jit(solution)/shard_map/ppermute | solution.py:76
  153.6 7.6 %collective-permute-start.47 = (bf16[64,1536]{1,0:T(8,128)(2,1)S(1)}, bf16[64,1536]{1,0:T(8,128)(2,1)S(1)}, u32[]{:S(2)}, u32[]{:S(2)}) collective-permute-start(bf16[64,1536]{1,0:T(8,128)(2,1)S(1)} %get-tuple-element.177), channel_id=1, source_target_pairs={{0,4},{4,0},{8,12},{12,8},{16,20},{20,16},{24,28},{28,24},{1,5},{5... | collective-permute-start | bytes 589832 | tf_op jit(solution)/shard_map/ppermute | solution.py:63
  159.5 1.7 collective-permute-start.45
  161.1 2.1 collective-permute-start.48
  164.2 4.5 %collective-permute-start.49 = (f32[4,512]{1,0:T(4,128)S(1)}, f32[4,512]{1,0:T(4,128)S(1)}, u32[]{:S(2)}, u32[]{:S(2)}) collective-permute-start(f32[4,512]{1,0:T(4,128)S(1)} %pad_maximum_fusion.11.refs_1_), channel_id=1, source_target_pairs={{0,1},{1,0},{2,3},{3,2},{4,5},{5,4},{6,7},{7,6},{8,9},{9,8},{10,11... | collective-permute-start | bytes 24584 | tf_op jit(solution)/shard_map/ppermute | solution.py:76
  164.9 4.5 %collective-permute-start.50 = (f32[4,512]{1,0:T(4,128)S(1)}, f32[4,512]{1,0:T(4,128)S(1)}, u32[]{:S(2)}, u32[]{:S(2)}) collective-permute-start(f32[4,512]{1,0:T(4,128)S(1)} %pad_maximum_fusion.11.refs_1_), channel_id=1, source_target_pairs={{0,2},{1,3},{2,0},{3,1},{4,6},{5,7},{6,4},{7,5},{8,10},{9,11},{10,... | collective-permute-start | bytes 24584 | tf_op jit(solution)/shard_map/ppermute | solution.py:76
  167.0 5.6 %collective-permute-start.51 = (f32[4,512]{1,0:T(4,128)S(1)}, f32[4,512]{1,0:T(4,128)S(1)}, u32[]{:S(2)}, u32[]{:S(2)}) collective-permute-start(f32[4,512]{1,0:T(4,128)S(1)} %pad_maximum_fusion.11.refs_1_), channel_id=1, source_target_pairs={{0,3},{1,2},{2,1},{3,0},{4,7},{5,6},{6,5},{7,4},{8,11},{9,10},{10,... | collective-permute-start | bytes 24584 | tf_op jit(solution)/shard_map/ppermute | solution.py:76
  178.7 4.5 %collective-permute-start.53 = (f32[4,512]{1,0:T(4,128)S(1)}, f32[4,512]{1,0:T(4,128)S(1)}, u32[]{:S(2)}, u32[]{:S(2)}) collective-permute-start(f32[4,512]{1,0:T(4,128)S(1)} %pad_maximum_fusion.12.refs_1_), channel_id=1, source_target_pairs={{0,1},{1,0},{2,3},{3,2},{4,5},{5,4},{6,7},{7,6},{8,9},{9,8},{10,11... | collective-permute-start | bytes 24584 | tf_op jit(solution)/shard_map/ppermute | solution.py:76
  178.8 5.0 %collective-permute-start.54 = (f32[4,512]{1,0:T(4,128)S(1)}, f32[4,512]{1,0:T(4,128)S(1)}, u32[]{:S(2)}, u32[]{:S(2)}) collective-permute-start(f32[4,512]{1,0:T(4,128)S(1)} %pad_maximum_fusion.12.refs_1_), channel_id=1, source_target_pairs={{0,2},{1,3},{2,0},{3,1},{4,6},{5,7},{6,4},{7,5},{8,10},{9,11},{10,... | collective-permute-start | bytes 24584 | tf_op jit(solution)/shard_map/ppermute | solution.py:76
  181.0 5.9 %collective-permute-start.55 = (f32[4,512]{1,0:T(4,128)S(1)}, f32[4,512]{1,0:T(4,128)S(1)}, u32[]{:S(2)}, u32[]{:S(2)}) collective-permute-start(f32[4,512]{1,0:T(4,128)S(1)} %pad_maximum_fusion.12.refs_1_), channel_id=1, source_target_pairs={{0,3},{1,2},{2,1},{3,0},{4,7},{5,6},{6,5},{7,4},{8,11},{9,10},{10,... | collective-permute-start | bytes 24584 | tf_op jit(solution)/shard_map/ppermute | solution.py:76
  194.0 14.8 %collective-permute-start.63 = (bf16[64,1536]{1,0:T(8,128)(2,1)S(1)}, bf16[64,1536]{1,0:T(8,128)(2,1)S(1)}, u32[]{:S(2)}, u32[]{:S(2)}) collective-permute-start(bf16[64,1536]{1,0:T(8,128)(2,1)S(1)} %get-tuple-element.210), channel_id=1, source_target_pairs={{0,4},{4,0},{8,12},{12,8},{16,20},{20,16},{24,28},{28,24},{1,5},{5... | collective-permute-start | bytes 589832 | tf_op jit(solution)/shard_map/ppermute | solution.py:63
  194.0 1.4 collective-permute-start.56
  195.5 4.5 %collective-permute-start.57 = (f32[4,1024]{1,0:T(4,128)S(1)}, f32[4,1024]{1,0:T(4,128)S(1)}, u32[]{:S(2)}, u32[]{:S(2)}) collective-permute-start(f32[4,1024]{1,0:T(4,128)S(1)} %pad_maximum_fusion.6.rest_0_), channel_id=1, source_target_pairs={{0,1},{1,0},{2,3},{3,2},{4,5},{5,4},{6,7},{7,6},{8,9},{9,8},{10,11... | collective-permute-start | bytes 49160 | tf_op jit(solution)/shard_map/ppermute | solution.py:76
  195.6 5.6 %collective-permute-start.58 = (f32[4,1024]{1,0:T(4,128)S(1)}, f32[4,1024]{1,0:T(4,128)S(1)}, u32[]{:S(2)}, u32[]{:S(2)}) collective-permute-start(f32[4,1024]{1,0:T(4,128)S(1)} %pad_maximum_fusion.6.rest_0_), channel_id=1, source_target_pairs={{0,2},{1,3},{2,0},{3,1},{4,6},{5,7},{6,4},{7,5},{8,10},{9,11},{10,... | collective-permute-start | bytes 49160 | tf_op jit(solution)/shard_map/ppermute | solution.py:76
  198.3 5.9 %collective-permute-start.59 = (f32[4,1024]{1,0:T(4,128)S(1)}, f32[4,1024]{1,0:T(4,128)S(1)}, u32[]{:S(2)}, u32[]{:S(2)}) collective-permute-start(f32[4,1024]{1,0:T(4,128)S(1)} %pad_maximum_fusion.6.rest_0_), channel_id=1, source_target_pairs={{0,3},{1,2},{2,1},{3,0},{4,7},{5,6},{6,5},{7,4},{8,11},{9,10},{10,... | collective-permute-start | bytes 49160 | tf_op jit(solution)/shard_map/ppermute | solution.py:76
  204.3 22.9 %collective-permute-start.62 = (bf16[512,256]{1,0:T(8,128)(2,1)S(1)}, bf16[512,256]{1,0:T(8,128)(2,1)S(1)}, u32[]{:S(2)}, u32[]{:S(2)}) collective-permute-start(bf16[512,256]{1,0:T(8,128)(2,1)S(1)} %cut_down.1.rest_0_), channel_id=1, source_target_pairs={{0,1},{1,0},{2,3},{3,2},{4,5},{5,4},{6,7},{7,6},{8,9},{9,8},{10,11... | collective-permute-start | bytes 786440 | tf_op jit(solution)/shard_map/ppermute | solution.py:76
  204.4 42.6 %collective-permute-start.60 = (bf16[512,256]{1,0:T(8,128)(2,1)S(1)}, bf16[512,256]{1,0:T(8,128)(2,1)S(1)}, u32[]{:S(2)}, u32[]{:S(2)}) collective-permute-start(bf16[512,256]{1,0:T(8,128)(2,1)S(1)} %cut_down.1.rest_0_), channel_id=1, source_target_pairs={{0,2},{1,3},{2,0},{3,1},{4,6},{5,7},{6,4},{7,5},{8,10},{9,11},{10,... | collective-permute-start | bytes 786440 | tf_op jit(solution)/shard_map/ppermute | solution.py:76
  206.7 40.3 %collective-permute-start.61 = (bf16[512,256]{1,0:T(8,128)(2,1)S(1)}, bf16[512,256]{1,0:T(8,128)(2,1)S(1)}, u32[]{:S(2)}, u32[]{:S(2)}) collective-permute-start(bf16[512,256]{1,0:T(8,128)(2,1)S(1)} %cut_down.1.rest_0_), channel_id=1, source_target_pairs={{0,3},{1,2},{2,1},{3,0},{4,7},{5,6},{6,5},{7,4},{8,11},{9,10},{10,... | collective-permute-start | bytes 786440 | tf_op jit(solution)/shard_map/ppermute | solution.py:76
  208.8 43.3 %collective-permute-start.64 = (bf16[64,1536]{1,0:T(8,128)(2,1)S(1)}, bf16[64,1536]{1,0:T(8,128)(2,1)S(1)}, u32[]{:S(2)}, u32[]{:S(2)}) collective-permute-start(bf16[64,1536]{1,0:T(8,128)(2,1)S(1)} %add_convert_fusion.2.rest_0_), channel_id=1, source_target_pairs={{0,1},{1,0},{2,3},{3,2},{4,5},{5,4},{6,7},{7,6},{8,9},{9,8},{10,11... | collective-permute-start | bytes 589832 | tf_op jit(solution)/shard_map/ppermute | solution.py:76
  208.9 44.5 %collective-permute-start.65 = (bf16[64,1536]{1,0:T(8,128)(2,1)S(1)}, bf16[64,1536]{1,0:T(8,128)(2,1)S(1)}, u32[]{:S(2)}, u32[]{:S(2)}) collective-permute-start(bf16[64,1536]{1,0:T(8,128)(2,1)S(1)} %add_convert_fusion.2.rest_0_), channel_id=1, source_target_pairs={{0,2},{1,3},{2,0},{3,1},{4,6},{5,7},{6,4},{7,5},{8,10},{9,11},{10,... | collective-permute-start | bytes 589832 | tf_op jit(solution)/shard_map/ppermute | solution.py:76
  227.2 26.2 %collective-permute-start.66 = (bf16[64,1536]{1,0:T(8,128)(2,1)S(1)}, bf16[64,1536]{1,0:T(8,128)(2,1)S(1)}, u32[]{:S(2)}, u32[]{:S(2)}) collective-permute-start(bf16[64,1536]{1,0:T(8,128)(2,1)S(1)} %add_convert_fusion.2.rest_0_), channel_id=1, source_target_pairs={{0,3},{1,2},{2,1},{3,0},{4,7},{5,6},{6,5},{7,4},{8,11},{9,10},{10,... | collective-permute-start | bytes 589832 | tf_op jit(solution)/shard_map/ppermute | solution.py:76
  253.4 8.0 %collective-permute-start.69 = (bf16[4608,128]{1,0:T(8,128)(2,1)}, bf16[4608,128]{1,0:T(8,128)(2,1)S(1)}, u32[]{:S(2)}, u32[]{:S(2)}) collective-permute-start(bf16[4608,128]{1,0:T(8,128)(2,1)} %copy-done.10), channel_id=1, source_target_pairs={{0,4},{4,0},{8,12},{12,8},{16,20},{20,16},{24,28},{28,24},{1,5},{5... | collective-permute-start | bytes 3538952 | tf_op jit(solution)/shard_map/ppermute | solution.py:63
  253.4 4.5 %collective-permute-start.68 = (f32[2,2,128,512]{3,2,1,0:T(8,128)S(1)}, f32[2,2,128,512]{3,2,1,0:T(8,128)S(1)}, u32[]{:S(2)}, u32[]{:S(2)}) collective-permute-start(f32[2,2,128,512]{3,2,1,0:T(8,128)S(1)} %back_input.1.rest_6_), channel_id=1, source_target_pairs={{0,4},{4,0},{8,12},{12,8},{16,20},{20,16},{24,28},{28,24},{1,5},{5... | collective-permute-start | bytes 3145736 | tf_op jit(solution)/shard_map/ppermute | solution.py:63
  253.9 4.0 %collective-permute-start.67 = (bf16[64,1024]{1,0:T(8,128)(2,1)S(1)}, bf16[64,1024]{1,0:T(8,128)(2,1)S(1)}, u32[]{:S(2)}, u32[]{:S(2)}) collective-permute-start(bf16[64,1024]{1,0:T(8,128)(2,1)S(1)} %copy-done.12), channel_id=1, source_target_pairs={{0,4},{4,0},{8,12},{12,8},{16,20},{20,16},{24,28},{28,24},{1,5},{5... | collective-permute-start | bytes 393224 | tf_op jit(solution)/shard_map/ppermute | solution.py:63
  (30 other events, 424.2 us)
Sparse Core Ops, SparseCore 0:
  40.8 118.6 all-gather.1
  164.3 64.0 all-reduce.4
